TPU v7x, 32 devices: a whole 2x2x4 slice. The times are simulated.
32 devices in a mesh: ctx: 16 (over z, y, core), tp: 2 (over x).
Axes of the slice: x: 2, y: 2, z: 4, core: 2. Of those that a mesh axis runs over, the one named last changes fastest.
Arguments:
- hidden_in: bfloat16 [2048, 1024], P('ctx'), may hold values from -6 to 6
- cotangent: bfloat16 [2048, 1024], P('ctx'), may hold values from -6 to 6
- gain_attn: float32 [1024], replicated, may hold values from 0.5 to 1.5
- gain_mlp: float32 [1024], replicated, may hold values from 0.5 to 1.5
- w_qkv: bfloat16 [1024, 3, 1024], P(None, None, 'tp'), may hold values from -0.25 to 0.25
- w_attn_out: bfloat16 [1024, 1024], P('tp'), may hold values from -1 to 1
- w_in: bfloat16 [1024, 2, 2624], P(None, None, 'tp'), may hold values from -0.1875 to 0.1875
- w_mlp_out: bfloat16 [2624, 1024], P('tp'), may hold values from -0.125 to 0.125
Outputs:
- output: bfloat16 [2048, 1024], P('ctx')
- grad_input: float32 [2048, 1024], P('ctx')
- grad_gain_attn: float32 [1024], P('ctx')
- grad_gain_mlp: float32 [1024], P('ctx')
- grad_w_qkv: float32 [1024, 3, 1024], P('ctx', None, 'tp')
- grad_w_attn_out: float32 [1024, 1024], P('tp', 'ctx')
- grad_w_in: float32 [1024, 2, 2624], P('ctx', None, 'tp')
- grad_w_mlp_out: float32 [2624, 1024], P('tp', 'ctx')
All inputs are finite; a program needn't handle non-finite values.
Results may differ from a plain program's by a relative error of at most 0.023.
The roundings to bfloat16 on the way count: a program that leaves them out, or rounds other values in their place, can miss the bound.
Values may be sent and summed in bfloat16 or wider, within the bound.
No kernel may reach another device: no remote copies, remote signals or barrier semaphores. Data moves between devices by JAX's collectives and lax.ppermute only.
A program may use at most 192 MiB of HBM per device.

v0:
```python
import math

import jax
import jax.numpy as jnp
from jax import lax
from jax.sharding import PartitionSpec as P

HD = 64


ROPE_BASE = 160000.0
NORM_EPS = 1e-05


def layer_norm(values, norm_gain):
    centred = values - jnp.mean(values, axis=-1, keepdims=True)
    spread = jnp.mean(centred * centred, axis=-1, keepdims=True)
    return centred * lax.rsqrt(spread + NORM_EPS) * norm_gain


def rope_tables(positions, head_width):
    inverse = ROPE_BASE ** (-(jnp.arange(head_width // 2).astype(jnp.float32) * 2.0) / head_width)
    angles = positions[:, None] * inverse[None, :]
    angles = jnp.concatenate([angles, angles], axis=-1)[:, None, :]
    return (jnp.cos(angles), jnp.sin(angles))


def rotate(values, cosine, sine_table):
    half_width = values.shape[-1] // 2
    turned = jnp.concatenate([-values[..., half_width:], values[..., :half_width]], axis=-1)
    return values * cosine + turned * sine_table


def rotate_back(gradient, cosine, sine_table):
    half_width = gradient.shape[-1] // 2
    scaled = gradient * sine_table
    turned = jnp.concatenate([scaled[..., half_width:], -scaled[..., :half_width]], axis=-1)
    return gradient * cosine + turned


def gated_gelu(projected):
    return jax.nn.gelu(projected[:, 0], approximate=False) * projected[:, 1]


def block_rows(row_total):
    return math.gcd(row_total, 1024)


def score_terms(
    query_block, grad_block, lse_block, delta_block, key_block, value_block, score_scale
):
    scores = (
        jnp.einsum("qhe,khe->qhk", query_block, key_block, preferred_element_type=jnp.float32)
        * score_scale
    )
    probabilities = jnp.exp(scores - lse_block[:, :, None])
    grad_probs = jnp.einsum(
        "qhe,khe->qhk", grad_block, value_block, preferred_element_type=jnp.float32
    )
    grad_scores = probabilities * (grad_probs - delta_block[:, :, None])
    return (probabilities.astype(jnp.bfloat16), grad_scores.astype(jnp.bfloat16))


def shards(hidden_in, cotangent, gain_attn, gain_mlp, w_qkv, w_attn_out, w_in, w_mlp_out):
    row_count = hidden_in.shape[0]
    head_count = w_qkv.shape[2] // HD
    score_scale = HD ** (-0.5)
    residual_in = hidden_in.astype(jnp.float32)
    normed_one, norm_one_back = jax.vjp(layer_norm, residual_in, gain_attn)
    attn_input = normed_one.astype(jnp.bfloat16)
    projected = jnp.einsum("td,dcf->tcf", attn_input, w_qkv, preferred_element_type=jnp.float32)
    positions = (lax.axis_index("ctx") * row_count + jnp.arange(row_count)).astype(jnp.float32)
    cosine, sine_table = rope_tables(positions, HD)
    queries = rotate(projected[:, 0].reshape(row_count, head_count, HD), cosine, sine_table).astype(
        jnp.bfloat16
    )
    keys_local = rotate(
        projected[:, 1].reshape(row_count, head_count, HD), cosine, sine_table
    ).astype(jnp.bfloat16)
    values_local = projected[:, 2].reshape(row_count, head_count, HD).astype(jnp.bfloat16)
    initial = (
        jnp.full((row_count, head_count), -1e30, jnp.float32),
        jnp.zeros((row_count, head_count), jnp.float32),
        jnp.zeros((row_count, head_count, HD), jnp.float32),
    )
    carried = initial
    key_part = lax.all_gather(keys_local, "ctx", axis=0, tiled=True)
    value_part = lax.all_gather(values_local, "ctx", axis=0, tiled=True)
    row_total = key_part.shape[0]
    block_size = block_rows(row_total)
    key_blocks = key_part.reshape(row_total // block_size, block_size, head_count, HD)
    value_blocks = value_part.reshape(row_total // block_size, block_size, head_count, HD)

    def forward_advance(running, blocks):
        running_max, run_total, accumulated = running
        key_block, value_block = blocks
        scores = (
            jnp.einsum("qhe,khe->qhk", queries, key_block, preferred_element_type=jnp.float32)
            * score_scale
        )
        new_max = jnp.maximum(running_max, jnp.max(scores, axis=-1))
        factor = jnp.exp(running_max - new_max)
        weights = jnp.exp(scores - new_max[:, :, None])
        run_total = run_total * factor + jnp.sum(weights, axis=-1)
        accumulated = accumulated * factor[:, :, None] + jnp.einsum(
            "qhk,khe->qhe",
            weights.astype(jnp.bfloat16),
            value_block,
            preferred_element_type=jnp.float32,
        )
        return ((new_max, run_total, accumulated), None)

    carried, unused = lax.scan(forward_advance, carried, (key_blocks, value_blocks))
    running_max, run_total, accumulated = carried
    attended = accumulated / run_total[:, :, None]
    log_total = running_max + jnp.log(run_total)
    attn_flat = attended.reshape(row_count, head_count * HD).astype(jnp.bfloat16)
    attn_branch = lax.psum(
        jnp.dot(attn_flat, w_attn_out, preferred_element_type=jnp.float32).astype(jnp.bfloat16),
        "tp",
    ).astype(jnp.float32)
    middle = residual_in + attn_branch
    normed_two, norm_two_back = jax.vjp(layer_norm, middle, gain_mlp)
    mlp_input = normed_two.astype(jnp.bfloat16)
    gate_up = jnp.einsum("td,dcf->tcf", mlp_input, w_in, preferred_element_type=jnp.float32)
    activated, gelu_back = jax.vjp(gated_gelu, gate_up)
    activated_low = activated.astype(jnp.bfloat16)
    mlp_branch = lax.psum(
        jnp.dot(activated_low, w_mlp_out, preferred_element_type=jnp.float32).astype(jnp.bfloat16),
        "tp",
    ).astype(jnp.float32)
    output = (middle + mlp_branch).astype(jnp.bfloat16)
    grad_w_mlp_out = jnp.einsum(
        "tf,td->fd", activated_low, cotangent, preferred_element_type=jnp.float32
    )
    grad_activated = jnp.einsum(
        "td,fd->tf", cotangent, w_mlp_out, preferred_element_type=jnp.float32
    )
    grad_gate_up = gelu_back(grad_activated)[0].astype(jnp.bfloat16)
    grad_w_in = jnp.einsum(
        "td,tcf->dcf", mlp_input, grad_gate_up, preferred_element_type=jnp.float32
    )
    grad_normed_two = lax.psum(
        jnp.einsum("tcf,dcf->td", grad_gate_up, w_in, preferred_element_type=jnp.float32).astype(
            jnp.bfloat16
        ),
        "tp",
    ).astype(jnp.float32)
    grad_middle_norm, grad_gain_mlp = norm_two_back(grad_normed_two)
    grad_middle = cotangent.astype(jnp.float32) + grad_middle_norm
    grad_middle_low = grad_middle.astype(jnp.bfloat16)
    grad_w_attn_out = jnp.einsum(
        "th,td->hd", attn_flat, grad_middle_low, preferred_element_type=jnp.float32
    )
    grad_heads = jnp.einsum(
        "td,hd->th", grad_middle_low, w_attn_out, preferred_element_type=jnp.float32
    )
    grad_heads = grad_heads.reshape(row_count, head_count, HD).astype(jnp.bfloat16)
    row_delta = jnp.sum(grad_heads.astype(jnp.float32) * attended, axis=-1)
    zero_heads = jnp.zeros((row_count, head_count, HD), jnp.float32)
    grad_query = zero_heads
    key_part = lax.all_gather(keys_local, "ctx", axis=0, tiled=True)
    value_part = lax.all_gather(values_local, "ctx", axis=0, tiled=True)
    row_total = key_part.shape[0]
    block_size = block_rows(row_total)
    key_blocks = key_part.reshape(row_total // block_size, block_size, head_count, HD)
    value_blocks = value_part.reshape(row_total // block_size, block_size, head_count, HD)

    def query_advance(running, blocks):
        key_block, value_block = blocks
        unused_probs, grad_scores = score_terms(
            queries, grad_heads, log_total, row_delta, key_block, value_block, score_scale
        )
        running = (
            running
            + jnp.einsum("qhk,khe->qhe", grad_scores, key_block, preferred_element_type=jnp.float32)
            * score_scale
        )
        return (running, None)

    grad_query, unused = lax.scan(query_advance, grad_query, (key_blocks, value_blocks))
    lse_all, delta_all = (
        lax.all_gather(log_total, "ctx", axis=0, tiled=True),
        lax.all_gather(row_delta, "ctx", axis=0, tiled=True),
    )
    carried = (zero_heads, zero_heads)
    query_part = lax.all_gather(queries, "ctx", axis=0, tiled=True)
    grad_part = lax.all_gather(grad_heads, "ctx", axis=0, tiled=True)
    row_total = query_part.shape[0]
    block_size = block_rows(row_total)
    query_blocks = query_part.reshape(row_total // block_size, block_size, head_count, HD)
    grad_blocks = grad_part.reshape(row_total // block_size, block_size, head_count, HD)
    lse_blocks = lse_all.reshape(row_total // block_size, block_size, head_count)
    delta_blocks = delta_all.reshape(row_total // block_size, block_size, head_count)

    def key_advance(running, blocks):
        grad_key, grad_value = running
        query_block, grad_block, lse_block, delta_block = blocks
        probs_low, grad_scores = score_terms(
            query_block, grad_block, lse_block, delta_block, keys_local, values_local, score_scale
        )
        grad_key = (
            grad_key
            + jnp.einsum(
                "qhk,qhe->khe", grad_scores, query_block, preferred_element_type=jnp.float32
            )
            * score_scale
        )
        grad_value = grad_value + jnp.einsum(
            "qhk,qhe->khe", probs_low, grad_block, preferred_element_type=jnp.float32
        )
        return ((grad_key, grad_value), None)

    carried, unused = lax.scan(
        key_advance, carried, (query_blocks, grad_blocks, lse_blocks, delta_blocks)
    )
    grad_keys, grad_values = carried
    grad_q_plain = rotate_back(grad_query, cosine, sine_table)
    grad_k_plain = rotate_back(grad_keys, cosine, sine_table)
    grad_projected = jnp.stack([grad_q_plain, grad_k_plain, grad_values], axis=1)
    grad_projected = grad_projected.reshape(row_count, 3, head_count * HD).astype(jnp.bfloat16)
    grad_w_qkv = jnp.einsum(
        "td,tcf->dcf", attn_input, grad_projected, preferred_element_type=jnp.float32
    )
    grad_normed_one = lax.psum(
        jnp.einsum("tcf,dcf->td", grad_projected, w_qkv, preferred_element_type=jnp.float32).astype(
            jnp.bfloat16
        ),
        "tp",
    ).astype(jnp.float32)
    grad_input_norm, grad_gain_attn = norm_one_back(grad_normed_one)
    grad_input = grad_middle + grad_input_norm
    summed = (
        lax.psum_scatter(grad_w_qkv, "ctx", scatter_dimension=0, tiled=True),
        lax.psum_scatter(grad_w_attn_out, "ctx", scatter_dimension=1, tiled=True),
        lax.psum_scatter(grad_w_in, "ctx", scatter_dimension=0, tiled=True),
        lax.psum_scatter(grad_w_mlp_out, "ctx", scatter_dimension=1, tiled=True),
        lax.psum_scatter(grad_gain_attn, "ctx", scatter_dimension=0, tiled=True),
        lax.psum_scatter(grad_gain_mlp, "ctx", scatter_dimension=0, tiled=True),
    )
    return (output, grad_input, summed[4], summed[5], summed[0], summed[1], summed[2], summed[3])


def solution(mesh):
    in_specs = (
        P("ctx", None),
        P("ctx", None),
        P(),
        P(),
        P(None, None, "tp"),
        P("tp", None),
        P(None, None, "tp"),
        P("tp", None),
    )
    out_specs = (
        P("ctx", None),
        P("ctx", None),
        P("ctx"),
        P("ctx"),
        P("ctx", None, "tp"),
        P("tp", "ctx"),
        P("ctx", None, "tp"),
        P("tp", "ctx"),
    )
    return jax.shard_map(shards, mesh=mesh, in_specs=in_specs, out_specs=out_specs, check_vma=False)
```

profile of v0, /device:TPU:0, one launch (start us, length us, event | category | flops | bytes accessed | tf_op | source)
XLA Modules:
  0.0 737.3 jit_solution(6647935614218018569)
XLA Ops:
  14.1 1.9 fusion.144
  17.0 1.8 copy.58
  21.9 36.2 %all-gather.7.cloned.1.call-done = bf16[2048,8,64]{0,2,1:T(8,128)(2,1)} async-done(((bf16[128,8,64]{0,2,1:T(8,128)(2,1)}), bf16[2048,8,64]{0,2,1:T(8,128)(2,1)}) %all-gather.7.cloned.1.call-update) | async-done | bytes 2097168 | tf_op jit(solution)/shard_map/all_gather | solution.py:88
  58.1 3.2 copy.90
  61.3 39.7 %all-gather.5.cloned.1.call-done = bf16[2048,8,64]{0,2,1:T(8,128)(2,1)} async-done(((bf16[128,8,64]{0,2,1:T(8,128)(2,1)}), bf16[2048,8,64]{0,2,1:T(8,128)(2,1)}) %all-gather.5.cloned.1.call-update) | async-done | bytes 2097168 | tf_op jit(solution)/shard_map/all_gather | solution.py:87
  101.0 3.2 copy.91
  104.2 10.0 %while.39 = (s32[]{:T(128)}, f32[128,8]{0,1:T(8,128)S(1)}, f32[128,8]{0,1:T(8,128)S(1)}, f32[128,8,64]{0,2,1:T(8,128)}, bf16[2,1024,8,64]{1,3,2,0:T(8,128)(2,1)}...) while((s32[]{:T(128)}, f32[128,8]{0,1:T(8,128)S(1)}, ...), condition=%wide.region_5.6_spmd.clone, body=%wide.region_2.5_spmd.clone.sunk | while | flops 277025792 | bytes 23789716 | solution.py:113
  104.2 2.2 bitcast_reduce_fusion.2
  108.8 2.2 bitcast_reduce_fusion.2
  111.7 2.5 fusion.199
  116.0 2.3 convolution_convert_fusion
  118.3 3.6 fusion.147
  121.9 18.7 %all-reduce.10.cloned.1.call-done = bf16[128,1024]{1,0:T(8,128)(2,1)} async-done(((bf16[128,1024]{1,0:T(8,128)(2,1)}), bf16[128,1024]{1,0:T(8,128)(2,1)}) %all-reduce.10.cloned.1.call-update) | async-done | bytes 262160 | tf_op jit(solution)/shard_map/psum | solution.py:118
  143.4 4.4 fusion.140
  153.6 22.7 %all-reduce.12.cloned.1.call-done = bf16[128,1024]{1,0:T(8,128)(2,1)} async-done(((bf16[128,1024]{1,0:T(8,128)(2,1)}), bf16[128,1024]{1,0:T(8,128)(2,1)}) %all-reduce.12.cloned.1.call-update) | async-done | bytes 262160 | tf_op jit(solution)/shard_map/psum | solution.py:143
  176.3 1.9 fusion.109
  182.1 2.4 convolution_convert_fusion.2
  186.3 33.2 %all-gather.9.cloned.1.call-done = bf16[2048,8,64]{0,2,1:T(8,128)(2,1)} async-done(((bf16[128,8,64]{0,2,1:T(8,128)(2,1)}), bf16[2048,8,64]{0,2,1:T(8,128)(2,1)}) %all-gather.9.cloned.1.call-update) | async-done | bytes 2097168 | tf_op jit(solution)/shard_map/all_gather | solution.py:187
  219.5 3.4 copy.89
  223.5 21.1 %all_gather.23 = f32[2048,8]{0,1:T(8,128)} all-gather(f32[128,8]{0,1:T(8,128)S(1)} %log_add_fusion), channel_id=1, replica_groups=mesh['ctx'=16,'tp'=2] {'ctx'}, dimensions={0}, use_global_device_ids=true | all-gather | bytes 69632 | tf_op jit(solution)/shard_map/all_gather | solution.py:183
  246.9 19.3 %all_gather.25 = f32[2048,8]{0,1:T(8,128)} all-gather(f32[128,8]{0,1:T(8,128)S(1)} %multiply_reduce_fusion.1), channel_id=1, replica_groups=mesh['ctx'=16,'tp'=2] {'ctx'}, dimensions={0}, use_global_device_ids=true | all-gather | bytes 69632 | tf_op jit(solution)/shard_map/all_gather | solution.py:184
  266.2 18.5 %while.40 = (s32[]{:T(128)}, f32[128,8,64]{0,2,1:T(8,128)}, bf16[2,1024,8,64]{1,3,2,0:T(8,128)(2,1)}, bf16[128,8,64]{0,2,1:T(8,128)(2,1)S(1)}, f32[128,8]{0,1:T(...) while((s32[]{:T(128)}, f32[128,8,64]{0,2,1:T(8,128)}, ...), condition=%wide.region_15.16_spmd.clone, body=%wide.region_14.15_spmd.clone.sunk | while | flops 408092672 | bytes 12347030 | solution.py:181
  266.2 4.0 fusion.205
  270.2 5.2 fusion.206
  275.4 4.0 fusion.205
  279.4 5.2 fusion.206
  284.6 3.3 copy.88
  287.9 32.2 %while.41 = (s32[]{:T(128)}, f32[128,8,64]{0,2,1:T(8,128)}, f32[128,8,64]{0,2,1:T(8,128)}, bf16[2,1024,8,64]{1,3,2,0:T(8,128)(2,1)}, bf16[128,8,64]{0,2,1:T(8,12...) while((s32[]{:T(128)}, f32[128,8,64]{0,2,1:T(8,128)}, ...), condition=%wide.region_17.18_spmd.clone, body=%wide.region_16.17_spmd.clone.sunk | while | flops 545587200 | bytes 18318988 | solution.py:214
  289.3 4.0 fusion.214
  293.3 6.5 fusion.215
  299.8 4.1 fusion.216
  305.3 4.0 fusion.214
  309.3 6.6 fusion.215
  315.9 4.2 fusion.216
  324.0 1.8 fusion.123
  329.1 2.8 fusion.78
  332.0 7.5 %fusion.130 = f32[1024,2,1312]{2,0,1:T(8,128)} fusion(f32[128,1,1312]{0,2,1:T(8,128)} %copy-done.7, f32[128,1,1312]{0,2,1:T(8,128)} %copy-done.8, bf16[128,1024]{1,0:T(8,128)(2,1)} %all-reduce.10.cloned.1.call-done, bf16[128,1024]{1,0:T(8,128)(2,1)S(1)} %copy-done.1, f32[1024]{0:T(1024)S(1)} %copy-done.21, f32[128]{0:T(128)S(1)} %copy-done.31, ...), kind=kOutput, calls=%fused_computation.174 | convolution fusion | flops 689455104 | bytes 12620800 | tf_op jit(solution)/shard_map/td,tcf->dcf/dot_general | solution.py:140
  340.4 2.8 fusion.148
  343.3 4.5 fusion.149
  348.7 4.7 fusion.125
  355.3 4.1 all-reduce.14.cloned.1.call-done
  361.9 33.7 %all-reduce.4 = (f32[1024]{0:T(1024)S(1)}, f32[1024]{0:T(1024)S(1)}) all-reduce(f32[1024]{0:T(1024)S(1)} %get-tuple-element.322, f32[1024]{0:T(1024)S(1)} %copy-done.26), channel_id=2, replica_groups=mesh['ctx'=16,'tp'=2] {'ctx'}, use_global_device_ids=true, to_apply=%region_22.23.clone | all-reduce | flops 2048 | bytes 16384
  396.7 2.9 add_add_fusion.2
  399.7 90.6 %reduce-scatter.9.cloned.1.call-done = f32[64,2,1312]{2,0,1:T(8,128)} async-done(((f32[1024,2,1312]{2,0,1:T(8,128)}), f32[64,2,1312]{2,0,1:T(8,128)}) %reduce-scatter.9.cloned.1.call-update) | async-done | bytes 671760 | tf_op jit(solution)/shard_map/reduce_scatter | solution.py:236
  490.3 2.5 copy.73
  492.8 63.2 %reduce-scatter.7.cloned.1.call-done = f32[512,64]{0,1:T(8,128)} async-done(((f32[512,1024]{0,1:T(8,128)}), f32[512,64]{0,1:T(8,128)}) %reduce-scatter.7.cloned.1.call-update) | async-done | bytes 131088 | tf_op jit(solution)/shard_map/reduce_scatter | solution.py:235
  556.0 85.3 %reduce-scatter.11.cloned.1.call-done = f32[1312,64]{0,1:T(8,128)} async-done(((f32[1312,1024]{0,1:T(8,128)}), f32[1312,64]{0,1:T(8,128)}) %reduce-scatter.11.cloned.1.call-update) | async-done | bytes 335888 | tf_op jit(solution)/shard_map/reduce_scatter | solution.py:237
  641.3 89.5 %reduce-scatter.5.cloned.1.call-done = f32[64,3,512]{2,0,1:T(8,128)} async-done(((f32[1024,3,512]{2,0,1:T(8,128)}), f32[64,3,512]{2,0,1:T(8,128)}) %reduce-scatter.5.cloned.1.call-update) | async-done | bytes 393232 | tf_op jit(solution)/shard_map/reduce_scatter | solution.py:234
  (177 shorter events, 49.4 us)
Async XLA Ops:
  7.2 3.6 copy-start
  7.2 50.9 %all-gather.7.cloned.1.call-start = ((), (), s32[]{:S(2)}) async-start(), calls=%async_computation.5 | async-start | bytes 2228224 | tf_op jit(solution)/shard_map/all_gather | solution.py:88
  12.3 0.9 copy-start.12
  14.0 86.9 %all-gather.5.cloned.1.call-start = ((), (), s32[]{:S(2)}) async-start(), calls=%async_computation.4 | async-start | bytes 2228224 | tf_op jit(solution)/shard_map/all_gather | solution.py:87
  19.0 2.8 copy-start.19
  19.0 2.7 copy-start.20
  21.8 118.8 %all-reduce.10.cloned.1.call-start = ((), (), s32[]{:S(2)}) async-start(), calls=%async_computation.6 | async-start | bytes 524288 | tf_op jit(solution)/shard_map/psum | solution.py:118
  104.2 2.9 copy-start.2
  108.8 2.9 copy-start.2
  114.3 33.6 %copy-start.3 = (bf16[128,8,64]{0,2,1:T(8,128)(2,1)}, bf16[128,8,64]{0,2,1:T(8,128)(2,1)S(1)}, u32[]{:S(2)}) copy-start(bf16[128,8,64]{0,2,1:T(8,128)(2,1)S(1)} %get-tuple-element.681) | copy-start | bytes 393220
  114.3 26.3 %copy-start.1 = (bf16[128,1024]{1,0:T(8,128)(2,1)S(1)}, bf16[128,1024]{1,0:T(8,128)(2,1)}, u32[]{:S(2)}) copy-start(bf16[128,1024]{1,0:T(8,128)(2,1)} %param.14) | copy-start | bytes 786436
  114.3 29.1 %copy-start.21 = (f32[1024]{0:T(1024)S(1)}, f32[1024]{0:T(1024)}, u32[]{:S(2)}) copy-start(f32[1024]{0:T(1024)} %param.17) | copy-start | bytes 12292
  118.3 58.0 %all-reduce.12.cloned.1.call-start = ((), (), s32[]{:S(2)}) async-start(), calls=%async_computation.7 | async-start | bytes 524288 | tf_op jit(solution)/shard_map/psum | solution.py:143
  141.6 6.2 copy-start.23
  143.3 7.9 %slice-start = ((s8[5373952]{0:T(1024)(128)(4,1)}), s8[4194304]{0:T(1024)(128)(4,1)S(1)}, s32[]{:S(2)}) async-start(s8[5373952]{0:T(1024)(128)(4,1)} %bitcast.332), calls=%async_computation.15 | async-start | bytes 8388608
  143.3 4.5 copy-start.29
  143.3 4.5 copy-start.9
  143.4 7.9 %slice-start.1 = ((s8[5373952]{0:T(1024)(128)(4,1)}), s8[1179648]{0:T(1024)(128)(4,1)S(1)}, s32[]{:S(2)}) async-start(s8[5373952]{0:T(1024)(128)(4,1)} %bitcast.332), calls=%async_computation.16 | async-start | bytes 2359296
  149.3 1.1 copy-start.8
  150.4 0.8 copy-start.7
  150.4 25.9 %copy-start.24 = (f32[128]{0:T(128)S(1)}, f32[128]{0:T(128)}, u32[]{:S(2)}) copy-start(f32[128]{0:T(128)} %copy-done.23) | copy-start | bytes 1540
  150.4 25.9 %copy-start.30 = (f32[128]{0:T(128)S(1)}, f32[128]{0:T(128)}, u32[]{:S(2)}) copy-start(f32[128]{0:T(128)} %copy-done.29) | copy-start | bytes 1540
  150.4 27.8 %copy-start.40 = (f32[128]{0:T(128)S(1)}, f32[128]{0:T(128)}, u32[]{:S(2)}) copy-start(f32[128]{0:T(128)} %copy-done.39) | copy-start | bytes 1540
  152.9 66.6 %all-gather.9.cloned.1.call-start = ((), (), s32[]{:S(2)}) async-start(), calls=%async_computation.8 | async-start | bytes 2228224 | tf_op jit(solution)/shard_map/all_gather | solution.py:187
  153.5 131.1 %all-gather.11.cloned.1.call-start = ((), (), s32[]{:S(2)}) async-start(), calls=%async_computation.9 | async-start | bytes 2228224 | tf_op jit(solution)/shard_map/all_gather | solution.py:188
  184.5 81.7 %copy-start.4 = (bf16[128,8,64]{0,2,1:T(8,128)(2,1)S(1)}, bf16[128,8,64]{0,2,1:T(8,128)(2,1)}, u32[]{:S(2)}) copy-start(bf16[128,8,64]{0,2,1:T(8,128)(2,1)} %copy-done.3) | copy-start | bytes 393220
  186.2 173.1 %all-reduce.14.cloned.1.call-start = ((), (), s32[]{:S(2)}) async-start(), calls=%async_computation.14 | async-start | bytes 1048576 | tf_op jit(solution)/shard_map/psum | solution.py:128
  219.5 25.0 %copy-start.5 = (bf16[1312,1024]{1,0:T(8,128)(2,1)S(1)}, bf16[1312,1024]{1,0:T(8,128)(2,1)}, u32[]{:S(2)}) copy-start(bf16[1312,1024]{1,0:T(8,128)(2,1)} %param.21) | copy-start | bytes 8060932
  219.5 25.0 %copy-start.10 = (bf16[128,1312]{0,1:T(8,128)(2,1)S(1)}, bf16[128,1312]{0,1:T(8,128)(2,1)}, u32[]{:S(2)}) copy-start(bf16[128,1312]{0,1:T(8,128)(2,1)} %get-tuple-element.387) | copy-start | bytes 1007620
  219.5 26.3 %copy-start.14 = (bf16[128,512]{0,1:T(8,128)(2,1)S(1)}, bf16[128,512]{0,1:T(8,128)(2,1)}, u32[]{:S(2)}) copy-start(bf16[128,512]{0,1:T(8,128)(2,1)} %copy.63) | copy-start | bytes 393220
  266.2 4.0 copy-start.28
  275.4 4.0 copy-start.28
  284.6 3.3 copy-start.6
  322.7 9.2 %copy-start.17 = (bf16[128,1,512]{2,0,1:T(8,128)(2,1)}, bf16[128,1,512]{2,0,1:T(8,128)(2,1)S(1)}, u32[]{:S(2)}) copy-start(bf16[128,1,512]{2,0,1:T(8,128)(2,1)S(1)} %copy.70) | copy-start | bytes 393220
  322.7 9.3 %copy-start.25 = (f32[128]{0:T(128)S(1)}, f32[128]{0:T(128)}, u32[]{:S(2)}) copy-start(f32[128]{0:T(128)} %copy-done.23) | copy-start | bytes 1540
  322.8 9.3 %copy-start.31 = (f32[128]{0:T(128)S(1)}, f32[128]{0:T(128)}, u32[]{:S(2)}) copy-start(f32[128]{0:T(128)} %copy-done.29) | copy-start | bytes 1540
  332.0 158.3 %reduce-scatter.9.cloned.1.call-start = ((), (), s32[]{:S(2)}) async-start(), calls=%async_computation.12 | async-start | bytes 12255232 | tf_op jit(solution)/shard_map/reduce_scatter | solution.py:236
  339.5 0.9 copy-start.16
  339.5 216.5 %reduce-scatter.7.cloned.1.call-start = ((), (), s32[]{:S(2)}) async-start(), calls=%async_computation.11 | async-start | bytes 2228224 | tf_op jit(solution)/shard_map/reduce_scatter | solution.py:235
  343.2 298.1 %reduce-scatter.11.cloned.1.call-start = ((), (), s32[]{:S(2)}) async-start(), calls=%async_computation.13 | async-start | bytes 6127616 | tf_op jit(solution)/shard_map/reduce_scatter | solution.py:237
  347.8 0.9 copy-start.18
  347.8 0.9 copy-start.22
  347.8 0.9 copy-start.33
  347.8 383.0 %reduce-scatter.5.cloned.1.call-start = ((), (), s32[]{:S(2)}) async-start(), calls=%async_computation.10 | async-start | bytes 6684672 | tf_op jit(solution)/shard_map/reduce_scatter | solution.py:234
  353.4 7.2 copy-start.38
  353.4 7.2 copy-start.34
  353.4 8.5 %copy-start.26 = (f32[1024]{0:T(1024)S(1)}, f32[1024]{0:T(1024)}, u32[]{:S(2)}) copy-start(f32[1024]{0:T(1024)} %get-tuple-element.320) | copy-start | bytes 12292
  353.4 43.3 %copy-start.36 = (f32[128]{0:T(128)S(1)}, f32[128]{0:T(128)}, u32[]{:S(2)}) copy-start(f32[128]{0:T(128)} %copy-done.35) | copy-start | bytes 1540
  (9 other events, 5.8 us)
Sparse Core Ops, SparseCore 0:
  14.2 43.8 all-gather.6
  60.8 40.1 all-gather.4
  118.4 22.1 all-reduce.9
  153.1 23.1 all-reduce.11
  178.3 41.1 all-gather.8
  221.6 40.4 all-gather.10
  332.1 27.2 all-reduce.13
  364.0 126.2 reduce-scatter.8
  494.6 61.3 reduce-scatter.6
  560.8 80.4 reduce-scatter.10
  646.4 84.4 reduce-scatter.4
where the time goes:
time: 739 us; the launch traced here: 737 us
  waiting for transfers between devices  484 us (65%)
  matrix products  95.9 us (13%)
  blocking collectives  74 us (10%)
  local copies, waits for them, and re-layouts  39.8 us (5%)
  other arithmetic  27.9 us (4%)
  between operations  15 us (2%)
    reduce_scatter x1, waiting for transfers between devices, shards(): lax.psum_scatter(grad_w_in, 'ctx', scatter_dimension=0, tiled=True)  90.6 us
    reduce_scatter x1, waiting for transfers between devices, shards(): lax.psum_scatter(grad_w_qkv, 'ctx', scatter_dimension=0, tiled=True)  89.5 us
    reduce_scatter x1, waiting for transfers between devices, shards(): lax.psum_scatter(grad_w_mlp_out, 'ctx', scatter_dimension=1, tiled=True)  85.3 us
    reduce_scatter x1, waiting for transfers between devices, shards(): lax.psum_scatter(grad_w_attn_out, 'ctx', scatter_dimension=1, tiled=True)  63.2 us
    all_gather x1, waiting for transfers between devices, shards(): key_part = lax.all_gather(keys_local, 'ctx', axis=0, tiled=True)  39.7 us
    all_gather x1, waiting for transfers between devices, shards(): value_part = lax.all_gather(values_local, 'ctx', axis=0, tiled=True)  36.2 us
    unnamed x1, blocking collectives  33.7 us
    all_gather x1, waiting for transfers between devices, shards(): query_part = lax.all_gather(queries, 'ctx', axis=0, tiled=True)  33.2 us
  transfers between devices with their start and end apart: 11, of which 10 were waited for; matrix products, arithmetic and copies ran while one was open for 10% of the time, Pallas kernels for 0%

commit v1 on v0

v1 whole, which is shorter than its diff:
```python
import functools

import jax
import jax.numpy as jnp
from jax import lax
from jax.experimental import pallas as pl
from jax.experimental.pallas import tpu as pltpu
from jax.sharding import PartitionSpec as P

HD = 64
HALF = HD // 2
ROPE_BASE = 160000.0
NORM_EPS = 1e-05
BF = jnp.bfloat16
F32 = jnp.float32
VMEM_LIMIT = 60 * 1024 * 1024


def dot(a, b, dims):
    return lax.dot_general(a, b, (dims, ((), ())), preferred_element_type=F32)


def nn(a, b):
    return dot(a, b, ((1,), (0,)))


def nt(a, b):
    return dot(a, b, ((1,), (1,)))


def key_loop(count, body):
    if count <= 2:
        for j in range(count):
            body(j)
    else:
        pl.loop(0, count)(body)


def load_rows(parts, row, out_ref):
    for j, (ref, first) in enumerate(parts):
        blocks, width = ref.shape[0], ref.shape[2]
        for b in range(blocks):
            out_ref[j, b * width : (b + 1) * width, :] = ref[b, first + row : first + row + HD, :].T


def load_columns(parts, row, out_ref):
    for j, (ref, first) in enumerate(parts):
        blocks, width = ref.shape[0], ref.shape[2]
        for b in range(blocks):
            out_ref[j, :, b * width : (b + 1) * width] = ref[b, first + row : first + row + HD, :]


def attend_kernel(part_count, own_ref, *refs):
    others = refs[: part_count - 1]
    out_ref, low_ref, lse_ref, k_scr, vt_scr, s_scr = refs[part_count - 1 :]
    blocks, width = own_ref.shape[0], own_ref.shape[2]
    parts = [(own_ref, HD)] + [(r, 0) for r in others]
    load_rows(parts, 0, k_scr)
    load_columns(parts, HD, vt_scr)
    pair = s_scr.shape[2] // width

    @pl.loop(0, blocks // pair)
    def query_block(i):
        qt = jnp.concatenate([own_ref[pair * i + b, :HD, :] for b in range(pair)], axis=1)

        def score(j, top):
            s = nn(k_scr[j], qt)
            s_scr[j] = s
            return jnp.maximum(top, jnp.max(s, axis=0, keepdims=True))

        top = jnp.full((1, pair * width), -jnp.inf, F32)
        top = lax.fori_loop(0, part_count, score, top, unroll=part_count <= 2)

        def weigh(j, carry):
            total, acc = carry
            p = jnp.exp(s_scr[j] - top)
            return total + jnp.sum(p, axis=0, keepdims=True), acc + nn(vt_scr[j], p.astype(BF))

        start = (jnp.zeros((1, pair * width), F32), jnp.zeros((HD, pair * width), F32))
        total, acc = lax.fori_loop(0, part_count, weigh, start, unroll=part_count <= 2)
        attended = acc / total
        lse = top + jnp.log(total)
        for b in range(pair):
            cut = slice(b * width, (b + 1) * width)
            out_ref[pair * i + b] = attended[:, cut]
            low_ref[pair * i + b] = attended[:, cut].astype(BF)
            lse_ref[pair * i + b] = lse[:, cut]


def attend(own, others):
    blocks, unused, width = own.shape
    part_count = 1 + len(others)
    keys = blocks * width
    pair = 2 if blocks % 2 == 0 else 1
    flops = 4 * keys * keys * part_count * HD
    return pl.pallas_call(
        functools.partial(attend_kernel, part_count),
        out_shape=(
            jax.ShapeDtypeStruct((blocks, HD, width), F32),
            jax.ShapeDtypeStruct((blocks, HD, width), BF),
            jax.ShapeDtypeStruct((blocks, 1, width), F32),
        ),
        scratch_shapes=[
            pltpu.VMEM((part_count, keys, HD), BF),
            pltpu.VMEM((part_count, HD, keys), BF),
            pltpu.VMEM((part_count, keys, pair * width), F32),
        ],
        compiler_params=pltpu.CompilerParams(vmem_limit_bytes=VMEM_LIMIT),
        cost_estimate=pl.CostEstimate(
            flops=flops, bytes_accessed=4 * own.size, transcendentals=keys * keys * part_count
        ),
        name="attend",
    )(own, *others)


def attend_back_kernel(part_count, own_ref, *refs):
    others = refs[: part_count - 1]
    (
        grad_ref,
        out_ref,
        lse_ref,
        dq_ref,
        dkv_ref,
        k_scr,
        v_scr,
        kt_scr,
        dk_scr,
        dv_scr,
    ) = refs[part_count - 1 :]
    blocks, width = own_ref.shape[0], own_ref.shape[2]
    parts = [(own_ref, HD)] + [(r, 0) for r in others]
    load_rows(parts, 0, k_scr)
    load_rows(parts, HD, v_scr)
    load_columns(parts, 0, kt_scr)
    dk_scr[...] = jnp.zeros_like(dk_scr)
    dv_scr[...] = jnp.zeros_like(dv_scr)
    pair = 2 if blocks % 2 == 0 else 1

    @pl.loop(0, blocks // pair)
    def query_block(i):
        span = range(pair)
        qt = jnp.concatenate([own_ref[pair * i + b, :HD, :] for b in span], axis=1)
        gt = jnp.concatenate([grad_ref[pair * i + b] for b in span], axis=1)
        ot = jnp.concatenate([out_ref[pair * i + b] for b in span], axis=1)
        lse = jnp.concatenate([lse_ref[pair * i + b] for b in span], axis=1)
        q, g = qt.T, gt.T
        delta = jnp.sum(gt.astype(F32) * ot, axis=0, keepdims=True)

        def one(j, dq):
            p = jnp.exp(nn(k_scr[j], qt) - lse)
            ds = (p * (nn(v_scr[j], gt) - delta)).astype(BF)
            dv_scr[j] += nn(p.astype(BF), g)
            dk_scr[j] += nn(ds, q)
            return dq + nn(kt_scr[j], ds)

        start = jnp.zeros((HD, pair * width), F32)
        dq = lax.fori_loop(0, part_count, one, start, unroll=part_count <= 2)
        for b in span:
            dq_ref[pair * i + b] = dq[:, b * width : (b + 1) * width] * (HD**-0.5)

    def finish(j):
        for b in range(blocks):
            rows = slice(b * width, (b + 1) * width)
            dkv_ref[j, b, :HD, :] = dk_scr[j, rows, :].T
            dkv_ref[j, b, HD:, :] = dv_scr[j, rows, :].T

    key_loop(part_count, finish)


def attend_back(own, others, grad, attended, lse):
    blocks, unused, width = own.shape
    part_count = 1 + len(others)
    keys = blocks * width
    flops = 10 * keys * keys * part_count * HD
    return pl.pallas_call(
        functools.partial(attend_back_kernel, part_count),
        out_shape=(
            jax.ShapeDtypeStruct((blocks, HD, width), F32),
            jax.ShapeDtypeStruct((part_count, blocks, 2 * HD, width), F32),
        ),
        scratch_shapes=[
            pltpu.VMEM((part_count, keys, HD), BF),
            pltpu.VMEM((part_count, keys, HD), BF),
            pltpu.VMEM((part_count, HD, keys), BF),
            pltpu.VMEM((part_count, keys, HD), F32),
            pltpu.VMEM((part_count, keys, HD), F32),
        ],
        compiler_params=pltpu.CompilerParams(vmem_limit_bytes=VMEM_LIMIT),
        cost_estimate=pl.CostEstimate(
            flops=flops, bytes_accessed=8 * own.size, transcendentals=keys * keys * part_count
        ),
        name="attend_back",
    )(own, *others, grad, attended, lse)


def head_weight_kernel(rows_ref, own_ref, other_ref, out_ref):
    blocks = rows_ref.shape[0]
    total = jnp.zeros((rows_ref.shape[2], own_ref.shape[1]), F32)
    for b in range(blocks):
        total += nt(rows_ref[b, 0], own_ref[b])
        total += nt(rows_ref[b, 1], other_ref[b])
    out_ref[...] = total.astype(BF)


def head_weight(rows, own, other):
    return pl.pallas_call(
        head_weight_kernel,
        out_shape=jax.ShapeDtypeStruct((rows.shape[2], own.shape[1]), BF),
        compiler_params=pltpu.CompilerParams(vmem_limit_bytes=VMEM_LIMIT),
        cost_estimate=pl.CostEstimate(
            flops=2 * rows.size * own.shape[1], bytes_accessed=2 * rows.size, transcendentals=0
        ),
        name="head_weight",
    )(rows, own, other)


def standardise(values):
    centred = values - jnp.mean(values, axis=-1, keepdims=True)
    spread = jnp.mean(centred * centred, axis=-1, keepdims=True)
    scale = lax.rsqrt(spread + NORM_EPS)
    return centred * scale, scale


def standardise_back(gradient, gain, normed, scale):
    y = gradient * gain
    along = jnp.mean(y * normed, axis=-1, keepdims=True)
    return scale * (y - jnp.mean(y, axis=-1, keepdims=True) - normed * along)


def gated_gelu(gate, up):
    return jax.nn.gelu(gate, approximate=False) * up


def layer(ctx_size, tp_size, hidden_in, cotangent, gain_attn, gain_mlp, w_qkv, w_attn_out, w_in, w_mlp_out):
    width = hidden_in.shape[0]
    model = hidden_in.shape[1]
    inner = w_qkv.shape[2]
    heads = inner // HD
    units = w_in.shape[2]
    chips = ctx_size // 2
    copies = chips // heads
    mine = model // ctx_size
    me = lax.axis_index("ctx")
    core = me % 2

    same_core = [[2 * p + k for p in range(chips)] for k in range(2)]
    head_groups = [
        [2 * (heads * g + p) + k for p in range(heads)] for g in range(copies) for k in range(2)
    ]

    def exchange(values):
        return lax.all_to_all(values, "ctx", 0, 0, axis_index_groups=head_groups)

    def swap_core(values):
        return lax.ppermute(values, "ctx", [(c, c ^ 1) for c in range(ctx_size)])

    def shift_keys(values, step):
        ring = 2 * copies
        pairs = []
        for c in range(ctx_size):
            g, p, k = c // (2 * heads), (c // 2) % heads, c % 2
            t = (2 * g + k + step) % ring
            pairs.append((c, 2 * (heads * (t // 2) + p) + t % 2))
        return lax.ppermute(values, "ctx", pairs)

    def add_tp(values):
        low = values.astype(BF)
        if tp_size == 2:
            other = lax.ppermute(low, "tp", [(0, 1), (1, 0)])
            return low.astype(F32) + other.astype(F32)
        return lax.psum(low, "tp").astype(F32)

    def sum_tp(values):
        if tp_size == 2:
            return values + lax.ppermute(values, "tp", [(0, 1), (1, 0)])
        return lax.psum(values, "tp")

    def choose(values_t):
        blocks = values_t.reshape(chips, 2, mine, width)
        keep = lax.dynamic_index_in_dim(blocks, core, 1, keepdims=False)
        give = lax.dynamic_index_in_dim(blocks, 1 - core, 1, keepdims=False)
        return keep.reshape(chips * mine, width), give.reshape(chips * mine, width)

    def scatter(values):
        return lax.psum_scatter(
            values, "ctx", scatter_dimension=0, tiled=True, axis_index_groups=same_core
        )

    residual_in = hidden_in.astype(F32)
    normed_one, scale_one = standardise(residual_in)
    attn_input = (normed_one * gain_attn).astype(BF)
    projected = jnp.einsum("dcf,td->cft", w_qkv, attn_input, preferred_element_type=F32)
    projected = projected.reshape(3, heads, HD, width)
    group_first = (me // (2 * heads)) * (2 * heads)
    block_ids = group_first + 2 * jnp.arange(heads) + core
    inverse = ROPE_BASE ** (-(jnp.arange(HALF).astype(F32) * 2.0) / HD)

    def tables(ids):
        positions = (ids[:, None] * width + jnp.arange(width)[None, :]).astype(F32)
        angles = positions[:, None, :] * inverse[None, :, None]
        return jnp.cos(angles), jnp.sin(angles)

    cos_one, sin_one = tables(me[None])
    cos_all, sin_all = tables(block_ids)

    def rotate(values, cosine, sine):
        first, second = values[:, :HALF], values[:, HALF:]
        return jnp.concatenate(
            [first * cosine - second * sine, second * cosine + first * sine], axis=1
        )

    def rotate_back(values, cosine, sine):
        first, second = values[:, :HALF], values[:, HALF:]
        return jnp.concatenate(
            [first * cosine + second * sine, second * cosine - first * sine], axis=1
        )

    score_scale = HD**-0.5
    queries = rotate(projected[0], cos_one, sin_one).astype(BF) * BF(score_scale)
    keys = rotate(projected[1], cos_one, sin_one).astype(BF)
    packed = jnp.concatenate([queries, keys, projected[2].astype(BF)], axis=1)
    own = exchange(packed)
    others = [shift_keys(own[:, HD:], step) for step in range(1, 2 * copies)]
    attended, attended_low, lse = attend(own, others)
    attn_flat_t = exchange(attended_low).reshape(inner, width)

    if copies == 1:
        keep_in, give_in = choose(attn_input.T)
        both_in = jnp.stack([keep_in, swap_core(give_in)])
        both_in, attn_flat_t = lax.optimization_barrier((both_in, attn_flat_t))
        rows_in = lax.all_gather(both_in, "ctx", axis=0, axis_index_groups=same_core)

    middle = residual_in + add_tp(dot(attn_flat_t, w_attn_out, ((0,), (0,))))
    normed_two, scale_two = standardise(middle)
    mlp_input = (normed_two * gain_mlp).astype(BF)
    gate_up = jnp.einsum("td,dcf->ctf", mlp_input, w_in, preferred_element_type=F32)
    activated, gelu_back = jax.vjp(gated_gelu, gate_up[0], gate_up[1])
    activated_low = activated.astype(BF)
    grad_activated = nt(cotangent, w_mlp_out)
    grad_gate, grad_up = gelu_back(grad_activated)
    grad_gate_up = jnp.stack([grad_gate, grad_up]).astype(BF)
    grad_normed_two = add_tp(
        jnp.einsum("ctf,dcf->td", grad_gate_up, w_in, preferred_element_type=F32)
    )
    output = (middle + add_tp(nn(activated_low, w_mlp_out))).astype(BF)

    keep_mlp, give_mlp = choose(mlp_input.T)
    rows_mlp = jnp.concatenate([keep_mlp, swap_core(give_mlp)], axis=1)
    columns_mlp = jnp.concatenate([grad_gate_up, swap_core(grad_gate_up)], axis=1)
    part_in = jnp.einsum("dt,ctf->dcf", rows_mlp, columns_mlp, preferred_element_type=F32)
    keep_cot, give_cot = choose(cotangent.T)
    rows_cot = jnp.concatenate([keep_cot, swap_core(give_cot)], axis=1)
    columns_cot = jnp.concatenate([activated_low, swap_core(activated_low)], axis=0)
    part_mlp = nn(rows_cot, columns_cot)
    grad_w_in = scatter(part_in.astype(BF).reshape(chips * mine, 2 * units)).astype(F32)
    grad_w_mlp_out = scatter(part_mlp.astype(BF)).astype(F32).T

    grad_middle = cotangent.astype(F32) + standardise_back(
        grad_normed_two, gain_mlp, normed_two, scale_two
    )
    grad_middle_low = grad_middle.astype(BF)
    grad_heads = nt(w_attn_out, grad_middle_low).astype(BF).reshape(heads, HD, width)
    grad_received = exchange(grad_heads)

    keep_out, give_out = choose(grad_middle_low.T)
    rows_out = jnp.concatenate([keep_out, swap_core(give_out)], axis=1)
    columns_out = jnp.concatenate([attn_flat_t, swap_core(attn_flat_t)], axis=1)
    part_out = nt(rows_out, columns_out)
    grad_w_attn_out = scatter(part_out.astype(BF)).astype(F32).T

    grad_q, grad_kv = attend_back(own, others, grad_received, attended, lse)
    total_kv = grad_kv[0]
    for step in range(1, 2 * copies):
        total_kv = total_kv + shift_keys(grad_kv[step], -step)
    grad_own = jnp.concatenate(
        [
            rotate_back(grad_q, cos_all, sin_all),
            rotate_back(total_kv[:, :HD], cos_all, sin_all),
            total_kv[:, HD:],
        ],
        axis=1,
    ).astype(BF)
    grad_back = exchange(grad_own).reshape(heads, 3, HD, width)
    grad_back = grad_back.transpose(1, 0, 2, 3).reshape(3, inner, width)
    grad_normed_one = add_tp(
        jnp.einsum("cft,dcf->td", grad_back, w_qkv, preferred_element_type=F32)
    )
    if copies == 1:
        part_qkv = head_weight(rows_in, grad_own, swap_core(grad_own))
        blocks_qkv = exchange(part_qkv.reshape(chips, mine, 3 * HD))
        blocks_qkv = blocks_qkv.reshape(heads, mine, 3, HD).astype(F32)
        grad_w_qkv = blocks_qkv.transpose(1, 2, 0, 3).reshape(mine, 3, inner)
    else:
        keep_in, give_in = choose(attn_input.T)
        rows_in = jnp.concatenate([keep_in, swap_core(give_in)], axis=1)
        columns_in = jnp.concatenate([grad_back, swap_core(grad_back)], axis=2)
        part_qkv = jnp.einsum("dt,cft->dcf", rows_in, columns_in, preferred_element_type=F32)
        grad_w_qkv = scatter(part_qkv.astype(BF).reshape(chips * mine, 3 * inner))
        grad_w_qkv = grad_w_qkv.astype(F32).reshape(mine, 3, inner)
    grad_input = grad_middle + standardise_back(grad_normed_one, gain_attn, normed_one, scale_one)

    first = me * mine
    rows_w_qkv = lax.dynamic_slice_in_dim(w_qkv, first, mine, 0).astype(F32)
    rows_w_in = lax.dynamic_slice_in_dim(w_in, first, mine, 0).astype(F32)
    grad_w_in = grad_w_in.reshape(mine, 2, units)
    grad_gains = sum_tp(
        jnp.stack(
            [
                jnp.sum(rows_w_qkv * grad_w_qkv, axis=(1, 2)),
                jnp.sum(rows_w_in * grad_w_in, axis=(1, 2)),
            ]
        )
    )
    grad_gain_attn = grad_gains[0] / lax.dynamic_slice_in_dim(gain_attn, first, mine, 0)
    grad_gain_mlp = grad_gains[1] / lax.dynamic_slice_in_dim(gain_mlp, first, mine, 0)
    return (
        output,
        grad_input,
        grad_gain_attn,
        grad_gain_mlp,
        grad_w_qkv,
        grad_w_attn_out,
        grad_w_in,
        grad_w_mlp_out,
    )


def solution(mesh):
    in_specs = (
        P("ctx", None),
        P("ctx", None),
        P(),
        P(),
        P(None, None, "tp"),
        P("tp", None),
        P(None, None, "tp"),
        P("tp", None),
    )
    out_specs = (
        P("ctx", None),
        P("ctx", None),
        P("ctx"),
        P("ctx"),
        P("ctx", None, "tp"),
        P("tp", "ctx"),
        P("ctx", None, "tp"),
        P("tp", "ctx"),
    )
    body = functools.partial(layer, mesh.shape["ctx"], mesh.shape["tp"])
    return jax.shard_map(body, mesh=mesh, in_specs=in_specs, out_specs=out_specs, check_vma=False)
```

time: 739 us -> 366 us (0.50)
  waiting for transfers between devices: 484 us -> 203 us
  matrix products: 95.9 us -> 24 us
  blocking collectives: 74 us -> 16 us
  starting transfers between devices: 0.67 us -> 28.7 us
  Pallas kernels: 0 us -> 19.6 us
  local copies, waits for them, and re-layouts: 39.8 us -> 30.2 us
    reduce_scatter x4 -> x2, waiting for transfers between devices: 329 us -> 63.3 us  [scatter(): lax.psum_scatter(values, 'ctx', scatter_dimension=0, tiled=True, axis_ind...]
    all_gather x4 -> x1, waiting for transfers between devices: 109 us -> 35.4 us  [layer(): lax.all_gather(both_in, 'ctx', axis=0, axis_index_groups=same_core)]
    dot_general x26 -> x11, matrix products: 95.9 us -> 24 us  [the longest x6 10.4 us: dot(): return lax.dot_general(a, b, (dims, ((), ())), preferred_element_type=F32)]
    unnamed x11 -> x5, waiting for transfers between devices: 0.7 us -> 47.8 us
    psum x3 -> x0, waiting for transfers between devices: 45.5 us -> none  [the longest x1 22.7 us: shards(): lax.psum(jnp.einsum('tcf,dcf->td', grad_gate_up, w_in, preferred_element_...]
    all_gather x2 -> x0, blocking collectives: 40.3 us -> none  [the longest x1 21.1 us: shards(): lax.all_gather(log_total, 'ctx', axis=0, tiled=True)]
    all_to_all x0 -> x4, waiting for transfers between devices: none -> 36.9 us  [exchange(): return lax.all_to_all(values, 'ctx', 0, 0, axis_index_groups=head_groups)]
    unnamed x1 -> x0, blocking collectives: 33.7 us -> none
  transfers between devices with their start and end apart: 11 -> 23, of which waited for: 10 -> 13; matrix products, arithmetic and copies ran while one was open for 10% -> 18% of each run, Pallas kernels for 0% -> 5%
where the time goes in v1:
time: 366 us; the launch traced here: 365 us
  waiting for transfers between devices  203 us (55%)
  local copies, waits for them, and re-layouts  30.2 us (8%)
  other arithmetic  28.9 us (8%)
  starting transfers between devices  28.7 us (8%)
  matrix products  24 us (7%)
  Pallas kernels  19.6 us (5%)
  blocking collectives  16 us (4%)
  between operations  14.2 us (4%)
    reduce_scatter x2, waiting for transfers between devices, scatter(): lax.psum_scatter(values, 'ctx', scatter_dimension=0, tiled=True, axis_ind...  63.3 us
    unnamed x5, waiting for transfers between devices  47.8 us
    all_to_all x4, waiting for transfers between devices, exchange(): return lax.all_to_all(values, 'ctx', 0, 0, axis_index_groups=head_groups)  36.9 us
    all_gather x1, waiting for transfers between devices, layer(): lax.all_gather(both_in, 'ctx', axis=0, axis_index_groups=same_core)  35.4 us
    all_to_all x4, starting transfers between devices, exchange(): return lax.all_to_all(values, 'ctx', 0, 0, axis_index_groups=head_groups)  20.1 us
    ppermute x4, waiting for transfers between devices, add_tp(): other = lax.ppermute(low, 'tp', [(0, 1), (1, 0)])  17.3 us
    all_to_all x1, blocking collectives, exchange(): return lax.all_to_all(values, 'ctx', 0, 0, axis_index_groups=head_groups)  16 us
    dot_general x6, matrix products, dot(): return lax.dot_general(a, b, (dims, ((), ())), preferred_element_type=F32)  10.4 us
  transfers between devices with their start and end apart: 23, of which 13 were waited for; matrix products, arithmetic and copies ran while one was open for 18% of the time, Pallas kernels for 5%

profile of v1, /device:TPU:0, one launch (start us, length us, event | category | flops | bytes accessed | tf_op | source)
XLA Modules:
  0.0 364.6 jit_solution(473666758692878803)
XLA Ops:
  9.6 2.7 convolution_bitcast_fusion.1
  14.9 1.7 copy.58
  16.9 1.7 pad_maximum_fusion.1
  18.5 7.3 %all-to-all-start = ((bf16[8,192,128]{2,1,0:T(8,128)(2,1)}), bf16[8,192,128]{2,1,0:T(8,128)(2,1)S(1)}, u32[]{:S(2)}, u32[]{:S(2)}) async-start(bf16[8,192,128]{2,1,0:T(8,128)(2,1)} %pad_maximum_fusion.1), calls=%async_computation | async-start | bytes 786432 | tf_op jit(solution)/shard_map/all_to_all | solution.py:252
  25.8 11.7 %all-to-all-done.own_ref = bf16[8,192,128]{2,1,0:T(8,128)(2,1)S(1)} async-done(((bf16[8,192,128]{2,1,0:T(8,128)(2,1)}), bf16[8,192,128]{2,1,0:T(8,128)(2,1)S(1)}, u32[]{:S(2)}, u32[]{:S(2)}) %all-to-all-start) | async-done | bytes 393248 | tf_op jit(solution)/shard_map/all_to_all | solution.py:252
  41.6 7.0 %attend.1 = (f32[8,64,128]{2,1,0:T(8,128)}, bf16[8,64,128]{2,1,0:T(8,128)(2,1)}, f32[8,1,128]{2,1,0:T(1,128)}) custom-call(bf16[8,192,128]{2,1,0:T(8,128)(2,1)} %copy-done.11, bf16[8,128,128]{2,1,0:T(8,128)(2,1)} %collective-permute-done.1.refs_0_), custom_call_target="tpu_custom_call" | custom-call | flops 536870912 | bytes 786432 | tf_op jit(solution)/shard_map/attend/pallas_call | solution.py:96
  48.6 4.0 %all-to-all-start.1 = ((bf16[8,64,128]{2,1,0:T(8,128)(2,1)}), bf16[8,64,128]{2,1,0:T(8,128)(2,1)}, u32[]{:S(2)}, u32[]{:S(2)}) async-start(bf16[8,64,128]{2,1,0:T(8,128)(2,1)} %get-tuple-element.15), calls=%async_computation.1 | async-start | bytes 262144 | tf_op jit(solution)/shard_map/all_to_all | solution.py:252
  54.3 5.9 %all-to-all-done.1 = bf16[8,64,128]{2,1,0:T(8,128)(2,1)} async-done(((bf16[8,64,128]{2,1,0:T(8,128)(2,1)}), bf16[8,64,128]{2,1,0:T(8,128)(2,1)}, u32[]{:S(2)}, u32[]{:S(2)}) %all-to-all-start.1) | async-done | bytes 131104 | tf_op jit(solution)/shard_map/all_to_all | solution.py:252
  60.1 1.6 convolution_convert_fusion.3
  61.8 1.5 collective-permute-start.2
  64.3 4.5 %collective-permute-done.2 = bf16[128,1024]{1,0:T(8,128)(2,1)S(1)} collective-permute-done((bf16[128,1024]{1,0:T(8,128)(2,1)S(1)}, bf16[128,1024]{1,0:T(8,128)(2,1)S(1)}, u32[]{:S(2)}, u32[]{:S(2)}) %collective-permute-start.2) | collective-permute-done | bytes 262176 | tf_op jit(solution)/shard_map/ppermute | solution.py:269
  69.3 4.4 %convolution_bitcast_fusion = f32[2,128,1312]{1,2,0:T(8,128)S(1)} fusion(bf16[1024,2,1312]{0,2,1:T(8,128)(2,1)} %param.14, f32[128,1024]{1,0:T(8,128)S(1)} %get-tuple-element.39, f32[1024]{0:T(1024)S(1)} %copy-done.13, f32[128]{0:T(128)S(1)} %add_rsqrt_fusion, f32[128]{0:T(128)S(1)} %broadcast_multiply_fusion.4), kind=kOutput, calls=%fused_computation.2 | convolution fusion | flops 688390144 | bytes 7246848 | tf_op jit(solution)/shard_map/td,dcf->ctf/dot_general | solution.py:336
  73.6 1.6 fusion.45
  76.5 1.5 collective-permute-start.4
  79.3 6.1 %collective-permute-done.4 = bf16[128,1024]{1,0:T(8,128)(2,1)S(1)} collective-permute-done((bf16[128,1024]{1,0:T(8,128)(2,1)S(1)}, bf16[128,1024]{1,0:T(8,128)(2,1)S(1)}, u32[]{:S(2)}, u32[]{:S(2)}) %collective-permute-start.4) | collective-permute-done | bytes 262176 | tf_op jit(solution)/shard_map/ppermute | solution.py:269
  86.3 1.9 collective-permute-done.3
  89.3 1.8 copy.65
  91.1 1.8 constant_dynamic-slice_fusion.1
  94.3 2.1 convolution_convert_fusion.2
  97.4 2.0 pad_maximum_fusion
  99.5 1.8 copy.64
  103.7 3.8 %convolution_convert_fusion = bf16[512,2,1312]{0,2,1:T(8,128)(2,1)} fusion(bf16[2,128,1312]{1,2,0:T(8,128)(2,1)} %collective-permute-done.9, bf16[1,128,1312]{1,2,0:T(8,128)(2,1)} %copy-done.4, bf16[1,128,1312]{1,2,0:T(8,128)(2,1)} %copy-done.3, bf16[512,128]{1,0:T(8,128)(2,1)S(1)} %collective-permute-done.8, bf16[512,128]{1,0:T(8,128)(2,1)S(1)} %bitcast.208), kind=kOutput, calls=%fused_computation | convolution fusion | flops 693764096 | bytes 4292608 | tf_op jit(solution)/shard_map/dt,ctf->dcf/dot_general | solution.py:350
  107.5 4.5 %copy.69 = bf16[512,2624]{1,0:T(8,128)(2,1)} copy(bf16[512,2624]{0,1:T(8,128)(2,1)} %bitcast.188) | data formatting | bytes 5373952
  112.0 2.4 fusion.7
  114.4 1.7 copy.59
  116.1 4.7 %all-to-all-start.2 = ((bf16[8,64,128]{2,1,0:T(8,128)(2,1)}), bf16[8,64,128]{2,1,0:T(8,128)(2,1)}, u32[]{:S(2)}, u32[]{:S(2)}) async-start(bf16[8,64,128]{2,1,0:T(8,128)(2,1)} %bitcast.200), calls=%async_computation.2 | async-start | bytes 262144 | tf_op jit(solution)/shard_map/all_to_all | solution.py:252
  121.5 7.1 %all-to-all-done.2.refs_1_ = bf16[8,64,128]{2,1,0:T(8,128)(2,1)} async-done(((bf16[8,64,128]{2,1,0:T(8,128)(2,1)}), bf16[8,64,128]{2,1,0:T(8,128)(2,1)}, u32[]{:S(2)}, u32[]{:S(2)}) %all-to-all-start.2) | async-done | bytes 131104 | tf_op jit(solution)/shard_map/all_to_all | solution.py:252
  128.6 8.9 %attend_back.1 = (f32[8,64,128]{2,1,0:T(8,128)}, f32[2,8,128,128]{3,2,1,0:T(8,128)}) custom-call(bf16[8,192,128]{2,1,0:T(8,128)(2,1)} %copy-done.11, bf16[8,128,128]{2,1,0:T(8,128)(2,1)} %collective-permute-done.1.refs_0_, bf16[8,64,128]{2,1,0:T(8,128)(2,1)} %all-to-all-done.2.refs_1_, f32[8,64,128]{2,1,0:T(8,128)} %get-tuple-element.17.refs_2_, ...), custom_call_target="tpu_custom_call" | custom-call | flops 1342177280 | bytes 1572864 | tf_op jit(solution)/shard_map/attend_back/pallas_call | solution.py:175
  137.5 1.9 slice_bitcast_fusion.1
  139.4 2.8 convolution_convert_fusion.1
  142.3 1.7 fusion.80
  143.9 1.5 fusion.79
  148.7 16.0 %all_to_all.25 = bf16[8,192,128]{2,1,0:T(8,128)(2,1)S(1)} all-to-all(bf16[8,192,128]{2,1,0:T(8,128)(2,1)S(1)} %fusion.75.own_ref), channel_id=1, replica_groups={{0,4,8,12,16,20,24,28},{2,6,10,14,18,22,26,30},{1,5,9,13,17,21,25,29},{..., dimensions={0} | all-to-all | bytes 786432 | tf_op jit(solution)/shard_map/all_to_all | solution.py:252
  164.7 1.9 fusion.6
  166.6 1.5 collective-permute-start.6
  168.0 1.5 convert_bitcast_fusion.2
  169.6 4.7 %collective-permute-done.6 = bf16[128,1024]{1,0:T(8,128)(2,1)} collective-permute-done((bf16[128,1024]{1,0:T(8,128)(2,1)}, bf16[128,1024]{1,0:T(8,128)(2,1)}, u32[]{:S(2)}, u32[]{:S(2)}) %collective-permute-start.6) | collective-permute-done | bytes 262176 | tf_op jit(solution)/shard_map/ppermute | solution.py:269
  175.6 35.4 %all-gather.3.cloned.1.call-done = bf16[16,512,128]{2,1,0:T(8,128)(2,1)} async-done(((bf16[2,512,128]{2,1,0:T(8,128)(2,1)}), bf16[16,512,128]{2,1,0:T(8,128)(2,1)}) %all-gather.3.cloned.1.call-update) | async-done | bytes 2097168 | tf_op jit(solution)/shard_map/all_gather | solution.py:331
  211.0 3.7 %head_weight.1 = bf16[512,192]{1,0:T(8,128)(2,1)} custom-call(bf16[8,2,512,128]{3,2,1,0:T(8,128)(2,1)} %bitcast.189, bf16[8,192,128]{2,1,0:T(8,128)(2,1)} %copy-done.7, bf16[8,192,128]{2,1,0:T(8,128)(2,1)} %collective-permute-done.7.other_ref), custom_call_target="tpu_custom_call" | custom-call | flops 402653184 | bytes 2097152 | tf_op jit(solution)/shard_map/head_weight/pallas_call | solution.py:206
  214.7 4.1 %all-to-all-start.4 = ((bf16[8,64,192]{2,1,0:T(8,128)(2,1)}), bf16[8,64,192]{2,1,0:T(8,128)(2,1)}, u32[]{:S(2)}, u32[]{:S(2)}) async-start(bf16[8,64,192]{2,1,0:T(8,128)(2,1)} %bitcast.196), calls=%async_computation.4 | async-start | bytes 524288 | tf_op jit(solution)/shard_map/all_to_all | solution.py:252
  218.7 2.1 fusion.40
  220.8 12.2 %all-to-all-done.4 = bf16[8,64,192]{2,1,0:T(8,128)(2,1)} async-done(((bf16[8,64,192]{2,1,0:T(8,128)(2,1)}), bf16[8,64,192]{2,1,0:T(8,128)(2,1)}, u32[]{:S(2)}, u32[]{:S(2)}) %all-to-all-start.4) | async-done | bytes 196640 | tf_op jit(solution)/shard_map/all_to_all | solution.py:252
  233.0 1.9 copy.62
  239.8 47.0 %reduce-scatter.10.cloned.1.call-done = bf16[64,2624]{1,0:T(8,128)(2,1)} async-done(((bf16[512,2624]{1,0:T(8,128)(2,1)}), bf16[64,2624]{1,0:T(8,128)(2,1)}) %reduce-scatter.10.cloned.1.call-update) | async-done | bytes 335888
  288.1 1.5 multiply_reduce_fusion
  289.7 1.5 collective-permute-start.10
  291.2 63.3 %reduce-scatter.8.cloned.1.call-done = bf16[64,1312]{1,0:T(8,128)(2,1)} async-done(((bf16[512,1312]{1,0:T(8,128)(2,1)}), bf16[64,1312]{1,0:T(8,128)(2,1)}) %reduce-scatter.8.cloned.1.call-update) | async-done | bytes 167952 | tf_op jit(solution)/shard_map/reduce_scatter | solution.py:285
  354.5 1.7 convert_bitcast_fusion.1
  (118 shorter events, 34.8 us)
Async XLA Ops:
  7.2 56.2 %copy-start = (bf16[1312,1024]{1,0:T(8,128)(2,1)S(1)}, bf16[1312,1024]{1,0:T(8,128)(2,1)}, u32[]{:S(2)}) copy-start(bf16[1312,1024]{1,0:T(8,128)(2,1)} %param.15) | copy-start | bytes 8060932
  12.3 26.1 %copy-start.2 = (bf16[128,1024]{1,0:T(8,128)(2,1)S(1)}, bf16[128,1024]{1,0:T(8,128)(2,1)}, u32[]{:S(2)}) copy-start(bf16[128,1024]{1,0:T(8,128)(2,1)} %param.8) | copy-start | bytes 786436
  12.3 26.1 %copy-start.15 = (f32[1024]{0:T(1024)S(1)}, f32[1024]{0:T(1024)}, u32[]{:S(2)}) copy-start(f32[1024]{0:T(1024)} %param.10) | copy-start | bytes 12292
  18.5 19.0 %all-to-all-start = ((bf16[8,192,128]{2,1,0:T(8,128)(2,1)}), bf16[8,192,128]{2,1,0:T(8,128)(2,1)S(1)}, u32[]{:S(2)}, u32[]{:S(2)}) async-start(bf16[8,192,128]{2,1,0:T(8,128)(2,1)} %pad_maximum_fusion.1), calls=%async_computation | async-start | bytes 786432 | tf_op jit(solution)/shard_map/all_to_all | solution.py:252
  37.5 0.8 copy-start.11
  38.3 3.4 collective-permute-start.1
  39.3 13.4 %copy-start.5 = (bf16[128,1024]{1,0:T(8,128)(2,1)S(1)}, bf16[128,1024]{1,0:T(8,128)(2,1)}, u32[]{:S(2)}) copy-start(bf16[128,1024]{1,0:T(8,128)(2,1)} %param.9) | copy-start | bytes 786436
  41.2 12.4 %copy-start.12 = (bf16[8,1,64,128]{3,2,1,0:T(8,128)(2,1)S(1)}, bf16[8,1,64,128]{3,2,1,0:T(8,128)(2,1)}, u32[]{:S(2)}) copy-start(bf16[8,1,64,128]{3,2,1,0:T(8,128)(2,1)} %get-tuple-element.56) | copy-start | bytes 393220
  41.2 12.3 %collective-permute-start = (bf16[512,128]{1,0:T(8,128)(2,1)}, bf16[512,128]{1,0:T(8,128)(2,1)S(1)}, u32[]{:S(2)}, u32[]{:S(2)}) collective-permute-start(bf16[512,128]{1,0:T(8,128)(2,1)} %bitcast.3), channel_id=1, source_target_pairs={{0,2},{2,0},{4,6},{6,4},{8,10},{10,8},{12,14},{14,12},{16,18},{18,... | collective-permute-start | bytes 393224 | tf_op jit(solution)/shard_map/ppermute | solution.py:255
  48.6 11.5 %all-to-all-start.1 = ((bf16[8,64,128]{2,1,0:T(8,128)(2,1)}), bf16[8,64,128]{2,1,0:T(8,128)(2,1)}, u32[]{:S(2)}, u32[]{:S(2)}) async-start(bf16[8,64,128]{2,1,0:T(8,128)(2,1)} %get-tuple-element.15), calls=%async_computation.1 | async-start | bytes 262144 | tf_op jit(solution)/shard_map/all_to_all | solution.py:252
  52.6 115.4 %reduce-scatter.6.cloned.1.call-start = ((), (), s32[]{:S(2)}) async-start(), calls=%async_computation.8 | async-start | bytes 589824 | tf_op jit(solution)/shard_map/reduce_scatter | solution.py:285
  61.8 7.5 %copy-start.13 = (f32[1024]{0:T(1024)S(1)}, f32[1024]{0:T(1024)}, u32[]{:S(2)}) copy-start(f32[1024]{0:T(1024)} %param.11) | copy-start | bytes 12292
  61.8 7.0 %collective-permute-start.2 = (bf16[128,1024]{1,0:T(8,128)(2,1)S(1)}, bf16[128,1024]{1,0:T(8,128)(2,1)S(1)}, u32[]{:S(2)}, u32[]{:S(2)}) collective-permute-start(bf16[128,1024]{1,0:T(8,128)(2,1)S(1)} %convolution_convert_fusion.3), channel_id=1, source_target_pairs={{0,1},{1,0},{2,3},{3,2},{4,5},{5,4},{6,7},{7,6},{8,9},{9,8},{10,11... | collective-permute-start | bytes 786440 | tf_op jit(solution)/shard_map/ppermute | solution.py:269
  64.2 28.7 %collective-permute-start.12 = (bf16[512,128]{1,0:T(8,128)(2,1)}, bf16[512,128]{1,0:T(8,128)(2,1)}, u32[]{:S(2)}, u32[]{:S(2)}) collective-permute-start(bf16[512,128]{1,0:T(8,128)(2,1)} %bitcast.10), channel_id=1, source_target_pairs={{0,2},{2,0},{4,6},{6,4},{8,10},{10,8},{12,14},{14,12},{16,18},{18,... | collective-permute-start | bytes 393224 | tf_op jit(solution)/shard_map/ppermute | solution.py:255
  69.2 6.2 %slice-start = ((s8[5373952]{0:T(1024)(128)(4,1)}), s8[4194304]{0:T(1024)(128)(4,1)S(1)}, s32[]{:S(2)}) async-start(s8[5373952]{0:T(1024)(128)(4,1)} %bitcast.184), calls=%async_computation.12 | async-start | bytes 8388608
  69.3 6.2 %slice-start.1 = ((s8[5373952]{0:T(1024)(128)(4,1)}), s8[1179648]{0:T(1024)(128)(4,1)S(1)}, s32[]{:S(2)}) async-start(s8[5373952]{0:T(1024)(128)(4,1)} %bitcast.184), calls=%async_computation.13 | async-start | bytes 2359296
  75.2 1.2 copy-start.3
  75.4 1.0 copy-start.4
  75.5 2.6 copy-start.9
  76.5 11.8 %copy-start.6 = (bf16[128,1024]{1,0:T(8,128)(2,1)S(1)}, bf16[128,1024]{1,0:T(8,128)(2,1)}, u32[]{:S(2)}) copy-start(bf16[128,1024]{1,0:T(8,128)(2,1)} %param.9) | copy-start | bytes 786436
  76.5 8.9 %collective-permute-start.4 = (bf16[128,1024]{1,0:T(8,128)(2,1)S(1)}, bf16[128,1024]{1,0:T(8,128)(2,1)S(1)}, u32[]{:S(2)}, u32[]{:S(2)}) collective-permute-start(bf16[128,1024]{1,0:T(8,128)(2,1)S(1)} %fusion.5), channel_id=1, source_target_pairs={{0,1},{1,0},{2,3},{3,2},{4,5},{5,4},{6,7},{7,6},{8,9},{9,8},{10,11... | collective-permute-start | bytes 786440 | tf_op jit(solution)/shard_map/ppermute | solution.py:269
  78.7 9.6 %collective-permute-start.3 = (bf16[128,1024]{1,0:T(8,128)(2,1)S(1)}, bf16[128,1024]{1,0:T(8,128)(2,1)S(1)}, u32[]{:S(2)}, u32[]{:S(2)}) collective-permute-start(bf16[128,1024]{1,0:T(8,128)(2,1)S(1)} %convolution_convert_fusion.4), channel_id=1, source_target_pairs={{0,1},{1,0},{2,3},{3,2},{4,5},{5,4},{6,7},{7,6},{8,9},{9,8},{10,11... | collective-permute-start | bytes 786440 | tf_op jit(solution)/shard_map/ppermute | solution.py:269
  92.9 1.3 collective-permute-start.11
  96.4 114.6 %all-gather.3.cloned.1.call-start = ((), (), s32[]{:S(2)}) async-start(), calls=%async_computation.10 | async-start | bytes 2359296 | tf_op jit(solution)/shard_map/all_gather | solution.py:331
  97.1 189.7 %reduce-scatter.10.cloned.1.call-start = ((), (), s32[]{:S(2)}) async-start(), calls=%async_computation.11 | async-start | bytes 3096576
  99.4 4.4 %collective-permute-start.9 = (bf16[2,128,1312]{1,2,0:T(8,128)(2,1)}, bf16[2,128,1312]{1,2,0:T(8,128)(2,1)}, u32[]{:S(2)}, u32[]{:S(2)}) collective-permute-start(bf16[2,128,1312]{1,2,0:T(8,128)(2,1)} %pad_maximum_fusion), channel_id=1, source_target_pairs={{0,2},{2,0},{4,6},{6,4},{8,10},{10,8},{12,14},{14,12},{16,18},{18,... | collective-permute-start | bytes 2015240 | tf_op jit(solution)/shard_map/ppermute | solution.py:255
  102.3 1.4 collective-permute-start.8
  116.1 12.5 %all-to-all-start.2 = ((bf16[8,64,128]{2,1,0:T(8,128)(2,1)}), bf16[8,64,128]{2,1,0:T(8,128)(2,1)}, u32[]{:S(2)}, u32[]{:S(2)}) async-start(bf16[8,64,128]{2,1,0:T(8,128)(2,1)} %bitcast.200), calls=%async_computation.2 | async-start | bytes 262144 | tf_op jit(solution)/shard_map/all_to_all | solution.py:252
  120.8 233.7 %reduce-scatter.8.cloned.1.call-start = ((), (), s32[]{:S(2)}) async-start(), calls=%async_computation.9 | async-start | bytes 1622016 | tf_op jit(solution)/shard_map/reduce_scatter | solution.py:285
  120.9 18.5 %collective-permute-start.14 = (bf16[128,1312]{0,1:T(8,128)(2,1)}, bf16[128,1312]{0,1:T(8,128)(2,1)}, u32[]{:S(2)}, u32[]{:S(2)}) collective-permute-start(bf16[128,1312]{0,1:T(8,128)(2,1)} %copy-done.9), channel_id=1, source_target_pairs={{0,2},{2,0},{4,6},{6,4},{8,10},{10,8},{12,14},{14,12},{16,18},{18,... | collective-permute-start | bytes 1007624 | tf_op jit(solution)/shard_map/ppermute | solution.py:255
  121.1 18.3 %collective-permute-start.13 = (bf16[512,128]{1,0:T(8,128)(2,1)}, bf16[512,128]{1,0:T(8,128)(2,1)}, u32[]{:S(2)}, u32[]{:S(2)}) collective-permute-start(bf16[512,128]{1,0:T(8,128)(2,1)} %bitcast.204), channel_id=1, source_target_pairs={{0,2},{2,0},{4,6},{6,4},{8,10},{10,8},{12,14},{14,12},{16,18},{18,... | collective-permute-start | bytes 393224 | tf_op jit(solution)/shard_map/ppermute | solution.py:255
  128.6 10.8 %copy-start.10 = (bf16[128,1312]{0,1:T(8,128)(2,1)S(1)}, bf16[128,1312]{0,1:T(8,128)(2,1)}, u32[]{:S(2)}) copy-start(bf16[128,1312]{0,1:T(8,128)(2,1)} %copy-done.9) | copy-start | bytes 1007620
  128.6 10.8 %copy-start.14 = (bf16[8,1,64,128]{3,2,1,0:T(8,128)(2,1)S(1)}, bf16[8,1,64,128]{3,2,1,0:T(8,128)(2,1)}, u32[]{:S(2)}) copy-start(bf16[8,1,64,128]{3,2,1,0:T(8,128)(2,1)} %get-tuple-element.50) | copy-start | bytes 393220
  139.4 6.1 %collective-permute-start.5 = (f32[8,128,128]{2,1,0:T(8,128)}, f32[8,128,128]{2,1,0:T(8,128)}, u32[]{:S(2)}, u32[]{:S(2)}) collective-permute-start(f32[8,128,128]{2,1,0:T(8,128)} %slice_bitcast_fusion.1), channel_id=1, source_target_pairs={{0,2},{2,0},{4,6},{6,4},{8,10},{10,8},{12,14},{14,12},{16,18},{18,... | collective-permute-start | bytes 1572872 | tf_op jit(solution)/shard_map/ppermute | solution.py:264
  142.3 22.5 %copy-start.1 = (bf16[1024,3,512]{2,0,1:T(8,128)(2,1)S(1)}, bf16[1024,3,512]{2,0,1:T(8,128)(2,1)}, u32[]{:S(2)}) copy-start(bf16[1024,3,512]{2,0,1:T(8,128)(2,1)} %param.12) | copy-start | bytes 9437188
  147.9 0.7 copy-start.7
  166.6 7.7 %collective-permute-start.6 = (bf16[128,1024]{1,0:T(8,128)(2,1)}, bf16[128,1024]{1,0:T(8,128)(2,1)}, u32[]{:S(2)}, u32[]{:S(2)}) collective-permute-start(bf16[128,1024]{1,0:T(8,128)(2,1)} %fusion.6), channel_id=1, source_target_pairs={{0,1},{1,0},{2,3},{3,2},{4,5},{5,4},{6,7},{7,6},{8,9},{9,8},{10,11... | collective-permute-start | bytes 786440 | tf_op jit(solution)/shard_map/ppermute | solution.py:269
  168.0 7.5 %collective-permute-start.7 = (bf16[8,192,128]{2,1,0:T(8,128)(2,1)}, bf16[8,192,128]{2,1,0:T(8,128)(2,1)}, u32[]{:S(2)}, u32[]{:S(2)}) collective-permute-start(bf16[8,192,128]{2,1,0:T(8,128)(2,1)} %copy-done.7), channel_id=1, source_target_pairs={{0,2},{2,0},{4,6},{6,4},{8,10},{10,8},{12,14},{14,12},{16,18},{18,... | collective-permute-start | bytes 1179656 | tf_op jit(solution)/shard_map/ppermute | solution.py:255
  214.7 18.4 %all-to-all-start.4 = ((bf16[8,64,192]{2,1,0:T(8,128)(2,1)}), bf16[8,64,192]{2,1,0:T(8,128)(2,1)}, u32[]{:S(2)}, u32[]{:S(2)}) async-start(bf16[8,64,192]{2,1,0:T(8,128)(2,1)} %bitcast.196), calls=%async_computation.4 | async-start | bytes 524288 | tf_op jit(solution)/shard_map/all_to_all | solution.py:252
  238.5 1.2 copy-start.8
  289.7 67.8 %collective-permute-start.10 = (f32[2,64]{1,0:T(2,128)S(1)}, f32[2,64]{1,0:T(2,128)S(1)}, u32[]{:S(2)}, u32[]{:S(2)}) collective-permute-start(f32[2,64]{1,0:T(2,128)S(1)} %pad_maximum_fusion.3), channel_id=1, source_target_pairs={{0,1},{1,0},{2,3},{3,2},{4,5},{5,4},{6,7},{7,6},{8,9},{9,8},{10,11... | collective-permute-start | bytes 1544 | tf_op jit(solution)/shard_map/ppermute | solution.py:275
Sparse Core Ops, SparseCore 0:
  96.5 63.2 reduce-scatter.5
  162.1 48.7 all-gather.2
  214.9 71.8 reduce-scatter.9
  290.5 64.0 reduce-scatter.7

commit v2 on v1

v2 whole, which is shorter than its diff:
```python
import functools
import math

import jax
import jax.numpy as jnp
from jax import lax
from jax.experimental import pallas as pl
from jax.experimental.pallas import tpu as pltpu
from jax.sharding import PartitionSpec as P

HD = 64
HALF = HD // 2
ROPE_BASE = 160000.0
NORM_EPS = 1e-05
BF = jnp.bfloat16
F32 = jnp.float32
VMEM_LIMIT = 60 * 1024 * 1024
MIDDLE_LIMIT = 32 * 1024 * 1024


def dot(a, b, dims):
    return lax.dot_general(a, b, (dims, ((), ())), preferred_element_type=F32)


def nn(a, b):
    return dot(a, b, ((1,), (0,)))


def nt(a, b):
    return dot(a, b, ((1,), (1,)))


def load_rows(parts, row, out_ref):
    for j, (ref, first) in enumerate(parts):
        blocks, width = ref.shape[0], ref.shape[2]
        for b in range(blocks):
            out_ref[j, b * width : (b + 1) * width, :] = ref[b, first + row : first + row + HD, :].T


def load_columns(parts, row, out_ref):
    for j, (ref, first) in enumerate(parts):
        blocks, width = ref.shape[0], ref.shape[2]
        for b in range(blocks):
            out_ref[j, :, b * width : (b + 1) * width] = ref[b, first + row : first + row + HD, :]


def attend_kernel(part_count, own_ref, *refs):
    others = refs[: part_count - 1]
    out_ref, low_ref, lse_ref, k_scr, vt_scr, s_scr = refs[part_count - 1 :]
    blocks, width = own_ref.shape[0], own_ref.shape[2]
    parts = [(r, HD) for r in (own_ref, *others)]
    load_rows(parts, 0, k_scr)
    load_columns(parts, HD, vt_scr)
    pair = s_scr.shape[2] // width

    @pl.loop(0, blocks // pair)
    def query_block(i):
        qt = jnp.concatenate([own_ref[pair * i + b, :HD, :] for b in range(pair)], axis=1)

        def score(j, top):
            s = nn(k_scr[j], qt)
            s_scr[j] = s
            return jnp.maximum(top, jnp.max(s, axis=0, keepdims=True))

        top = jnp.full((1, pair * width), -jnp.inf, F32)
        top = lax.fori_loop(0, part_count, score, top, unroll=part_count <= 2)

        def weigh(j, carry):
            total, acc = carry
            p = jnp.exp(s_scr[j] - top)
            return total + jnp.sum(p, axis=0, keepdims=True), acc + nn(vt_scr[j], p.astype(BF))

        start = (jnp.zeros((1, pair * width), F32), jnp.zeros((HD, pair * width), F32))
        total, acc = lax.fori_loop(0, part_count, weigh, start, unroll=part_count <= 2)
        attended = acc / total
        lse = top + jnp.log(total)
        for b in range(pair):
            cut = slice(b * width, (b + 1) * width)
            out_ref[pair * i + b] = attended[:, cut]
            low_ref[pair * i + b] = attended[:, cut].astype(BF)
            lse_ref[pair * i + b] = lse[:, cut]


def attend(own, others):
    blocks, unused, width = own.shape
    part_count = 1 + len(others)
    keys = blocks * width
    pair = 2 if blocks % 2 == 0 else 1
    flops = 4 * keys * keys * part_count * HD
    return pl.pallas_call(
        functools.partial(attend_kernel, part_count),
        out_shape=(
            jax.ShapeDtypeStruct((blocks, HD, width), F32),
            jax.ShapeDtypeStruct((blocks, HD, width), BF),
            jax.ShapeDtypeStruct((blocks, 1, width), F32),
        ),
        scratch_shapes=[
            pltpu.VMEM((part_count, keys, HD), BF),
            pltpu.VMEM((part_count, HD, keys), BF),
            pltpu.VMEM((part_count, keys, pair * width), F32),
        ],
        compiler_params=pltpu.CompilerParams(vmem_limit_bytes=VMEM_LIMIT),
        cost_estimate=pl.CostEstimate(
            flops=flops, bytes_accessed=4 * own.size, transcendentals=keys * keys * part_count
        ),
        name="attend",
    )(own, *others)


def turn_back(values, cosine, sine):
    first, second = values[:HALF], values[HALF:]
    return jnp.concatenate([first * cosine + second * sine, second * cosine - first * sine], axis=0)


def attend_back_kernel(part_count, own_ref, *refs):
    others = refs[: part_count - 1]
    refs = refs[part_count - 1 :]
    grad_ref, out_ref, lse_ref, cos_ref, sin_ref = refs[:5]
    dq_ref, dkv_ref = refs[5:7]
    dkv_others = refs[7 : 6 + part_count]
    k_scr, v_scr, kt_scr, dk_scr, dv_scr = refs[6 + part_count :]
    blocks, width = own_ref.shape[0], own_ref.shape[2]
    parts = [(r, HD) for r in (own_ref, *others)]
    load_rows(parts, 0, k_scr)
    load_rows(parts, HD, v_scr)
    load_columns(parts, 0, kt_scr)
    dk_scr[...] = jnp.zeros_like(dk_scr)
    dv_scr[...] = jnp.zeros_like(dv_scr)
    pair = 2 if blocks % 2 == 0 else 1

    @pl.loop(0, blocks // pair)
    def query_block(i):
        span = range(pair)
        qt = jnp.concatenate([own_ref[pair * i + b, :HD, :] for b in span], axis=1)
        gt = jnp.concatenate(
            [
                (grad_ref[0, pair * i + b].astype(F32) + grad_ref[1, pair * i + b].astype(F32)).astype(BF)
                for b in span
            ],
            axis=1,
        )
        ot = jnp.concatenate([out_ref[pair * i + b] for b in span], axis=1)
        lse = jnp.concatenate([lse_ref[pair * i + b] for b in span], axis=1)
        q, g = qt.T, gt.T
        delta = jnp.sum(gt.astype(F32) * ot, axis=0, keepdims=True)

        def one(j, dq):
            p = jnp.exp(nn(k_scr[j], qt) - lse)
            ds = (p * (nn(v_scr[j], gt) - delta)).astype(BF)
            dv_scr[j] += nn(p.astype(BF), g)
            dk_scr[j] += nn(ds, q)
            return dq + nn(kt_scr[j], ds)

        start = jnp.zeros((HD, pair * width), F32)
        dq = lax.fori_loop(0, part_count, one, start, unroll=part_count <= 2)
        for b in span:
            at = pair * i + b
            block = dq[:, b * width : (b + 1) * width] * (HD**-0.5)
            dq_ref[at] = turn_back(block, cos_ref[at], sin_ref[at]).astype(BF)

    for j, ref in enumerate((dkv_ref, *dkv_others)):
        for b in range(blocks):
            rows = slice(b * width, (b + 1) * width)
            ref[b, :HD, :] = dk_scr[j, rows, :].T
            ref[b, HD:, :] = dv_scr[j, rows, :].T


def attend_back(own, others, grad, attended, lse, cosine, sine):
    blocks, unused, width = own.shape
    part_count = 1 + len(others)
    keys = blocks * width
    flops = 10 * keys * keys * part_count * HD
    terms = jax.ShapeDtypeStruct((blocks, 2 * HD, width), F32)
    return pl.pallas_call(
        functools.partial(attend_back_kernel, part_count),
        out_shape=(jax.ShapeDtypeStruct((blocks, HD, width), BF), *[terms] * part_count),
        scratch_shapes=[
            pltpu.VMEM((part_count, keys, HD), BF),
            pltpu.VMEM((part_count, keys, HD), BF),
            pltpu.VMEM((part_count, HD, keys), BF),
            pltpu.VMEM((part_count, keys, HD), F32),
            pltpu.VMEM((part_count, keys, HD), F32),
        ],
        compiler_params=pltpu.CompilerParams(vmem_limit_bytes=VMEM_LIMIT),
        cost_estimate=pl.CostEstimate(
            flops=flops, bytes_accessed=8 * own.size, transcendentals=keys * keys * part_count
        ),
        name="attend_back",
    )(own, *others, grad, attended, lse, cosine, sine)


def combine_kernel(count, dq_ref, *refs):
    terms, (cos_ref, sin_ref, out_ref) = refs[:count], refs[count:]
    for b in range(dq_ref.shape[0]):
        total = terms[0][b]
        for ref in terms[1:]:
            total = total + ref[b]
        out_ref[b, :HD] = dq_ref[b]
        out_ref[b, HD : 2 * HD] = turn_back(total[:HD], cos_ref[b], sin_ref[b]).astype(BF)
        out_ref[b, 2 * HD :] = total[HD:].astype(BF)


def combine(dq, terms, cosine, sine):
    blocks, unused, width = dq.shape
    return pl.pallas_call(
        functools.partial(combine_kernel, len(terms)),
        out_shape=jax.ShapeDtypeStruct((blocks, 3 * HD, width), BF),
        compiler_params=pltpu.CompilerParams(vmem_limit_bytes=VMEM_LIMIT),
        name="combine",
    )(dq, *terms, cosine, sine)


def standardise(values):
    centred = values - jnp.mean(values, axis=-1, keepdims=True)
    spread = jnp.mean(centred * centred, axis=-1, keepdims=True)
    scale = lax.rsqrt(spread + NORM_EPS)
    return centred * scale, scale


def standardise_back(gradient, gain, normed, scale):
    y = gradient * gain
    along = jnp.mean(y * normed, axis=-1, keepdims=True)
    return scale * (y - jnp.mean(y, axis=-1, keepdims=True) - normed * along)


def project_kernel(hidden_ref, gain_ref, cos_ref, sin_ref, w_ref, packed_ref, input_ref):
    c = pl.program_id(0)
    heads = packed_ref.shape[0]

    @pl.when(c == 0)
    def norm():
        normed, unused = standardise(hidden_ref[...].astype(F32))
        input_ref[...] = (normed * gain_ref[...]).astype(BF)

    rows = nn(input_ref[...], w_ref[0]).T

    @pl.when(c == 2)
    def plain():
        for h in range(heads):
            packed_ref[h, 2 * HD :] = rows[h * HD : (h + 1) * HD].astype(BF)

    @pl.when(c < 2)
    def turned():
        cosine, sine = cos_ref[...], sin_ref[...]
        factor = jnp.where(c == 0, HD**-0.5, 1.0).astype(F32)
        at = pl.multiple_of(c * HD, HD)
        for h in range(heads):
            first, second = rows[h * HD : h * HD + HALF], rows[h * HD + HALF : (h + 1) * HD]
            both = jnp.concatenate(
                [first * cosine - second * sine, second * cosine + first * sine], axis=0
            )
            packed_ref[h, pl.ds(at, HD)] = (both * factor).astype(BF)


def project(hidden, gain, cosine, sine, weights):
    width, model = hidden.shape
    inner = weights.shape[2]
    heads = inner // HD

    def whole(*shape):
        return pl.BlockSpec(shape, lambda c: (0,) * len(shape))

    return pl.pallas_call(
        project_kernel,
        grid=(3,),
        in_specs=[
            whole(width, model),
            whole(1, model),
            whole(HALF, width),
            whole(HALF, width),
            pl.BlockSpec((1, model, inner), lambda c: (c, 0, 0)),
        ],
        out_specs=(whole(heads, 3 * HD, width), whole(width, model)),
        out_shape=(
            jax.ShapeDtypeStruct((heads, 3 * HD, width), BF),
            jax.ShapeDtypeStruct((width, model), BF),
        ),
        compiler_params=pltpu.CompilerParams(vmem_limit_bytes=VMEM_LIMIT),
        name="project",
    )(hidden, gain, cosine, sine, weights)


def middle_kernel(
    tp_ref,
    attn_ref,
    hidden_ref,
    cot_ref,
    gain_ref,
    own_ref,
    other_ref,
    w_in_ref,
    grad_act_ref,
    middle_ref,
    input_ref,
    act_ref,
    grad_ref,
    part_ref,
    heads_ref,
):
    tp = tp_ref[0]
    branch = nn(attn_ref[tp].T, own_ref[...]) + nn(attn_ref[1 - tp].T, other_ref[...])
    middle = hidden_ref[...].astype(F32) + branch
    middle_ref[...] = middle
    normed, scale = standardise(middle)
    gain = gain_ref[...]
    mlp_input = (normed * gain).astype(BF)
    input_ref[...] = mlp_input
    gate, up = nt(mlp_input, w_in_ref[0]), nt(mlp_input, w_in_ref[1])
    share = 0.5 * (1.0 + lax.erf(gate * (0.5**0.5)))
    slope = share + gate * jnp.exp(-0.5 * gate * gate) * ((2.0 * math.pi) ** -0.5)
    bent = gate * share
    grad_act = grad_act_ref[...]
    act_ref[...] = (bent * up).astype(BF)
    grad_gate = (slope * up * grad_act).astype(BF)
    grad_up = (bent * grad_act).astype(BF)
    grad_ref[0] = grad_gate
    grad_ref[1] = grad_up
    part = nn(grad_gate, w_in_ref[0]) + nn(grad_up, w_in_ref[1])
    part_ref[...] = part.astype(BF)
    grad = 0.5 * cot_ref[...].astype(F32) + standardise_back(part, gain, normed, scale)
    grad = grad.astype(BF)
    shape = heads_ref.shape[1:]
    heads_ref[tp] = nt(own_ref[...], grad).astype(BF).reshape(shape)
    heads_ref[1 - tp] = nt(other_ref[...], grad).astype(BF).reshape(shape)


def middle_part(tp, attn, hidden, cotangent, gain, own, other, w_in, grad_act):
    width, model = hidden.shape
    units = w_in.shape[1]
    inner = own.shape[0]
    vmem = pl.BlockSpec(memory_space=pltpu.VMEM)
    return pl.pallas_call(
        middle_kernel,
        in_specs=[pl.BlockSpec(memory_space=pltpu.SMEM)] + [vmem] * 8,
        out_shape=(
            jax.ShapeDtypeStruct((width, model), F32),
            jax.ShapeDtypeStruct((width, model), BF),
            jax.ShapeDtypeStruct((width, units), BF),
            jax.ShapeDtypeStruct((2, width, units), BF),
            jax.ShapeDtypeStruct((width, model), BF),
            jax.ShapeDtypeStruct((2, inner // HD, HD, width), BF),
        ),
        compiler_params=pltpu.CompilerParams(vmem_limit_bytes=MIDDLE_LIMIT),
        cost_estimate=pl.CostEstimate(
            flops=8 * width * model * (units + inner),
            bytes_accessed=2 * w_in.size + 4 * own.size,
            transcendentals=2 * width * units,
        ),
        name="middle_part",
    )(tp, attn, hidden, cotangent, gain, own, other, w_in, grad_act)


def project_back_kernel(grad_ref, w_ref, out_ref):
    heads = grad_ref.shape[0]
    total = jnp.zeros(out_ref.shape, F32)
    for c in range(3):
        rows = jnp.concatenate([grad_ref[h, c * HD : (c + 1) * HD, :] for h in range(heads)], axis=0)
        total += nt(rows.T, w_ref[c])
    out_ref[...] = total.astype(BF)


def project_back(grad, weights):
    width = grad.shape[2]
    return pl.pallas_call(
        project_back_kernel,
        out_shape=jax.ShapeDtypeStruct((width, weights.shape[1]), BF),
        compiler_params=pltpu.CompilerParams(vmem_limit_bytes=MIDDLE_LIMIT),
        cost_estimate=pl.CostEstimate(
            flops=2 * width * weights.size, bytes_accessed=2 * weights.size, transcendentals=0
        ),
        name="project_back",
    )(grad, weights)


def head_weight_kernel(count, ids_ref, own_ref, other_ref, *refs):
    out_ref = refs[count]
    width = own_ref.shape[2]
    total = jnp.zeros((refs[0].shape[0], own_ref.shape[1]), F32)
    whole = count if refs[count - 1].shape == refs[0].shape else count - 2
    for b in range(whole):
        at = ids_ref[b]
        total += nt(refs[b][:, :width], own_ref[at])
        total += nt(refs[b][:, width:], other_ref[at])
    if whole < count:
        at = ids_ref[whole]
        rows = jnp.concatenate([refs[whole][...], refs[whole + 1][...]], axis=0)
        total += nt(rows[:, :width], own_ref[at])
        total += nt(rows[:, width:], other_ref[at])
    out_ref[...] = total.astype(BF)


def head_weight(ids, own, other, rows):
    count = len(rows)
    vmem = pl.BlockSpec(memory_space=pltpu.VMEM)
    return pl.pallas_call(
        functools.partial(head_weight_kernel, count),
        in_specs=[pl.BlockSpec(memory_space=pltpu.SMEM)] + [vmem] * (2 + count),
        out_specs=vmem,
        out_shape=jax.ShapeDtypeStruct((rows[0].shape[0], own.shape[1]), BF),
        compiler_params=pltpu.CompilerParams(vmem_limit_bytes=VMEM_LIMIT),
        cost_estimate=pl.CostEstimate(
            flops=2 * count * rows[0].size * own.shape[1],
            bytes_accessed=2 * count * rows[0].size,
            transcendentals=0,
        ),
        name="head_weight",
    )(ids, own, other, *rows)


def mlp_weight_kernel(rows_in_ref, rows_out_ref, own_ref, other_ref, act_ref, act_other_ref, out_ref):
    chips, unused, mine, units = out_ref.shape
    for c in range(2):
        columns = jnp.concatenate([own_ref[c], other_ref[c]], axis=0)
        out_ref[:, c] = nn(rows_in_ref[...], columns).astype(BF).reshape(chips, mine, units)
    columns = jnp.concatenate([act_ref[...], act_other_ref[...]], axis=0)
    out_ref[:, 2] = nn(rows_out_ref[...], columns).astype(BF).reshape(chips, mine, units)


def mlp_weight(chips, rows_in, rows_out, own, other, act, act_other):
    mine = rows_in.shape[0] // chips
    units = act.shape[1]
    return pl.pallas_call(
        mlp_weight_kernel,
        out_shape=jax.ShapeDtypeStruct((chips, 3, mine, units), BF),
        compiler_params=pltpu.CompilerParams(vmem_limit_bytes=VMEM_LIMIT),
        cost_estimate=pl.CostEstimate(
            flops=6 * rows_in.size * units,
            bytes_accessed=6 * chips * mine * units + 12 * act.size,
            transcendentals=0,
        ),
        name="mlp_weight",
    )(rows_in, rows_out, own, other, act, act_other)


def layer(ctx_size, tp_size, hidden_in, cotangent, gain_attn, gain_mlp, w_qkv, w_attn_out, w_in, w_mlp_out):
    width = hidden_in.shape[0]
    model = hidden_in.shape[1]
    inner = w_qkv.shape[2]
    heads = inner // HD
    units = w_in.shape[2]
    chips = ctx_size // 2
    copies = chips // heads
    mine = model // ctx_size
    me = lax.axis_index("ctx")
    core = me % 2

    same_core = [[2 * p + k for p in range(chips)] for k in range(2)]
    head_groups = [
        [2 * (heads * g + p) + k for p in range(heads)] for g in range(copies) for k in range(2)
    ]

    wide_groups = [
        [(2 * (heads * g + p) + k) * tp_size + t for t in range(tp_size) for p in range(heads)]
        for g in range(copies)
        for k in range(2)
    ]

    def exchange_wide(values):
        return lax.all_to_all(values, ("ctx", "tp"), 0, 0, axis_index_groups=wide_groups)

    def exchange(values):
        return lax.all_to_all(values, "ctx", 0, 0, axis_index_groups=head_groups)

    def swap_core(values):
        return lax.ppermute(values, "ctx", [(c, c ^ 1) for c in range(ctx_size)])

    def shift_keys(values, step):
        ring = 2 * copies
        pairs = []
        for c in range(ctx_size):
            g, p, k = c // (2 * heads), (c // 2) % heads, c % 2
            t = (2 * g + k + step) % ring
            pairs.append((c, 2 * (heads * (t // 2) + p) + t % 2))
        return lax.ppermute(values, "ctx", pairs)

    def swap_tp(values):
        return lax.ppermute(values, "tp", [(0, 1), (1, 0)])

    def add_tp(low):
        return low.astype(F32) + swap_tp(low).astype(F32)

    def after(values, *earlier):
        return lax.optimization_barrier((values, earlier))[0]

    def ring_chip(position):
        position = position % chips
        up = 2 * position
        return jnp.where(position < chips // 2, up, 2 * chips - 1 - up)

    ring = [2 * q if q < chips // 2 else 2 * chips - 1 - 2 * q for q in range(chips)]
    place = {p: q for q, p in enumerate(ring)}

    def turn(values, step):
        pairs = [
            (2 * p + k, 2 * ring[(place[p] + step) % chips] + k)
            for p in range(chips)
            for k in range(2)
        ]
        return lax.ppermute(values, "ctx", pairs)

    chip = me // 2
    position = jnp.where(chip % 2 == 0, chip // 2, chips - 1 - chip // 2)
    ringed = copies == 1

    def picker(chip_ids):
        wanted = ((2 * chip_ids + core) * mine)[:, None] + jnp.arange(mine)[None, :]
        return (wanted.reshape(-1, 1) == jnp.arange(model)[None, :]).astype(BF)

    pick_plain = picker(jnp.arange(chips))
    pick_ring = picker(ring_chip(position + jnp.arange(chips))) if ringed else pick_plain

    def rows_of(pick, values):
        both = jnp.concatenate([values, swap_core(values)], axis=0)
        return nt(pick, both).astype(BF)

    class Sum:
        def __init__(self, parts):
            self.parts, self.right, self.left, self.step = parts, None, None, 0

        def advance(self, *earlier):
            self.step += 1
            half = chips // 2
            cut = self.parts.shape[-2] // 2
            right, left = self.parts[half + 1 - self.step], self.parts[half - 1 + self.step]
            if self.step == 1:
                right, left = right[..., :cut, :], left[..., cut:, :]
            elif self.step == 2:
                first = right[..., :cut, :].astype(F32) + self.right.astype(F32)
                right = jnp.concatenate([first.astype(BF), right[..., cut:, :]], axis=-2)
                last = left[..., cut:, :].astype(F32) + self.left.astype(F32)
                left = jnp.concatenate([left[..., :cut, :], last.astype(BF)], axis=-2)
            else:
                right = (right.astype(F32) + self.right.astype(F32)).astype(BF)
                left = (left.astype(F32) + self.left.astype(F32)).astype(BF)
            right, left = after((right, left), *earlier)
            self.right, self.left = turn(right, 1), turn(left, -1)

        def result(self):
            total = self.parts[0].astype(F32) + self.right.astype(F32)
            return total + self.left.astype(F32)

    def scatter(parts):
        flat = parts.reshape(parts.shape[0], -1)
        summed = lax.psum_scatter(
            flat, "ctx", scatter_dimension=0, tiled=True, axis_index_groups=same_core
        )
        return summed.reshape(parts.shape[1:]).astype(F32)

    group_first = (me // (2 * heads)) * (2 * heads)
    block_ids = group_first + 2 * jnp.arange(heads) + core
    inverse = ROPE_BASE ** (-(jnp.arange(HALF).astype(F32) * 2.0) / HD)

    def tables(ids):
        positions = (ids[:, None] * width + jnp.arange(width)[None, :]).astype(F32)
        angles = positions[:, None, :] * inverse[None, :, None]
        return jnp.cos(angles), jnp.sin(angles)

    tp = lax.axis_index("tp")
    tp_list = tp.astype(jnp.int32).reshape(1)
    cos_one, sin_one = tables(me[None])
    w_three = w_qkv.transpose(1, 0, 2)
    w_pair = w_in.transpose(1, 2, 0)

    packed, attn_input = project(hidden_in, gain_attn[None], cos_one[0], sin_one[0], w_three)
    own = exchange(packed)
    w_out_other = swap_tp(after(w_attn_out, packed))
    later_cot = after(cotangent, packed)
    cos_all, sin_all = tables(after(block_ids, packed))
    rows_in = rows_of(pick_plain, after(attn_input, packed))
    rows_cot = rows_of(pick_ring, later_cot)
    grad_activated = nt(later_cot, w_mlp_out)
    own = after(own, rows_in, rows_cot, grad_activated, cos_all, sin_all)
    others = [shift_keys(own, step) for step in range(1, 2 * copies)]

    gathered = [rows_in]
    right = left = rows_in

    def gather_step(step, *earlier):
        nonlocal right, left
        right, left = after((right, left), *earlier)
        if 2 * step == chips:
            cut = right.shape[0] // 2
            right, left = right[:cut], left[cut:]
        right, left = turn(right, 1), turn(left, -1)
        gathered.extend([right, left])

    if ringed:
        gather_step(1, own)
    attended, attended_low, lse = attend(own, others)
    twice = jnp.concatenate([attended_low] * tp_size, axis=0)
    if ringed:
        gather_step(2, twice)
    attn_all = exchange_wide(twice).reshape(tp_size, inner, width)
    if ringed:
        attn_all = after(attn_all, right, left)
        gather_step(3, attn_all)
    middle, mlp_input, activated_low, grad_gate_up, part_two, head_terms = middle_part(
        tp_list,
        attn_all,
        hidden_in,
        cotangent,
        gain_mlp[None],
        w_attn_out,
        w_out_other,
        w_pair,
        grad_activated,
    )
    if ringed:
        gather_step(4, head_terms)
    grad_received = exchange_wide(head_terms.reshape(tp_size * heads, HD, width))

    rows_mlp = rows_of(pick_ring, mlp_input)
    parts_mlp = mlp_weight(
        chips,
        rows_mlp,
        rows_cot,
        grad_gate_up,
        swap_core(grad_gate_up),
        activated_low,
        swap_core(activated_low),
    )
    grad_received = after(grad_received, parts_mlp)
    if ringed:
        sum_mlp = Sum(parts_mlp)
        sum_mlp.advance()
    grad_received = grad_received.reshape(tp_size, heads, HD, width)
    dq, *grad_kv = attend_back(own, others, grad_received, attended, lse, cos_all, sin_all)

    normed_two, scale_two = standardise(middle)
    grad_middle = cotangent.astype(F32) + standardise_back(
        add_tp(part_two), gain_mlp, normed_two, scale_two
    )
    grad_middle_low = grad_middle.astype(BF)
    output = (middle + add_tp(nn(activated_low, w_mlp_out).astype(BF))).astype(BF)
    attn_flat_t = lax.dynamic_index_in_dim(attn_all, tp, 0, keepdims=False)
    rows_out = rows_of(pick_ring, after(grad_middle_low, dq))
    columns_out = jnp.concatenate([attn_flat_t, swap_core(attn_flat_t)], axis=1)
    parts_out = nt(rows_out, columns_out).astype(BF).reshape(chips, mine, inner)

    terms = [grad_kv[0]]
    for step in range(1, 2 * copies):
        terms.append(shift_keys(grad_kv[step], -step))
    if ringed:
        sum_mlp.advance(dq)
    grad_own = combine(dq, terms, cos_all, sin_all)
    grad_back = exchange(grad_own)
    if ringed:
        sum_out = Sum(parts_out)
        sum_out.advance(grad_own)
        steps = [0]
        for step in range(1, chips // 2 + 1):
            steps.extend([-step, step])
        ids = ring_chip(position + jnp.array(steps[:chips])).astype(jnp.int32)
        part_qkv = head_weight(ids, grad_own, swap_core(grad_own), gathered)
        sum_mlp.advance(part_qkv)
        sum_out.advance(part_qkv)
        grad_back = after(grad_back, part_qkv)
    part_one = project_back(grad_back, w_three)
    grad_normed_one = add_tp(part_one)
    if ringed:
        blocks_qkv = exchange(after(part_qkv, part_one).reshape(chips, mine, 3 * HD))
        sum_mlp.advance(part_one)
        sum_out.advance(part_one)
        blocks_qkv = blocks_qkv.reshape(heads, mine, 3, HD).astype(F32)
        grad_w_qkv = blocks_qkv.transpose(1, 2, 0, 3).reshape(mine, 3, inner)
        sum_out.advance(grad_w_qkv)
        grad_mlp, grad_out = sum_mlp.result(), sum_out.result()
    else:
        grad_back = grad_back.reshape(heads, 3, HD, width)
        grad_back = grad_back.transpose(1, 0, 2, 3).reshape(3, inner, width)
        columns_in = jnp.concatenate([grad_back, swap_core(grad_back)], axis=2)
        part_qkv = jnp.einsum("dt,cft->dcf", rows_in, columns_in, preferred_element_type=F32)
        grad_w_qkv = scatter(part_qkv.astype(BF).reshape(chips, mine, 3, inner))
        grad_mlp = scatter(parts_mlp)
        grad_out = scatter(parts_out)
    normed_one, scale_one = standardise(hidden_in.astype(F32))
    grad_input = grad_middle + standardise_back(grad_normed_one, gain_attn, normed_one, scale_one)
    grad_w_in = jnp.stack([grad_mlp[0], grad_mlp[1]], axis=1)
    grad_w_mlp_out = grad_mlp[2].T
    grad_w_attn_out = grad_out.T

    first = me * mine
    rows_w_qkv = lax.dynamic_slice_in_dim(w_qkv, first, mine, 0).astype(F32)
    rows_w_in = lax.dynamic_slice_in_dim(w_in, first, mine, 0).astype(F32)
    gain_terms = jnp.stack(
        [
            jnp.sum(rows_w_qkv * grad_w_qkv, axis=(1, 2)),
            jnp.sum(rows_w_in * grad_w_in, axis=(1, 2)),
        ]
    )
    grad_gains = gain_terms + swap_tp(gain_terms)
    grad_gain_attn = grad_gains[0] / lax.dynamic_slice_in_dim(gain_attn, first, mine, 0)
    grad_gain_mlp = grad_gains[1] / lax.dynamic_slice_in_dim(gain_mlp, first, mine, 0)
    return (
        output,
        grad_input,
        grad_gain_attn,
        grad_gain_mlp,
        grad_w_qkv,
        grad_w_attn_out,
        grad_w_in,
        grad_w_mlp_out,
    )


def solution(mesh):
    in_specs = (
        P("ctx", None),
        P("ctx", None),
        P(),
        P(),
        P(None, None, "tp"),
        P("tp", None),
        P(None, None, "tp"),
        P("tp", None),
    )
    out_specs = (
        P("ctx", None),
        P("ctx", None),
        P("ctx"),
        P("ctx"),
        P("ctx", None, "tp"),
        P("tp", "ctx"),
        P("ctx", None, "tp"),
        P("tp", "ctx"),
    )
    body = functools.partial(layer, mesh.shape["ctx"], mesh.shape["tp"])
    return jax.shard_map(body, mesh=mesh, in_specs=in_specs, out_specs=out_specs, check_vma=False)
```

time: 366 us -> 226 us (0.62)
  waiting for transfers between devices: 203 us -> 37.2 us
  starting transfers between devices: 28.7 us -> 61.2 us
  Pallas kernels: 19.6 us -> 38.6 us
  blocking collectives: 16 us -> 0 us
  local copies, waits for them, and re-layouts: 30.2 us -> 43.4 us
  between operations: 14.2 us -> 1.05 us
  matrix products: 24 us -> 12.9 us
    reduce_scatter x2 -> x0, waiting for transfers between devices: 63.3 us -> none  [scatter(): lax.psum_scatter(values, 'ctx', scatter_dimension=0, tiled=True, axis_ind...]
    unnamed x5 -> x0, waiting for transfers between devices: 47.8 us -> none
    all_gather x1 -> x0, waiting for transfers between devices: 35.4 us -> none  [layer(): lax.all_gather(both_in, 'ctx', axis=0, axis_index_groups=same_core)]
    all_to_all x4 -> x3, waiting for transfers between devices: 36.9 us -> 3.36 us  [exchange(): return lax.all_to_all(values, 'ctx', 0, 0, axis_index_groups=head_groups)]
    ppermute x5 -> x29, starting transfers between devices: 6.7 us -> 33.7 us  [the longest x24 28 us: turn(): return lax.ppermute(values, 'ctx', pairs)]
    pallas_call x1 -> x6, Pallas kernels: 3.71 us -> 22.7 us  [the longest x1 6.01 us: middle_part(): pl.pallas_call(middle_kernel, in_specs=[pl.BlockSpec(memory_space=pltpu.S...]
    ppermute x5 -> x29, waiting for transfers between devices: 17.3 us -> 33.9 us  [the longest x24 21.3 us: turn(): return lax.ppermute(values, 'ctx', pairs)]
    all_to_all x1 -> x0, blocking collectives: 16 us -> none  [exchange(): return lax.all_to_all(values, 'ctx', 0, 0, axis_index_groups=head_groups)]
  transfers between devices with their start and end apart: 23 -> 44, of which waited for: 13 -> 8; matrix products, arithmetic and copies ran while one was open for 18% -> 31% of each run, Pallas kernels for 5% -> 13%
where the time goes in v2:
time: 226 us; the launch traced here: 223 us
  starting transfers between devices  61.2 us (27%)
  local copies, waits for them, and re-layouts  43.4 us (19%)
  Pallas kernels  38.6 us (17%)
  waiting for transfers between devices  37.2 us (16%)
  other arithmetic  29.1 us (13%)
  matrix products  12.9 us (6%)
    ppermute x24, starting transfers between devices, turn(): return lax.ppermute(values, 'ctx', pairs)  28 us
    ppermute x24, waiting for transfers between devices, turn(): return lax.ppermute(values, 'ctx', pairs)  21.3 us
    unnamed x75, local copies, waits for them, and re-layouts  19.4 us
    all_to_all x3, starting transfers between devices, exchange(): return lax.all_to_all(values, 'ctx', 0, 0, axis_index_groups=head_groups)  16.9 us
    dot_general x6, matrix products, dot(): return lax.dot_general(a, b, (dims, ((), ())), preferred_element_type=F32)  12.9 us
    ppermute x5, waiting for transfers between devices, swap_tp(): return lax.ppermute(values, 'tp', [(0, 1), (1, 0)])  12.6 us
    all_to_all x2, starting transfers between devices, exchange_wide(): lax.all_to_all(values, ('ctx', 'tp'), 0, 0, axis_index_groups=wide_groups)  9.36 us
    pallas_call x1, Pallas kernels, attend_back(): pl.pallas_call(functools.partial(attend_back_kernel, part_count), out_sha...  8.9 us
  transfers between devices with their start and end apart: 44, of which 8 were waited for; matrix products, arithmetic and copies ran while one was open for 31% of the time, Pallas kernels for 13%

profile of v2, /device:TPU:0, one launch (start us, length us, event | category | flops | bytes accessed | tf_op | source)
XLA Modules:
  0.0 223.4 jit_solution(1014284985570265680)
XLA Ops:
  1.4 4.6 %project.1 = (bf16[8,192,128]{2,1,0:T(8,128)(2,1)}, bf16[128,1024]{1,0:T(8,128)(2,1)}) custom-call(bf16[128,1024]{1,0:T(8,128)(2,1)} %hidden_ref.3, f32[1,1024]{1,0:T(1,128)} %bitcast.79, f32[32,128]{1,0:T(8,128)} %get-tuple-element.172.cos_ref, f32[32,128]{1,0:T(8,128)} %get-tuple-element.171.sin_ref, bf16[3,1024,512]{2,1,0:T(8,128)(2,1)} %bitcast.70), custom_call_target="tpu_custom_call" | custom-call | tf_op jit(solution)/shard_map/project/pallas_call | solution.py:263
  6.0 7.3 %all-to-all-start = ((bf16[8,192,128]{2,1,0:T(8,128)(2,1)}), bf16[8,192,128]{2,1,0:T(8,128)(2,1)S(1)}, u32[]{:S(2)}, u32[]{:S(2)}) async-start(bf16[8,192,128]{2,1,0:T(8,128)(2,1)} %get-tuple-element.56), calls=%async_computation | async-start | bytes 786432 | tf_op jit(solution)/shard_map/all_to_all | solution.py:462
  15.3 1.7 fusion.61
  17.2 2.2 fusion.5.rows_out_ref
  19.4 2.2 fusion.4.refs_0_
  21.6 3.4 %all-to-all-done.own_ref = bf16[8,192,128]{2,1,0:T(8,128)(2,1)S(1)} async-done(((bf16[8,192,128]{2,1,0:T(8,128)(2,1)}), bf16[8,192,128]{2,1,0:T(8,128)(2,1)S(1)}, u32[]{:S(2)}, u32[]{:S(2)}) %all-to-all-start) | async-done | bytes 393248 | tf_op jit(solution)/shard_map/all_to_all | solution.py:462
  29.8 7.0 %attend.1 = (f32[8,64,128]{2,1,0:T(8,128)}, bf16[8,64,128]{2,1,0:T(8,128)(2,1)}, f32[8,1,128]{2,1,0:T(1,128)}) custom-call(bf16[8,192,128]{2,1,0:T(8,128)(2,1)} %copy-done.27, bf16[8,192,128]{2,1,0:T(8,128)(2,1)} %copy-done.32), custom_call_target="tpu_custom_call" | custom-call | flops 536870912 | bytes 786432 | tf_op jit(solution)/shard_map/attend/pallas_call | solution.py:90
  36.8 1.6 constant_dynamic-update-slice_fusion.1
  38.4 1.6 constant_dynamic-update-slice_fusion
  40.0 3.7 %all-to-all-start.1 = ((bf16[16,64,128]{2,1,0:T(8,128)(2,1)}), bf16[16,64,128]{2,1,0:T(8,128)(2,1)S(1)}, u32[]{:S(2)}, u32[]{:S(2)}) async-start(bf16[16,64,128]{2,1,0:T(8,128)(2,1)} %constant_dynamic-update-slice_fusion), calls=%async_computation.1 | async-start | bytes 524288 | tf_op jit(solution)/shard_map/all_to_all | solution.py:459
  43.9 2.0 collective-permute-start.5
  45.9 2.2 copy.30.grad_act_ref
  48.2 2.2 constant_dynamic-slice_fusion
  50.4 4.2 %collective-permute-done.5.refs_3_ = bf16[512,256]{1,0:T(8,128)(2,1)} collective-permute-done((bf16[512,256]{1,0:T(8,128)(2,1)}, bf16[512,256]{1,0:T(8,128)(2,1)}, u32[]{:S(2)}, u32[]{:S(2)}) %collective-permute-start.5) | collective-permute-done | bytes 262176 | tf_op jit(solution)/shard_map/ppermute | solution.py:499
  54.5 1.7 collective-permute-done.6.refs_4_
  57.0 2.5 %copy-done.3 = bf16[1024,2,1312]{0,2,1:T(8,128)(2,1)S(1)} copy-done((bf16[1024,2,1312]{0,2,1:T(8,128)(2,1)S(1)}, bf16[1024,2,1312]{0,2,1:T(8,128)(2,1)}, u32[]{:S(2)}) %copy-start.3) | copy-done | bytes 5373976
  63.7 6.0 %middle_part.1 = (f32[128,1024]{1,0:T(8,128)S(1)}, bf16[128,1024]{1,0:T(8,128)(2,1)}, bf16[128,1312]{1,0:T(8,128)(2,1)}, bf16[2,128,1312]{2,1,0:T(8,128)(2,1)S(1...) custom-call(s32[1]{0:T(128)} %bitcast.tp_ref, bf16[2,512,128]{2,1,0:T(8,128)(2,1)S(1)} %bitcast.74, ...), custom_call_target="tpu_custom_call" | custom-call | flops 1912602624 | bytes 7471104 | tf_op jit(solution)/shard_map/middle_part/pallas_call | solution.py:332
  69.8 2.6 %convolution_convert_fusion.1 = bf16[128,1024]{1,0:T(8,128)(2,1)} fusion(bf16[128,1312]{1,0:T(8,128)(2,1)} %get-tuple-element.70.act_ref, bf16[1312,1024]{1,0:T(8,128)(2,1)S(1)} %copy-done), kind=kOutput, calls=%fused_computation.11 | convolution fusion | flops 344064000 | bytes 3284992 | tf_op jit(solution)/shard_map/dot_general | solution.py:22
  72.7 2.2 copy.31
  75.2 5.6 %all-to-all-start.2 = ((bf16[16,64,128]{2,1,0:T(8,128)(2,1)}), bf16[16,64,128]{2,1,0:T(8,128)(2,1)}, u32[]{:S(2)}, u32[]{:S(2)}) async-start(bf16[16,64,128]{2,1,0:T(8,128)(2,1)} %bitcast.75), calls=%async_computation.2 | async-start | bytes 524288 | tf_op jit(solution)/shard_map/all_to_all | solution.py:459
  80.8 1.9 collective-permute-start.8
  84.9 12.6 %collective-permute-done.9 = bf16[128,1024]{1,0:T(8,128)(2,1)S(1)} collective-permute-done((bf16[128,1024]{1,0:T(8,128)(2,1)}, bf16[128,1024]{1,0:T(8,128)(2,1)S(1)}, u32[]{:S(2)}, u32[]{:S(2)}) %collective-permute-start.9) | collective-permute-done | bytes 262176 | tf_op jit(solution)/shard_map/ppermute | solution.py:477
  99.4 1.7 collective-permute-start.15
  101.1 2.2 %fusion.6.rows_in_ref = bf16[512,256]{1,0:T(8,128)(2,1)} fusion(s32[512]{0:T(512)S(1)} %add.249, bf16[128,1024]{1,0:T(8,128)(2,1)} %collective-permute-done.10, bf16[128,1024]{1,0:T(8,128)(2,1)} %get-tuple-element.73), kind=kOutput, calls=%fused_computation.9 | convolution fusion | flops 270139392 | bytes 788480 | tf_op jit(solution)/shard_map/dot_general | solution.py:22
  103.9 2.3 %copy.32.other_ref = bf16[2,128,1312]{2,1,0:T(8,128)(2,1)} copy(bf16[2,128,1312]{1,2,0:T(8,128)(2,1)} %collective-permute-done.11) | data formatting | bytes 1343488 | tf_op jit(solution)/shard_map/ppermute | solution.py:465
  106.2 5.1 %mlp_weight.1 = bf16[8,3,64,1312]{3,2,1,0:T(8,128)(2,1)} custom-call(bf16[512,256]{1,0:T(8,128)(2,1)} %fusion.6.rows_in_ref, bf16[512,256]{1,0:T(8,128)(2,1)} %fusion.5.rows_out_ref, bf16[2,128,1312]{2,1,0:T(8,128)(2,1)} %copy-done.4, bf16[2,128,1312]{2,1,0:T(8,128)(2,1)} %copy.32.other_ref, bf16[128,1312]{1,0:T(8,128)(2,1)} %get-tuple-element.70.act_ref, ...), custom_call_target="tpu_custom_call" | custom-call | flops 1031798784 | bytes 6045696 | tf_op jit(solution)/shard_map/mlp_weight/pallas_call | solution.py:422
  111.3 2.5 %slice_bitcast_fusion.2 = (bf16[3,64,1312]{2,1,0:T(8,128)(2,1)}, bf16[3,64,1312]{2,1,0:T(8,128)(2,1)S(1)}, bf16[3,64,1312]{2,1,0:T(8,128)(2,1)}) fusion(bf16[8,3,64,1312]{3,2,1,0:T(8,128)(2,1)} %mlp_weight.1), kind=kLoop, calls=%fused_computation.37 | loop fusion | bytes 3022848 | tf_op jit(solution)/shard_map/squeeze | solution.py:524
  116.1 2.3 %fusion.58 = (bf16[128,1024]{1,0:T(8,128)(2,1)}, f32[128,1024]{1,0:T(8,128)}, bf16[128,1024]{1,0:T(8,128)(2,1)}) fusion(f32[128]{0:T(128)S(1)} %broadcast_multiply_fusion.3, f32[128,1024]{1,0:T(8,128)S(1)} %get-tuple-element.69, f32[128]{0:T(128)S(1)} %broadcast_multiply_fusion.5, f32[128]{0:T(128)S(1)} %broadcast_multiply_fusion.4, ...), kind=kLoop, calls=%fused_computation.134 | loop fusion | flops 2359296 | bytes 2889728 | tf_op jit(solution)/shard_map/convert_element_type | solution.py:633
  118.4 8.9 %attend_back.1 = (bf16[8,64,128]{2,1,0:T(8,128)(2,1)}, f32[8,128,128]{2,1,0:T(8,128)}, f32[8,128,128]{2,1,0:T(8,128)}) custom-call(bf16[8,192,128]{2,1,0:T(8,128)(2,1)} %copy-done.27, bf16[8,192,128]{2,1,0:T(8,128)(2,1)} %copy-done.32, bf16[2,8,64,128]{3,2,1,0:T(8,128)(2,1)} %bitcast.7.refs_1_, f32[8,64,128]{2,1,0:T(8,128)} %get-tuple-element.76.refs_2_, ...), custom_call_target="tpu_custom_call" | custom-call | flops 1342177280 | bytes 1572864 | tf_op jit(solution)/shard_map/attend_back/pallas_call | solution.py:174
  130.0 7.2 %collective-permute-done.20 = bf16[3,32,1312]{2,1,0:T(8,128)(2,1)S(1)} collective-permute-done((bf16[3,32,1312]{2,1,0:T(8,128)(2,1)S(1)}, bf16[3,32,1312]{2,1,0:T(8,128)(2,1)S(1)}, u32[]{:S(2)}, u32[]{:S(2)}) %collective-permute-start.20) | collective-permute-done | bytes 251936 | tf_op jit(solution)/shard_map/ppermute | solution.py:499
  141.8 2.0 convolution_convert_fusion
  144.5 2.1 combine.1.own_ref
  151.9 5.4 %all-to-all-start.3 = ((bf16[8,192,128]{2,1,0:T(8,128)(2,1)}), bf16[8,192,128]{2,1,0:T(8,128)(2,1)S(1)}, u32[]{:S(2)}, u32[]{:S(2)}) async-start(bf16[8,192,128]{2,1,0:T(8,128)(2,1)} %combine.1.own_ref), calls=%async_computation.3 | async-start | bytes 786432 | tf_op jit(solution)/shard_map/all_to_all | solution.py:462
  157.4 2.0 collective-permute-start.18
  160.9 6.5 %collective-permute-done.18.refs_8_ = bf16[256,256]{1,0:T(8,128)(2,1)} collective-permute-done((bf16[256,256]{1,0:T(8,128)(2,1)}, bf16[256,256]{1,0:T(8,128)(2,1)}, u32[]{:S(2)}, u32[]{:S(2)}) %collective-permute-start.18) | collective-permute-done | bytes 131104 | tf_op jit(solution)/shard_map/ppermute | solution.py:499
  168.2 3.7 %head_weight.1 = bf16[512,192]{1,0:T(8,128)(2,1)} custom-call(s32[8]{0:T(128)} %compare_select_fusion.4.ids_ref, bf16[8,192,128]{2,1,0:T(8,128)(2,1)} %combine.1.own_ref, bf16[8,192,128]{2,1,0:T(8,128)(2,1)} %copy-done.28, bf16[512,256]{1,0:T(8,128)(2,1)} %fusion.4.refs_0_, bf16[512,256]{1,0:T(8,128)(2,1)} %collective-permute-done.3.refs_1_, ...), custom_call_target="tpu_custom_call" | custom-call | flops 452984832 | bytes 2359296 | tf_op jit(solution)/shard_map/head_weight/pallas_call | solution.py:395
  171.9 4.5 %collective-permute-start.33 = (bf16[64,512]{1,0:T(8,128)(2,1)S(1)}, bf16[64,512]{1,0:T(8,128)(2,1)S(1)}, u32[]{:S(2)}, u32[]{:S(2)}) collective-permute-start(bf16[64,512]{1,0:T(8,128)(2,1)S(1)} %copy-done.30), channel_id=1, source_target_pairs={{0,8},{2,10},{4,0},{6,2},{8,16},{10,18},{12,4},{14,6},{16,24},{18,... | collective-permute-start | bytes 196616 | tf_op jit(solution)/shard_map/ppermute | solution.py:499
  176.4 2.8 %fusion.9 = (bf16[3,64,1312]{2,1,0:T(8,128)(2,1)}, bf16[3,64,1312]{2,1,0:T(8,128)(2,1)}) fusion(bf16[3,64,1312]{2,1,0:T(8,128)(2,1)} %collective-permute-done.23, bf16[8,3,64,1312]{3,2,1,0:T(8,128)(2,1)} %mlp_weight.1, bf16[3,64,1312]{2,1,0:T(8,128)(2,1)} %collective-permute-done.22), kind=kLoop, calls=%fused_computation.15 | loop fusion | flops 2015232 | bytes 3022848 | tf_op jit(solution)/shard_map/convert_element_type | solution.py:534
  179.1 2.0 collective-permute-start.24
  183.4 1.9 copy-done.1
  187.5 2.1 collective-permute-start.35
  189.6 2.1 copy.37
  192.4 4.2 %all-to-all-start.4 = ((bf16[8,64,192]{2,1,0:T(8,128)(2,1)}), bf16[8,64,192]{2,1,0:T(8,128)(2,1)S(1)}, u32[]{:S(2)}, u32[]{:S(2)}) async-start(bf16[8,64,192]{2,1,0:T(8,128)(2,1)} %bitcast.78), calls=%async_computation.4 | async-start | bytes 524288 | tf_op jit(solution)/shard_map/all_to_all | solution.py:462
  196.6 1.6 add_convert_fusion.3
  198.2 2.8 %fusion.8 = (bf16[3,64,1312]{2,1,0:T(8,128)(2,1)}, bf16[3,64,1312]{2,1,0:T(8,128)(2,1)}) fusion(bf16[3,64,1312]{2,1,0:T(8,128)(2,1)} %collective-permute-done.25, bf16[8,3,64,1312]{3,2,1,0:T(8,128)(2,1)} %mlp_weight.1, bf16[3,64,1312]{2,1,0:T(8,128)(2,1)} %collective-permute-done.24), kind=kLoop, calls=%fused_computation.13 | loop fusion | flops 2015232 | bytes 3022848 | tf_op jit(solution)/shard_map/convert_element_type | solution.py:534
  201.0 2.0 collective-permute-start.26
  204.5 2.0 fusion.25
  211.1 1.9 collective-permute-start.37
  (194 shorter events, 57.8 us)
Async XLA Ops:
  0.6 14.6 %copy-start = (bf16[1312,1024]{1,0:T(8,128)(2,1)S(1)}, bf16[1312,1024]{1,0:T(8,128)(2,1)}, u32[]{:S(2)}) copy-start(bf16[1312,1024]{1,0:T(8,128)(2,1)} %param.16) | copy-start | bytes 8060932
  1.4 11.8 %copy-start.6 = (bf16[128,1024]{1,0:T(8,128)(2,1)S(1)}, bf16[128,1024]{1,0:T(8,128)(2,1)}, u32[]{:S(2)}) copy-start(bf16[128,1024]{1,0:T(8,128)(2,1)} %cot_ref.1) | copy-start | bytes 786436
  6.0 19.0 %all-to-all-start = ((bf16[8,192,128]{2,1,0:T(8,128)(2,1)}), bf16[8,192,128]{2,1,0:T(8,128)(2,1)S(1)}, u32[]{:S(2)}, u32[]{:S(2)}) async-start(bf16[8,192,128]{2,1,0:T(8,128)(2,1)} %get-tuple-element.56), calls=%async_computation | async-start | bytes 786432 | tf_op jit(solution)/shard_map/all_to_all | solution.py:462
  13.3 3.9 %collective-permute-start.1 = (bf16[128,1024]{1,0:T(8,128)(2,1)S(1)}, bf16[128,1024]{1,0:T(8,128)(2,1)}, u32[]{:S(2)}, u32[]{:S(2)}) collective-permute-start(bf16[128,1024]{1,0:T(8,128)(2,1)S(1)} %copy-done.6), channel_id=1, source_target_pairs={{0,2},{2,0},{4,6},{6,4},{8,10},{10,8},{12,14},{14,12},{16,18},{18,... | collective-permute-start | bytes 786440 | tf_op jit(solution)/shard_map/ppermute | solution.py:465
  13.4 6.1 %collective-permute-start = (bf16[128,1024]{1,0:T(8,128)(2,1)}, bf16[128,1024]{1,0:T(8,128)(2,1)}, u32[]{:S(2)}, u32[]{:S(2)}) collective-permute-start(bf16[128,1024]{1,0:T(8,128)(2,1)} %get-tuple-element.58), channel_id=1, source_target_pairs={{0,2},{2,0},{4,6},{6,4},{8,10},{10,8},{12,14},{14,12},{16,18},{18,... | collective-permute-start | bytes 786440 | tf_op jit(solution)/shard_map/ppermute | solution.py:465
  25.0 4.0 %collective-permute-start.2 = (bf16[8,192,128]{2,1,0:T(8,128)(2,1)S(1)}, bf16[8,192,128]{2,1,0:T(8,128)(2,1)S(1)}, u32[]{:S(2)}, u32[]{:S(2)}) collective-permute-start(bf16[8,192,128]{2,1,0:T(8,128)(2,1)S(1)} %all-to-all-done.own_ref), channel_id=1, source_target_pairs={{0,2},{2,0},{4,6},{6,4},{8,10},{10,8},{12,14},{14,12},{16,18},{18,... | collective-permute-start | bytes 1179656 | tf_op jit(solution)/shard_map/ppermute | solution.py:474
  25.0 32.0 %collective-permute-start.7 = (bf16[512,1024]{1,0:T(8,128)(2,1)}, bf16[512,1024]{1,0:T(8,128)(2,1)}, u32[]{:S(2)}, u32[]{:S(2)}) collective-permute-start(bf16[512,1024]{1,0:T(8,128)(2,1)} %own_ref.1), channel_id=1, source_target_pairs={{0,1},{1,0},{2,3},{3,2},{4,5},{5,4},{6,7},{7,6},{8,9},{9,8},{10,11... | collective-permute-start | bytes 3145736 | tf_op jit(solution)/shard_map/ppermute | solution.py:477
  27.0 16.9 %collective-permute-start.3 = (bf16[512,256]{1,0:T(8,128)(2,1)}, bf16[512,256]{1,0:T(8,128)(2,1)}, u32[]{:S(2)}, u32[]{:S(2)}) collective-permute-start(bf16[512,256]{1,0:T(8,128)(2,1)} %fusion.4.refs_0_), channel_id=1, source_target_pairs={{0,8},{2,10},{4,0},{6,2},{8,16},{10,18},{12,4},{14,6},{16,24},{18,... | collective-permute-start | bytes 786440 | tf_op jit(solution)/shard_map/ppermute | solution.py:499
  27.9 15.9 %collective-permute-start.4 = (bf16[512,256]{1,0:T(8,128)(2,1)}, bf16[512,256]{1,0:T(8,128)(2,1)}, u32[]{:S(2)}, u32[]{:S(2)}) collective-permute-start(bf16[512,256]{1,0:T(8,128)(2,1)} %fusion.4.refs_0_), channel_id=1, source_target_pairs={{0,4},{2,6},{4,12},{6,14},{8,0},{10,2},{12,20},{14,22},{16,8},{18,... | collective-permute-start | bytes 786440 | tf_op jit(solution)/shard_map/ppermute | solution.py:499
  40.0 16.3 %all-to-all-start.1 = ((bf16[16,64,128]{2,1,0:T(8,128)(2,1)}), bf16[16,64,128]{2,1,0:T(8,128)(2,1)S(1)}, u32[]{:S(2)}, u32[]{:S(2)}) async-start(bf16[16,64,128]{2,1,0:T(8,128)(2,1)} %constant_dynamic-update-slice_fusion), calls=%async_computation.1 | async-start | bytes 524288 | tf_op jit(solution)/shard_map/all_to_all | solution.py:459
  43.9 10.7 %collective-permute-start.5 = (bf16[512,256]{1,0:T(8,128)(2,1)}, bf16[512,256]{1,0:T(8,128)(2,1)}, u32[]{:S(2)}, u32[]{:S(2)}) collective-permute-start(bf16[512,256]{1,0:T(8,128)(2,1)} %collective-permute-done.3.refs_1_), channel_id=1, source_target_pairs={{0,8},{2,10},{4,0},{6,2},{8,16},{10,18},{12,4},{14,6},{16,24},{18,... | collective-permute-start | bytes 786440 | tf_op jit(solution)/shard_map/ppermute | solution.py:499
  45.8 10.4 %collective-permute-start.6 = (bf16[512,256]{1,0:T(8,128)(2,1)}, bf16[512,256]{1,0:T(8,128)(2,1)}, u32[]{:S(2)}, u32[]{:S(2)}) collective-permute-start(bf16[512,256]{1,0:T(8,128)(2,1)} %collective-permute-done.4.refs_2_), channel_id=1, source_target_pairs={{0,4},{2,6},{4,12},{6,14},{8,0},{10,2},{12,20},{14,22},{16,8},{18,... | collective-permute-start | bytes 786440 | tf_op jit(solution)/shard_map/ppermute | solution.py:499
  45.9 11.0 %copy-start.17 = (f32[1024]{0:T(1024)S(1)}, f32[1024]{0:T(1024)}, u32[]{:S(2)}) copy-start(f32[1024]{0:T(1024)} %param.12) | copy-start | bytes 12292
  69.8 36.4 %collective-permute-start.12 = (bf16[128,1312]{1,0:T(8,128)(2,1)}, bf16[128,1312]{1,0:T(8,128)(2,1)}, u32[]{:S(2)}, u32[]{:S(2)}) collective-permute-start(bf16[128,1312]{1,0:T(8,128)(2,1)} %get-tuple-element.70.act_ref), channel_id=1, source_target_pairs={{0,2},{2,0},{4,6},{6,4},{8,10},{10,8},{12,14},{14,12},{16,18},{18,... | collective-permute-start | bytes 1007624 | tf_op jit(solution)/shard_map/ppermute | solution.py:465
  72.4 27.0 %collective-permute-start.10 = (bf16[128,1024]{1,0:T(8,128)(2,1)}, bf16[128,1024]{1,0:T(8,128)(2,1)}, u32[]{:S(2)}, u32[]{:S(2)}) collective-permute-start(bf16[128,1024]{1,0:T(8,128)(2,1)} %get-tuple-element.73), channel_id=1, source_target_pairs={{0,2},{2,0},{4,6},{6,4},{8,10},{10,8},{12,14},{14,12},{16,18},{18,... | collective-permute-start | bytes 786440 | tf_op jit(solution)/shard_map/ppermute | solution.py:465
  74.9 28.4 %collective-permute-start.11 = (bf16[2,128,1312]{1,2,0:T(8,128)(2,1)}, bf16[2,128,1312]{1,2,0:T(8,128)(2,1)}, u32[]{:S(2)}, u32[]{:S(2)}) collective-permute-start(bf16[2,128,1312]{1,2,0:T(8,128)(2,1)} %copy.31), channel_id=1, source_target_pairs={{0,2},{2,0},{4,6},{6,4},{8,10},{10,8},{12,14},{14,12},{16,18},{18,... | collective-permute-start | bytes 2015240 | tf_op jit(solution)/shard_map/ppermute | solution.py:465
  75.2 43.2 %all-to-all-start.2 = ((bf16[16,64,128]{2,1,0:T(8,128)(2,1)}), bf16[16,64,128]{2,1,0:T(8,128)(2,1)}, u32[]{:S(2)}, u32[]{:S(2)}) async-start(bf16[16,64,128]{2,1,0:T(8,128)(2,1)} %bitcast.75), calls=%async_computation.2 | async-start | bytes 524288 | tf_op jit(solution)/shard_map/all_to_all | solution.py:459
  80.8 35.2 %collective-permute-start.8 = (bf16[128,1024]{1,0:T(8,128)(2,1)}, bf16[128,1024]{1,0:T(8,128)(2,1)}, u32[]{:S(2)}, u32[]{:S(2)}) collective-permute-start(bf16[128,1024]{1,0:T(8,128)(2,1)} %convolution_convert_fusion.1), channel_id=1, source_target_pairs={{0,1},{1,0},{2,3},{3,2},{4,5},{5,4},{6,7},{7,6},{8,9},{9,8},{10,11... | collective-permute-start | bytes 786440 | tf_op jit(solution)/shard_map/ppermute | solution.py:477
  83.0 14.4 %collective-permute-start.9 = (bf16[128,1024]{1,0:T(8,128)(2,1)}, bf16[128,1024]{1,0:T(8,128)(2,1)S(1)}, u32[]{:S(2)}, u32[]{:S(2)}) collective-permute-start(bf16[128,1024]{1,0:T(8,128)(2,1)} %copy-done.13), channel_id=1, source_target_pairs={{0,1},{1,0},{2,3},{3,2},{4,5},{5,4},{6,7},{7,6},{8,9},{9,8},{10,11... | collective-permute-start | bytes 786440 | tf_op jit(solution)/shard_map/ppermute | solution.py:477
  97.5 41.6 %collective-permute-start.30 = (bf16[512,128]{1,0:T(8,128)(2,1)}, bf16[512,128]{1,0:T(8,128)(2,1)}, u32[]{:S(2)}, u32[]{:S(2)}) collective-permute-start(bf16[512,128]{1,0:T(8,128)(2,1)} %dynamic-slice_bitcast_fusion), channel_id=1, source_target_pairs={{0,2},{2,0},{4,6},{6,4},{8,10},{10,8},{12,14},{14,12},{16,18},{18,... | collective-permute-start | bytes 393224 | tf_op jit(solution)/shard_map/ppermute | solution.py:465
  99.4 47.8 %collective-permute-start.15 = (bf16[512,256]{1,0:T(8,128)(2,1)}, bf16[512,256]{1,0:T(8,128)(2,1)}, u32[]{:S(2)}, u32[]{:S(2)}) collective-permute-start(bf16[512,256]{1,0:T(8,128)(2,1)} %collective-permute-done.5.refs_3_), channel_id=1, source_target_pairs={{0,8},{2,10},{4,0},{6,2},{8,16},{10,18},{12,4},{14,6},{16,24},{18,... | collective-permute-start | bytes 786440 | tf_op jit(solution)/shard_map/ppermute | solution.py:499
  103.3 45.5 %collective-permute-start.16 = (bf16[512,256]{1,0:T(8,128)(2,1)}, bf16[512,256]{1,0:T(8,128)(2,1)}, u32[]{:S(2)}, u32[]{:S(2)}) collective-permute-start(bf16[512,256]{1,0:T(8,128)(2,1)} %collective-permute-done.6.refs_4_), channel_id=1, source_target_pairs={{0,4},{2,6},{4,12},{6,14},{8,0},{10,2},{12,20},{14,22},{16,8},{18,... | collective-permute-start | bytes 786440 | tf_op jit(solution)/shard_map/ppermute | solution.py:499
  114.6 13.8 %collective-permute-start.21 = (bf16[3,32,1312]{2,1,0:T(8,128)(2,1)}, bf16[3,32,1312]{2,1,0:T(8,128)(2,1)}, u32[]{:S(2)}, u32[]{:S(2)}) collective-permute-start(bf16[3,32,1312]{2,1,0:T(8,128)(2,1)} %get-tuple-element.88), channel_id=1, source_target_pairs={{0,4},{2,6},{4,12},{6,14},{8,0},{10,2},{12,20},{14,22},{16,8},{18,... | collective-permute-start | bytes 755720 | tf_op jit(solution)/shard_map/ppermute | solution.py:499
  127.3 12.3 %collective-permute-start.29 = (bf16[128,1024]{1,0:T(8,128)(2,1)}, bf16[128,1024]{1,0:T(8,128)(2,1)S(1)}, u32[]{:S(2)}, u32[]{:S(2)}) collective-permute-start(bf16[128,1024]{1,0:T(8,128)(2,1)} %get-tuple-element.95), channel_id=1, source_target_pairs={{0,2},{2,0},{4,6},{6,4},{8,10},{10,8},{12,14},{14,12},{16,18},{18,... | collective-permute-start | bytes 786440 | tf_op jit(solution)/shard_map/ppermute | solution.py:465
  128.4 8.9 %collective-permute-start.20 = (bf16[3,32,1312]{2,1,0:T(8,128)(2,1)S(1)}, bf16[3,32,1312]{2,1,0:T(8,128)(2,1)S(1)}, u32[]{:S(2)}, u32[]{:S(2)}) collective-permute-start(bf16[3,32,1312]{2,1,0:T(8,128)(2,1)S(1)} %copy-done.29), channel_id=1, source_target_pairs={{0,8},{2,10},{4,0},{6,2},{8,16},{10,18},{12,4},{14,6},{16,24},{18,... | collective-permute-start | bytes 755720 | tf_op jit(solution)/shard_map/ppermute | solution.py:499
  137.3 7.2 %collective-permute-start.13 = (f32[8,128,128]{2,1,0:T(8,128)}, f32[8,128,128]{2,1,0:T(8,128)}, u32[]{:S(2)}, u32[]{:S(2)}) collective-permute-start(f32[8,128,128]{2,1,0:T(8,128)} %get-tuple-element.80), channel_id=1, source_target_pairs={{0,2},{2,0},{4,6},{6,4},{8,10},{10,8},{12,14},{14,12},{16,18},{18,... | collective-permute-start | bytes 1572872 | tf_op jit(solution)/shard_map/ppermute | solution.py:474
  139.1 37.3 %collective-permute-start.22 = (bf16[3,64,1312]{2,1,0:T(8,128)(2,1)}, bf16[3,64,1312]{2,1,0:T(8,128)(2,1)}, u32[]{:S(2)}, u32[]{:S(2)}) collective-permute-start(bf16[3,64,1312]{2,1,0:T(8,128)(2,1)} %pad_maximum_fusion.1), channel_id=1, source_target_pairs={{0,8},{2,10},{4,0},{6,2},{8,16},{10,18},{12,4},{14,6},{16,24},{18,... | collective-permute-start | bytes 1511432 | tf_op jit(solution)/shard_map/ppermute | solution.py:499
  140.3 36.0 %collective-permute-start.23 = (bf16[3,64,1312]{2,1,0:T(8,128)(2,1)}, bf16[3,64,1312]{2,1,0:T(8,128)(2,1)}, u32[]{:S(2)}, u32[]{:S(2)}) collective-permute-start(bf16[3,64,1312]{2,1,0:T(8,128)(2,1)} %pad_maximum_fusion.2), channel_id=1, source_target_pairs={{0,4},{2,6},{4,12},{6,14},{8,0},{10,2},{12,20},{14,22},{16,8},{18,... | collective-permute-start | bytes 1511432 | tf_op jit(solution)/shard_map/ppermute | solution.py:499
  146.6 10.8 %collective-permute-start.31 = (bf16[32,512]{1,0:T(8,128)(2,1)}, bf16[32,512]{1,0:T(8,128)(2,1)}, u32[]{:S(2)}, u32[]{:S(2)}) collective-permute-start(bf16[32,512]{1,0:T(8,128)(2,1)} %get-tuple-element.96), channel_id=1, source_target_pairs={{0,8},{2,10},{4,0},{6,2},{8,16},{10,18},{12,4},{14,6},{16,24},{18,... | collective-permute-start | bytes 98312 | tf_op jit(solution)/shard_map/ppermute | solution.py:499
  147.2 12.3 %collective-permute-start.32 = (bf16[32,512]{1,0:T(8,128)(2,1)}, bf16[32,512]{1,0:T(8,128)(2,1)}, u32[]{:S(2)}, u32[]{:S(2)}) collective-permute-start(bf16[32,512]{1,0:T(8,128)(2,1)} %get-tuple-element.97), channel_id=1, source_target_pairs={{0,4},{2,6},{4,12},{6,14},{8,0},{10,2},{12,20},{14,22},{16,8},{18,... | collective-permute-start | bytes 98312 | tf_op jit(solution)/shard_map/ppermute | solution.py:499
  149.8 11.1 %collective-permute-start.17 = (bf16[256,256]{1,0:T(8,128)(2,1)S(1)}, bf16[256,256]{1,0:T(8,128)(2,1)}, u32[]{:S(2)}, u32[]{:S(2)}) collective-permute-start(bf16[256,256]{1,0:T(8,128)(2,1)S(1)} %slice.118), channel_id=1, source_target_pairs={{0,8},{2,10},{4,0},{6,2},{8,16},{10,18},{12,4},{14,6},{16,24},{18,... | collective-permute-start | bytes 393224 | tf_op jit(solution)/shard_map/ppermute | solution.py:499
  151.9 30.7 %all-to-all-start.3 = ((bf16[8,192,128]{2,1,0:T(8,128)(2,1)}), bf16[8,192,128]{2,1,0:T(8,128)(2,1)S(1)}, u32[]{:S(2)}, u32[]{:S(2)}) async-start(bf16[8,192,128]{2,1,0:T(8,128)(2,1)} %combine.1.own_ref), calls=%async_computation.3 | async-start | bytes 786432 | tf_op jit(solution)/shard_map/all_to_all | solution.py:462
  157.4 10.0 %collective-permute-start.18 = (bf16[256,256]{1,0:T(8,128)(2,1)}, bf16[256,256]{1,0:T(8,128)(2,1)}, u32[]{:S(2)}, u32[]{:S(2)}) collective-permute-start(bf16[256,256]{1,0:T(8,128)(2,1)} %slice.119), channel_id=1, source_target_pairs={{0,4},{2,6},{4,12},{6,14},{8,0},{10,2},{12,20},{14,22},{16,8},{18,... | collective-permute-start | bytes 393224 | tf_op jit(solution)/shard_map/ppermute | solution.py:499
  159.4 8.0 %collective-permute-start.14 = (bf16[8,192,128]{2,1,0:T(8,128)(2,1)}, bf16[8,192,128]{2,1,0:T(8,128)(2,1)S(1)}, u32[]{:S(2)}, u32[]{:S(2)}) collective-permute-start(bf16[8,192,128]{2,1,0:T(8,128)(2,1)} %combine.1.own_ref), channel_id=1, source_target_pairs={{0,2},{2,0},{4,6},{6,4},{8,10},{10,8},{12,14},{14,12},{16,18},{18,... | collective-permute-start | bytes 1179656 | tf_op jit(solution)/shard_map/ppermute | solution.py:465
  160.9 11.0 %copy-start.30 = (bf16[64,512]{1,0:T(8,128)(2,1)S(1)}, bf16[64,512]{1,0:T(8,128)(2,1)}, u32[]{:S(2)}) copy-start(bf16[64,512]{1,0:T(8,128)(2,1)} %pad_maximum_fusion.3) | copy-start | bytes 196612
  171.9 9.3 %collective-permute-start.33 = (bf16[64,512]{1,0:T(8,128)(2,1)S(1)}, bf16[64,512]{1,0:T(8,128)(2,1)S(1)}, u32[]{:S(2)}, u32[]{:S(2)}) collective-permute-start(bf16[64,512]{1,0:T(8,128)(2,1)S(1)} %copy-done.30), channel_id=1, source_target_pairs={{0,8},{2,10},{4,0},{6,2},{8,16},{10,18},{12,4},{14,6},{16,24},{18,... | collective-permute-start | bytes 196616 | tf_op jit(solution)/shard_map/ppermute | solution.py:499
  176.3 4.8 %collective-permute-start.34 = (bf16[64,512]{1,0:T(8,128)(2,1)S(1)}, bf16[64,512]{1,0:T(8,128)(2,1)S(1)}, u32[]{:S(2)}, u32[]{:S(2)}) collective-permute-start(bf16[64,512]{1,0:T(8,128)(2,1)S(1)} %pad_maximum_fusion.4), channel_id=1, source_target_pairs={{0,4},{2,6},{4,12},{6,14},{8,0},{10,2},{12,20},{14,22},{16,8},{18,... | collective-permute-start | bytes 196616 | tf_op jit(solution)/shard_map/ppermute | solution.py:499
  179.1 19.1 %collective-permute-start.24 = (bf16[3,64,1312]{2,1,0:T(8,128)(2,1)}, bf16[3,64,1312]{2,1,0:T(8,128)(2,1)}, u32[]{:S(2)}, u32[]{:S(2)}) collective-permute-start(bf16[3,64,1312]{2,1,0:T(8,128)(2,1)} %get-tuple-element.91), channel_id=1, source_target_pairs={{0,8},{2,10},{4,0},{6,2},{8,16},{10,18},{12,4},{14,6},{16,24},{18,... | collective-permute-start | bytes 1511432 | tf_op jit(solution)/shard_map/ppermute | solution.py:499
  181.1 17.1 %collective-permute-start.25 = (bf16[3,64,1312]{2,1,0:T(8,128)(2,1)}, bf16[3,64,1312]{2,1,0:T(8,128)(2,1)}, u32[]{:S(2)}, u32[]{:S(2)}) collective-permute-start(bf16[3,64,1312]{2,1,0:T(8,128)(2,1)} %get-tuple-element.92), channel_id=1, source_target_pairs={{0,4},{2,6},{4,12},{6,14},{8,0},{10,2},{12,20},{14,22},{16,8},{18,... | collective-permute-start | bytes 1511432 | tf_op jit(solution)/shard_map/ppermute | solution.py:499
  187.5 9.1 %collective-permute-start.35 = (bf16[64,512]{1,0:T(8,128)(2,1)}, bf16[64,512]{1,0:T(8,128)(2,1)}, u32[]{:S(2)}, u32[]{:S(2)}) collective-permute-start(bf16[64,512]{1,0:T(8,128)(2,1)} %get-tuple-element.100), channel_id=1, source_target_pairs={{0,8},{2,10},{4,0},{6,2},{8,16},{10,18},{12,4},{14,6},{16,24},{18,... | collective-permute-start | bytes 196616 | tf_op jit(solution)/shard_map/ppermute | solution.py:499
  189.5 7.1 %collective-permute-start.36 = (bf16[64,512]{1,0:T(8,128)(2,1)S(1)}, bf16[64,512]{1,0:T(8,128)(2,1)}, u32[]{:S(2)}, u32[]{:S(2)}) collective-permute-start(bf16[64,512]{1,0:T(8,128)(2,1)S(1)} %get-tuple-element.101), channel_id=1, source_target_pairs={{0,4},{2,6},{4,12},{6,14},{8,0},{10,2},{12,20},{14,22},{16,8},{18,... | collective-permute-start | bytes 196616 | tf_op jit(solution)/shard_map/ppermute | solution.py:499
  191.7 11.6 %collective-permute-start.19 = (bf16[128,1024]{1,0:T(8,128)(2,1)S(1)}, bf16[128,1024]{1,0:T(8,128)(2,1)}, u32[]{:S(2)}, u32[]{:S(2)}) collective-permute-start(bf16[128,1024]{1,0:T(8,128)(2,1)S(1)} %project_back.1), channel_id=1, source_target_pairs={{0,1},{1,0},{2,3},{3,2},{4,5},{5,4},{6,7},{7,6},{8,9},{9,8},{10,11... | collective-permute-start | bytes 786440 | tf_op jit(solution)/shard_map/ppermute | solution.py:477
  192.4 14.1 %all-to-all-start.4 = ((bf16[8,64,192]{2,1,0:T(8,128)(2,1)}), bf16[8,64,192]{2,1,0:T(8,128)(2,1)S(1)}, u32[]{:S(2)}, u32[]{:S(2)}) async-start(bf16[8,64,192]{2,1,0:T(8,128)(2,1)} %bitcast.78), calls=%async_computation.4 | async-start | bytes 524288 | tf_op jit(solution)/shard_map/all_to_all | solution.py:462
  201.0 13.6 %collective-permute-start.26 = (bf16[3,64,1312]{2,1,0:T(8,128)(2,1)}, bf16[3,64,1312]{2,1,0:T(8,128)(2,1)}, u32[]{:S(2)}, u32[]{:S(2)}) collective-permute-start(bf16[3,64,1312]{2,1,0:T(8,128)(2,1)} %get-tuple-element.93), channel_id=1, source_target_pairs={{0,8},{2,10},{4,0},{6,2},{8,16},{10,18},{12,4},{14,6},{16,24},{18,... | collective-permute-start | bytes 1511432 | tf_op jit(solution)/shard_map/ppermute | solution.py:499
  203.0 12.7 %collective-permute-start.27 = (bf16[3,64,1312]{2,1,0:T(8,128)(2,1)}, bf16[3,64,1312]{2,1,0:T(8,128)(2,1)}, u32[]{:S(2)}, u32[]{:S(2)}) collective-permute-start(bf16[3,64,1312]{2,1,0:T(8,128)(2,1)} %get-tuple-element.94), channel_id=1, source_target_pairs={{0,4},{2,6},{4,12},{6,14},{8,0},{10,2},{12,20},{14,22},{16,8},{18,... | collective-permute-start | bytes 1511432 | tf_op jit(solution)/shard_map/ppermute | solution.py:499
  211.1 8.8 %collective-permute-start.37 = (bf16[64,512]{1,0:T(8,128)(2,1)}, bf16[64,512]{1,0:T(8,128)(2,1)S(1)}, u32[]{:S(2)}, u32[]{:S(2)}) collective-permute-start(bf16[64,512]{1,0:T(8,128)(2,1)} %get-tuple-element.102), channel_id=1, source_target_pairs={{0,8},{2,10},{4,0},{6,2},{8,16},{10,18},{12,4},{14,6},{16,24},{18,... | collective-permute-start | bytes 196616 | tf_op jit(solution)/shard_map/ppermute | solution.py:499
  212.9 7.0 %collective-permute-start.38 = (bf16[64,512]{1,0:T(8,128)(2,1)S(1)}, bf16[64,512]{1,0:T(8,128)(2,1)S(1)}, u32[]{:S(2)}, u32[]{:S(2)}) collective-permute-start(bf16[64,512]{1,0:T(8,128)(2,1)S(1)} %get-tuple-element.103), channel_id=1, source_target_pairs={{0,4},{2,6},{4,12},{6,14},{8,0},{10,2},{12,20},{14,22},{16,8},{18,... | collective-permute-start | bytes 196616 | tf_op jit(solution)/shard_map/ppermute | solution.py:499
  218.6 4.3 %collective-permute-start.28 = (f32[2,64]{1,0:T(2,128)S(1)}, f32[2,64]{1,0:T(2,128)S(1)}, u32[]{:S(2)}, u32[]{:S(2)}) collective-permute-start(f32[2,64]{1,0:T(2,128)S(1)} %pad_maximum_fusion.5), channel_id=1, source_target_pairs={{0,1},{1,0},{2,3},{3,2},{4,5},{5,4},{6,7},{7,6},{8,9},{9,8},{10,11... | collective-permute-start | bytes 1544 | tf_op jit(solution)/shard_map/ppermute | solution.py:477
  (32 other events, 85.2 us)

commit v3 on v2

v3 whole, which is shorter than its diff:
```python
import functools
import math

import jax
import jax.numpy as jnp
from jax import lax
from jax.experimental import pallas as pl
from jax.experimental.pallas import tpu as pltpu
from jax.sharding import PartitionSpec as P

HD = 64
HALF = HD // 2
ROPE_BASE = 160000.0
NORM_EPS = 1e-05
BF = jnp.bfloat16
F32 = jnp.float32
GRANT = 60 * 1024 * 1024


def dot(a, b, dims):
    return lax.dot_general(a, b, (dims, ((), ())), preferred_element_type=F32)


def nn(a, b):
    return dot(a, b, ((1,), (0,)))


def nt(a, b):
    return dot(a, b, ((1,), (1,)))


def staged(body, ins, outs, name, scratch=(), late=0, scalars=0, cost=None, far=0):
    arrays = ins[scalars:]
    count = len(arrays)

    def kernel(*refs):
        front, refs = refs[:scalars], refs[scalars:]
        given, refs = refs[:count], refs[count:]
        results, refs = refs[: len(outs)], refs[len(outs) :]
        held, sems, rest = refs[:count], refs[count], refs[count + 1 :]
        copies = [pltpu.make_async_copy(g, h, sems.at[i]) for i, (g, h) in enumerate(zip(given, held))]
        for copy in copies:
            copy.start()
        for copy in copies[: count - late]:
            copy.wait()
        body(*front, *held, *results, *rest, *[copy.wait for copy in copies[count - late :]])

    vmem, hbm = pl.BlockSpec(memory_space=pltpu.VMEM), pl.BlockSpec(memory_space=pltpu.HBM)
    specs = [vmem] * (len(outs) - far) + [hbm] * far
    return pl.pallas_call(
        kernel,
        in_specs=[pl.BlockSpec(memory_space=pltpu.SMEM)] * scalars + [hbm] * count,
        out_specs=specs,
        out_shape=outs,
        scratch_shapes=[
            *[pltpu.VMEM(v.shape, v.dtype) for v in arrays],
            pltpu.SemaphoreType.DMA((count,)),
            *scratch,
        ],
        compiler_params=pltpu.CompilerParams(vmem_limit_bytes=GRANT),
        cost_estimate=cost,
        name=name,
    )(*ins)


def work(flops, byte_count, transcendentals=0):
    return pl.CostEstimate(flops=flops, bytes_accessed=byte_count, transcendentals=transcendentals)


def shaped(shape, dtype):
    return jax.ShapeDtypeStruct(shape, dtype)


def load_rows(parts, row, out_ref):
    for j, (ref, first) in enumerate(parts):
        blocks, width = ref.shape[0], ref.shape[2]
        for b in range(blocks):
            out_ref[j, b * width : (b + 1) * width, :] = ref[b, first + row : first + row + HD, :].T


def load_columns(parts, row, out_ref):
    for j, (ref, first) in enumerate(parts):
        blocks, width = ref.shape[0], ref.shape[2]
        for b in range(blocks):
            out_ref[j, :, b * width : (b + 1) * width] = ref[b, first + row : first + row + HD, :]


def attend_kernel(part_count, own_ref, *refs):
    others = refs[: part_count - 1]
    out_ref, low_ref, lse_ref, k_scr, vt_scr, s_scr = refs[part_count - 1 :]
    blocks, width = own_ref.shape[0], own_ref.shape[2]
    parts = [(r, HD) for r in (own_ref, *others)]
    load_rows(parts, 0, k_scr)
    load_columns(parts, HD, vt_scr)
    pair = s_scr.shape[2] // width

    @pl.loop(0, blocks // pair)
    def query_block(i):
        qt = jnp.concatenate([own_ref[pair * i + b, :HD, :] for b in range(pair)], axis=1)

        def score(j, top):
            s = nn(k_scr[j], qt)
            s_scr[j] = s
            return jnp.maximum(top, jnp.max(s, axis=0, keepdims=True))

        top = jnp.full((1, pair * width), -jnp.inf, F32)
        top = lax.fori_loop(0, part_count, score, top, unroll=part_count <= 2)

        def weigh(j, carry):
            total, acc = carry
            p = jnp.exp(s_scr[j] - top)
            return total + jnp.sum(p, axis=0, keepdims=True), acc + nn(vt_scr[j], p.astype(BF))

        start = (jnp.zeros((1, pair * width), F32), jnp.zeros((HD, pair * width), F32))
        total, acc = lax.fori_loop(0, part_count, weigh, start, unroll=part_count <= 2)
        attended = acc / total
        lse = top + jnp.log(total)
        for b in range(pair):
            cut = slice(b * width, (b + 1) * width)
            out_ref[pair * i + b] = attended[:, cut]
            for t in range(low_ref.shape[0]):
                low_ref[t, pair * i + b] = attended[:, cut].astype(BF)
            lse_ref[pair * i + b] = lse[:, cut]


def attend(tp_size, own, others):
    blocks, unused, width = own.shape
    part_count = 1 + len(others)
    keys = blocks * width
    pair = 2 if blocks % 2 == 0 else 1
    flops = 4 * keys * keys * part_count * HD
    return staged(
        functools.partial(attend_kernel, part_count),
        [own, *others],
        [
            shaped((blocks, HD, width), F32),
            shaped((tp_size, blocks, HD, width), BF),
            shaped((blocks, 1, width), F32),
        ],
        "attend",
        [
            pltpu.VMEM((part_count, keys, HD), BF),
            pltpu.VMEM((part_count, HD, keys), BF),
            pltpu.VMEM((part_count, keys, pair * width), F32),
        ],
        cost=work(flops, 4 * own.size, keys * keys * part_count),
    )


def turn_back(values, cosine, sine):
    first, second = values[:HALF], values[HALF:]
    return jnp.concatenate([first * cosine + second * sine, second * cosine - first * sine], axis=0)


def attend_back_kernel(part_count, own_ref, *refs):
    others = refs[: part_count - 1]
    refs = refs[part_count - 1 :]
    grad_ref, out_ref, lse_ref, cos_ref, sin_ref = refs[:5]
    dq_ref, dkv_ref = refs[5:7]
    dkv_others = refs[7 : 6 + part_count]
    k_scr, v_scr, kt_scr, dk_scr, dv_scr = refs[6 + part_count :]
    blocks, width = own_ref.shape[0], own_ref.shape[2]
    parts = [(r, HD) for r in (own_ref, *others)]
    load_rows(parts, 0, k_scr)
    load_rows(parts, HD, v_scr)
    load_columns(parts, 0, kt_scr)
    dk_scr[...] = jnp.zeros_like(dk_scr)
    dv_scr[...] = jnp.zeros_like(dv_scr)
    pair = 2 if blocks % 2 == 0 else 1

    @pl.loop(0, blocks // pair)
    def query_block(i):
        span = range(pair)
        qt = jnp.concatenate([own_ref[pair * i + b, :HD, :] for b in span], axis=1)
        gt = jnp.concatenate(
            [
                (grad_ref[0, pair * i + b].astype(F32) + grad_ref[1, pair * i + b].astype(F32)).astype(BF)
                for b in span
            ],
            axis=1,
        )
        ot = jnp.concatenate([out_ref[pair * i + b] for b in span], axis=1)
        lse = jnp.concatenate([lse_ref[pair * i + b] for b in span], axis=1)
        q, g = qt.T, gt.T
        delta = jnp.sum(gt.astype(F32) * ot, axis=0, keepdims=True)

        def one(j, dq):
            p = jnp.exp(nn(k_scr[j], qt) - lse)
            ds = (p * (nn(v_scr[j], gt) - delta)).astype(BF)
            dv_scr[j] += nn(p.astype(BF), g)
            dk_scr[j] += nn(ds, q)
            return dq + nn(kt_scr[j], ds)

        start = jnp.zeros((HD, pair * width), F32)
        dq = lax.fori_loop(0, part_count, one, start, unroll=part_count <= 2)
        for b in span:
            at = pair * i + b
            block = dq[:, b * width : (b + 1) * width] * (HD**-0.5)
            dq_ref[at] = turn_back(block, cos_ref[at], sin_ref[at]).astype(BF)

    for j, ref in enumerate((dkv_ref, *dkv_others)):
        for b in range(blocks):
            rows = slice(b * width, (b + 1) * width)
            ref[b, :HD, :] = dk_scr[j, rows, :].T
            ref[b, HD:, :] = dv_scr[j, rows, :].T


def attend_back(own, others, grad, attended, lse, cosine, sine):
    blocks, unused, width = own.shape
    part_count = 1 + len(others)
    keys = blocks * width
    flops = 10 * keys * keys * part_count * HD
    return staged(
        functools.partial(attend_back_kernel, part_count),
        [own, *others, grad, attended, lse, cosine, sine],
        [shaped((blocks, HD, width), BF)] + [shaped((blocks, 2 * HD, width), F32)] * part_count,
        "attend_back",
        [
            pltpu.VMEM((part_count, keys, HD), BF),
            pltpu.VMEM((part_count, keys, HD), BF),
            pltpu.VMEM((part_count, HD, keys), BF),
            pltpu.VMEM((part_count, keys, HD), F32),
            pltpu.VMEM((part_count, keys, HD), F32),
        ],
        cost=work(flops, 8 * own.size, keys * keys * part_count),
    )


def combine_kernel(count, dq_ref, *refs):
    terms, (cos_ref, sin_ref, out_ref) = refs[:count], refs[count:]
    for b in range(dq_ref.shape[0]):
        total = terms[0][b]
        for ref in terms[1:]:
            total = total + ref[b]
        out_ref[b, :HD] = dq_ref[b]
        out_ref[b, HD : 2 * HD] = turn_back(total[:HD], cos_ref[b], sin_ref[b]).astype(BF)
        out_ref[b, 2 * HD :] = total[HD:].astype(BF)


def combine(dq, terms, cosine, sine):
    blocks, unused, width = dq.shape
    return staged(
        functools.partial(combine_kernel, len(terms)),
        [dq, *terms, cosine, sine],
        [shaped((blocks, 3 * HD, width), BF)],
        "combine",
        cost=work(dq.size, 20 * dq.size),
    )[0]


def standardise(values):
    centred = values - jnp.mean(values, axis=-1, keepdims=True)
    spread = jnp.mean(centred * centred, axis=-1, keepdims=True)
    scale = lax.rsqrt(spread + NORM_EPS)
    return centred * scale, scale


def standardise_back(gradient, gain, normed, scale):
    y = gradient * gain
    along = jnp.mean(y * normed, axis=-1, keepdims=True)
    return scale * (y - jnp.mean(y, axis=-1, keepdims=True) - normed * along)


def project_kernel(hidden_ref, gain_ref, cos_ref, sin_ref, *refs):
    weights, (packed_ref, input_ref), waits = refs[:3], refs[3:5], refs[5:]
    normed, unused = standardise(hidden_ref[...].astype(F32))
    attn_input = (normed * gain_ref[...]).astype(BF)
    input_ref[...] = attn_input
    cosine, sine = cos_ref[...], sin_ref[...]
    for c in range(3):
        waits[c]()
        rows = nn(attn_input, weights[c][0]).T
        for h in range(packed_ref.shape[0]):
            block = rows[h * HD : (h + 1) * HD]
            if c < 2:
                first, second = block[:HALF], block[HALF:]
                block = jnp.concatenate(
                    [first * cosine - second * sine, second * cosine + first * sine], axis=0
                )
            if c == 0:
                block = block * (HD**-0.5)
            packed_ref[h, c * HD : (c + 1) * HD] = block.astype(BF)


def project(hidden, gain, cosine, sine, weights):
    width, model = hidden.shape
    heads = weights.shape[2] // HD
    hbm, vmem = pl.BlockSpec(memory_space=pltpu.HBM), pl.BlockSpec(memory_space=pltpu.VMEM)

    def kernel(h_ref, g_ref, c_ref, s_ref, w_ref, packed_ref, input_ref, h_scr, w_scr, sems):
        copies = [pltpu.make_async_copy(h_ref, h_scr, sems.at[3])]
        copies += [pltpu.make_async_copy(w_ref.at[c], w_scr.at[c], sems.at[c]) for c in range(3)]
        for copy in copies:
            copy.start()
        copies[0].wait()
        blocks = [w_scr.at[pl.ds(c, 1)] for c in range(3)]
        waits = [copy.wait for copy in copies[1:]]
        project_kernel(h_scr, g_ref, c_ref, s_ref, *blocks, packed_ref, input_ref, *waits)

    return pl.pallas_call(
        kernel,
        in_specs=[hbm, vmem, vmem, vmem, hbm],
        out_specs=(vmem, vmem),
        out_shape=(shaped((heads, 3 * HD, width), BF), shaped((width, model), BF)),
        scratch_shapes=[
            pltpu.VMEM(hidden.shape, BF),
            pltpu.VMEM(weights.shape, BF),
            pltpu.SemaphoreType.DMA((4,)),
        ],
        compiler_params=pltpu.CompilerParams(vmem_limit_bytes=GRANT),
        name="project",
    )(hidden, gain, cosine, sine, weights)


def unit_back_kernel(cot_ref, w_ref, out_ref):
    out_ref[...] = nt(cot_ref[...], w_ref[...])


def unit_back(cotangent, weights):
    width, units = cotangent.shape[0], weights.shape[0]
    return staged(
        unit_back_kernel,
        [cotangent, weights],
        [shaped((width, units), F32)],
        "unit_back",
        cost=work(2 * width * weights.size, 2 * weights.size),
    )[0]


def middle_kernel(
    tp_ref,
    attn_ref,
    hidden_ref,
    cot_ref,
    gain_ref,
    own_ref,
    other_ref,
    grad_act_ref,
    w_in_ref,
    middle_ref,
    input_ref,
    gated_ref,
    act_ref,
    part_ref,
    heads_ref,
    wait_units,
):
    tp = tp_ref[0]
    branch = nn(attn_ref[tp].T, own_ref[...]) + nn(attn_ref[1 - tp].T, other_ref[...])
    middle = hidden_ref[...].astype(F32) + branch
    middle_ref[...] = middle
    normed, scale = standardise(middle)
    gain = gain_ref[...]
    mlp_input = (normed * gain).astype(BF)
    input_ref[...] = mlp_input
    wait_units()
    gate, up = nt(mlp_input, w_in_ref[0]), nt(mlp_input, w_in_ref[1])
    share = 0.5 * (1.0 + lax.erf(gate * (0.5**0.5)))
    slope = share + gate * jnp.exp(-0.5 * gate * gate) * ((2.0 * math.pi) ** -0.5)
    bent = gate * share
    grad_act = grad_act_ref[...]
    grad_gate = (slope * up * grad_act).astype(BF)
    grad_up = (bent * grad_act).astype(BF)
    units = grad_gate.shape[1]
    gated_ref[:, :units] = grad_gate
    gated_ref[:, units : 2 * units] = grad_up
    activated = (bent * up).astype(BF)
    gated_ref[:, 2 * units :] = activated
    act_ref[...] = activated
    part = nn(grad_gate, w_in_ref[0]) + nn(grad_up, w_in_ref[1])
    part_ref[...] = part.astype(BF)
    grad = 0.5 * cot_ref[...].astype(F32) + standardise_back(part, gain, normed, scale)
    grad = grad.astype(BF)
    shape = heads_ref.shape[1:]
    heads_ref[tp] = nt(own_ref[...], grad).astype(BF).reshape(shape)
    heads_ref[1 - tp] = nt(other_ref[...], grad).astype(BF).reshape(shape)


def middle_part(tp, attn, hidden, cotangent, gain, own, other, grad_act, w_in):
    width, model = hidden.shape
    units = w_in.shape[1]
    inner = own.shape[0]
    return staged(
        middle_kernel,
        [tp, attn, hidden, cotangent, gain, own, other, grad_act, w_in],
        [
            shaped((width, model), F32),
            shaped((width, model), BF),
            shaped((width, 3 * units), BF),
            shaped((width, units), BF),
            shaped((width, model), BF),
            shaped((2, inner // HD, HD, width), BF),
        ],
        "middle_part",
        late=1,
        scalars=1,
        cost=work(8 * width * model * (units + inner), 2 * w_in.size, 2 * width * units),
    )


def project_back_kernel(grad_ref, w_ref, out_ref):
    heads = grad_ref.shape[0]
    total = jnp.zeros(out_ref.shape, F32)
    for c in range(3):
        rows = jnp.concatenate([grad_ref[h, c * HD : (c + 1) * HD, :] for h in range(heads)], axis=0)
        total += nt(rows.T, w_ref[c])
    out_ref[...] = total.astype(BF)


def project_back(grad, weights):
    width = grad.shape[2]
    return staged(
        project_back_kernel,
        [grad, weights],
        [shaped((width, weights.shape[1]), BF)],
        "project_back",
        cost=work(2 * width * weights.size, 2 * weights.size),
    )[0]


def picked(pick_ref, own_ref, other_ref):
    values = jnp.concatenate([own_ref[...], other_ref[...]], axis=0)
    return nt(pick_ref[...], values).astype(BF)


def pick_kernel(pick_ref, own_ref, other_ref, out_ref):
    out_ref[...] = picked(pick_ref, own_ref, other_ref)


def pick_rows(pick, own, other):
    rows, width = pick.shape[0], own.shape[0]
    return staged(
        pick_kernel,
        [pick, own, other],
        [shaped((rows, 2 * width), BF)],
        "pick_rows",
        cost=work(4 * rows * own.size, 6 * own.size),
    )[0]


def head_weight_kernel(ids_ref, own_ref, other_ref, *refs):
    rows, out_ref = refs[:-1], refs[-1]
    width = own_ref.shape[2]
    total = jnp.zeros((rows[0].shape[0], own_ref.shape[1]), F32)
    for b, ref in enumerate(rows):
        at = ids_ref[b]
        total += nt(ref[:, :width], own_ref[at])
        total += nt(ref[:, width:], other_ref[at])
    out_ref[...] = total.astype(BF)


def head_weight(ids, own, other, rows):
    count = len(rows)
    return staged(
        head_weight_kernel,
        [ids, own, other, *rows],
        [shaped((rows[0].shape[0], own.shape[1]), BF)],
        "head_weight",
        scalars=1,
        cost=work(2 * count * rows[0].size * own.shape[1], 2 * count * rows[0].size),
    )[0]


def mlp_weight_kernel(sizes, pick_ref, *refs):
    given, outs = refs[:6], refs[6 : 6 + len(sizes)]
    total_scr, sems, wait_own, wait_other = refs[6 + len(sizes) :]
    in_own, in_other, cot_own, cot_other, own_ref, other_ref = given
    units = own_ref.shape[1] // 3
    rows_in = picked(pick_ref, in_own, in_other)
    rows_out = picked(pick_ref, cot_own, cot_other)
    wait_own()
    wait_other()
    columns = jnp.concatenate([own_ref[...], other_ref[...]], axis=0)
    total_scr[:, : 2 * units] = nn(rows_in, columns[:, : 2 * units]).astype(BF)
    total_scr[:, 2 * units :] = nn(rows_out, columns[:, 2 * units :]).astype(BF)
    copies, first = [], 0
    for r, ref in enumerate(outs):
        copies.append(pltpu.make_async_copy(total_scr.at[pl.ds(first, sizes[r])], ref, sems.at[r]))
        first += sizes[r]
    for copy in copies:
        copy.start()
    for copy in copies:
        copy.wait()


def mlp_weight(sizes, pick, in_own, in_other, cot_own, cot_other, own, other):
    rows, columns = sum(sizes), own.shape[1]
    return staged(
        functools.partial(mlp_weight_kernel, sizes),
        [pick, in_own, in_other, cot_own, cot_other, own, other],
        [shaped((size, columns), BF) for size in sizes],
        "mlp_weight",
        [pltpu.VMEM((rows, columns), BF), pltpu.SemaphoreType.DMA((len(sizes),))],
        late=2,
        cost=work(4 * rows * own.size, 2 * rows * columns + 8 * own.size),
        far=len(sizes),
    )


def out_weight_kernel(pick_ref, own_ref, other_ref, attn_ref, attn_other_ref, *outs):
    rows = picked(pick_ref, own_ref, other_ref)
    columns = jnp.concatenate([attn_ref[...], attn_other_ref[...]], axis=1)
    total = nt(rows, columns).astype(BF)
    first = 0
    for ref in outs:
        ref[...] = total[first : first + ref.shape[0]]
        first += ref.shape[0]


def out_weight(sizes, pick, own, other, attn, attn_other):
    return staged(
        out_weight_kernel,
        [pick, own, other, attn, attn_other],
        [shaped((size, attn.shape[0]), BF) for size in sizes],
        "out_weight",
        cost=work(4 * sum(sizes) * attn.size, 8 * own.size),
    )


def finish_qkv_kernel(first_ref, blocks_ref, w_ref, out_ref, gain_ref, w_scr, sem):
    mine = out_ref.shape[1]
    rows = pl.ds(pl.multiple_of(first_ref[0], mine), mine)
    copy = pltpu.make_async_copy(w_ref.at[:, rows, :], w_scr, sem)
    copy.start()
    for c in range(3):
        for h in range(blocks_ref.shape[0]):
            cut = slice(h * HD, (h + 1) * HD)
            out_ref[c, :, cut] = blocks_ref[h, :, c * HD : (c + 1) * HD].astype(F32)
    copy.wait()
    total = jnp.zeros((mine, 1), F32)
    for c in range(3):
        total += jnp.sum(out_ref[c] * w_scr[c].astype(F32), axis=1, keepdims=True)
    gain_ref[...] = total


def finish_qkv(first, blocks, weights):
    heads, mine, unused = blocks.shape
    inner = weights.shape[2]
    vmem, hbm = pl.BlockSpec(memory_space=pltpu.VMEM), pl.BlockSpec(memory_space=pltpu.HBM)
    return pl.pallas_call(
        finish_qkv_kernel,
        in_specs=[pl.BlockSpec(memory_space=pltpu.SMEM), vmem, hbm],
        out_specs=(vmem, vmem),
        out_shape=(shaped((3, mine, inner), F32), shaped((mine, 1), F32)),
        scratch_shapes=[pltpu.VMEM((3, mine, inner), BF), pltpu.SemaphoreType.DMA],
        compiler_params=pltpu.CompilerParams(vmem_limit_bytes=GRANT),
        name="finish_qkv",
    )(first, blocks, weights)


def finish_mlp_kernel(own_ref, right_ref, left_ref, w_ref, in_ref, out_ref, gain_ref):
    units = out_ref.shape[1]
    total = own_ref[...].astype(F32) + right_ref[...].astype(F32) + left_ref[...].astype(F32)
    out_ref[...] = total[:, 2 * units :]
    in_ref[:, 0, :] = total[:, :units]
    in_ref[:, 1, :] = total[:, units : 2 * units]
    gain_ref[...] = jnp.sum(total[:, : 2 * units] * w_ref[...].astype(F32), axis=1, keepdims=True)


def finish_mlp(own, right, left, rows):
    mine, units = own.shape[0], own.shape[1] // 3
    return staged(
        finish_mlp_kernel,
        [own, right, left, rows],
        [shaped((mine, 2, units), F32), shaped((mine, units), F32), shaped((mine, 1), F32)],
        "finish_mlp",
        cost=work(8 * own.size, 14 * own.size),
    )


def middle_back_kernel(middle_ref, cot_ref, gain_ref, own_ref, other_ref, out_ref, low_ref):
    normed, scale = standardise(middle_ref[...])
    part = own_ref[...].astype(F32) + other_ref[...].astype(F32)
    grad = cot_ref[...].astype(F32) + standardise_back(part, gain_ref[...], normed, scale)
    out_ref[...] = grad
    low_ref[...] = grad.astype(BF)


def middle_back(middle, cotangent, gain, own, other):
    return staged(
        middle_back_kernel,
        [middle, cotangent, gain, own, other],
        [shaped(middle.shape, F32), shaped(middle.shape, BF)],
        "middle_back",
        cost=work(20 * middle.size, 16 * middle.size),
    )


def input_back_kernel(hidden_ref, gain_ref, own_ref, grad_ref, other_ref, out_ref):
    normed, scale = standardise(hidden_ref[...].astype(F32))
    part = own_ref[...].astype(F32) + other_ref[...].astype(F32)
    out_ref[...] = grad_ref[...] + standardise_back(part, gain_ref[...], normed, scale)


def input_back(hidden, gain, own, grad, other):
    return staged(
        input_back_kernel,
        [hidden, gain, own, grad, other],
        [shaped(grad.shape, F32)],
        "input_back",
        cost=work(20 * grad.size, 14 * grad.size),
    )[0]


def layer(ctx_size, tp_size, hidden_in, cotangent, gain_attn, gain_mlp, w_qkv, w_attn_out, w_in, w_mlp_out):
    width = hidden_in.shape[0]
    model = hidden_in.shape[1]
    inner = w_qkv.shape[2]
    heads = inner // HD
    units = w_in.shape[2]
    chips = ctx_size // 2
    copies = chips // heads
    mine = model // ctx_size
    me = lax.axis_index("ctx")
    core = me % 2

    same_core = [[2 * p + k for p in range(chips)] for k in range(2)]
    head_groups = [
        [2 * (heads * g + p) + k for p in range(heads)] for g in range(copies) for k in range(2)
    ]

    wide_groups = [
        [(2 * (heads * g + p) + k) * tp_size + t for t in range(tp_size) for p in range(heads)]
        for g in range(copies)
        for k in range(2)
    ]

    def exchange_wide(values):
        return lax.all_to_all(values, ("ctx", "tp"), 0, 0, axis_index_groups=wide_groups)

    def exchange(values):
        return lax.all_to_all(values, "ctx", 0, 0, axis_index_groups=head_groups)

    def swap_core(values):
        return lax.ppermute(values, "ctx", [(c, c ^ 1) for c in range(ctx_size)])

    def shift_keys(values, step):
        ring = 2 * copies
        pairs = []
        for c in range(ctx_size):
            g, p, k = c // (2 * heads), (c // 2) % heads, c % 2
            t = (2 * g + k + step) % ring
            pairs.append((c, 2 * (heads * (t // 2) + p) + t % 2))
        return lax.ppermute(values, "ctx", pairs)

    def swap_tp(values):
        return lax.ppermute(values, "tp", [(0, 1), (1, 0)])

    def add_tp(low):
        return low.astype(F32) + swap_tp(low).astype(F32)

    def after(values, *earlier):
        return lax.optimization_barrier((values, earlier))[0]

    def ring_chip(position):
        position = position % chips
        up = 2 * position
        return jnp.where(position < chips // 2, up, 2 * chips - 1 - up)

    ring = [2 * q if q < chips // 2 else 2 * chips - 1 - 2 * q for q in range(chips)]
    place = {p: q for q, p in enumerate(ring)}

    def turn(values, step):
        pairs = [
            (2 * p + k, 2 * ring[(place[p] + step) % chips] + k)
            for p in range(chips)
            for k in range(2)
        ]
        return lax.ppermute(values, "ctx", pairs)

    chip = me // 2
    position = jnp.where(chip % 2 == 0, chip // 2, chips - 1 - chip // 2)
    ringed = copies == 1

    def picker(chip_ids):
        wanted = ((2 * chip_ids + core) * mine)[:, None] + jnp.arange(mine)[None, :]
        return (wanted.reshape(-1, 1) == jnp.arange(model)[None, :]).astype(BF)

    class Sum:
        def __init__(self, blocks):
            half = chips // 2
            self.own, self.step = blocks[0], 0
            self.rights = [blocks[half], *blocks[half - 1 : 0 : -1]]
            self.lefts = [blocks[half + 1], *blocks[half + 2 :]]

        def advance(self, *earlier):
            right, left = self.rights[self.step], self.lefts[self.step]
            if self.step == 1:
                cut = self.right.shape[-2]
                first = right[..., :cut, :].astype(F32) + self.right.astype(F32)
                right = jnp.concatenate([first.astype(BF), right[..., cut:, :]], axis=-2)
                last = left[..., cut:, :].astype(F32) + self.left.astype(F32)
                left = jnp.concatenate([left[..., :cut, :], last.astype(BF)], axis=-2)
            elif self.step > 1:
                right = (right.astype(F32) + self.right.astype(F32)).astype(BF)
                left = (left.astype(F32) + self.left.astype(F32)).astype(BF)
            self.step += 1
            right, left = after((right, left), *earlier)
            self.right, self.left = turn(right, 1), turn(left, -1)
            return right, left

        def result(self):
            total = self.own.astype(F32) + self.right.astype(F32)
            return total + self.left.astype(F32)

    def scatter(parts):
        flat = parts.reshape(chips, -1)
        summed = lax.psum_scatter(
            flat, "ctx", scatter_dimension=0, tiled=True, axis_index_groups=same_core
        )
        return summed.reshape((mine,) + parts.shape[1:]).astype(F32)

    group_first = (me // (2 * heads)) * (2 * heads)
    block_ids = group_first + 2 * jnp.arange(heads) + core
    inverse = ROPE_BASE ** (-(jnp.arange(HALF).astype(F32) * 2.0) / HD)

    def tables(ids):
        positions = (ids[:, None] * width + jnp.arange(width)[None, :]).astype(F32)
        angles = positions[:, None, :] * inverse[None, :, None]
        return jnp.cos(angles), jnp.sin(angles)

    tp = lax.axis_index("tp")
    tp_list = tp.astype(jnp.int32).reshape(1)
    cos_one, sin_one = tables(me[None])
    w_three = w_qkv.transpose(1, 0, 2)
    w_pair = w_in.transpose(1, 2, 0)

    packed, attn_input = project(hidden_in, gain_attn[None], cos_one[0], sin_one[0], w_three)
    own = exchange(packed)
    w_out_other = swap_tp(w_attn_out)
    later_cot = after(cotangent, packed)
    cot_other = swap_core(later_cot)
    later_input = after(attn_input, packed)
    rows_in = pick_rows(
        picker(after(jnp.arange(chips), packed)), later_input, swap_core(later_input)
    )
    gathered = [rows_in]
    right = left = rows_in

    def gather_step(step, *earlier):
        nonlocal right, left
        if 2 * step == chips:
            right = turn(after(right, *earlier), 1)
            gathered.append(right)
            return
        right, left = after((right, left), *earlier)
        right, left = turn(right, 1), turn(left, -1)
        gathered.extend([right, left])

    if ringed:
        gather_step(1)
    cos_all, sin_all = tables(after(block_ids, rows_in))
    grad_activated = unit_back(after(later_cot, rows_in), w_mlp_out)
    order = after(jnp.arange(chips), rows_in)
    pick_ring = picker(ring_chip(position + order) if ringed else order)
    own = after(own, grad_activated, cos_all, sin_all, pick_ring)
    others = [shift_keys(own, step) for step in range(1, 2 * copies)]
    attended, attended_low, lse = attend(tp_size, own, others)
    attn_all = exchange_wide(attended_low.reshape(tp_size * heads, HD, width))
    if ringed:
        gather_step(2, attended_low)
    rows_w_in = lax.dynamic_slice_in_dim(after(w_in, attended_low), me * mine, mine, 0)
    rows_w_in = rows_w_in.reshape(mine, 2 * units)
    attn_all = after(attn_all, rows_w_in).reshape(tp_size, inner, width)
    if ringed:
        gather_step(3, attn_all)
    middle, mlp_input, gated, activated_low, part_two, head_terms = middle_part(
        tp_list,
        attn_all,
        hidden_in,
        cotangent,
        gain_mlp[None],
        w_attn_out,
        w_out_other,
        grad_activated,
        w_pair,
    )
    grad_received = exchange_wide(head_terms.reshape(tp_size * heads, HD, width))

    half = chips // 2
    sizes = [mine] * half + [mine // 2, mine // 2] + [mine] * (half - 1) if ringed else [chips * mine]
    parts_mlp = mlp_weight(
        sizes,
        pick_ring,
        mlp_input,
        swap_core(mlp_input),
        cotangent,
        cot_other,
        gated,
        swap_core(gated),
    )
    grad_received = after(grad_received, parts_mlp)
    if ringed:
        sum_mlp = Sum(parts_mlp)
        sum_mlp.advance()
        gather_step(4, grad_received)
    grad_received = grad_received.reshape(tp_size, heads, HD, width)
    dq, *grad_kv = attend_back(own, others, grad_received, attended, lse, cos_all, sin_all)

    part_two = after(part_two, parts_mlp)
    part_two_other = swap_tp(part_two)
    terms = [grad_kv[0]]
    for step in range(1, 2 * copies):
        terms.append(shift_keys(grad_kv[step], -step))
    if ringed:
        sent = sum_mlp.advance(dq)
        terms[0] = after(terms[0], sent)
    grad_own = combine(dq, terms, cos_all, sin_all)
    grad_back = exchange(grad_own)

    later_two = after(part_two_other, grad_own)
    grad_middle, grad_middle_low = middle_back(middle, cotangent, gain_mlp[None], part_two, later_two)
    attn_flat_t = lax.dynamic_index_in_dim(after(attn_all, grad_own), tp, 0, keepdims=False)
    parts_out = out_weight(
        sizes,
        pick_ring,
        grad_middle_low,
        swap_core(grad_middle_low),
        attn_flat_t,
        swap_core(attn_flat_t),
    )
    if ringed:
        sum_out = Sum(parts_out)
        sum_out.advance()
        steps = [0]
        for step in range(1, chips // 2 + 1):
            steps.extend([-step, step])
        ids = ring_chip(position + jnp.array(steps[:chips])).astype(jnp.int32)
        part_qkv = head_weight(ids, grad_own, swap_core(grad_own), gathered)
        grad_back = after(grad_back, part_qkv)
    part_one = project_back(grad_back, w_three)
    part_one_other = swap_tp(part_one)
    first = me * mine
    if ringed:
        blocks_qkv = exchange(after(part_qkv, part_one).reshape(chips, mine, 3 * HD))
        sent = sum_mlp.advance(part_one)
        sum_out.advance(sent)
        mlp_part = nn(after(activated_low, sent), w_mlp_out).astype(BF)
        output = (middle + add_tp(mlp_part)).astype(BF)
        part_one_other = after(part_one_other, mlp_part)
        grad_input = input_back(hidden_in, gain_attn[None], part_one, grad_middle, part_one_other)
        grad_w_qkv, gain_one = finish_qkv(
            first.astype(jnp.int32).reshape(1), after(blocks_qkv, grad_input), w_three
        )
        sum_out.advance(grad_input)
        sum_mlp.advance(gain_one)
        sum_out.advance(gain_one)
        grad_w_qkv = grad_w_qkv.transpose(1, 0, 2)
        grad_w_attn_out = sum_out.result().T
        grad_w_in, grad_w_mlp_out, gain_two = finish_mlp(
            sum_mlp.own, sum_mlp.right, sum_mlp.left, rows_w_in
        )
    else:
        output = (middle + add_tp(nn(activated_low, w_mlp_out).astype(BF))).astype(BF)
        grad_input = input_back(hidden_in, gain_attn[None], part_one, grad_middle, part_one_other)
        grad_back = grad_back.reshape(heads, 3, HD, width)
        grad_back = grad_back.transpose(1, 0, 2, 3).reshape(3, inner, width)
        columns_in = jnp.concatenate([grad_back, swap_core(grad_back)], axis=2)
        part_qkv = jnp.einsum("dt,cft->dcf", rows_in, columns_in, preferred_element_type=F32)
        grad_w_qkv = scatter(part_qkv.astype(BF))
        grad_mlp = scatter(parts_mlp[0])
        grad_w_in = grad_mlp[:, : 2 * units].reshape(mine, 2, units)
        grad_w_mlp_out = grad_mlp[:, 2 * units :]
        grad_w_attn_out = scatter(parts_out[0]).T
        rows_w_qkv = lax.dynamic_slice_in_dim(w_qkv, first, mine, 0)
        gain_one = jnp.sum(rows_w_qkv.astype(F32) * grad_w_qkv, axis=(1, 2))[:, None]
        gain_two = jnp.sum(rows_w_in.astype(F32) * grad_mlp[:, : 2 * units], axis=1)[:, None]

    def scale_gradient(term, gain):
        term = term[:, 0]
        return (term + swap_tp(term)) / lax.dynamic_slice_in_dim(gain, first, mine, 0)

    return (
        output,
        grad_input,
        scale_gradient(gain_one, gain_attn),
        scale_gradient(gain_two, gain_mlp),
        grad_w_qkv,
        grad_w_attn_out,
        grad_w_in,
        grad_w_mlp_out.T,
    )


def solution(mesh):
    in_specs = (
        P("ctx", None),
        P("ctx", None),
        P(),
        P(),
        P(None, None, "tp"),
        P("tp", None),
        P(None, None, "tp"),
        P("tp", None),
    )
    out_specs = (
        P("ctx", None),
        P("ctx", None),
        P("ctx"),
        P("ctx"),
        P("ctx", None, "tp"),
        P("tp", "ctx"),
        P("ctx", None, "tp"),
        P("tp", "ctx"),
    )
    body = functools.partial(layer, mesh.shape["ctx"], mesh.shape["tp"])
    return jax.shard_map(body, mesh=mesh, in_specs=in_specs, out_specs=out_specs, check_vma=False)
```

time: 226 us -> 197 us (0.87)
  Pallas kernels: 38.6 us -> 64.8 us
  local copies, waits for them, and re-layouts: 43.4 us -> 18.1 us
  matrix products: 12.9 us -> 0.58 us
  waiting for transfers between devices: 37.2 us -> 26.7 us
  other arithmetic: 29.1 us -> 20.7 us
    pallas_call x8 -> x15, Pallas kernels: 38.6 us -> 64.8 us  [the longest x13 58.1 us: staged(): pl.pallas_call(kernel, in_specs=[pl.BlockSpec(memory_space=pltpu.SMEM)] *...]
    dot_general x6 -> x1, matrix products: 12.9 us -> 0.58 us  [dot(): return lax.dot_general(a, b, (dims, ((), ())), preferred_element_type=F32)]
    unnamed x75 -> x78, local copies, waits for them, and re-layouts: 19.4 us -> 8.46 us
    ppermute x5 -> x6, waiting for transfers between devices: 12.6 us -> 2.33 us  [swap_tp(): return lax.ppermute(values, 'tp', [(0, 1), (1, 0)])]
    all_to_all x2, waiting for transfers between devices: 0.01 us -> 7.82 us  [exchange_wide(): lax.all_to_all(values, ('ctx', 'tp'), 0, 0, axis_index_groups=wide_groups)]
    ppermute x24 -> x23, waiting for transfers between devices: 21.3 us -> 14.6 us  [turn(): return lax.ppermute(values, 'ctx', pairs)]
    convert_element_type x4, other arithmetic: 8.68 us -> 3.01 us  [advance(): left = (left.astype(F32) + self.left.astype(F32)).astype(BF)]
    reduce_sum x7 -> x0, other arithmetic: 4.11 us -> none  [the longest x2 2.4 us: standardise_back(): return scale * (y - jnp.mean(y, axis=-1, keepdims=True) - normed * along)]
  transfers between devices with their start and end apart: 44 -> 43, of which waited for: 8 -> 12; matrix products, arithmetic and copies ran while one was open for 31% -> 14% of each run, Pallas kernels for 13% -> 25%
where the time goes in v3:
time: 197 us; the launch traced here: 196 us
  Pallas kernels  64.8 us (33%)
  starting transfers between devices  63.4 us (32%)
  waiting for transfers between devices  26.7 us (14%)
  other arithmetic  20.7 us (11%)
  local copies, waits for them, and re-layouts  18.1 us (9%)
    pallas_call x13, Pallas kernels, staged(): pl.pallas_call(kernel, in_specs=[pl.BlockSpec(memory_space=pltpu.SMEM)] *...  58.1 us
    ppermute x23, starting transfers between devices, turn(): return lax.ppermute(values, 'ctx', pairs)  28.9 us
    all_to_all x3, starting transfers between devices, exchange(): return lax.all_to_all(values, 'ctx', 0, 0, axis_index_groups=head_groups)  16.6 us
    ppermute x23, waiting for transfers between devices, turn(): return lax.ppermute(values, 'ctx', pairs)  14.6 us
    all_to_all x2, starting transfers between devices, exchange_wide(): lax.all_to_all(values, ('ctx', 'tp'), 0, 0, axis_index_groups=wide_groups)  9.65 us
    unnamed x78, local copies, waits for them, and re-layouts  8.46 us
    all_to_all x2, waiting for transfers between devices, exchange_wide(): lax.all_to_all(values, ('ctx', 'tp'), 0, 0, axis_index_groups=wide_groups)  7.82 us
    ppermute x6, starting transfers between devices, swap_tp(): return lax.ppermute(values, 'tp', [(0, 1), (1, 0)])  6.63 us
  transfers between devices with their start and end apart: 43, of which 12 were waited for; matrix products, arithmetic and copies ran while one was open for 14% of the time, Pallas kernels for 25%

profile of v3, /device:TPU:0, one launch (start us, length us, event | category | flops | bytes accessed | tf_op | source)
XLA Modules:
  0.0 195.7 jit_solution(7385776449572985950)
XLA Ops:
  1.4 4.1 %project.1 = (bf16[8,192,128]{2,1,0:T(8,128)(2,1)}, bf16[128,1024]{1,0:T(8,128)(2,1)}) custom-call(bf16[128,1024]{1,0:T(8,128)(2,1)} %refs_0_.2, f32[1,1024]{1,0:T(1,128)} %bitcast.31, f32[32,128]{1,0:T(8,128)} %get-tuple-element.173.c_ref, f32[32,128]{1,0:T(8,128)} %get-tuple-element.172.s_ref, bf16[3,1024,512]{2,1,0:T(8,128)(2,1)} %bitcast.20), custom_call_target="tpu_custom_call" | custom-call | tf_op jit(solution)/shard_map/project/pallas_call | solution.py:300
  5.5 7.3 %all-to-all-start = ((bf16[8,192,128]{2,1,0:T(8,128)(2,1)}), bf16[8,192,128]{2,1,0:T(8,128)(2,1)S(1)}, u32[]{:S(2)}, u32[]{:S(2)}) async-start(bf16[8,192,128]{2,1,0:T(8,128)(2,1)} %get-tuple-element.89), calls=%async_computation | async-start | bytes 786432 | tf_op jit(solution)/shard_map/all_to_all | solution.py:632
  12.8 1.6 collective-permute-start.2
  16.4 2.6 %pick_rows.1.refs_3_ = bf16[512,256]{1,0:T(8,128)(2,1)} custom-call(bf16[512,1024]{1,0:T(8,128)(2,1)} %fusion.refs_0_, bf16[128,1024]{1,0:T(8,128)(2,1)} %get-tuple-element.93.refs_1_, bf16[128,1024]{1,0:T(8,128)(2,1)} %copy-done.25), custom_call_target="tpu_custom_call" | custom-call | flops 268435456 | bytes 786432 | tf_op jit(solution)/shard_map/pick_rows/pallas_call | solution.py:50
  20.5 1.2 multiply_sine_fusion
  21.7 3.8 %unit_back.1.refs_7_ = f32[128,1312]{1,0:T(8,128)} custom-call(bf16[128,1024]{1,0:T(8,128)(2,1)} %refs_1_.3, bf16[1312,1024]{1,0:T(8,128)(2,1)} %refs_1_.2), custom_call_target="tpu_custom_call" | custom-call | flops 343932928 | bytes 2686976 | tf_op jit(solution)/shard_map/unit_back/pallas_call | solution.py:50
  25.7 1.6 collective-permute-done.1.refs_1_
  28.0 7.1 %attend.1 = (f32[8,64,128]{2,1,0:T(8,128)}, bf16[2,8,64,128]{3,2,1,0:T(8,128)(2,1)}, f32[8,1,128]{2,1,0:T(1,128)}) custom-call(bf16[8,192,128]{2,1,0:T(8,128)(2,1)} %copy-done.21, bf16[8,192,128]{2,1,0:T(8,128)(2,1)} %copy-done.37), custom_call_target="tpu_custom_call" | custom-call | flops 536870912 | bytes 786432 | tf_op jit(solution)/shard_map/attend/pallas_call | solution.py:50
  35.1 6.1 %all-to-all-start.1 = ((bf16[16,64,128]{2,1,0:T(8,128)(2,1)}), bf16[16,64,128]{2,1,0:T(8,128)(2,1)S(1)}, u32[]{:S(2)}, u32[]{:S(2)}) async-start(bf16[16,64,128]{2,1,0:T(8,128)(2,1)} %bitcast.30), calls=%async_computation.1 | async-start | bytes 524288 | tf_op jit(solution)/shard_map/all_to_all | solution.py:629
  41.3 1.3 constant_dynamic-slice_fusion
  43.6 7.8 %all-to-all-done.1 = bf16[16,64,128]{2,1,0:T(8,128)(2,1)S(1)} async-done(((bf16[16,64,128]{2,1,0:T(8,128)(2,1)}), bf16[16,64,128]{2,1,0:T(8,128)(2,1)S(1)}, u32[]{:S(2)}, u32[]{:S(2)}) %all-to-all-start.1) | async-done | bytes 262176 | tf_op jit(solution)/shard_map/all_to_all | solution.py:629
  52.5 8.2 %middle_part.1 = (f32[128,1024]{1,0:T(8,128)}, bf16[128,1024]{1,0:T(8,128)(2,1)}, bf16[128,3936]{1,0:T(8,128)(2,1)}, bf16[128,1312]{1,0:T(8,128)(2,1)}, bf16[128...) custom-call(s32[1]{0:T(128)} %bitcast.refs_0_, bf16[2,512,128]{2,1,0:T(8,128)(2,1)} %bitcast.25, ...), custom_call_target="tpu_custom_call" | custom-call | flops 1912602624 | bytes 5373952 | tf_op jit(solution)/shard_map/middle_part/pallas_call | solution.py:50
  60.7 1.9 copy.20
  62.7 3.5 %all-to-all-start.2 = ((bf16[16,64,128]{2,1,0:T(8,128)(2,1)}), bf16[16,64,128]{2,1,0:T(8,128)(2,1)S(1)}, u32[]{:S(2)}, u32[]{:S(2)}) async-start(bf16[16,64,128]{2,1,0:T(8,128)(2,1)} %bitcast.29), calls=%async_computation.2 | async-start | bytes 524288 | tf_op jit(solution)/shard_map/all_to_all | solution.py:629
  66.9 1.8 collective-permute-start.12
  69.0 1.7 copy.21.refs_6_
  72.1 5.9 %mlp_weight.1 = (bf16[64,3936]{1,0:T(8,128)(2,1)}, bf16[64,3936]{1,0:T(8,128)(2,1)}, bf16[64,3936]{1,0:T(8,128)(2,1)}, bf16[64,3936]{1,0:T(8,128)(2,1)}, bf16[32...) custom-call(bf16[512,1024]{1,0:T(8,128)(2,1)} %fusion.1.refs_0_, ...), custom_call_target="tpu_custom_call" | custom-call | flops 1031798784 | bytes 8060928 | tf_op jit(solution)/shard_map/mlp_weight/pallas_call | solution.py:50
  78.0 1.8 collective-permute-start.7
  79.8 2.3 %collective-permute-start.14 = (bf16[512,256]{1,0:T(8,128)(2,1)}, bf16[512,256]{1,0:T(8,128)(2,1)S(1)}, u32[]{:S(2)}, u32[]{:S(2)}) collective-permute-start(bf16[512,256]{1,0:T(8,128)(2,1)} %collective-permute-done.12.refs_4_), channel_id=1, source_target_pairs={{0,8},{2,10},{4,0},{6,2},{8,16},{10,18},{12,4},{14,6},{16,24},{18,... | collective-permute-start | bytes 786440 | tf_op jit(solution)/shard_map/ppermute | solution.py:669
  84.2 2.1 %collective-permute-start.6 = (bf16[32,3936]{1,0:T(8,128)(2,1)}, bf16[32,3936]{1,0:T(8,128)(2,1)S(1)}, u32[]{:S(2)}, u32[]{:S(2)}) collective-permute-start(bf16[32,3936]{1,0:T(8,128)(2,1)} %get-tuple-element.109), channel_id=1, source_target_pairs={{0,8},{2,10},{4,0},{6,2},{8,16},{10,18},{12,4},{14,6},{16,24},{18,... | collective-permute-start | bytes 755720 | tf_op jit(solution)/shard_map/ppermute | solution.py:669
  86.3 8.9 %attend_back.1 = (bf16[8,64,128]{2,1,0:T(8,128)(2,1)}, f32[8,128,128]{2,1,0:T(8,128)}, f32[8,128,128]{2,1,0:T(8,128)}) custom-call(bf16[8,192,128]{2,1,0:T(8,128)(2,1)} %copy-done.21, bf16[8,192,128]{2,1,0:T(8,128)(2,1)} %copy-done.37, bf16[2,8,64,128]{3,2,1,0:T(8,128)(2,1)} %bitcast.28, f32[8,64,128]{2,1,0:T(8,128)} %get-tuple-element.118.refs_3_, ...), custom_call_target="tpu_custom_call" | custom-call | flops 1342177280 | bytes 1572864 | tf_op jit(solution)/shard_map/attend_back/pallas_call | solution.py:50
  97.3 2.0 %collective-permute-start.16 = (bf16[512,256]{1,0:T(8,128)(2,1)S(1)}, bf16[512,256]{1,0:T(8,128)(2,1)}, u32[]{:S(2)}, u32[]{:S(2)}) collective-permute-start(bf16[512,256]{1,0:T(8,128)(2,1)S(1)} %collective-permute-done.14.refs_6_), channel_id=1, source_target_pairs={{0,8},{2,10},{4,0},{6,2},{8,16},{10,18},{12,4},{14,6},{16,24},{18,... | collective-permute-start | bytes 786440 | tf_op jit(solution)/shard_map/ppermute | solution.py:669
  99.3 1.6 collective-permute-start.20
  101.5 4.7 %collective-permute-done.16.refs_8_ = bf16[512,256]{1,0:T(8,128)(2,1)} collective-permute-done((bf16[512,256]{1,0:T(8,128)(2,1)S(1)}, bf16[512,256]{1,0:T(8,128)(2,1)}, u32[]{:S(2)}, u32[]{:S(2)}) %collective-permute-start.16) | collective-permute-done | bytes 262176 | tf_op jit(solution)/shard_map/ppermute | solution.py:669
  106.2 1.6 collective-permute-start.18
  108.6 2.2 %combine.1.refs_1_ = bf16[8,192,128]{2,1,0:T(8,128)(2,1)} custom-call(bf16[8,64,128]{2,1,0:T(8,128)(2,1)} %get-tuple-element.120.refs_0_, f32[8,128,128]{2,1,0:T(8,128)} %get-tuple-element.124.refs_1_, f32[8,128,128]{2,1,0:T(8,128)} %copy-done.12, f32[8,32,128]{2,1,0:T(8,128)} %get-tuple-element.171.refs_5_.refs_3_, ...), custom_call_target="tpu_custom_call" | custom-call | flops 65536 | bytes 1310720 | tf_op jit(solution)/shard_map/combine/pallas_call | solution.py:50
  110.8 4.5 %all-to-all-start.3 = ((bf16[8,192,128]{2,1,0:T(8,128)(2,1)}), bf16[8,192,128]{2,1,0:T(8,128)(2,1)S(1)}, u32[]{:S(2)}, u32[]{:S(2)}) async-start(bf16[8,192,128]{2,1,0:T(8,128)(2,1)} %combine.1.refs_1_), calls=%async_computation.3 | async-start | bytes 786432 | tf_op jit(solution)/shard_map/all_to_all | solution.py:632
  115.4 2.6 %middle_back.1 = (f32[128,1024]{1,0:T(8,128)}, bf16[128,1024]{1,0:T(8,128)(2,1)}) custom-call(f32[128,1024]{1,0:T(8,128)} %get-tuple-element.101.refs_0_, bf16[128,1024]{1,0:T(8,128)(2,1)} %refs_1_.3, f32[1,1024]{1,0:T(1,128)} %bitcast.34, bf16[128,1024]{1,0:T(8,128)(2,1)} %get-tuple-element.138.refs_3_, bf16[128,1024]{1,0:T(8,128)(2,1)} %collective-permute-done.20.refs_4_), custom_call_target="tpu_custom_call" | custom-call | flops 2621440 | bytes 2097152 | tf_op jit(solution)/shard_map/middle_back/pallas_call | solution.py:50
  120.9 3.0 %out_weight.1 = (bf16[64,512]{1,0:T(8,128)(2,1)}, bf16[64,512]{1,0:T(8,128)(2,1)}, bf16[64,512]{1,0:T(8,128)(2,1)}, bf16[64,512]{1,0:T(8,128)(2,1)}, bf16[32,512...) custom-call(bf16[512,1024]{1,0:T(8,128)(2,1)} %fusion.1.refs_0_, ...), custom_call_target="tpu_custom_call" | custom-call | flops 134217728 | bytes 1048576 | tf_op jit(solution)/shard_map/out_weight/pallas_call | solution.py:50
  123.9 2.1 %collective-permute-start.31 = (bf16[32,512]{1,0:T(8,128)(2,1)}, bf16[32,512]{1,0:T(8,128)(2,1)S(1)}, u32[]{:S(2)}, u32[]{:S(2)}) collective-permute-start(bf16[32,512]{1,0:T(8,128)(2,1)} %get-tuple-element.159), channel_id=1, source_target_pairs={{0,4},{2,6},{4,12},{6,14},{8,0},{10,2},{12,20},{14,22},{16,8},{18,... | collective-permute-start | bytes 98312 | tf_op jit(solution)/shard_map/ppermute | solution.py:669
  127.9 1.9 collective-permute-start.30
  131.3 1.6 collective-permute-done.30
  135.8 4.5 %head_weight.1 = bf16[512,192]{1,0:T(8,128)(2,1)} custom-call(s32[8]{0:T(128)} %compare_select_fusion.4.refs_0_, bf16[8,192,128]{2,1,0:T(8,128)(2,1)} %combine.1.refs_1_, bf16[8,192,128]{2,1,0:T(8,128)(2,1)} %copy-done.22, bf16[512,256]{1,0:T(8,128)(2,1)} %pick_rows.1.refs_3_, bf16[512,256]{1,0:T(8,128)(2,1)} %collective-permute-done.12.refs_4_, ...), custom_call_target="tpu_custom_call" | custom-call | flops 402653184 | bytes 2097152 | tf_op jit(solution)/shard_map/head_weight/pallas_call | solution.py:50
  141.0 4.1 %project_back.1.refs_2_ = bf16[128,1024]{1,0:T(8,128)(2,1)} custom-call(bf16[8,192,128]{2,1,0:T(8,128)(2,1)} %copy-done.6, bf16[3,1024,512]{2,1,0:T(8,128)(2,1)} %bitcast.21), custom_call_target="tpu_custom_call" | custom-call | flops 402653184 | bytes 3145728 | tf_op jit(solution)/shard_map/project_back/pallas_call | solution.py:50
  146.0 3.1 %collective-permute-start.24 = (bf16[64,3936]{1,0:T(8,128)(2,1)}, bf16[64,3936]{1,0:T(8,128)(2,1)}, u32[]{:S(2)}, u32[]{:S(2)}) collective-permute-start(bf16[64,3936]{1,0:T(8,128)(2,1)} %add_convert_fusion.2), channel_id=1, source_target_pairs={{0,4},{2,6},{4,12},{6,14},{8,0},{10,2},{12,20},{14,22},{16,8},{18,... | collective-permute-start | bytes 1511432 | tf_op jit(solution)/shard_map/ppermute | solution.py:669
  149.2 2.0 %collective-permute-start.33 = (bf16[64,512]{1,0:T(8,128)(2,1)}, bf16[64,512]{1,0:T(8,128)(2,1)}, u32[]{:S(2)}, u32[]{:S(2)}) collective-permute-start(bf16[64,512]{1,0:T(8,128)(2,1)} %pad_maximum_fusion.3), channel_id=1, source_target_pairs={{0,4},{2,6},{4,12},{6,14},{8,0},{10,2},{12,20},{14,22},{16,8},{18,... | collective-permute-start | bytes 196616 | tf_op jit(solution)/shard_map/ppermute | solution.py:669
  151.8 4.8 %all-to-all-start.4 = ((bf16[8,64,192]{2,1,0:T(8,128)(2,1)}), bf16[8,64,192]{2,1,0:T(8,128)(2,1)S(1)}, u32[]{:S(2)}, u32[]{:S(2)}) async-start(bf16[8,64,192]{2,1,0:T(8,128)(2,1)} %bitcast.27), calls=%async_computation.4 | async-start | bytes 524288 | tf_op jit(solution)/shard_map/all_to_all | solution.py:632
  156.6 5.1 %collective-permute-done.33 = bf16[64,512]{1,0:T(8,128)(2,1)} collective-permute-done((bf16[64,512]{1,0:T(8,128)(2,1)}, bf16[64,512]{1,0:T(8,128)(2,1)}, u32[]{:S(2)}, u32[]{:S(2)}) %collective-permute-start.33) | collective-permute-done | bytes 65568 | tf_op jit(solution)/shard_map/ppermute | solution.py:669
  164.4 2.5 %input_back.1 = f32[128,1024]{1,0:T(8,128)} custom-call(bf16[128,1024]{1,0:T(8,128)(2,1)} %refs_0_.2, f32[1,1024]{1,0:T(1,128)} %bitcast.32, bf16[128,1024]{1,0:T(8,128)(2,1)} %project_back.1.refs_2_, f32[128,1024]{1,0:T(8,128)} %get-tuple-element.140.refs_3_, bf16[128,1024]{1,0:T(8,128)(2,1)} %collective-permute-done.21.refs_4_), custom_call_target="tpu_custom_call" | custom-call | flops 2621440 | bytes 1835008 | tf_op jit(solution)/shard_map/input_back/pallas_call | solution.py:50
  167.0 2.8 %collective-permute-start.35 = (bf16[64,512]{1,0:T(8,128)(2,1)S(1)}, bf16[64,512]{1,0:T(8,128)(2,1)S(1)}, u32[]{:S(2)}, u32[]{:S(2)}) collective-permute-start(bf16[64,512]{1,0:T(8,128)(2,1)S(1)} %add_convert_fusion.9), channel_id=1, source_target_pairs={{0,4},{2,6},{4,12},{6,14},{8,0},{10,2},{12,20},{14,22},{16,8},{18,... | collective-permute-start | bytes 196616 | tf_op jit(solution)/shard_map/ppermute | solution.py:669
  171.3 2.7 %finish_qkv.1 = (f32[3,64,512]{2,1,0:T(8,128)}, f32[64,1]{1,0:T(8,128)}) custom-call(s32[1]{0:T(128)} %bitcast.10.first_ref, bf16[8,64,192]{2,1,0:T(8,128)(2,1)} %copy-done.7, bf16[3,1024,512]{2,1,0:T(8,128)(2,1)} %bitcast.22), custom_call_target="tpu_custom_call" | custom-call | tf_op jit(solution)/shard_map/finish_qkv/pallas_call | solution.py:540
  176.9 1.7 collective-permute-start.26
  182.4 1.3 dynamic-slice_divide_fusion.1
  183.6 1.8 collective-permute-done.25.refs_1_
  187.1 2.8 %finish_mlp.1 = (f32[64,2,1312]{2,1,0:T(2,128)}, f32[64,1312]{1,0:T(8,128)}, f32[64,1]{1,0:T(8,128)}) custom-call(bf16[64,3936]{1,0:T(8,128)(2,1)} %get-tuple-element.113.refs_0_, bf16[64,3936]{1,0:T(8,128)(2,1)} %copy-done.13, bf16[64,3936]{1,0:T(8,128)(2,1)} %copy-done.14, bf16[64,2624]{1,0:T(8,128)(2,1)} %copy.22.refs_3_), custom_call_target="tpu_custom_call" | custom-call | flops 2015232 | bytes 3526656 | tf_op jit(solution)/shard_map/finish_mlp/pallas_call | solution.py:50
  190.8 1.3 collective-permute-start.27
  192.8 1.6 collective-permute-done.27
  194.4 1.3 dynamic-slice_divide_fusion
  (181 shorter events, 40.8 us)
Async XLA Ops:
  5.5 20.0 %all-to-all-start = ((bf16[8,192,128]{2,1,0:T(8,128)(2,1)}), bf16[8,192,128]{2,1,0:T(8,128)(2,1)S(1)}, u32[]{:S(2)}, u32[]{:S(2)}) async-start(bf16[8,192,128]{2,1,0:T(8,128)(2,1)} %get-tuple-element.89), calls=%async_computation | async-start | bytes 786432 | tf_op jit(solution)/shard_map/all_to_all | solution.py:632
  12.8 2.9 %collective-permute-start = (bf16[128,1024]{1,0:T(8,128)(2,1)}, bf16[128,1024]{1,0:T(8,128)(2,1)S(1)}, u32[]{:S(2)}, u32[]{:S(2)}) collective-permute-start(bf16[128,1024]{1,0:T(8,128)(2,1)} %get-tuple-element.93.refs_1_), channel_id=1, source_target_pairs={{0,2},{2,0},{4,6},{6,4},{8,10},{10,8},{12,14},{14,12},{16,18},{18,... | collective-permute-start | bytes 786440 | tf_op jit(solution)/shard_map/ppermute | solution.py:635
  12.8 38.6 %collective-permute-start.2 = (bf16[512,1024]{1,0:T(8,128)(2,1)S(1)}, bf16[512,1024]{1,0:T(8,128)(2,1)S(1)}, u32[]{:S(2)}, u32[]{:S(2)}) collective-permute-start(bf16[512,1024]{1,0:T(8,128)(2,1)S(1)} %copy-done.9), channel_id=1, source_target_pairs={{0,1},{1,0},{2,3},{3,2},{4,5},{5,4},{6,7},{7,6},{8,9},{9,8},{10,11... | collective-permute-start | bytes 3145736 | tf_op jit(solution)/shard_map/ppermute | solution.py:647
  25.5 1.8 collective-permute-start.1
  35.1 16.3 %all-to-all-start.1 = ((bf16[16,64,128]{2,1,0:T(8,128)(2,1)}), bf16[16,64,128]{2,1,0:T(8,128)(2,1)S(1)}, u32[]{:S(2)}, u32[]{:S(2)}) async-start(bf16[16,64,128]{2,1,0:T(8,128)(2,1)} %bitcast.30), calls=%async_computation.1 | async-start | bytes 524288 | tf_op jit(solution)/shard_map/all_to_all | solution.py:629
  62.7 6.3 %collective-permute-start.5 = (bf16[128,3936]{0,1:T(8,128)(2,1)S(1)}, bf16[128,3936]{0,1:T(8,128)(2,1)S(1)}, u32[]{:S(2)}, u32[]{:S(2)}) collective-permute-start(bf16[128,3936]{0,1:T(8,128)(2,1)S(1)} %copy.20), channel_id=1, source_target_pairs={{0,2},{2,0},{4,6},{6,4},{8,10},{10,8},{12,14},{14,12},{16,18},{18,... | collective-permute-start | bytes 3022856 | tf_op jit(solution)/shard_map/ppermute | solution.py:635
  62.7 21.4 %all-to-all-start.2 = ((bf16[16,64,128]{2,1,0:T(8,128)(2,1)}), bf16[16,64,128]{2,1,0:T(8,128)(2,1)S(1)}, u32[]{:S(2)}, u32[]{:S(2)}) async-start(bf16[16,64,128]{2,1,0:T(8,128)(2,1)} %bitcast.29), calls=%async_computation.2 | async-start | bytes 524288 | tf_op jit(solution)/shard_map/all_to_all | solution.py:629
  66.3 4.4 %collective-permute-start.4 = (bf16[128,1024]{1,0:T(8,128)(2,1)S(1)}, bf16[128,1024]{1,0:T(8,128)(2,1)S(1)}, u32[]{:S(2)}, u32[]{:S(2)}) collective-permute-start(bf16[128,1024]{1,0:T(8,128)(2,1)S(1)} %copy-done.1), channel_id=1, source_target_pairs={{0,2},{2,0},{4,6},{6,4},{8,10},{10,8},{12,14},{14,12},{16,18},{18,... | collective-permute-start | bytes 786440 | tf_op jit(solution)/shard_map/ppermute | solution.py:635
  66.8 3.8 %collective-permute-start.3 = (bf16[128,1024]{1,0:T(8,128)(2,1)}, bf16[128,1024]{1,0:T(8,128)(2,1)S(1)}, u32[]{:S(2)}, u32[]{:S(2)}) collective-permute-start(bf16[128,1024]{1,0:T(8,128)(2,1)} %get-tuple-element.103.refs_1_), channel_id=1, source_target_pairs={{0,2},{2,0},{4,6},{6,4},{8,10},{10,8},{12,14},{14,12},{16,18},{18,... | collective-permute-start | bytes 786440 | tf_op jit(solution)/shard_map/ppermute | solution.py:635
  66.9 12.9 %collective-permute-start.12 = (bf16[512,256]{1,0:T(8,128)(2,1)S(1)}, bf16[512,256]{1,0:T(8,128)(2,1)}, u32[]{:S(2)}, u32[]{:S(2)}) collective-permute-start(bf16[512,256]{1,0:T(8,128)(2,1)S(1)} %copy-done.8), channel_id=1, source_target_pairs={{0,8},{2,10},{4,0},{6,2},{8,16},{10,18},{12,4},{14,6},{16,24},{18,... | collective-permute-start | bytes 786440 | tf_op jit(solution)/shard_map/ppermute | solution.py:669
  68.7 11.1 %collective-permute-start.13 = (bf16[512,256]{1,0:T(8,128)(2,1)S(1)}, bf16[512,256]{1,0:T(8,128)(2,1)}, u32[]{:S(2)}, u32[]{:S(2)}) collective-permute-start(bf16[512,256]{1,0:T(8,128)(2,1)S(1)} %copy-done.8), channel_id=1, source_target_pairs={{0,4},{2,6},{4,12},{6,14},{8,0},{10,2},{12,20},{14,22},{16,8},{18,... | collective-permute-start | bytes 786440 | tf_op jit(solution)/shard_map/ppermute | solution.py:669
  78.0 17.3 %collective-permute-start.7 = (bf16[32,3936]{1,0:T(8,128)(2,1)}, bf16[32,3936]{1,0:T(8,128)(2,1)S(1)}, u32[]{:S(2)}, u32[]{:S(2)}) collective-permute-start(bf16[32,3936]{1,0:T(8,128)(2,1)} %get-tuple-element.111), channel_id=1, source_target_pairs={{0,4},{2,6},{4,12},{6,14},{8,0},{10,2},{12,20},{14,22},{16,8},{18,... | collective-permute-start | bytes 755720 | tf_op jit(solution)/shard_map/ppermute | solution.py:669
  79.8 17.4 %collective-permute-start.14 = (bf16[512,256]{1,0:T(8,128)(2,1)}, bf16[512,256]{1,0:T(8,128)(2,1)S(1)}, u32[]{:S(2)}, u32[]{:S(2)}) collective-permute-start(bf16[512,256]{1,0:T(8,128)(2,1)} %collective-permute-done.12.refs_4_), channel_id=1, source_target_pairs={{0,8},{2,10},{4,0},{6,2},{8,16},{10,18},{12,4},{14,6},{16,24},{18,... | collective-permute-start | bytes 786440 | tf_op jit(solution)/shard_map/ppermute | solution.py:669
  82.2 15.1 %collective-permute-start.15 = (bf16[512,256]{1,0:T(8,128)(2,1)}, bf16[512,256]{1,0:T(8,128)(2,1)}, u32[]{:S(2)}, u32[]{:S(2)}) collective-permute-start(bf16[512,256]{1,0:T(8,128)(2,1)} %collective-permute-done.13.refs_5_), channel_id=1, source_target_pairs={{0,4},{2,6},{4,12},{6,14},{8,0},{10,2},{12,20},{14,22},{16,8},{18,... | collective-permute-start | bytes 786440 | tf_op jit(solution)/shard_map/ppermute | solution.py:669
  84.2 12.0 %collective-permute-start.6 = (bf16[32,3936]{1,0:T(8,128)(2,1)}, bf16[32,3936]{1,0:T(8,128)(2,1)S(1)}, u32[]{:S(2)}, u32[]{:S(2)}) collective-permute-start(bf16[32,3936]{1,0:T(8,128)(2,1)} %get-tuple-element.109), channel_id=1, source_target_pairs={{0,8},{2,10},{4,0},{6,2},{8,16},{10,18},{12,4},{14,6},{16,24},{18,... | collective-permute-start | bytes 755720 | tf_op jit(solution)/shard_map/ppermute | solution.py:669
  95.2 12.5 %collective-permute-start.10 = (f32[8,128,128]{2,1,0:T(8,128)}, f32[8,128,128]{2,1,0:T(8,128)S(1)}, u32[]{:S(2)}, u32[]{:S(2)}) collective-permute-start(f32[8,128,128]{2,1,0:T(8,128)} %get-tuple-element.125), channel_id=1, source_target_pairs={{0,2},{2,0},{4,6},{6,4},{8,10},{10,8},{12,14},{14,12},{16,18},{18,... | collective-permute-start | bytes 1572872 | tf_op jit(solution)/shard_map/ppermute | solution.py:644
  95.4 19.9 %copy-start.5 = (bf16[16,64,128]{2,1,0:T(8,128)(2,1)S(1)}, bf16[16,64,128]{2,1,0:T(8,128)(2,1)}, u32[]{:S(2)}) copy-start(bf16[16,64,128]{2,1,0:T(8,128)(2,1)} %copy-done.4) | copy-start | bytes 786436
  96.3 22.3 %copy-start.18 = (bf16[64,3936]{1,0:T(8,128)(2,1)S(1)}, bf16[64,3936]{1,0:T(8,128)(2,1)}, u32[]{:S(2)}) copy-start(bf16[64,3936]{1,0:T(8,128)(2,1)} %get-tuple-element.115) | copy-start | bytes 1511428
  97.2 20.9 %collective-permute-start.9 = (bf16[64,3936]{1,0:T(8,128)(2,1)}, bf16[64,3936]{1,0:T(8,128)(2,1)S(1)}, u32[]{:S(2)}, u32[]{:S(2)}) collective-permute-start(bf16[64,3936]{1,0:T(8,128)(2,1)} %pad_maximum_fusion.1), channel_id=1, source_target_pairs={{0,4},{2,6},{4,12},{6,14},{8,0},{10,2},{12,20},{14,22},{16,8},{18,... | collective-permute-start | bytes 1511432 | tf_op jit(solution)/shard_map/ppermute | solution.py:669
  97.3 8.9 %collective-permute-start.16 = (bf16[512,256]{1,0:T(8,128)(2,1)S(1)}, bf16[512,256]{1,0:T(8,128)(2,1)}, u32[]{:S(2)}, u32[]{:S(2)}) collective-permute-start(bf16[512,256]{1,0:T(8,128)(2,1)S(1)} %collective-permute-done.14.refs_6_), channel_id=1, source_target_pairs={{0,8},{2,10},{4,0},{6,2},{8,16},{10,18},{12,4},{14,6},{16,24},{18,... | collective-permute-start | bytes 786440 | tf_op jit(solution)/shard_map/ppermute | solution.py:669
  99.3 16.1 %collective-permute-start.20 = (bf16[128,1024]{1,0:T(8,128)(2,1)S(1)}, bf16[128,1024]{1,0:T(8,128)(2,1)}, u32[]{:S(2)}, u32[]{:S(2)}) collective-permute-start(bf16[128,1024]{1,0:T(8,128)(2,1)S(1)} %copy-done.24), channel_id=1, source_target_pairs={{0,1},{1,0},{2,3},{3,2},{4,5},{5,4},{6,7},{7,6},{8,9},{9,8},{10,11... | collective-permute-start | bytes 786440 | tf_op jit(solution)/shard_map/ppermute | solution.py:647
  101.4 33.6 %collective-permute-start.17 = (bf16[512,256]{1,0:T(8,128)(2,1)}, bf16[512,256]{1,0:T(8,128)(2,1)}, u32[]{:S(2)}, u32[]{:S(2)}) collective-permute-start(bf16[512,256]{1,0:T(8,128)(2,1)} %collective-permute-done.15.refs_7_), channel_id=1, source_target_pairs={{0,4},{2,6},{4,12},{6,14},{8,0},{10,2},{12,20},{14,22},{16,8},{18,... | collective-permute-start | bytes 786440 | tf_op jit(solution)/shard_map/ppermute | solution.py:669
  106.2 28.8 %collective-permute-start.18 = (bf16[512,256]{1,0:T(8,128)(2,1)}, bf16[512,256]{1,0:T(8,128)(2,1)}, u32[]{:S(2)}, u32[]{:S(2)}) collective-permute-start(bf16[512,256]{1,0:T(8,128)(2,1)} %collective-permute-done.16.refs_8_), channel_id=1, source_target_pairs={{0,8},{2,10},{4,0},{6,2},{8,16},{10,18},{12,4},{14,6},{16,24},{18,... | collective-permute-start | bytes 786440 | tf_op jit(solution)/shard_map/ppermute | solution.py:669
  107.8 18.5 %collective-permute-start.8 = (bf16[64,3936]{1,0:T(8,128)(2,1)}, bf16[64,3936]{1,0:T(8,128)(2,1)S(1)}, u32[]{:S(2)}, u32[]{:S(2)}) collective-permute-start(bf16[64,3936]{1,0:T(8,128)(2,1)} %pad_maximum_fusion), channel_id=1, source_target_pairs={{0,8},{2,10},{4,0},{6,2},{8,16},{10,18},{12,4},{14,6},{16,24},{18,... | collective-permute-start | bytes 1511432 | tf_op jit(solution)/shard_map/ppermute | solution.py:669
  110.8 29.4 %all-to-all-start.3 = ((bf16[8,192,128]{2,1,0:T(8,128)(2,1)}), bf16[8,192,128]{2,1,0:T(8,128)(2,1)S(1)}, u32[]{:S(2)}, u32[]{:S(2)}) async-start(bf16[8,192,128]{2,1,0:T(8,128)(2,1)} %combine.1.refs_1_), calls=%async_computation.3 | async-start | bytes 786432 | tf_op jit(solution)/shard_map/all_to_all | solution.py:632
  115.3 4.2 %collective-permute-start.29 = (bf16[512,128]{1,0:T(8,128)(2,1)S(1)}, bf16[512,128]{1,0:T(8,128)(2,1)S(1)}, u32[]{:S(2)}, u32[]{:S(2)}) collective-permute-start(bf16[512,128]{1,0:T(8,128)(2,1)S(1)} %dynamic-slice_bitcast_fusion.refs_3_), channel_id=1, source_target_pairs={{0,2},{2,0},{4,6},{6,4},{8,10},{10,8},{12,14},{14,12},{16,18},{18,... | collective-permute-start | bytes 393224 | tf_op jit(solution)/shard_map/ppermute | solution.py:635
  118.1 1.9 collective-permute-start.28
  119.6 15.4 %collective-permute-start.11 = (bf16[8,192,128]{2,1,0:T(8,128)(2,1)S(1)}, bf16[8,192,128]{2,1,0:T(8,128)(2,1)S(1)}, u32[]{:S(2)}, u32[]{:S(2)}) collective-permute-start(bf16[8,192,128]{2,1,0:T(8,128)(2,1)S(1)} %copy-done.2), channel_id=1, source_target_pairs={{0,2},{2,0},{4,6},{6,4},{8,10},{10,8},{12,14},{14,12},{16,18},{18,... | collective-permute-start | bytes 1179656 | tf_op jit(solution)/shard_map/ppermute | solution.py:635
  123.9 6.6 %collective-permute-start.31 = (bf16[32,512]{1,0:T(8,128)(2,1)}, bf16[32,512]{1,0:T(8,128)(2,1)S(1)}, u32[]{:S(2)}, u32[]{:S(2)}) collective-permute-start(bf16[32,512]{1,0:T(8,128)(2,1)} %get-tuple-element.159), channel_id=1, source_target_pairs={{0,4},{2,6},{4,12},{6,14},{8,0},{10,2},{12,20},{14,22},{16,8},{18,... | collective-permute-start | bytes 98312 | tf_op jit(solution)/shard_map/ppermute | solution.py:669
  127.9 5.1 %collective-permute-start.30 = (bf16[32,512]{1,0:T(8,128)(2,1)}, bf16[32,512]{1,0:T(8,128)(2,1)S(1)}, u32[]{:S(2)}, u32[]{:S(2)}) collective-permute-start(bf16[32,512]{1,0:T(8,128)(2,1)} %get-tuple-element.157), channel_id=1, source_target_pairs={{0,8},{2,10},{4,0},{6,2},{8,16},{10,18},{12,4},{14,6},{16,24},{18,... | collective-permute-start | bytes 98312 | tf_op jit(solution)/shard_map/ppermute | solution.py:669
  145.1 18.5 %copy-start.35 = (bf16[64,512]{1,0:T(8,128)(2,1)S(1)}, bf16[64,512]{1,0:T(8,128)(2,1)}, u32[]{:S(2)}) copy-start(bf16[64,512]{1,0:T(8,128)(2,1)} %get-tuple-element.153) | copy-start | bytes 196612
  145.1 19.3 %collective-permute-start.21 = (bf16[128,1024]{1,0:T(8,128)(2,1)}, bf16[128,1024]{1,0:T(8,128)(2,1)}, u32[]{:S(2)}, u32[]{:S(2)}) collective-permute-start(bf16[128,1024]{1,0:T(8,128)(2,1)} %project_back.1.refs_2_), channel_id=1, source_target_pairs={{0,1},{1,0},{2,3},{3,2},{4,5},{5,4},{6,7},{7,6},{8,9},{9,8},{10,11... | collective-permute-start | bytes 786440 | tf_op jit(solution)/shard_map/ppermute | solution.py:647
  146.0 28.0 %collective-permute-start.24 = (bf16[64,3936]{1,0:T(8,128)(2,1)}, bf16[64,3936]{1,0:T(8,128)(2,1)}, u32[]{:S(2)}, u32[]{:S(2)}) collective-permute-start(bf16[64,3936]{1,0:T(8,128)(2,1)} %add_convert_fusion.2), channel_id=1, source_target_pairs={{0,4},{2,6},{4,12},{6,14},{8,0},{10,2},{12,20},{14,22},{16,8},{18,... | collective-permute-start | bytes 1511432 | tf_op jit(solution)/shard_map/ppermute | solution.py:669
  149.2 26.1 %collective-permute-start.23 = (bf16[64,3936]{1,0:T(8,128)(2,1)}, bf16[64,3936]{1,0:T(8,128)(2,1)}, u32[]{:S(2)}, u32[]{:S(2)}) collective-permute-start(bf16[64,3936]{1,0:T(8,128)(2,1)} %add_convert_fusion.3), channel_id=1, source_target_pairs={{0,8},{2,10},{4,0},{6,2},{8,16},{10,18},{12,4},{14,6},{16,24},{18,... | collective-permute-start | bytes 1511432 | tf_op jit(solution)/shard_map/ppermute | solution.py:669
  149.2 12.5 %collective-permute-start.33 = (bf16[64,512]{1,0:T(8,128)(2,1)}, bf16[64,512]{1,0:T(8,128)(2,1)}, u32[]{:S(2)}, u32[]{:S(2)}) collective-permute-start(bf16[64,512]{1,0:T(8,128)(2,1)} %pad_maximum_fusion.3), channel_id=1, source_target_pairs={{0,4},{2,6},{4,12},{6,14},{8,0},{10,2},{12,20},{14,22},{16,8},{18,... | collective-permute-start | bytes 196616 | tf_op jit(solution)/shard_map/ppermute | solution.py:669
  151.2 12.3 %collective-permute-start.32 = (bf16[64,512]{1,0:T(8,128)(2,1)}, bf16[64,512]{1,0:T(8,128)(2,1)}, u32[]{:S(2)}, u32[]{:S(2)}) collective-permute-start(bf16[64,512]{1,0:T(8,128)(2,1)} %pad_maximum_fusion.2), channel_id=1, source_target_pairs={{0,8},{2,10},{4,0},{6,2},{8,16},{10,18},{12,4},{14,6},{16,24},{18,... | collective-permute-start | bytes 196616 | tf_op jit(solution)/shard_map/ppermute | solution.py:669
  151.2 18.6 %copy-start.3 = (f32[128,1024]{1,0:T(8,128)S(1)}, f32[128,1024]{1,0:T(8,128)}, u32[]{:S(2)}) copy-start(f32[128,1024]{1,0:T(8,128)} %get-tuple-element.101.refs_0_) | copy-start | bytes 1572868
  151.8 18.8 %all-to-all-start.4 = ((bf16[8,64,192]{2,1,0:T(8,128)(2,1)}), bf16[8,64,192]{2,1,0:T(8,128)(2,1)S(1)}, u32[]{:S(2)}, u32[]{:S(2)}) async-start(bf16[8,64,192]{2,1,0:T(8,128)(2,1)} %bitcast.27), calls=%async_computation.4 | async-start | bytes 524288 | tf_op jit(solution)/shard_map/all_to_all | solution.py:632
  161.7 8.2 %collective-permute-start.19 = (bf16[128,1024]{1,0:T(8,128)(2,1)S(1)}, bf16[128,1024]{1,0:T(8,128)(2,1)S(1)}, u32[]{:S(2)}, u32[]{:S(2)}) collective-permute-start(bf16[128,1024]{1,0:T(8,128)(2,1)S(1)} %convolution_convert_fusion), channel_id=1, source_target_pairs={{0,1},{1,0},{2,3},{3,2},{4,5},{5,4},{6,7},{7,6},{8,9},{9,8},{10,11... | collective-permute-start | bytes 786440 | tf_op jit(solution)/shard_map/ppermute | solution.py:647
  167.0 11.6 %collective-permute-start.35 = (bf16[64,512]{1,0:T(8,128)(2,1)S(1)}, bf16[64,512]{1,0:T(8,128)(2,1)S(1)}, u32[]{:S(2)}, u32[]{:S(2)}) collective-permute-start(bf16[64,512]{1,0:T(8,128)(2,1)S(1)} %add_convert_fusion.9), channel_id=1, source_target_pairs={{0,4},{2,6},{4,12},{6,14},{8,0},{10,2},{12,20},{14,22},{16,8},{18,... | collective-permute-start | bytes 196616 | tf_op jit(solution)/shard_map/ppermute | solution.py:669
  169.8 8.8 %collective-permute-start.34 = (bf16[64,512]{1,0:T(8,128)(2,1)S(1)}, bf16[64,512]{1,0:T(8,128)(2,1)S(1)}, u32[]{:S(2)}, u32[]{:S(2)}) collective-permute-start(bf16[64,512]{1,0:T(8,128)(2,1)S(1)} %add_convert_fusion.10), channel_id=1, source_target_pairs={{0,8},{2,10},{4,0},{6,2},{8,16},{10,18},{12,4},{14,6},{16,24},{18,... | collective-permute-start | bytes 196616 | tf_op jit(solution)/shard_map/ppermute | solution.py:669
  174.0 18.1 %copy-start.32 = (bf16[64,512]{1,0:T(8,128)(2,1)S(1)}, bf16[64,512]{1,0:T(8,128)(2,1)}, u32[]{:S(2)}) copy-start(bf16[64,512]{1,0:T(8,128)(2,1)} %get-tuple-element.151) | copy-start | bytes 196612
  176.4 9.1 %collective-permute-start.25 = (bf16[64,3936]{1,0:T(8,128)(2,1)S(1)}, bf16[64,3936]{1,0:T(8,128)(2,1)S(1)}, u32[]{:S(2)}, u32[]{:S(2)}) collective-permute-start(bf16[64,3936]{1,0:T(8,128)(2,1)S(1)} %add_convert_fusion.1), channel_id=1, source_target_pairs={{0,8},{2,10},{4,0},{6,2},{8,16},{10,18},{12,4},{14,6},{16,24},{18,... | collective-permute-start | bytes 1511432 | tf_op jit(solution)/shard_map/ppermute | solution.py:669
  176.9 9.0 %collective-permute-start.26 = (bf16[64,3936]{1,0:T(8,128)(2,1)S(1)}, bf16[64,3936]{1,0:T(8,128)(2,1)S(1)}, u32[]{:S(2)}, u32[]{:S(2)}) collective-permute-start(bf16[64,3936]{1,0:T(8,128)(2,1)S(1)} %add_convert_fusion), channel_id=1, source_target_pairs={{0,4},{2,6},{4,12},{6,14},{8,0},{10,2},{12,20},{14,22},{16,8},{18,... | collective-permute-start | bytes 1511432 | tf_op jit(solution)/shard_map/ppermute | solution.py:669
  178.8 3.6 %collective-permute-start.22 = (f32[64]{0:T(128)S(1)}, f32[64]{0:T(128)S(1)}, u32[]{:S(2)}, u32[]{:S(2)}) collective-permute-start(f32[64]{0:T(128)S(1)} %reduce), channel_id=1, source_target_pairs={{0,1},{1,0},{2,3},{3,2},{4,5},{5,4},{6,7},{7,6},{8,9},{9,8},{10,11... | collective-permute-start | bytes 776 | tf_op jit(solution)/shard_map/ppermute | solution.py:647
  179.7 12.4 %collective-permute-start.36 = (bf16[64,512]{1,0:T(8,128)(2,1)S(1)}, bf16[64,512]{1,0:T(8,128)(2,1)S(1)}, u32[]{:S(2)}, u32[]{:S(2)}) collective-permute-start(bf16[64,512]{1,0:T(8,128)(2,1)S(1)} %add_convert_fusion.8), channel_id=1, source_target_pairs={{0,8},{2,10},{4,0},{6,2},{8,16},{10,18},{12,4},{14,6},{16,24},{18,... | collective-permute-start | bytes 196616 | tf_op jit(solution)/shard_map/ppermute | solution.py:669
  180.8 11.3 %collective-permute-start.37 = (bf16[64,512]{1,0:T(8,128)(2,1)S(1)}, bf16[64,512]{1,0:T(8,128)(2,1)S(1)}, u32[]{:S(2)}, u32[]{:S(2)}) collective-permute-start(bf16[64,512]{1,0:T(8,128)(2,1)S(1)} %add_convert_fusion.7), channel_id=1, source_target_pairs={{0,4},{2,6},{4,12},{6,14},{8,0},{10,2},{12,20},{14,22},{16,8},{18,... | collective-permute-start | bytes 196616 | tf_op jit(solution)/shard_map/ppermute | solution.py:669
  190.8 3.6 %collective-permute-start.27 = (f32[64]{0:T(128)S(1)}, f32[64]{0:T(128)S(1)}, u32[]{:S(2)}, u32[]{:S(2)}) collective-permute-start(f32[64]{0:T(128)S(1)} %reduce.1), channel_id=1, source_target_pairs={{0,1},{1,0},{2,3},{3,2},{4,5},{5,4},{6,7},{7,6},{8,9},{9,8},{10,11... | collective-permute-start | bytes 776 | tf_op jit(solution)/shard_map/ppermute | solution.py:647
  (34 other events, 178.2 us)

commit v4 on v3

--- a/solution.py
+++ b/solution.py
@@ -61,6 +61,10 @@
         cost_estimate=cost,
         name=name,
     )(*ins)
+
+
+def whole_lanes(size):
+    return -(-size // 128) * 128
 
 
 def work(flops, byte_count, transcendentals=0):
@@ -308,6 +312,7 @@
             pltpu.SemaphoreType.DMA((4,)),
         ],
         compiler_params=pltpu.CompilerParams(vmem_limit_bytes=GRANT),
+        cost_estimate=work(2 * width * weights.size, 2 * weights.size),
         name="project",
     )(hidden, gain, cosine, sine, weights)
 
@@ -338,21 +343,24 @@
     grad_act_ref,
     w_in_ref,
     middle_ref,
-    input_ref,
-    gated_ref,
+    mid_ref,
     act_ref,
     part_ref,
     heads_ref,
     wait_units,
 ):
     tp = tp_ref[0]
-    branch = nn(attn_ref[tp].T, own_ref[...]) + nn(attn_ref[1 - tp].T, other_ref[...])
+    attn_own = attn_ref[tp].T
+    branch = nn(attn_own, own_ref[...]) + nn(attn_ref[1 - tp].T, other_ref[...])
     middle = hidden_ref[...].astype(F32) + branch
     middle_ref[...] = middle
     normed, scale = standardise(middle)
     gain = gain_ref[...]
     mlp_input = (normed * gain).astype(BF)
-    input_ref[...] = mlp_input
+    model, inner = mlp_input.shape[1], attn_own.shape[1]
+    first = model + inner
+    mid_ref[:, :model] = mlp_input
+    mid_ref[:, model:first] = attn_own
     wait_units()
     gate, up = nt(mlp_input, w_in_ref[0]), nt(mlp_input, w_in_ref[1])
     share = 0.5 * (1.0 + lax.erf(gate * (0.5**0.5)))
@@ -362,11 +370,14 @@
     grad_gate = (slope * up * grad_act).astype(BF)
     grad_up = (bent * grad_act).astype(BF)
     units = grad_gate.shape[1]
-    gated_ref[:, :units] = grad_gate
-    gated_ref[:, units : 2 * units] = grad_up
+    mid_ref[:, first : first + units] = grad_gate
+    mid_ref[:, first + units : first + 2 * units] = grad_up
     activated = (bent * up).astype(BF)
-    gated_ref[:, 2 * units :] = activated
+    mid_ref[:, first + 2 * units : first + 3 * units] = activated
     act_ref[...] = activated
+    last = first + 3 * units
+    if last < mid_ref.shape[1]:
+        mid_ref[:, last:] = jnp.zeros((activated.shape[0], mid_ref.shape[1] - last), BF)
     part = nn(grad_gate, w_in_ref[0]) + nn(grad_up, w_in_ref[1])
     part_ref[...] = part.astype(BF)
     grad = 0.5 * cot_ref[...].astype(F32) + standardise_back(part, gain, normed, scale)
@@ -385,8 +396,7 @@
         [tp, attn, hidden, cotangent, gain, own, other, grad_act, w_in],
         [
             shaped((width, model), F32),
-            shaped((width, model), BF),
-            shaped((width, 3 * units), BF),
+            shaped((width, whole_lanes(model + inner + 3 * units)), BF),
             shaped((width, units), BF),
             shaped((width, model), BF),
             shaped((2, inner // HD, HD, width), BF),
@@ -423,97 +433,146 @@
     return nt(pick_ref[...], values).astype(BF)
 
 
-def pick_kernel(pick_ref, own_ref, other_ref, out_ref):
-    out_ref[...] = picked(pick_ref, own_ref, other_ref)
-
-
-def pick_rows(pick, own, other):
-    rows, width = pick.shape[0], own.shape[0]
-    return staged(
-        pick_kernel,
-        [pick, own, other],
-        [shaped((rows, 2 * width), BF)],
-        "pick_rows",
-        cost=work(4 * rows * own.size, 6 * own.size),
-    )[0]
-
-
-def head_weight_kernel(ids_ref, own_ref, other_ref, *refs):
-    rows, out_ref = refs[:-1], refs[-1]
-    width = own_ref.shape[2]
-    total = jnp.zeros((rows[0].shape[0], own_ref.shape[1]), F32)
-    for b, ref in enumerate(rows):
-        at = ids_ref[b]
-        total += nt(ref[:, :width], own_ref[at])
-        total += nt(ref[:, width:], other_ref[at])
-    out_ref[...] = total.astype(BF)
-
-
-def head_weight(ids, own, other, rows):
+def head_weight_kernel(mine, ids_ref, grad_ref, *refs):
+    rows, keep_ref, give_ref, total_scr = refs[:-3], *refs[-3:]
     count = len(rows)
-    return staged(
-        head_weight_kernel,
-        [ids, own, other, *rows],
-        [shaped((rows[0].shape[0], own.shape[1]), BF)],
+    core = ids_ref[count]
+    grads = jnp.concatenate([grad_ref[ids_ref[b]] for b in range(count)], axis=1)
+    inputs = jnp.concatenate([ref[...] for ref in rows], axis=0)
+    total_scr[...] = nn(grads, inputs).T
+    for b in range(keep_ref.shape[0]):
+        keep = pl.multiple_of((2 * b + core) * mine, mine)
+        give = pl.multiple_of((2 * b + 1 - core) * mine, mine)
+        keep_ref[b] = total_scr[pl.ds(keep, mine), :].astype(BF)
+        give_ref[b] = total_scr[pl.ds(give, mine), :].astype(BF)
+
+
+def head_weight(chips, ids, grad, rows):
+    width, model = rows[0].shape
+    columns = grad.shape[1]
+    mine = model // (2 * chips)
+    return staged(
+        functools.partial(head_weight_kernel, mine),
+        [ids, grad, *rows],
+        [shaped((chips, mine, columns), BF)] * 2,
         "head_weight",
+        [pltpu.VMEM((model, columns), F32)],
         scalars=1,
-        cost=work(2 * count * rows[0].size * own.shape[1], 2 * count * rows[0].size),
-    )[0]
-
-
-def mlp_weight_kernel(sizes, pick_ref, *refs):
-    given, outs = refs[:6], refs[6 : 6 + len(sizes)]
-    total_scr, sems, wait_own, wait_other = refs[6 + len(sizes) :]
-    in_own, in_other, cot_own, cot_other, own_ref, other_ref = given
-    units = own_ref.shape[1] // 3
-    rows_in = picked(pick_ref, in_own, in_other)
-    rows_out = picked(pick_ref, cot_own, cot_other)
-    wait_own()
-    wait_other()
-    columns = jnp.concatenate([own_ref[...], other_ref[...]], axis=0)
-    total_scr[:, : 2 * units] = nn(rows_in, columns[:, : 2 * units]).astype(BF)
-    total_scr[:, 2 * units :] = nn(rows_out, columns[:, 2 * units :]).astype(BF)
-    copies, first = [], 0
+        cost=work(2 * len(rows) * rows[0].size * columns, 2 * len(rows) * rows[0].size),
+    )
+
+
+def mlp_weight_kernel(sizes, inner, units, pick_ref, *refs):
+    cot_own, cot_other, own_ref, other_ref = refs[:4]
+    outs = refs[4 : 4 + len(sizes)]
+    total_scr, sems = refs[4 + len(sizes) :]
+    model = cot_own.shape[1]
+    first = model + inner
+    cot_both = jnp.concatenate([cot_own[...], cot_other[...]], axis=0)
+    both = jnp.concatenate([own_ref[...], other_ref[...]], axis=0)
+    columns = both[:, first : first + 3 * units]
+    copies, start, done, rows = [], 0, 0, total_scr.shape[0]
     for r, ref in enumerate(outs):
-        copies.append(pltpu.make_async_copy(total_scr.at[pl.ds(first, sizes[r])], ref, sems.at[r]))
-        first += sizes[r]
-    for copy in copies:
-        copy.start()
+        while start + sizes[r] > done:
+            cut = slice(done, done + rows // 2)
+            in_rows = nt(pick_ref[cut], both[:, :model]).astype(BF)
+            cot_rows = nt(pick_ref[cut], cot_both).astype(BF)
+            total_scr[cut, : 2 * units] = nn(in_rows, columns[:, : 2 * units]).astype(BF)
+            total_scr[cut, 2 * units : 3 * units] = nn(cot_rows, columns[:, 2 * units :]).astype(BF)
+            if 3 * units < total_scr.shape[1]:
+                rest = total_scr.shape[1] - 3 * units
+                total_scr[cut, 3 * units :] = jnp.zeros((rows // 2, rest), BF)
+            done += rows // 2
+        copies.append(pltpu.make_async_copy(total_scr.at[pl.ds(start, sizes[r])], ref, sems.at[r]))
+        copies[-1].start()
+        start += sizes[r]
     for copy in copies:
         copy.wait()
 
 
-def mlp_weight(sizes, pick, in_own, in_other, cot_own, cot_other, own, other):
-    rows, columns = sum(sizes), own.shape[1]
-    return staged(
-        functools.partial(mlp_weight_kernel, sizes),
-        [pick, in_own, in_other, cot_own, cot_other, own, other],
+def mlp_weight(sizes, inner, units, pick, cot_own, cot_other, own, other):
+    rows, columns = sum(sizes), whole_lanes(3 * units)
+    return staged(
+        functools.partial(mlp_weight_kernel, sizes, inner, units),
+        [pick, cot_own, cot_other, own, other],
         [shaped((size, columns), BF) for size in sizes],
         "mlp_weight",
         [pltpu.VMEM((rows, columns), BF), pltpu.SemaphoreType.DMA((len(sizes),))],
-        late=2,
         cost=work(4 * rows * own.size, 2 * rows * columns + 8 * own.size),
         far=len(sizes),
     )
 
 
-def out_weight_kernel(pick_ref, own_ref, other_ref, attn_ref, attn_other_ref, *outs):
-    rows = picked(pick_ref, own_ref, other_ref)
-    columns = jnp.concatenate([attn_ref[...], attn_other_ref[...]], axis=1)
-    total = nt(rows, columns).astype(BF)
-    first = 0
-    for ref in outs:
-        ref[...] = total[first : first + ref.shape[0]]
-        first += ref.shape[0]
-
-
-def out_weight(sizes, pick, own, other, attn, attn_other):
-    return staged(
-        out_weight_kernel,
-        [pick, own, other, attn, attn_other],
-        [shaped((size, attn.shape[0]), BF) for size in sizes],
-        "out_weight",
-        cost=work(4 * sum(sizes) * attn.size, 8 * own.size),
+def out_weight_kernel(mine, pick_ref, own_ref, other_ref, attn_ref, attn_other_ref, *outs):
+    both = jnp.concatenate([own_ref[...], other_ref[...]], axis=0)
+    rows = nt(pick_ref[...], both).astype(BF)
+    total = nn(rows, jnp.concatenate([attn_ref[...], attn_other_ref[...]], axis=0)).astype(BF)
+    for r, ref in enumerate(outs):
+        ref[...] = total[r * ref.shape[0] : (r + 1) * ref.shape[0]]
+
+
+def out_weight(count, inner, pick, own, other, mid, mid_other):
+    rows, (width, model) = pick.shape[0], own.shape
+    vmem, hbm = pl.BlockSpec(memory_space=pltpu.VMEM), pl.BlockSpec(memory_space=pltpu.HBM)
+
+    def kernel(pick_ref, own_ref, other_ref, mid_ref, mid_other_ref, *refs):
+        outs, held, sems = refs[:count], refs[count : count + 5], refs[count + 5]
+        columns = pl.ds(model, inner)
+        given = [pick_ref, own_ref, other_ref, mid_ref.at[:, columns], mid_other_ref.at[:, columns]]
+        copies = [pltpu.make_async_copy(g, h, sems.at[i]) for i, (g, h) in enumerate(zip(given, held))]
+        for copy in copies:
+            copy.start()
+        for copy in copies:
+            copy.wait()
+        out_weight_kernel(rows // count, *held, *outs)
+
+    return pl.pallas_call(
+        kernel,
+        in_specs=[hbm] * 5,
+        out_specs=[vmem] * count,
+        out_shape=[shaped((rows // count, inner), BF)] * count,
+        scratch_shapes=[
+            pltpu.VMEM(pick.shape, BF),
+            pltpu.VMEM(own.shape, BF),
+            pltpu.VMEM(own.shape, BF),
+            pltpu.VMEM((width, inner), BF),
+            pltpu.VMEM((width, inner), BF),
+            pltpu.SemaphoreType.DMA((5,)),
+        ],
+        compiler_params=pltpu.CompilerParams(vmem_limit_bytes=GRANT),
+        cost_estimate=work(4 * rows * own.size, 8 * own.size),
+        name="out_weight",
+    )(pick, own, other, mid, mid_other)
+
+
+def ring_add_kernel(carried, *refs):
+    for side in range(2):
+        block, got, narrow = refs[3 * side : 3 * side + 3]
+        out = refs[6 + side]
+        wide, rows = block.shape[1], got.shape[0]
+        total = block[...].astype(F32)
+        if rows == block.shape[0]:
+            out[:, :wide] = (total + got[:, :wide].astype(F32)).astype(BF)
+        elif side == 0:
+            out[:rows, :wide] = (total[:rows] + got[...].astype(F32)).astype(BF)
+            out[rows:, :wide] = block[rows:, :]
+        else:
+            out[:rows, :wide] = block[:rows, :]
+            out[rows:, :wide] = (total[rows:] + got[...].astype(F32)).astype(BF)
+        if carried:
+            out[:, wide:] = (narrow[...].astype(F32) + got[:, wide:].astype(F32)).astype(BF)
+        else:
+            out[:, wide:] = narrow[...]
+
+
+def ring_add(carried, *arrays):
+    rows, columns = arrays[0].shape[0], arrays[0].shape[1] + arrays[2].shape[1]
+    return staged(
+        functools.partial(ring_add_kernel, carried),
+        list(arrays),
+        [shaped((rows, columns), BF)] * 2,
+        "ring_add",
+        cost=work(4 * rows * columns, 12 * rows * columns),
     )
 
 
@@ -544,25 +603,30 @@
         out_shape=(shaped((3, mine, inner), F32), shaped((mine, 1), F32)),
         scratch_shapes=[pltpu.VMEM((3, mine, inner), BF), pltpu.SemaphoreType.DMA],
         compiler_params=pltpu.CompilerParams(vmem_limit_bytes=GRANT),
+        cost_estimate=work(2 * blocks.size, 10 * blocks.size),
         name="finish_qkv",
     )(first, blocks, weights)
 
 
-def finish_mlp_kernel(own_ref, right_ref, left_ref, w_ref, in_ref, out_ref, gain_ref):
+def finish_mlp_kernel(own_ref, right_ref, left_ref, w_ref, gain_ref, in_ref, out_ref, gains_ref):
     units = out_ref.shape[1]
-    total = own_ref[...].astype(F32) + right_ref[...].astype(F32) + left_ref[...].astype(F32)
-    out_ref[...] = total[:, 2 * units :]
+    wide = own_ref.shape[1]
+    total = own_ref[...].astype(F32) + right_ref[:, :wide].astype(F32) + left_ref[:, :wide].astype(F32)
+    out_ref[...] = total[:, 2 * units : 3 * units]
     in_ref[:, 0, :] = total[:, :units]
     in_ref[:, 1, :] = total[:, units : 2 * units]
-    gain_ref[...] = jnp.sum(total[:, : 2 * units] * w_ref[...].astype(F32), axis=1, keepdims=True)
-
-
-def finish_mlp(own, right, left, rows):
-    mine, units = own.shape[0], own.shape[1] // 3
+    term = jnp.sum(total[:, : 2 * units] * w_ref[...].astype(F32), axis=1, keepdims=True)
+    mine = term.shape[0]
+    gains_ref[0:1] = jnp.broadcast_to(gain_ref[...], (mine, 128)).T[0:1]
+    gains_ref[1:2] = jnp.broadcast_to(term, (mine, 128)).T[0:1]
+
+
+def finish_mlp(units, own, right, left, rows, gain):
+    mine = own.shape[0]
     return staged(
         finish_mlp_kernel,
-        [own, right, left, rows],
-        [shaped((mine, 2, units), F32), shaped((mine, units), F32), shaped((mine, 1), F32)],
+        [own, right, left, rows, gain],
+        [shaped((mine, 2, units), F32), shaped((mine, units), F32), shaped((2, mine), F32)],
         "finish_mlp",
         cost=work(8 * own.size, 14 * own.size),
     )
@@ -676,33 +740,6 @@
         wanted = ((2 * chip_ids + core) * mine)[:, None] + jnp.arange(mine)[None, :]
         return (wanted.reshape(-1, 1) == jnp.arange(model)[None, :]).astype(BF)
 
-    class Sum:
-        def __init__(self, blocks):
-            half = chips // 2
-            self.own, self.step = blocks[0], 0
-            self.rights = [blocks[half], *blocks[half - 1 : 0 : -1]]
-            self.lefts = [blocks[half + 1], *blocks[half + 2 :]]
-
-        def advance(self, *earlier):
-            right, left = self.rights[self.step], self.lefts[self.step]
-            if self.step == 1:
-                cut = self.right.shape[-2]
-                first = right[..., :cut, :].astype(F32) + self.right.astype(F32)
-                right = jnp.concatenate([first.astype(BF), right[..., cut:, :]], axis=-2)
-                last = left[..., cut:, :].astype(F32) + self.left.astype(F32)
-                left = jnp.concatenate([left[..., :cut, :], last.astype(BF)], axis=-2)
-            elif self.step > 1:
-                right = (right.astype(F32) + self.right.astype(F32)).astype(BF)
-                left = (left.astype(F32) + self.left.astype(F32)).astype(BF)
-            self.step += 1
-            right, left = after((right, left), *earlier)
-            self.right, self.left = turn(right, 1), turn(left, -1)
-            return right, left
-
-        def result(self):
-            total = self.own.astype(F32) + self.right.astype(F32)
-            return total + self.left.astype(F32)
-
     def scatter(parts):
         flat = parts.reshape(chips, -1)
         summed = lax.psum_scatter(
@@ -730,12 +767,11 @@
     w_out_other = swap_tp(w_attn_out)
     later_cot = after(cotangent, packed)
     cot_other = swap_core(later_cot)
-    later_input = after(attn_input, packed)
-    rows_in = pick_rows(
-        picker(after(jnp.arange(chips), packed)), later_input, swap_core(later_input)
-    )
-    gathered = [rows_in]
-    right = left = rows_in
+    cos_all, sin_all = tables(after(block_ids, packed))
+    order = after(jnp.arange(chips), packed)
+    pick = picker(ring_chip(position + order) if ringed else order)
+    gathered = [attn_input]
+    right = left = after(attn_input, cos_all, sin_all, pick)
 
     def gather_step(step, *earlier):
         nonlocal right, left
@@ -749,22 +785,22 @@
 
     if ringed:
         gather_step(1)
-    cos_all, sin_all = tables(after(block_ids, rows_in))
-    grad_activated = unit_back(after(later_cot, rows_in), w_mlp_out)
-    order = after(jnp.arange(chips), rows_in)
-    pick_ring = picker(ring_chip(position + order) if ringed else order)
-    own = after(own, grad_activated, cos_all, sin_all, pick_ring)
+    own = after(own, cos_all, sin_all, pick)
     others = [shift_keys(own, step) for step in range(1, 2 * copies)]
     attended, attended_low, lse = attend(tp_size, own, others)
+    if ringed:
+        attended_low = after(attended_low, right, left)
     attn_all = exchange_wide(attended_low.reshape(tp_size * heads, HD, width))
+    grad_activated = unit_back(after(cotangent, attended_low), w_mlp_out)
     if ringed:
         gather_step(2, attended_low)
     rows_w_in = lax.dynamic_slice_in_dim(after(w_in, attended_low), me * mine, mine, 0)
     rows_w_in = rows_w_in.reshape(mine, 2 * units)
-    attn_all = after(attn_all, rows_w_in).reshape(tp_size, inner, width)
+    attn_all = after(attn_all, rows_w_in, grad_activated, right, left)
+    attn_all = attn_all.reshape(tp_size, inner, width)
     if ringed:
         gather_step(3, attn_all)
-    middle, mlp_input, gated, activated_low, part_two, head_terms = middle_part(
+    middle, mid, activated_low, part_two, head_terms = middle_part(
         tp_list,
         attn_all,
         hidden_in,
@@ -776,105 +812,116 @@
         w_pair,
     )
     grad_received = exchange_wide(head_terms.reshape(tp_size * heads, HD, width))
+    if ringed:
+        gather_step(4, head_terms)
 
     half = chips // 2
     sizes = [mine] * half + [mine // 2, mine // 2] + [mine] * (half - 1) if ringed else [chips * mine]
-    parts_mlp = mlp_weight(
-        sizes,
-        pick_ring,
-        mlp_input,
-        swap_core(mlp_input),
-        cotangent,
-        cot_other,
-        gated,
-        swap_core(gated),
-    )
-    grad_received = after(grad_received, parts_mlp)
+    mid_other = swap_core(mid)
+    parts_mlp = mlp_weight(sizes, inner, units, pick, cotangent, cot_other, mid, mid_other)
     if ringed:
-        sum_mlp = Sum(parts_mlp)
-        sum_mlp.advance()
-        gather_step(4, grad_received)
+        mlp_rights = parts_mlp[half::-1]
+        mlp_lefts = parts_mlp[half + 1 :]
+        got_right, got_left = turn(mlp_rights[0], 1), turn(mlp_lefts[0], -1)
+    part_two_other = swap_tp(part_two)
+    later_two = after(part_two_other, parts_mlp)
+    grad_middle, grad_middle_low = middle_back(middle, cotangent, gain_mlp[None], part_two, later_two)
+    parts_out = out_weight(
+        chips if ringed else 1,
+        inner,
+        pick,
+        grad_middle_low,
+        swap_core(grad_middle_low),
+        mid,
+        mid_other,
+    )
+    grad_received = after(grad_received, parts_mlp, parts_out, right, left)
     grad_received = grad_received.reshape(tp_size, heads, HD, width)
     dq, *grad_kv = attend_back(own, others, grad_received, attended, lse, cos_all, sin_all)
 
-    part_two = after(part_two, parts_mlp)
-    part_two_other = swap_tp(part_two)
+    if ringed:
+        grad_kv = after(grad_kv, got_right, got_left)
     terms = [grad_kv[0]]
     for step in range(1, 2 * copies):
         terms.append(shift_keys(grad_kv[step], -step))
     if ringed:
-        sent = sum_mlp.advance(dq)
+
+        def ring_step(step, *earlier):
+            nonlocal got_right, got_left
+            sent = ring_add(
+                step > 1,
+                mlp_rights[step],
+                after(got_right, *earlier),
+                parts_out[half + 1 - step],
+                mlp_lefts[step],
+                got_left,
+                parts_out[half + step],
+            )
+            got_right, got_left = turn(sent[0], 1), turn(sent[1], -1)
+            return sent
+
+        sent = ring_step(1, dq)
         terms[0] = after(terms[0], sent)
     grad_own = combine(dq, terms, cos_all, sin_all)
     grad_back = exchange(grad_own)
-
-    later_two = after(part_two_other, grad_own)
-    grad_middle, grad_middle_low = middle_back(middle, cotangent, gain_mlp[None], part_two, later_two)
-    attn_flat_t = lax.dynamic_index_in_dim(after(attn_all, grad_own), tp, 0, keepdims=False)
-    parts_out = out_weight(
-        sizes,
-        pick_ring,
-        grad_middle_low,
-        swap_core(grad_middle_low),
-        attn_flat_t,
-        swap_core(attn_flat_t),
-    )
     if ringed:
-        sum_out = Sum(parts_out)
-        sum_out.advance()
         steps = [0]
-        for step in range(1, chips // 2 + 1):
+        for step in range(1, half + 1):
             steps.extend([-step, step])
-        ids = ring_chip(position + jnp.array(steps[:chips])).astype(jnp.int32)
-        part_qkv = head_weight(ids, grad_own, swap_core(grad_own), gathered)
-        grad_back = after(grad_back, part_qkv)
+        ids = ring_chip(position + jnp.array(steps[:chips]))
+        ids = jnp.concatenate([ids, core[None]]).astype(jnp.int32)
+        keep_qkv, give_qkv = head_weight(chips, ids, grad_own, gathered)
+        given_qkv = swap_core(give_qkv)
+        sent = ring_step(2, keep_qkv)
+        part_qkv = (keep_qkv.astype(F32) + given_qkv.astype(F32)).astype(BF)
+        blocks_qkv = exchange(after(part_qkv, sent))
+        mlp_part = nn(after(activated_low, sent), w_mlp_out).astype(BF)
+        grad_back = after(grad_back, part_qkv, mlp_part, sent)
     part_one = project_back(grad_back, w_three)
     part_one_other = swap_tp(part_one)
     first = me * mine
     if ringed:
-        blocks_qkv = exchange(after(part_qkv, part_one).reshape(chips, mine, 3 * HD))
-        sent = sum_mlp.advance(part_one)
-        sum_out.advance(sent)
-        mlp_part = nn(after(activated_low, sent), w_mlp_out).astype(BF)
-        output = (middle + add_tp(mlp_part)).astype(BF)
-        part_one_other = after(part_one_other, mlp_part)
+        sent = ring_step(3, part_one_other, blocks_qkv)
+        output = (middle + add_tp(after(mlp_part, sent))).astype(BF)
+        part_one_other = after(part_one_other, sent)
         grad_input = input_back(hidden_in, gain_attn[None], part_one, grad_middle, part_one_other)
         grad_w_qkv, gain_one = finish_qkv(
-            first.astype(jnp.int32).reshape(1), after(blocks_qkv, grad_input), w_three
+            first.astype(jnp.int32).reshape(1), blocks_qkv, w_three
         )
-        sum_out.advance(grad_input)
-        sum_mlp.advance(gain_one)
-        sum_out.advance(gain_one)
+        wide = mlp_rights[0].shape[1]
+        last = parts_out[1].astype(F32) + got_right[:, wide:].astype(F32)
+        last = turn(last.astype(BF), 1)
+        grad_w_in, grad_w_mlp_out, gains = finish_mlp(
+            units, parts_mlp[0], got_right, got_left, rows_w_in, gain_one
+        )
+        grad_out = parts_out[0].astype(F32) + got_left[:, wide:].astype(F32)
+        grad_w_attn_out = (grad_out + last.astype(F32)).T
         grad_w_qkv = grad_w_qkv.transpose(1, 0, 2)
-        grad_w_attn_out = sum_out.result().T
-        grad_w_in, grad_w_mlp_out, gain_two = finish_mlp(
-            sum_mlp.own, sum_mlp.right, sum_mlp.left, rows_w_in
-        )
     else:
         output = (middle + add_tp(nn(activated_low, w_mlp_out).astype(BF))).astype(BF)
         grad_input = input_back(hidden_in, gain_attn[None], part_one, grad_middle, part_one_other)
         grad_back = grad_back.reshape(heads, 3, HD, width)
         grad_back = grad_back.transpose(1, 0, 2, 3).reshape(3, inner, width)
         columns_in = jnp.concatenate([grad_back, swap_core(grad_back)], axis=2)
+        rows_in = jnp.concatenate([attn_input, swap_core(attn_input)], axis=0)
+        rows_in = nt(pick, rows_in).astype(BF)
         part_qkv = jnp.einsum("dt,cft->dcf", rows_in, columns_in, preferred_element_type=F32)
         grad_w_qkv = scatter(part_qkv.astype(BF))
         grad_mlp = scatter(parts_mlp[0])
         grad_w_in = grad_mlp[:, : 2 * units].reshape(mine, 2, units)
-        grad_w_mlp_out = grad_mlp[:, 2 * units :]
+        grad_w_mlp_out = grad_mlp[:, 2 * units : 3 * units]
         grad_w_attn_out = scatter(parts_out[0]).T
         rows_w_qkv = lax.dynamic_slice_in_dim(w_qkv, first, mine, 0)
-        gain_one = jnp.sum(rows_w_qkv.astype(F32) * grad_w_qkv, axis=(1, 2))[:, None]
-        gain_two = jnp.sum(rows_w_in.astype(F32) * grad_mlp[:, : 2 * units], axis=1)[:, None]
-
-    def scale_gradient(term, gain):
-        term = term[:, 0]
-        return (term + swap_tp(term)) / lax.dynamic_slice_in_dim(gain, first, mine, 0)
-
+        gain_one = jnp.sum(rows_w_qkv.astype(F32) * grad_w_qkv, axis=(1, 2))
+        gain_two = jnp.sum(rows_w_in.astype(F32) * grad_mlp[:, : 2 * units], axis=1)
+        gains = jnp.stack([gain_one, gain_two])
+
+    gains = gains + swap_tp(gains)
     return (
         output,
         grad_input,
-        scale_gradient(gain_one, gain_attn),
-        scale_gradient(gain_two, gain_mlp),
+        gains[0] / lax.dynamic_slice_in_dim(gain_attn, first, mine, 0),
+        gains[1] / lax.dynamic_slice_in_dim(gain_mlp, first, mine, 0),
         grad_w_qkv,
         grad_w_attn_out,
         grad_w_in,

time: 197 us -> 177 us (0.90)
  starting transfers between devices: 63.4 us -> 51.3 us
  other arithmetic: 20.7 us -> 10.9 us
  local copies, waits for them, and re-layouts: 18.1 us -> 9.91 us
  Pallas kernels: 64.8 us -> 70.1 us
  waiting for transfers between devices: 26.7 us -> 30.7 us
    all_to_all x3, waiting for transfers between devices: 0.01 us -> 14.8 us  [exchange(): return lax.all_to_all(values, 'ctx', 0, 0, axis_index_groups=head_groups)]
    ppermute x23 -> x16, starting transfers between devices: 28.9 us -> 17.9 us  [turn(): return lax.ppermute(values, 'ctx', pairs)]
    all_to_all x2, waiting for transfers between devices: 7.82 us -> 0.01 us  [exchange_wide(): lax.all_to_all(values, ('ctx', 'tp'), 0, 0, axis_index_groups=wide_groups)]
    convert_element_type x13 -> x3, other arithmetic: 8.42 us -> 3.37 us  [the longest x1 1.72 us: layer(): part_qkv = (keep_qkv.astype(F32) + given_qkv.astype(F32)).astype(BF)]
    slice x4 -> x0, local copies, waits for them, and re-layouts: 3.51 us -> none  [the longest x2 1.78 us: advance(): right = jnp.concatenate([first.astype(BF), right[..., cut:, :]], axis=-2)]
    pallas_call x0 -> x1, Pallas kernels: none -> 3.04 us  [out_weight(): pl.pallas_call(kernel, in_specs=[hbm] * 5, out_specs=[vmem] * count, out_...]
    concatenate x4 -> x1, other arithmetic: 2.93 us -> 0.59 us  [layer(): ids = jnp.concatenate([ids, core[None]]).astype(jnp.int32)]
    pallas_call x13 -> x14, Pallas kernels: 58.1 us -> 60.3 us  [staged(): pl.pallas_call(kernel, in_specs=[pl.BlockSpec(memory_space=pltpu.SMEM)] *...]
  transfers between devices with their start and end apart: 43 -> 32, of which waited for: 12 -> 14; matrix products, arithmetic and copies ran while one was open for 14% -> 7% of each run, Pallas kernels for 25% -> 30%
where the time goes in v4:
time: 177 us; the launch traced here: 175 us
  Pallas kernels  70.1 us (40%)
  starting transfers between devices  51.3 us (29%)
  waiting for transfers between devices  30.7 us (17%)
  other arithmetic  10.9 us (6%)
  local copies, waits for them, and re-layouts  9.91 us (6%)
    pallas_call x14, Pallas kernels, staged(): pl.pallas_call(kernel, in_specs=[pl.BlockSpec(memory_space=pltpu.SMEM)] *...  60.3 us
    ppermute x16, starting transfers between devices, turn(): return lax.ppermute(values, 'ctx', pairs)  17.9 us
    all_to_all x3, starting transfers between devices, exchange(): return lax.all_to_all(values, 'ctx', 0, 0, axis_index_groups=head_groups)  17.1 us
    all_to_all x3, waiting for transfers between devices, exchange(): return lax.all_to_all(values, 'ctx', 0, 0, axis_index_groups=head_groups)  14.8 us
    ppermute x16, waiting for transfers between devices, turn(): return lax.ppermute(values, 'ctx', pairs)  14.6 us
    all_to_all x2, starting transfers between devices, exchange_wide(): lax.all_to_all(values, ('ctx', 'tp'), 0, 0, axis_index_groups=wide_groups)  8.42 us
    unnamed x54, local copies, waits for them, and re-layouts  7.51 us
    ppermute x5, starting transfers between devices, swap_tp(): return lax.ppermute(values, 'tp', [(0, 1), (1, 0)])  7.07 us
  transfers between devices with their start and end apart: 32, of which 14 were waited for; matrix products, arithmetic and copies ran while one was open for 7% of the time, Pallas kernels for 30%

profile of v4, /device:TPU:0, one launch (start us, length us, event | category | flops | bytes accessed | tf_op | source)
XLA Modules:
  0.0 175.5 jit_solution(595764924819604889)
XLA Ops:
  1.4 4.1 %project.1 = (bf16[8,192,128]{2,1,0:T(8,128)(2,1)}, bf16[128,1024]{1,0:T(8,128)(2,1)}) custom-call(bf16[128,1024]{1,0:T(8,128)(2,1)} %refs_0_.2, f32[1,1024]{1,0:T(1,128)} %bitcast.31, f32[32,128]{1,0:T(8,128)} %get-tuple-element.161.c_ref, f32[32,128]{1,0:T(8,128)} %get-tuple-element.160.s_ref, bf16[3,1024,512]{2,1,0:T(8,128)(2,1)} %bitcast.22), custom_call_target="tpu_custom_call" | custom-call | flops 402653184 | bytes 3145728 | tf_op jit(solution)/shard_map/project/pallas_call | solution.py:304
  5.5 7.3 %all-to-all-start = ((bf16[8,192,128]{2,1,0:T(8,128)(2,1)}), bf16[8,192,128]{2,1,0:T(8,128)(2,1)S(1)}, u32[]{:S(2)}, u32[]{:S(2)}) async-start(bf16[8,192,128]{2,1,0:T(8,128)(2,1)} %get-tuple-element.82), calls=%async_computation | async-start | bytes 786432 | tf_op jit(solution)/shard_map/all_to_all | solution.py:696
  12.8 1.6 collective-permute-start.5
  15.8 1.2 multiply_sine_fusion
  17.0 7.4 %all-to-all-done.refs_0_ = bf16[8,192,128]{2,1,0:T(8,128)(2,1)S(1)} async-done(((bf16[8,192,128]{2,1,0:T(8,128)(2,1)}), bf16[8,192,128]{2,1,0:T(8,128)(2,1)S(1)}, u32[]{:S(2)}, u32[]{:S(2)}) %all-to-all-start) | async-done | bytes 393248 | tf_op jit(solution)/shard_map/all_to_all | solution.py:696
  27.3 7.1 %attend.1 = (f32[8,64,128]{2,1,0:T(8,128)}, bf16[2,8,64,128]{3,2,1,0:T(8,128)(2,1)}, f32[8,1,128]{2,1,0:T(1,128)}) custom-call(bf16[8,192,128]{2,1,0:T(8,128)(2,1)} %copy-done.11, bf16[8,192,128]{2,1,0:T(8,128)(2,1)} %copy-done.24), custom_call_target="tpu_custom_call" | custom-call | flops 536870912 | bytes 786432 | tf_op jit(solution)/shard_map/attend/pallas_call | solution.py:50
  34.4 4.7 %all-to-all-start.1 = ((bf16[16,64,128]{2,1,0:T(8,128)(2,1)}), bf16[16,64,128]{2,1,0:T(8,128)(2,1)S(1)}, u32[]{:S(2)}, u32[]{:S(2)}) async-start(bf16[16,64,128]{2,1,0:T(8,128)(2,1)} %bitcast.30), calls=%async_computation.1 | async-start | bytes 524288 | tf_op jit(solution)/shard_map/all_to_all | solution.py:693
  39.1 1.9 %collective-permute-start.3 = (bf16[128,1024]{1,0:T(8,128)(2,1)S(1)}, bf16[128,1024]{1,0:T(8,128)(2,1)}, u32[]{:S(2)}, u32[]{:S(2)}) collective-permute-start(bf16[128,1024]{1,0:T(8,128)(2,1)S(1)} %collective-permute-done.1.refs_3_), channel_id=1, source_target_pairs={{0,8},{2,10},{4,0},{6,2},{8,16},{10,18},{12,4},{14,6},{16,24},{18,... | collective-permute-start | bytes 786440 | tf_op jit(solution)/shard_map/ppermute | solution.py:733
  41.1 1.3 constant_dynamic-slice_fusion
  43.5 3.8 %unit_back.1.refs_7_ = f32[128,1312]{1,0:T(8,128)} custom-call(bf16[128,1024]{1,0:T(8,128)(2,1)} %refs_1_.5, bf16[1312,1024]{1,0:T(8,128)(2,1)} %refs_1_.3), custom_call_target="tpu_custom_call" | custom-call | flops 343932928 | bytes 2686976 | tf_op jit(solution)/shard_map/unit_back/pallas_call | solution.py:50
  47.2 2.7 %collective-permute-done.3.refs_5_ = bf16[128,1024]{1,0:T(8,128)(2,1)} collective-permute-done((bf16[128,1024]{1,0:T(8,128)(2,1)S(1)}, bf16[128,1024]{1,0:T(8,128)(2,1)}, u32[]{:S(2)}, u32[]{:S(2)}) %collective-permute-start.3) | collective-permute-done | bytes 262176 | tf_op jit(solution)/shard_map/ppermute | solution.py:733
  50.0 1.8 %collective-permute-done.4.refs_6_ = bf16[128,1024]{1,0:T(8,128)(2,1)} collective-permute-done((bf16[128,1024]{1,0:T(8,128)(2,1)}, bf16[128,1024]{1,0:T(8,128)(2,1)}, u32[]{:S(2)}, u32[]{:S(2)}) %collective-permute-start.4) | collective-permute-done | bytes 262176 | tf_op jit(solution)/shard_map/ppermute | solution.py:733
  52.8 8.4 %middle_part.1 = (f32[128,1024]{1,0:T(8,128)}, bf16[128,5504]{1,0:T(8,128)(2,1)}, bf16[128,1312]{1,0:T(8,128)(2,1)}, bf16[128,1024]{1,0:T(8,128)(2,1)}, bf16[2,8,64,128]{3,2,1,0:T(8,128)(2,1)}) custom-call(s32[1]{0:T(128)} %bitcast.refs_0_, bf16[2,512,128]{2,1,0:T(8,128)(2,1)} %bitcast.27, bf16[128,1024]{1,0:T(8,128)(2,1)} %refs_0_.2, ...), custom_call_target="tpu_custom_call" | custom-call | flops 1912602624 | bytes 5373952 | tf_op jit(solution)/shard_map/middle_part/pallas_call | solution.py:50
  61.8 1.5 collective-permute-start.9
  63.3 2.5 %collective-permute-start.11 = (bf16[128,1024]{1,0:T(8,128)(2,1)}, bf16[128,1024]{1,0:T(8,128)(2,1)S(1)}, u32[]{:S(2)}, u32[]{:S(2)}) collective-permute-start(bf16[128,1024]{1,0:T(8,128)(2,1)} %collective-permute-done.3.refs_5_), channel_id=1, source_target_pairs={{0,8},{2,10},{4,0},{6,2},{8,16},{10,18},{12,4},{14,6},{16,24},{18,... | collective-permute-start | bytes 786440 | tf_op jit(solution)/shard_map/ppermute | solution.py:733
  65.8 3.8 %all-to-all-start.2 = ((bf16[16,64,128]{2,1,0:T(8,128)(2,1)}), bf16[16,64,128]{2,1,0:T(8,128)(2,1)S(1)}, u32[]{:S(2)}, u32[]{:S(2)}) async-start(bf16[16,64,128]{2,1,0:T(8,128)(2,1)} %bitcast.28), calls=%async_computation.2 | async-start | bytes 524288 | tf_op jit(solution)/shard_map/all_to_all | solution.py:693
  71.3 5.8 %mlp_weight.1 = (bf16[64,3968]{1,0:T(8,128)(2,1)}, bf16[64,3968]{1,0:T(8,128)(2,1)}, bf16[64,3968]{1,0:T(8,128)(2,1)}, bf16[64,3968]{1,0:T(8,128)(2,1)}, bf16[32...) custom-call(bf16[512,1024]{1,0:T(8,128)(2,1)} %fusion.refs_0_.pick_r, ...), custom_call_target="tpu_custom_call" | custom-call | flops 1442840576 | bytes 9699328 | tf_op jit(solution)/shard_map/mlp_weight/pallas_call | solution.py:50
  77.8 2.6 %middle_back.1 = (f32[128,1024]{1,0:T(8,128)}, bf16[128,1024]{1,0:T(8,128)(2,1)}) custom-call(f32[128,1024]{1,0:T(8,128)} %get-tuple-element.97.refs_0_, bf16[128,1024]{1,0:T(8,128)(2,1)} %refs_1_.5, f32[1,1024]{1,0:T(1,128)} %bitcast.34, bf16[128,1024]{1,0:T(8,128)(2,1)} %get-tuple-element.111.refs_3_, bf16[128,1024]{1,0:T(8,128)(2,1)} %copy-done.14), custom_call_target="tpu_custom_call" | custom-call | flops 2621440 | bytes 2097152 | tf_op jit(solution)/shard_map/middle_back/pallas_call | solution.py:50
  80.5 2.0 %collective-permute-start.13 = (bf16[128,1024]{1,0:T(8,128)(2,1)}, bf16[128,1024]{1,0:T(8,128)(2,1)S(1)}, u32[]{:S(2)}, u32[]{:S(2)}) collective-permute-start(bf16[128,1024]{1,0:T(8,128)(2,1)} %collective-permute-done.4.refs_6_), channel_id=1, source_target_pairs={{0,4},{2,6},{4,12},{6,14},{8,0},{10,2},{12,20},{14,22},{16,8},{18,... | collective-permute-start | bytes 786440 | tf_op jit(solution)/shard_map/ppermute | solution.py:733
  82.6 1.9 %collective-permute-start.14 = (bf16[32,3968]{1,0:T(8,128)(2,1)}, bf16[32,3968]{1,0:T(8,128)(2,1)S(1)}, u32[]{:S(2)}, u32[]{:S(2)}) collective-permute-start(bf16[32,3968]{1,0:T(8,128)(2,1)} %get-tuple-element.107), channel_id=1, source_target_pairs={{0,4},{2,6},{4,12},{6,14},{8,0},{10,2},{12,20},{14,22},{16,8},{18,... | collective-permute-start | bytes 761864 | tf_op jit(solution)/shard_map/ppermute | solution.py:733
  85.5 3.0 %out_weight.1 = (bf16[64,512]{1,0:T(8,128)(2,1)}, bf16[64,512]{1,0:T(8,128)(2,1)}, bf16[64,512]{1,0:T(8,128)(2,1)}, bf16[64,512]{1,0:T(8,128)(2,1)}, bf16[64,512...) custom-call(bf16[512,1024]{1,0:T(8,128)(2,1)} %fusion.refs_0_.pick_ref, ...), custom_call_target="tpu_custom_call" | custom-call | flops 268435456 | bytes 1048576 | tf_op jit(solution)/shard_map/out_weight/pallas_call | solution.py:529
  88.5 1.4 collective-permute-done.13.refs_8_
  90.0 1.7 collective-permute-done.12.refs_9_
  91.7 9.0 %attend_back.1 = (bf16[8,64,128]{2,1,0:T(8,128)(2,1)}, f32[8,128,128]{2,1,0:T(8,128)}, f32[8,128,128]{2,1,0:T(8,128)}) custom-call(bf16[8,192,128]{2,1,0:T(8,128)(2,1)} %copy-done.11, bf16[8,192,128]{2,1,0:T(8,128)(2,1)} %copy-done.24, bf16[2,8,64,128]{3,2,1,0:T(8,128)(2,1)} %bitcast.29, f32[8,64,128]{2,1,0:T(8,128)} %get-tuple-element.126.refs_3_, ...), custom_call_target="tpu_custom_call" | custom-call | flops 1342177280 | bytes 1572864 | tf_op jit(solution)/shard_map/attend_back/pallas_call | solution.py:50
  101.5 2.6 %ring_add.3 = (bf16[64,4480]{1,0:T(8,128)(2,1)}, bf16[64,4480]{1,0:T(8,128)(2,1)}) custom-call(bf16[64,3968]{1,0:T(8,128)(2,1)} %get-tuple-element.102.refs_0_, bf16[32,3968]{1,0:T(8,128)(2,1)} %copy-done.21, bf16[64,512]{1,0:T(8,128)(2,1)} %get-tuple-element.118.refs_2_, bf16[64,3968]{1,0:T(8,128)(2,1)} %get-tuple-element.108.refs_3_, ...), custom_call_target="tpu_custom_call" | custom-call | flops 1146880 | bytes 3440640 | tf_op jit(solution)/shard_map/ring_add/pallas_call | solution.py:50
  104.9 1.3 collective-permute-start.17
  107.0 2.2 %combine.1.refs_1_ = bf16[8,192,128]{2,1,0:T(8,128)(2,1)} custom-call(bf16[8,64,128]{2,1,0:T(8,128)(2,1)} %get-tuple-element.128.refs_0_, f32[8,128,128]{2,1,0:T(8,128)} %get-tuple-element.135.refs_1_, f32[8,128,128]{2,1,0:T(8,128)} %copy-done.10, f32[8,32,128]{2,1,0:T(8,128)} %get-tuple-element.157.refs_5_.refs_3_, ...), custom_call_target="tpu_custom_call" | custom-call | flops 65536 | bytes 1310720 | tf_op jit(solution)/shard_map/combine/pallas_call | solution.py:50
  109.1 4.8 %all-to-all-start.3 = ((bf16[8,192,128]{2,1,0:T(8,128)(2,1)}), bf16[8,192,128]{2,1,0:T(8,128)(2,1)S(1)}, u32[]{:S(2)}, u32[]{:S(2)}) async-start(bf16[8,192,128]{2,1,0:T(8,128)(2,1)} %combine.1.refs_1_), calls=%async_computation.3 | async-start | bytes 786432 | tf_op jit(solution)/shard_map/all_to_all | solution.py:696
  114.6 4.1 %head_weight.1 = (bf16[8,64,192]{2,1,0:T(8,128)(2,1)}, bf16[8,64,192]{2,1,0:T(8,128)(2,1)}) custom-call(s32[9]{0:T(128)} %pad_add_fusion.refs_0_, bf16[8,192,128]{2,1,0:T(8,128)(2,1)} %combine.1.refs_1_, bf16[128,1024]{1,0:T(8,128)(2,1)} %get-tuple-element.90.refs_2_, bf16[128,1024]{1,0:T(8,128)(2,1)} %copy-done.16, ...), custom_call_target="tpu_custom_call" | custom-call | flops 402653184 | bytes 2097152 | tf_op jit(solution)/shard_map/head_weight/pallas_call | solution.py:50
  120.7 2.8 %ring_add.4 = (bf16[64,4480]{1,0:T(8,128)(2,1)}, bf16[64,4480]{1,0:T(8,128)(2,1)}) custom-call(bf16[64,3968]{1,0:T(8,128)(2,1)} %get-tuple-element.101.refs_0_, bf16[64,4480]{1,0:T(8,128)(2,1)} %collective-permute-done.15.refs_1_, bf16[64,512]{1,0:T(8,128)(2,1)} %get-tuple-element.117.refs_2_, bf16[64,3968]{1,0:T(8,128)(2,1)} %get-tuple-element.109.refs_3_, ...), custom_call_target="tpu_custom_call" | custom-call | flops 1146880 | bytes 3440640 | tf_op jit(solution)/shard_map/ring_add/pallas_call | solution.py:50
  123.5 2.5 %collective-permute-start.18 = (bf16[64,4480]{1,0:T(8,128)(2,1)}, bf16[64,4480]{1,0:T(8,128)(2,1)}, u32[]{:S(2)}, u32[]{:S(2)}) collective-permute-start(bf16[64,4480]{1,0:T(8,128)(2,1)} %get-tuple-element.139), channel_id=1, source_target_pairs={{0,8},{2,10},{4,0},{6,2},{8,16},{10,18},{12,4},{14,6},{16,24},{18,... | collective-permute-start | bytes 1720328 | tf_op jit(solution)/shard_map/ppermute | solution.py:733
  126.0 1.7 add_convert_fusion.1
  127.7 2.3 %all-to-all-done.3.refs_0_ = bf16[8,192,128]{2,1,0:T(8,128)(2,1)S(1)} async-done(((bf16[8,192,128]{2,1,0:T(8,128)(2,1)}), bf16[8,192,128]{2,1,0:T(8,128)(2,1)S(1)}, u32[]{:S(2)}, u32[]{:S(2)}) %all-to-all-start.3) | async-done | bytes 393248 | tf_op jit(solution)/shard_map/all_to_all | solution.py:696
  130.0 5.0 %all-to-all-start.4 = ((bf16[8,64,192]{2,1,0:T(8,128)(2,1)}), bf16[8,64,192]{2,1,0:T(8,128)(2,1)}, u32[]{:S(2)}, u32[]{:S(2)}) async-start(bf16[8,64,192]{2,1,0:T(8,128)(2,1)} %add_convert_fusion.1), calls=%async_computation.4 | async-start | bytes 524288 | tf_op jit(solution)/shard_map/all_to_all | solution.py:696
  135.0 1.6 convolution_convert_fusion
  136.6 3.9 %project_back.1.refs_2_ = bf16[128,1024]{1,0:T(8,128)(2,1)} custom-call(bf16[8,192,128]{2,1,0:T(8,128)(2,1)} %copy-done.3, bf16[3,1024,512]{2,1,0:T(8,128)(2,1)} %bitcast.23), custom_call_target="tpu_custom_call" | custom-call | flops 402653184 | bytes 3145728 | tf_op jit(solution)/shard_map/project_back/pallas_call | solution.py:50
  140.5 1.3 collective-permute-start.20
  141.8 5.1 %all-to-all-done.4.blocks_ref = bf16[8,64,192]{2,1,0:T(8,128)(2,1)} async-done(((bf16[8,64,192]{2,1,0:T(8,128)(2,1)}), bf16[8,64,192]{2,1,0:T(8,128)(2,1)}, u32[]{:S(2)}, u32[]{:S(2)}) %all-to-all-start.4) | async-done | bytes 196640 | tf_op jit(solution)/shard_map/all_to_all | solution.py:696
  147.2 2.9 %ring_add.5 = (bf16[64,4480]{1,0:T(8,128)(2,1)}, bf16[64,4480]{1,0:T(8,128)(2,1)}) custom-call(bf16[64,3968]{1,0:T(8,128)(2,1)} %get-tuple-element.106.refs_0_, bf16[64,4480]{1,0:T(8,128)(2,1)} %collective-permute-done.18.refs_1_, bf16[64,512]{1,0:T(8,128)(2,1)} %get-tuple-element.116.refs_2_, bf16[64,3968]{1,0:T(8,128)(2,1)} %get-tuple-element.110.refs_3_, ...), custom_call_target="tpu_custom_call" | custom-call | flops 1146880 | bytes 3440640 | tf_op jit(solution)/shard_map/ring_add/pallas_call | solution.py:50
  150.0 2.1 %collective-permute-start.23 = (bf16[64,4480]{1,0:T(8,128)(2,1)}, bf16[64,4480]{1,0:T(8,128)(2,1)S(1)}, u32[]{:S(2)}, u32[]{:S(2)}) collective-permute-start(bf16[64,4480]{1,0:T(8,128)(2,1)} %get-tuple-element.146), channel_id=1, source_target_pairs={{0,8},{2,10},{4,0},{6,2},{8,16},{10,18},{12,4},{14,6},{16,24},{18,... | collective-permute-start | bytes 1720328 | tf_op jit(solution)/shard_map/ppermute | solution.py:733
  152.2 1.2 collective-permute-start.22
  153.4 2.6 %finish_qkv.1 = (f32[3,64,512]{2,1,0:T(8,128)}, f32[64,1]{1,0:T(8,128)}) custom-call(s32[1]{0:T(128)} %bitcast.11.first_ref, bf16[8,64,192]{2,1,0:T(8,128)(2,1)} %all-to-all-done.4.blocks_ref, bf16[3,1024,512]{2,1,0:T(8,128)(2,1)} %bitcast.24), custom_call_target="tpu_custom_call" | custom-call | flops 196608 | bytes 983040 | tf_op jit(solution)/shard_map/finish_qkv/pallas_call | solution.py:599
  156.1 2.6 %input_back.1 = f32[128,1024]{1,0:T(8,128)} custom-call(bf16[128,1024]{1,0:T(8,128)(2,1)} %refs_0_.2, f32[1,1024]{1,0:T(1,128)} %bitcast.32, bf16[128,1024]{1,0:T(8,128)(2,1)} %project_back.1.refs_2_, f32[128,1024]{1,0:T(8,128)} %get-tuple-element.149.refs_3_, bf16[128,1024]{1,0:T(8,128)(2,1)} %copy-done.12), custom_call_target="tpu_custom_call" | custom-call | flops 2621440 | bytes 1835008 | tf_op jit(solution)/shard_map/input_back/pallas_call | solution.py:50
  159.5 3.9 %collective-permute-done.23.refs_1_ = bf16[64,4480]{1,0:T(8,128)(2,1)S(1)} collective-permute-done((bf16[64,4480]{1,0:T(8,128)(2,1)}, bf16[64,4480]{1,0:T(8,128)(2,1)S(1)}, u32[]{:S(2)}, u32[]{:S(2)}) %collective-permute-start.23) | collective-permute-done | bytes 573472 | tf_op jit(solution)/shard_map/ppermute | solution.py:733
  164.5 2.8 %finish_mlp.1 = (f32[64,2,1312]{2,1,0:T(2,128)}, f32[64,1312]{1,0:T(8,128)}, f32[2,64]{1,0:T(2,128)}) custom-call(bf16[64,3968]{1,0:T(8,128)(2,1)} %get-tuple-element.105.refs_0_, bf16[64,4480]{1,0:T(8,128)(2,1)} %copy-done.9, bf16[64,4480]{1,0:T(8,128)(2,1)} %copy-done.8, bf16[64,2624]{1,0:T(8,128)(2,1)} %copy.18.refs_3_, f32[64,1]{1,0:T(8,128)} %get-tuple-element.151.refs_4_), custom_call_target="tpu_custom_call" | custom-call | flops 2031616 | bytes 3555328 | tf_op jit(solution)/shard_map/finish_mlp/pallas_call | solution.py:50
  167.3 1.5 collective-permute-start.25
  171.6 1.3 bitcast_divide_fusion
  173.9 1.5 add_bitcast_fusion
  (109 shorter events, 22.5 us)
Async XLA Ops:
  0.6 12.2 %copy-start.6 = (bf16[512,1024]{1,0:T(8,128)(2,1)S(1)}, bf16[512,1024]{1,0:T(8,128)(2,1)}, u32[]{:S(2)}) copy-start(bf16[512,1024]{1,0:T(8,128)(2,1)} %refs_5_.1) | copy-start | bytes 3145732
  5.5 19.0 %all-to-all-start = ((bf16[8,192,128]{2,1,0:T(8,128)(2,1)}), bf16[8,192,128]{2,1,0:T(8,128)(2,1)S(1)}, u32[]{:S(2)}, u32[]{:S(2)}) async-start(bf16[8,192,128]{2,1,0:T(8,128)(2,1)} %get-tuple-element.82), calls=%async_computation | async-start | bytes 786432 | tf_op jit(solution)/shard_map/all_to_all | solution.py:696
  12.8 39.0 %collective-permute-start.5 = (bf16[512,1024]{1,0:T(8,128)(2,1)S(1)}, bf16[512,1024]{1,0:T(8,128)(2,1)S(1)}, u32[]{:S(2)}, u32[]{:S(2)}) collective-permute-start(bf16[512,1024]{1,0:T(8,128)(2,1)S(1)} %copy-done.6), channel_id=1, source_target_pairs={{0,1},{1,0},{2,3},{3,2},{4,5},{5,4},{6,7},{7,6},{8,9},{9,8},{10,11... | collective-permute-start | bytes 3145736 | tf_op jit(solution)/shard_map/ppermute | solution.py:711
  24.5 2.0 %copy-start.11 = (bf16[8,192,128]{2,1,0:T(8,128)(2,1)}, bf16[8,192,128]{2,1,0:T(8,128)(2,1)S(1)}, u32[]{:S(2)}) copy-start(bf16[8,192,128]{2,1,0:T(8,128)(2,1)S(1)} %all-to-all-done.refs_0_) | copy-start | bytes 1179652
  24.5 2.0 %collective-permute-start = (bf16[8,192,128]{2,1,0:T(8,128)(2,1)S(1)}, bf16[8,192,128]{2,1,0:T(8,128)(2,1)S(1)}, u32[]{:S(2)}, u32[]{:S(2)}) collective-permute-start(bf16[8,192,128]{2,1,0:T(8,128)(2,1)S(1)} %all-to-all-done.refs_0_), channel_id=1, source_target_pairs={{0,2},{2,0},{4,6},{6,4},{8,10},{10,8},{12,14},{14,12},{16,18},{18,... | collective-permute-start | bytes 1179656 | tf_op jit(solution)/shard_map/ppermute | solution.py:708
  24.5 9.9 %collective-permute-start.1 = (bf16[128,1024]{1,0:T(8,128)(2,1)}, bf16[128,1024]{1,0:T(8,128)(2,1)S(1)}, u32[]{:S(2)}, u32[]{:S(2)}) collective-permute-start(bf16[128,1024]{1,0:T(8,128)(2,1)} %get-tuple-element.90.refs_2_), channel_id=1, source_target_pairs={{0,8},{2,10},{4,0},{6,2},{8,16},{10,18},{12,4},{14,6},{16,24},{18,... | collective-permute-start | bytes 786440 | tf_op jit(solution)/shard_map/ppermute | solution.py:733
  25.4 9.0 %collective-permute-start.2 = (bf16[128,1024]{1,0:T(8,128)(2,1)}, bf16[128,1024]{1,0:T(8,128)(2,1)}, u32[]{:S(2)}, u32[]{:S(2)}) collective-permute-start(bf16[128,1024]{1,0:T(8,128)(2,1)} %get-tuple-element.90.refs_2_), channel_id=1, source_target_pairs={{0,4},{2,6},{4,12},{6,14},{8,0},{10,2},{12,20},{14,22},{16,8},{18,... | collective-permute-start | bytes 786440 | tf_op jit(solution)/shard_map/ppermute | solution.py:733
  34.4 12.9 %copy-start.16 = (bf16[128,1024]{1,0:T(8,128)(2,1)}, bf16[128,1024]{1,0:T(8,128)(2,1)S(1)}, u32[]{:S(2)}) copy-start(bf16[128,1024]{1,0:T(8,128)(2,1)S(1)} %collective-permute-done.1.refs_3_) | copy-start | bytes 786436
  34.4 17.4 %all-to-all-start.1 = ((bf16[16,64,128]{2,1,0:T(8,128)(2,1)}), bf16[16,64,128]{2,1,0:T(8,128)(2,1)S(1)}, u32[]{:S(2)}, u32[]{:S(2)}) async-start(bf16[16,64,128]{2,1,0:T(8,128)(2,1)} %bitcast.30), calls=%async_computation.1 | async-start | bytes 524288 | tf_op jit(solution)/shard_map/all_to_all | solution.py:693
  39.1 10.9 %collective-permute-start.3 = (bf16[128,1024]{1,0:T(8,128)(2,1)S(1)}, bf16[128,1024]{1,0:T(8,128)(2,1)}, u32[]{:S(2)}, u32[]{:S(2)}) collective-permute-start(bf16[128,1024]{1,0:T(8,128)(2,1)S(1)} %collective-permute-done.1.refs_3_), channel_id=1, source_target_pairs={{0,8},{2,10},{4,0},{6,2},{8,16},{10,18},{12,4},{14,6},{16,24},{18,... | collective-permute-start | bytes 786440 | tf_op jit(solution)/shard_map/ppermute | solution.py:733
  41.0 10.8 %collective-permute-start.4 = (bf16[128,1024]{1,0:T(8,128)(2,1)}, bf16[128,1024]{1,0:T(8,128)(2,1)}, u32[]{:S(2)}, u32[]{:S(2)}) collective-permute-start(bf16[128,1024]{1,0:T(8,128)(2,1)} %collective-permute-done.2.refs_4_), channel_id=1, source_target_pairs={{0,4},{2,6},{4,12},{6,14},{8,0},{10,2},{12,20},{14,22},{16,8},{18,... | collective-permute-start | bytes 786440 | tf_op jit(solution)/shard_map/ppermute | solution.py:733
  52.8 8.5 %copy-start.1 = (bf16[128,1024]{1,0:T(8,128)(2,1)S(1)}, bf16[128,1024]{1,0:T(8,128)(2,1)}, u32[]{:S(2)}) copy-start(bf16[128,1024]{1,0:T(8,128)(2,1)} %refs_1_.5) | copy-start | bytes 786436
  61.2 8.3 %collective-permute-start.7 = (bf16[128,5504]{1,0:T(8,128)(2,1)}, bf16[128,5504]{1,0:T(8,128)(2,1)S(1)}, u32[]{:S(2)}, u32[]{:S(2)}) collective-permute-start(bf16[128,5504]{1,0:T(8,128)(2,1)} %get-tuple-element.100.refs_3_.mid_ref), channel_id=1, source_target_pairs={{0,2},{2,0},{4,6},{6,4},{8,10},{10,8},{12,14},{14,12},{16,18},{18,... | collective-permute-start | bytes 4227080 | tf_op jit(solution)/shard_map/ppermute | solution.py:699
  61.3 8.2 %collective-permute-start.6 = (bf16[128,1024]{1,0:T(8,128)(2,1)S(1)}, bf16[128,1024]{1,0:T(8,128)(2,1)S(1)}, u32[]{:S(2)}, u32[]{:S(2)}) collective-permute-start(bf16[128,1024]{1,0:T(8,128)(2,1)S(1)} %copy-done.1), channel_id=1, source_target_pairs={{0,2},{2,0},{4,6},{6,4},{8,10},{10,8},{12,14},{14,12},{16,18},{18,... | collective-permute-start | bytes 786440 | tf_op jit(solution)/shard_map/ppermute | solution.py:699
  61.8 15.3 %collective-permute-start.9 = (bf16[128,1024]{1,0:T(8,128)(2,1)}, bf16[128,1024]{1,0:T(8,128)(2,1)S(1)}, u32[]{:S(2)}, u32[]{:S(2)}) collective-permute-start(bf16[128,1024]{1,0:T(8,128)(2,1)} %get-tuple-element.111.refs_3_), channel_id=1, source_target_pairs={{0,1},{1,0},{2,3},{3,2},{4,5},{5,4},{6,7},{7,6},{8,9},{9,8},{10,11... | collective-permute-start | bytes 786440 | tf_op jit(solution)/shard_map/ppermute | solution.py:711
  63.3 19.3 %collective-permute-start.11 = (bf16[128,1024]{1,0:T(8,128)(2,1)}, bf16[128,1024]{1,0:T(8,128)(2,1)S(1)}, u32[]{:S(2)}, u32[]{:S(2)}) collective-permute-start(bf16[128,1024]{1,0:T(8,128)(2,1)} %collective-permute-done.3.refs_5_), channel_id=1, source_target_pairs={{0,8},{2,10},{4,0},{6,2},{8,16},{10,18},{12,4},{14,6},{16,24},{18,... | collective-permute-start | bytes 786440 | tf_op jit(solution)/shard_map/ppermute | solution.py:733
  65.8 24.2 %all-to-all-start.2 = ((bf16[16,64,128]{2,1,0:T(8,128)(2,1)}), bf16[16,64,128]{2,1,0:T(8,128)(2,1)S(1)}, u32[]{:S(2)}, u32[]{:S(2)}) async-start(bf16[16,64,128]{2,1,0:T(8,128)(2,1)} %bitcast.28), calls=%async_computation.2 | async-start | bytes 524288 | tf_op jit(solution)/shard_map/all_to_all | solution.py:693
  70.2 1.1 copy-start.4
  80.5 4.3 %collective-permute-start.10 = (bf16[128,1024]{1,0:T(8,128)(2,1)}, bf16[128,1024]{1,0:T(8,128)(2,1)S(1)}, u32[]{:S(2)}, u32[]{:S(2)}) collective-permute-start(bf16[128,1024]{1,0:T(8,128)(2,1)} %get-tuple-element.113.own_ref), channel_id=1, source_target_pairs={{0,2},{2,0},{4,6},{6,4},{8,10},{10,8},{12,14},{14,12},{16,18},{18,... | collective-permute-start | bytes 786440 | tf_op jit(solution)/shard_map/ppermute | solution.py:699
  80.5 9.4 %collective-permute-start.13 = (bf16[128,1024]{1,0:T(8,128)(2,1)}, bf16[128,1024]{1,0:T(8,128)(2,1)S(1)}, u32[]{:S(2)}, u32[]{:S(2)}) collective-permute-start(bf16[128,1024]{1,0:T(8,128)(2,1)} %collective-permute-done.4.refs_6_), channel_id=1, source_target_pairs={{0,4},{2,6},{4,12},{6,14},{8,0},{10,2},{12,20},{14,22},{16,8},{18,... | collective-permute-start | bytes 786440 | tf_op jit(solution)/shard_map/ppermute | solution.py:733
  82.5 32.0 %copy-start.17 = (bf16[128,1024]{1,0:T(8,128)(2,1)}, bf16[128,1024]{1,0:T(8,128)(2,1)S(1)}, u32[]{:S(2)}) copy-start(bf16[128,1024]{1,0:T(8,128)(2,1)S(1)} %collective-permute-done.11.refs_7_) | copy-start | bytes 786436
  82.5 9.2 %collective-permute-start.12 = (bf16[128,1024]{1,0:T(8,128)(2,1)S(1)}, bf16[128,1024]{1,0:T(8,128)(2,1)S(1)}, u32[]{:S(2)}, u32[]{:S(2)}) collective-permute-start(bf16[128,1024]{1,0:T(8,128)(2,1)S(1)} %collective-permute-done.11.refs_7_), channel_id=1, source_target_pairs={{0,8},{2,10},{4,0},{6,2},{8,16},{10,18},{12,4},{14,6},{16,24},{18,... | collective-permute-start | bytes 786440 | tf_op jit(solution)/shard_map/ppermute | solution.py:733
  82.6 18.1 %collective-permute-start.14 = (bf16[32,3968]{1,0:T(8,128)(2,1)}, bf16[32,3968]{1,0:T(8,128)(2,1)S(1)}, u32[]{:S(2)}, u32[]{:S(2)}) collective-permute-start(bf16[32,3968]{1,0:T(8,128)(2,1)} %get-tuple-element.107), channel_id=1, source_target_pairs={{0,4},{2,6},{4,12},{6,14},{8,0},{10,2},{12,20},{14,22},{16,8},{18,... | collective-permute-start | bytes 761864 | tf_op jit(solution)/shard_map/ppermute | solution.py:733
  84.6 16.2 %collective-permute-start.8 = (bf16[32,3968]{1,0:T(8,128)(2,1)}, bf16[32,3968]{1,0:T(8,128)(2,1)S(1)}, u32[]{:S(2)}, u32[]{:S(2)}) collective-permute-start(bf16[32,3968]{1,0:T(8,128)(2,1)} %get-tuple-element.103), channel_id=1, source_target_pairs={{0,8},{2,10},{4,0},{6,2},{8,16},{10,18},{12,4},{14,6},{16,24},{18,... | collective-permute-start | bytes 761864 | tf_op jit(solution)/shard_map/ppermute | solution.py:733
  90.0 24.0 %copy-start.18 = (bf16[128,1024]{1,0:T(8,128)(2,1)}, bf16[128,1024]{1,0:T(8,128)(2,1)S(1)}, u32[]{:S(2)}) copy-start(bf16[128,1024]{1,0:T(8,128)(2,1)S(1)} %collective-permute-done.13.refs_8_) | copy-start | bytes 786436
  90.0 1.7 copy-start.15
  91.7 12.4 %copy-start.19 = (bf16[128,1024]{1,0:T(8,128)(2,1)}, bf16[128,1024]{1,0:T(8,128)(2,1)S(1)}, u32[]{:S(2)}) copy-start(bf16[128,1024]{1,0:T(8,128)(2,1)S(1)} %collective-permute-done.12.refs_9_) | copy-start | bytes 786436
  100.7 13.2 %copy-start.26 = (s32[8]{0:T(128)S(1)}, s32[8]{0:T(128)}, u32[]{:S(2)}) copy-start(s32[8]{0:T(128)} %constant.99.clone) | copy-start | bytes 100
  100.8 5.4 %collective-permute-start.16 = (f32[8,128,128]{2,1,0:T(8,128)}, f32[8,128,128]{2,1,0:T(8,128)S(1)}, u32[]{:S(2)}, u32[]{:S(2)}) collective-permute-start(f32[8,128,128]{2,1,0:T(8,128)} %get-tuple-element.136), channel_id=1, source_target_pairs={{0,2},{2,0},{4,6},{6,4},{8,10},{10,8},{12,14},{14,12},{16,18},{18,... | collective-permute-start | bytes 1572872 | tf_op jit(solution)/shard_map/ppermute | solution.py:708
  104.1 15.6 %collective-permute-start.15 = (bf16[64,4480]{1,0:T(8,128)(2,1)}, bf16[64,4480]{1,0:T(8,128)(2,1)}, u32[]{:S(2)}, u32[]{:S(2)}) collective-permute-start(bf16[64,4480]{1,0:T(8,128)(2,1)} %get-tuple-element.130), channel_id=1, source_target_pairs={{0,8},{2,10},{4,0},{6,2},{8,16},{10,18},{12,4},{14,6},{16,24},{18,... | collective-permute-start | bytes 1720328 | tf_op jit(solution)/shard_map/ppermute | solution.py:733
  104.9 15.8 %collective-permute-start.17 = (bf16[64,4480]{1,0:T(8,128)(2,1)}, bf16[64,4480]{1,0:T(8,128)(2,1)}, u32[]{:S(2)}, u32[]{:S(2)}) collective-permute-start(bf16[64,4480]{1,0:T(8,128)(2,1)} %get-tuple-element.134), channel_id=1, source_target_pairs={{0,4},{2,6},{4,12},{6,14},{8,0},{10,2},{12,20},{14,22},{16,8},{18,... | collective-permute-start | bytes 1720328 | tf_op jit(solution)/shard_map/ppermute | solution.py:733
  109.1 20.8 %all-to-all-start.3 = ((bf16[8,192,128]{2,1,0:T(8,128)(2,1)}), bf16[8,192,128]{2,1,0:T(8,128)(2,1)S(1)}, u32[]{:S(2)}, u32[]{:S(2)}) async-start(bf16[8,192,128]{2,1,0:T(8,128)(2,1)} %combine.1.refs_1_), calls=%async_computation.3 | async-start | bytes 786432 | tf_op jit(solution)/shard_map/all_to_all | solution.py:696
  114.6 20.5 %copy-start = (bf16[1312,1024]{1,0:T(8,128)(2,1)S(1)}, bf16[1312,1024]{1,0:T(8,128)(2,1)}, u32[]{:S(2)}) copy-start(bf16[1312,1024]{1,0:T(8,128)(2,1)} %refs_1_.3) | copy-start | bytes 8060932
  118.6 7.4 %collective-permute-start.19 = (bf16[8,64,192]{2,1,0:T(8,128)(2,1)}, bf16[8,64,192]{2,1,0:T(8,128)(2,1)S(1)}, u32[]{:S(2)}, u32[]{:S(2)}) collective-permute-start(bf16[8,64,192]{2,1,0:T(8,128)(2,1)} %get-tuple-element.142), channel_id=1, source_target_pairs={{0,2},{2,0},{4,6},{6,4},{8,10},{10,8},{12,14},{14,12},{16,18},{18,... | collective-permute-start | bytes 589832 | tf_op jit(solution)/shard_map/ppermute | solution.py:699
  123.5 23.4 %collective-permute-start.18 = (bf16[64,4480]{1,0:T(8,128)(2,1)}, bf16[64,4480]{1,0:T(8,128)(2,1)}, u32[]{:S(2)}, u32[]{:S(2)}) collective-permute-start(bf16[64,4480]{1,0:T(8,128)(2,1)} %get-tuple-element.139), channel_id=1, source_target_pairs={{0,8},{2,10},{4,0},{6,2},{8,16},{10,18},{12,4},{14,6},{16,24},{18,... | collective-permute-start | bytes 1720328 | tf_op jit(solution)/shard_map/ppermute | solution.py:733
  126.0 21.2 %collective-permute-start.21 = (bf16[64,4480]{1,0:T(8,128)(2,1)}, bf16[64,4480]{1,0:T(8,128)(2,1)}, u32[]{:S(2)}, u32[]{:S(2)}) collective-permute-start(bf16[64,4480]{1,0:T(8,128)(2,1)} %get-tuple-element.140), channel_id=1, source_target_pairs={{0,4},{2,6},{4,12},{6,14},{8,0},{10,2},{12,20},{14,22},{16,8},{18,... | collective-permute-start | bytes 1720328 | tf_op jit(solution)/shard_map/ppermute | solution.py:733
  130.0 6.6 %copy-start.3 = (bf16[8,192,128]{2,1,0:T(8,128)(2,1)}, bf16[8,192,128]{2,1,0:T(8,128)(2,1)S(1)}, u32[]{:S(2)}) copy-start(bf16[8,192,128]{2,1,0:T(8,128)(2,1)S(1)} %all-to-all-done.3.refs_0_) | copy-start | bytes 1179652
  130.0 16.9 %all-to-all-start.4 = ((bf16[8,64,192]{2,1,0:T(8,128)(2,1)}), bf16[8,64,192]{2,1,0:T(8,128)(2,1)}, u32[]{:S(2)}, u32[]{:S(2)}) async-start(bf16[8,64,192]{2,1,0:T(8,128)(2,1)} %add_convert_fusion.1), calls=%async_computation.4 | async-start | bytes 524288 | tf_op jit(solution)/shard_map/all_to_all | solution.py:696
  140.5 6.6 %collective-permute-start.20 = (bf16[128,1024]{1,0:T(8,128)(2,1)}, bf16[128,1024]{1,0:T(8,128)(2,1)S(1)}, u32[]{:S(2)}, u32[]{:S(2)}) collective-permute-start(bf16[128,1024]{1,0:T(8,128)(2,1)} %project_back.1.refs_2_), channel_id=1, source_target_pairs={{0,1},{1,0},{2,3},{3,2},{4,5},{5,4},{6,7},{7,6},{8,9},{9,8},{10,11... | collective-permute-start | bytes 786440 | tf_op jit(solution)/shard_map/ppermute | solution.py:711
  147.2 8.9 %copy-start.12 = (bf16[128,1024]{1,0:T(8,128)(2,1)}, bf16[128,1024]{1,0:T(8,128)(2,1)S(1)}, u32[]{:S(2)}) copy-start(bf16[128,1024]{1,0:T(8,128)(2,1)S(1)} %collective-permute-done.20.refs_4_) | copy-start | bytes 786436
  150.0 8.6 %copy-start.2 = (f32[128,1024]{1,0:T(8,128)S(1)}, f32[128,1024]{1,0:T(8,128)}, u32[]{:S(2)}) copy-start(f32[128,1024]{1,0:T(8,128)} %get-tuple-element.97.refs_0_) | copy-start | bytes 1572868
  150.0 13.4 %collective-permute-start.23 = (bf16[64,4480]{1,0:T(8,128)(2,1)}, bf16[64,4480]{1,0:T(8,128)(2,1)S(1)}, u32[]{:S(2)}, u32[]{:S(2)}) collective-permute-start(bf16[64,4480]{1,0:T(8,128)(2,1)} %get-tuple-element.146), channel_id=1, source_target_pairs={{0,8},{2,10},{4,0},{6,2},{8,16},{10,18},{12,4},{14,6},{16,24},{18,... | collective-permute-start | bytes 1720328 | tf_op jit(solution)/shard_map/ppermute | solution.py:733
  152.1 11.4 %collective-permute-start.24 = (bf16[64,4480]{1,0:T(8,128)(2,1)}, bf16[64,4480]{1,0:T(8,128)(2,1)S(1)}, u32[]{:S(2)}, u32[]{:S(2)}) collective-permute-start(bf16[64,4480]{1,0:T(8,128)(2,1)} %get-tuple-element.147), channel_id=1, source_target_pairs={{0,4},{2,6},{4,12},{6,14},{8,0},{10,2},{12,20},{14,22},{16,8},{18,... | collective-permute-start | bytes 1720328 | tf_op jit(solution)/shard_map/ppermute | solution.py:733
  152.2 6.5 %collective-permute-start.22 = (bf16[128,1024]{1,0:T(8,128)(2,1)S(1)}, bf16[128,1024]{1,0:T(8,128)(2,1)S(1)}, u32[]{:S(2)}, u32[]{:S(2)}) collective-permute-start(bf16[128,1024]{1,0:T(8,128)(2,1)S(1)} %convolution_convert_fusion), channel_id=1, source_target_pairs={{0,1},{1,0},{2,3},{3,2},{4,5},{5,4},{6,7},{7,6},{8,9},{9,8},{10,11... | collective-permute-start | bytes 786440 | tf_op jit(solution)/shard_map/ppermute | solution.py:711
  156.1 12.7 %copy-start.23 = (bf16[64,512]{1,0:T(8,128)(2,1)S(1)}, bf16[64,512]{1,0:T(8,128)(2,1)}, u32[]{:S(2)}) copy-start(bf16[64,512]{1,0:T(8,128)(2,1)} %get-tuple-element.115) | copy-start | bytes 196612
  156.1 17.9 %copy-start.22 = (bf16[64,512]{1,0:T(8,128)(2,1)S(1)}, bf16[64,512]{1,0:T(8,128)(2,1)}, u32[]{:S(2)}) copy-start(bf16[64,512]{1,0:T(8,128)(2,1)} %get-tuple-element.114) | copy-start | bytes 196612
  167.3 3.7 %collective-permute-start.25 = (f32[2,64]{1,0:T(2,128)}, f32[2,64]{1,0:T(2,128)S(1)}, u32[]{:S(2)}, u32[]{:S(2)}) collective-permute-start(f32[2,64]{1,0:T(2,128)} %get-tuple-element.152), channel_id=1, source_target_pairs={{0,1},{1,0},{2,3},{3,2},{4,5},{5,4},{6,7},{7,6},{8,9},{9,8},{10,11... | collective-permute-start | bytes 1544 | tf_op jit(solution)/shard_map/ppermute | solution.py:711
  169.6 4.3 %collective-permute-start.26 = (bf16[64,512]{1,0:T(8,128)(2,1)S(1)}, bf16[64,512]{1,0:T(8,128)(2,1)S(1)}, u32[]{:S(2)}, u32[]{:S(2)}) collective-permute-start(bf16[64,512]{1,0:T(8,128)(2,1)S(1)} %add_convert_fusion.2), channel_id=1, source_target_pairs={{0,8},{2,10},{4,0},{6,2},{8,16},{10,18},{12,4},{14,6},{16,24},{18,... | collective-permute-start | bytes 196616 | tf_op jit(solution)/shard_map/ppermute | solution.py:733
  (11 other events, 8.7 us)

commit v5 on v4

--- a/solution.py
+++ b/solution.py
@@ -45,7 +45,7 @@
             copy.wait()
         body(*front, *held, *results, *rest, *[copy.wait for copy in copies[count - late :]])
 
-    vmem, hbm = pl.BlockSpec(memory_space=pltpu.VMEM), pl.BlockSpec(memory_space=pltpu.HBM)
+    vmem, hbm = pl.BlockSpec(memory_space=pltpu.VMEM), pl.BlockSpec(memory_space=pl.ANY)
     specs = [vmem] * (len(outs) - far) + [hbm] * far
     return pl.pallas_call(
         kernel,
@@ -98,7 +98,7 @@
     load_columns(parts, HD, vt_scr)
     pair = s_scr.shape[2] // width
 
-    @pl.loop(0, blocks // pair)
+    @pl.loop(0, blocks // pair, unroll=True)
     def query_block(i):
         qt = jnp.concatenate([own_ref[pair * i + b, :HD, :] for b in range(pair)], axis=1)
 
@@ -172,7 +172,7 @@
     dv_scr[...] = jnp.zeros_like(dv_scr)
     pair = 2 if blocks % 2 == 0 else 1
 
-    @pl.loop(0, blocks // pair)
+    @pl.loop(0, blocks // pair, unroll=True)
     def query_block(i):
         span = range(pair)
         qt = jnp.concatenate([own_ref[pair * i + b, :HD, :] for b in span], axis=1)
@@ -362,7 +362,8 @@
     mid_ref[:, :model] = mlp_input
     mid_ref[:, model:first] = attn_own
     wait_units()
-    gate, up = nt(mlp_input, w_in_ref[0]), nt(mlp_input, w_in_ref[1])
+    turned = mlp_input.T
+    gate, up = nn(w_in_ref[0], turned).T, nn(w_in_ref[1], turned).T
     share = 0.5 * (1.0 + lax.erf(gate * (0.5**0.5)))
     slope = share + gate * jnp.exp(-0.5 * gate * gate) * ((2.0 * math.pi) ** -0.5)
     bent = gate * share
@@ -513,7 +514,7 @@
 
 def out_weight(count, inner, pick, own, other, mid, mid_other):
     rows, (width, model) = pick.shape[0], own.shape
-    vmem, hbm = pl.BlockSpec(memory_space=pltpu.VMEM), pl.BlockSpec(memory_space=pltpu.HBM)
+    vmem, hbm = pl.BlockSpec(memory_space=pltpu.VMEM), pl.BlockSpec(memory_space=pl.ANY)
 
     def kernel(pick_ref, own_ref, other_ref, mid_ref, mid_other_ref, *refs):
         outs, held, sems = refs[:count], refs[count : count + 5], refs[count + 5]
@@ -545,10 +546,16 @@
     )(pick, own, other, mid, mid_other)
 
 
-def ring_add_kernel(carried, *refs):
+def ring_add_kernel(count, *refs):
+    outs, scratch, sems = refs[2 * count : 2 * count + 2], refs[2 * count + 2], refs[2 * count + 3]
+    waits = refs[2 * count + 4 :]
+    copies = []
     for side in range(2):
-        block, got, narrow = refs[3 * side : 3 * side + 3]
-        out = refs[6 + side]
+        given = refs[count * side : count * (side + 1)]
+        for wait in waits[count * side : count * (side + 1)]:
+            wait()
+        block, got = given[:2]
+        out = scratch.at[side]
         wide, rows = block.shape[1], got.shape[0]
         total = block[...].astype(F32)
         if rows == block.shape[0]:
@@ -559,20 +566,28 @@
         else:
             out[:rows, :wide] = block[:rows, :]
             out[rows:, :wide] = (total[rows:] + got[...].astype(F32)).astype(BF)
-        if carried:
-            out[:, wide:] = (narrow[...].astype(F32) + got[:, wide:].astype(F32)).astype(BF)
-        else:
-            out[:, wide:] = narrow[...]
-
-
-def ring_add(carried, *arrays):
-    rows, columns = arrays[0].shape[0], arrays[0].shape[1] + arrays[2].shape[1]
-    return staged(
-        functools.partial(ring_add_kernel, carried),
-        list(arrays),
+        if count == 3 and got.shape[1] > wide:
+            out[:, wide:] = (given[2][...].astype(F32) + got[:, wide:].astype(F32)).astype(BF)
+        elif count == 3:
+            out[:, wide:] = given[2][...]
+        copies.append(pltpu.make_async_copy(out, outs[side], sems.at[side]))
+        copies[-1].start()
+    for copy in copies:
+        copy.wait()
+
+
+def ring_add(right, left):
+    rows = right[0].shape[0]
+    columns = right[0].shape[1] + (right[2].shape[1] if len(right) == 3 else 0)
+    return staged(
+        functools.partial(ring_add_kernel, len(right)),
+        [*right, *left],
         [shaped((rows, columns), BF)] * 2,
         "ring_add",
+        [pltpu.VMEM((2, rows, columns), BF), pltpu.SemaphoreType.DMA((2,))],
+        late=2 * len(right),
         cost=work(4 * rows * columns, 12 * rows * columns),
+        far=2,
     )
 
 
@@ -608,7 +623,7 @@
     )(first, blocks, weights)
 
 
-def finish_mlp_kernel(own_ref, right_ref, left_ref, w_ref, gain_ref, in_ref, out_ref, gains_ref):
+def finish_mlp_kernel(own_ref, right_ref, left_ref, w_ref, gain_ref, inverse_ref, in_ref, out_ref, gains_ref):
     units = out_ref.shape[1]
     wide = own_ref.shape[1]
     total = own_ref[...].astype(F32) + right_ref[:, :wide].astype(F32) + left_ref[:, :wide].astype(F32)
@@ -617,15 +632,16 @@
     in_ref[:, 1, :] = total[:, units : 2 * units]
     term = jnp.sum(total[:, : 2 * units] * w_ref[...].astype(F32), axis=1, keepdims=True)
     mine = term.shape[0]
-    gains_ref[0:1] = jnp.broadcast_to(gain_ref[...], (mine, 128)).T[0:1]
-    gains_ref[1:2] = jnp.broadcast_to(term, (mine, 128)).T[0:1]
-
-
-def finish_mlp(units, own, right, left, rows, gain):
+    inverse = inverse_ref[...]
+    gains_ref[0:1] = jnp.broadcast_to(gain_ref[...], (mine, 128)).T[0:1] * inverse[0:1]
+    gains_ref[1:2] = jnp.broadcast_to(term, (mine, 128)).T[0:1] * inverse[1:2]
+
+
+def finish_mlp(units, own, right, left, rows, gain, inverse):
     mine = own.shape[0]
     return staged(
         finish_mlp_kernel,
-        [own, right, left, rows, gain],
+        [own, right, left, rows, gain, inverse],
         [shaped((mine, 2, units), F32), shaped((mine, units), F32), shaped((2, mine), F32)],
         "finish_mlp",
         cost=work(8 * own.size, 14 * own.size),
@@ -764,6 +780,9 @@
 
     packed, attn_input = project(hidden_in, gain_attn[None], cos_one[0], sin_one[0], w_three)
     own = exchange(packed)
+    first = me * mine
+    both_gains = after(jnp.stack([gain_attn, gain_mlp]), packed)
+    gain_inverse = 1.0 / lax.dynamic_slice_in_dim(both_gains, first, mine, 1)
     w_out_other = swap_tp(w_attn_out)
     later_cot = after(cotangent, packed)
     cot_other = swap_core(later_cot)
@@ -796,8 +815,7 @@
         gather_step(2, attended_low)
     rows_w_in = lax.dynamic_slice_in_dim(after(w_in, attended_low), me * mine, mine, 0)
     rows_w_in = rows_w_in.reshape(mine, 2 * units)
-    attn_all = after(attn_all, rows_w_in, grad_activated, right, left)
-    attn_all = attn_all.reshape(tp_size, inner, width)
+    attn_all = after(attn_all, rows_w_in, grad_activated, right, left).reshape(tp_size, inner, width)
     if ringed:
         gather_step(3, attn_all)
     middle, mid, activated_low, part_two, head_terms = middle_part(
@@ -811,9 +829,10 @@
         grad_activated,
         w_pair,
     )
+    if ringed:
+        results = (middle, mid, activated_low, part_two, head_terms)
+        middle, mid, activated_low, part_two, head_terms = after(results, right, left)
     grad_received = exchange_wide(head_terms.reshape(tp_size * heads, HD, width))
-    if ringed:
-        gather_step(4, head_terms)
 
     half = chips // 2
     sizes = [mine] * half + [mine // 2, mine // 2] + [mine] * (half - 1) if ringed else [chips * mine]
@@ -823,48 +842,49 @@
         mlp_rights = parts_mlp[half::-1]
         mlp_lefts = parts_mlp[half + 1 :]
         got_right, got_left = turn(mlp_rights[0], 1), turn(mlp_lefts[0], -1)
-    part_two_other = swap_tp(part_two)
+    part_two_other = swap_tp(after(part_two, mid_other))
     later_two = after(part_two_other, parts_mlp)
     grad_middle, grad_middle_low = middle_back(middle, cotangent, gain_mlp[None], part_two, later_two)
+    grad_received = after(grad_received, parts_mlp, right, left, grad_middle_low)
+    if ringed:
+        gather_step(4, parts_mlp)
+    grad_received = grad_received.reshape(tp_size, heads, HD, width)
+    dq, *grad_kv = attend_back(own, others, grad_received, attended, lse, cos_all, sin_all)
+
+    low_other = swap_core(grad_middle_low)
+    if ringed:
+        grad_kv = after(grad_kv, got_right, got_left, right, low_other)
+    terms = [grad_kv[0]]
+    for step in range(1, 2 * copies):
+        terms.append(shift_keys(grad_kv[step], -step))
     parts_out = out_weight(
         chips if ringed else 1,
         inner,
         pick,
-        grad_middle_low,
-        swap_core(grad_middle_low),
+        after(grad_middle_low, dq),
+        low_other,
         mid,
         mid_other,
     )
-    grad_received = after(grad_received, parts_mlp, parts_out, right, left)
-    grad_received = grad_received.reshape(tp_size, heads, HD, width)
-    dq, *grad_kv = attend_back(own, others, grad_received, attended, lse, cos_all, sin_all)
-
-    if ringed:
-        grad_kv = after(grad_kv, got_right, got_left)
-    terms = [grad_kv[0]]
-    for step in range(1, 2 * copies):
-        terms.append(shift_keys(grad_kv[step], -step))
-    if ringed:
-
-        def ring_step(step, *earlier):
+    if ringed:
+
+        def ring_step(step, narrow, *earlier):
             nonlocal got_right, got_left
-            sent = ring_add(
-                step > 1,
-                mlp_rights[step],
-                after(got_right, *earlier),
-                parts_out[half + 1 - step],
-                mlp_lefts[step],
-                got_left,
-                parts_out[half + step],
-            )
+            rights = [mlp_rights[step], after(got_right, *earlier)]
+            lefts = [mlp_lefts[step], got_left]
+            if narrow:
+                rights.append(parts_out[half - step])
+                lefts.append(parts_out[half + step])
+            sent = ring_add(rights, lefts)
             got_right, got_left = turn(sent[0], 1), turn(sent[1], -1)
             return sent
 
-        sent = ring_step(1, dq)
+        sent = ring_step(1, True, dq)
         terms[0] = after(terms[0], sent)
     grad_own = combine(dq, terms, cos_all, sin_all)
     grad_back = exchange(grad_own)
     if ringed:
+        direct = turn(after(parts_out[half], sent), half)
         steps = [0]
         for step in range(1, half + 1):
             steps.extend([-step, step])
@@ -872,30 +892,28 @@
         ids = jnp.concatenate([ids, core[None]]).astype(jnp.int32)
         keep_qkv, give_qkv = head_weight(chips, ids, grad_own, gathered)
         given_qkv = swap_core(give_qkv)
-        sent = ring_step(2, keep_qkv)
+        sent = ring_step(2, True, keep_qkv)
         part_qkv = (keep_qkv.astype(F32) + given_qkv.astype(F32)).astype(BF)
         blocks_qkv = exchange(after(part_qkv, sent))
-        mlp_part = nn(after(activated_low, sent), w_mlp_out).astype(BF)
-        grad_back = after(grad_back, part_qkv, mlp_part, sent)
+        grad_back = after(grad_back, part_qkv, sent)
     part_one = project_back(grad_back, w_three)
     part_one_other = swap_tp(part_one)
-    first = me * mine
-    if ringed:
-        sent = ring_step(3, part_one_other, blocks_qkv)
-        output = (middle + add_tp(after(mlp_part, sent))).astype(BF)
+    if ringed:
+        mlp_part = nn(after(activated_low, part_one), w_mlp_out).astype(BF)
+        sent = ring_step(3, True, part_one_other, direct, mlp_part)
+        output = (middle + add_tp(mlp_part)).astype(BF)
         part_one_other = after(part_one_other, sent)
         grad_input = input_back(hidden_in, gain_attn[None], part_one, grad_middle, part_one_other)
         grad_w_qkv, gain_one = finish_qkv(
             first.astype(jnp.int32).reshape(1), blocks_qkv, w_three
         )
         wide = mlp_rights[0].shape[1]
-        last = parts_out[1].astype(F32) + got_right[:, wide:].astype(F32)
-        last = turn(last.astype(BF), 1)
         grad_w_in, grad_w_mlp_out, gains = finish_mlp(
-            units, parts_mlp[0], got_right, got_left, rows_w_in, gain_one
+            units, parts_mlp[0], got_right, got_left, rows_w_in, gain_one, gain_inverse
         )
-        grad_out = parts_out[0].astype(F32) + got_left[:, wide:].astype(F32)
-        grad_w_attn_out = (grad_out + last.astype(F32)).T
+        grad_out = parts_out[0].astype(F32) + direct.astype(F32)
+        grad_out = grad_out + got_right[:, wide:].astype(F32) + got_left[:, wide:].astype(F32)
+        grad_w_attn_out = grad_out.T
         grad_w_qkv = grad_w_qkv.transpose(1, 0, 2)
     else:
         output = (middle + add_tp(nn(activated_low, w_mlp_out).astype(BF))).astype(BF)
@@ -914,14 +932,14 @@
         rows_w_qkv = lax.dynamic_slice_in_dim(w_qkv, first, mine, 0)
         gain_one = jnp.sum(rows_w_qkv.astype(F32) * grad_w_qkv, axis=(1, 2))
         gain_two = jnp.sum(rows_w_in.astype(F32) * grad_mlp[:, : 2 * units], axis=1)
-        gains = jnp.stack([gain_one, gain_two])
+        gains = jnp.stack([gain_one, gain_two]) * gain_inverse
 
     gains = gains + swap_tp(gains)
     return (
         output,
         grad_input,
-        gains[0] / lax.dynamic_slice_in_dim(gain_attn, first, mine, 0),
-        gains[1] / lax.dynamic_slice_in_dim(gain_mlp, first, mine, 0),
+        gains[0],
+        gains[1],
         grad_w_qkv,
         grad_w_attn_out,
         grad_w_in,

time: 177 us -> 169 us (0.955)
  waiting for transfers between devices: 30.7 us -> 23.8 us
  starting transfers between devices: 51.3 us -> 54.7 us
  Pallas kernels: 70.1 us -> 67 us
    all_to_all x3, waiting for transfers between devices: 14.8 us -> 8.46 us  [exchange(): return lax.all_to_all(values, 'ctx', 0, 0, axis_index_groups=head_groups)]
    ppermute x16, waiting for transfers between devices: 14.6 us -> 9.58 us  [turn(): return lax.ppermute(values, 'ctx', pairs)]
    ppermute x5, waiting for transfers between devices: 1.21 us -> 5.73 us  [swap_tp(): return lax.ppermute(values, 'tp', [(0, 1), (1, 0)])]
    ppermute x16, starting transfers between devices: 17.9 us -> 21.6 us  [turn(): return lax.ppermute(values, 'ctx', pairs)]
    pallas_call x14, Pallas kernels: 60.3 us -> 57.3 us  [staged(): pl.pallas_call(kernel, in_specs=[pl.BlockSpec(memory_space=pltpu.SMEM)] *...]
    unnamed x54 -> x66, local copies, waits for them, and re-layouts: 7.51 us -> 7.98 us
  transfers between devices with their start and end apart: 32 -> 32, of which waited for: 14 -> 12; matrix products, arithmetic and copies ran while one was open for 7% -> 7% of each run, Pallas kernels for 30% -> 36%
where the time goes in v5:
time: 169 us; the launch traced here: 168 us
  Pallas kernels  67 us (40%)
  starting transfers between devices  54.7 us (32%)
  waiting for transfers between devices  23.8 us (14%)
  local copies, waits for them, and re-layouts  10.9 us (6%)
  other arithmetic  9.39 us (6%)
    pallas_call x14, Pallas kernels, staged(): pl.pallas_call(kernel, in_specs=[pl.BlockSpec(memory_space=pltpu.SMEM)] *...  57.3 us
    ppermute x16, starting transfers between devices, turn(): return lax.ppermute(values, 'ctx', pairs)  21.6 us
    all_to_all x3, starting transfers between devices, exchange(): return lax.all_to_all(values, 'ctx', 0, 0, axis_index_groups=head_groups)  16.4 us
    ppermute x16, waiting for transfers between devices, turn(): return lax.ppermute(values, 'ctx', pairs)  9.58 us
    all_to_all x2, starting transfers between devices, exchange_wide(): lax.all_to_all(values, ('ctx', 'tp'), 0, 0, axis_index_groups=wide_groups)  9.53 us
    all_to_all x3, waiting for transfers between devices, exchange(): return lax.all_to_all(values, 'ctx', 0, 0, axis_index_groups=head_groups)  8.46 us
    unnamed x66, local copies, waits for them, and re-layouts  7.98 us
    ppermute x5, starting transfers between devices, swap_tp(): return lax.ppermute(values, 'tp', [(0, 1), (1, 0)])  6.51 us
  transfers between devices with their start and end apart: 32, of which 12 were waited for; matrix products, arithmetic and copies ran while one was open for 7% of the time, Pallas kernels for 36%

profile of v5, /device:TPU:0, one launch (start us, length us, event | category | flops | bytes accessed | tf_op | source)
XLA Modules:
  0.0 167.7 jit_solution(6522120521439617712)
XLA Ops:
  1.4 4.1 %project.1 = (bf16[8,192,128]{2,1,0:T(8,128)(2,1)}, bf16[128,1024]{1,0:T(8,128)(2,1)}) custom-call(bf16[128,1024]{1,0:T(8,128)(2,1)} %refs_0_.2, f32[1,1024]{1,0:T(1,128)} %bitcast.34, f32[32,128]{1,0:T(8,128)} %get-tuple-element.177.c_ref, f32[32,128]{1,0:T(8,128)} %get-tuple-element.176.s_ref, bf16[3,1024,512]{2,1,0:T(8,128)(2,1)} %bitcast.22), custom_call_target="tpu_custom_call" | custom-call | flops 402653184 | bytes 3145728 | tf_op jit(solution)/shard_map/project/pallas_call | solution.py:304
  5.5 7.3 %all-to-all-start = ((bf16[8,192,128]{2,1,0:T(8,128)(2,1)}), bf16[8,192,128]{2,1,0:T(8,128)(2,1)S(1)}, u32[]{:S(2)}, u32[]{:S(2)}) async-start(bf16[8,192,128]{2,1,0:T(8,128)(2,1)} %get-tuple-element.90), calls=%async_computation | async-start | bytes 786432 | tf_op jit(solution)/shard_map/all_to_all | solution.py:712
  12.8 1.6 collective-permute-start.5
  14.6 1.2 fusion.refs_0_.pick_ref
  15.8 1.2 multiply_sine_fusion
  17.1 7.4 %all-to-all-done.refs_0_ = bf16[8,192,128]{2,1,0:T(8,128)(2,1)S(1)} async-done(((bf16[8,192,128]{2,1,0:T(8,128)(2,1)}), bf16[8,192,128]{2,1,0:T(8,128)(2,1)S(1)}, u32[]{:S(2)}, u32[]{:S(2)}) %all-to-all-start) | async-done | bytes 393248 | tf_op jit(solution)/shard_map/all_to_all | solution.py:712
  25.4 1.1 collective-permute-start.2
  27.3 6.0 %attend.1 = (f32[8,64,128]{2,1,0:T(8,128)}, bf16[2,8,64,128]{3,2,1,0:T(8,128)(2,1)}, f32[8,1,128]{2,1,0:T(1,128)}) custom-call(bf16[8,192,128]{2,1,0:T(8,128)(2,1)} %copy-done.14, bf16[8,192,128]{2,1,0:T(8,128)(2,1)} %copy-done.29), custom_call_target="tpu_custom_call" | custom-call | flops 536870912 | bytes 786432 | tf_op jit(solution)/shard_map/attend/pallas_call | solution.py:50
  34.2 4.3 %all-to-all-start.1 = ((bf16[16,64,128]{2,1,0:T(8,128)(2,1)}), bf16[16,64,128]{2,1,0:T(8,128)(2,1)S(1)}, u32[]{:S(2)}, u32[]{:S(2)}) async-start(bf16[16,64,128]{2,1,0:T(8,128)(2,1)} %bitcast.30), calls=%async_computation.1 | async-start | bytes 524288 | tf_op jit(solution)/shard_map/all_to_all | solution.py:709
  38.5 1.9 %collective-permute-start.3 = (bf16[128,1024]{1,0:T(8,128)(2,1)}, bf16[128,1024]{1,0:T(8,128)(2,1)S(1)}, u32[]{:S(2)}, u32[]{:S(2)}) collective-permute-start(bf16[128,1024]{1,0:T(8,128)(2,1)} %collective-permute-done.1.refs_3_), channel_id=1, source_target_pairs={{0,8},{2,10},{4,0},{6,2},{8,16},{10,18},{12,4},{14,6},{16,24},{18,... | collective-permute-start | bytes 786440 | tf_op jit(solution)/shard_map/ppermute | solution.py:749
  40.6 1.3 constant_dynamic-slice_fusion
  41.9 1.0 copy.18.refs_3_
  42.9 3.8 %unit_back.1.refs_7_ = f32[128,1312]{1,0:T(8,128)} custom-call(bf16[128,1024]{1,0:T(8,128)(2,1)} %refs_1_.5, bf16[1312,1024]{1,0:T(8,128)(2,1)} %refs_1_.3), custom_call_target="tpu_custom_call" | custom-call | flops 343932928 | bytes 2686976 | tf_op jit(solution)/shard_map/unit_back/pallas_call | solution.py:50
  46.7 2.2 %collective-permute-done.3.refs_5_ = bf16[128,1024]{1,0:T(8,128)(2,1)S(1)} collective-permute-done((bf16[128,1024]{1,0:T(8,128)(2,1)}, bf16[128,1024]{1,0:T(8,128)(2,1)S(1)}, u32[]{:S(2)}, u32[]{:S(2)}) %collective-permute-start.3) | collective-permute-done | bytes 262176 | tf_op jit(solution)/shard_map/ppermute | solution.py:749
  48.8 1.8 %collective-permute-done.4.refs_6_ = bf16[128,1024]{1,0:T(8,128)(2,1)S(1)} collective-permute-done((bf16[128,1024]{1,0:T(8,128)(2,1)}, bf16[128,1024]{1,0:T(8,128)(2,1)S(1)}, u32[]{:S(2)}, u32[]{:S(2)}) %collective-permute-start.4) | collective-permute-done | bytes 262176 | tf_op jit(solution)/shard_map/ppermute | solution.py:749
  50.6 2.5 %collective-permute-start.6 = (bf16[128,1024]{1,0:T(8,128)(2,1)S(1)}, bf16[128,1024]{1,0:T(8,128)(2,1)S(1)}, u32[]{:S(2)}, u32[]{:S(2)}) collective-permute-start(bf16[128,1024]{1,0:T(8,128)(2,1)S(1)} %collective-permute-done.3.refs_5_), channel_id=1, source_target_pairs={{0,8},{2,10},{4,0},{6,2},{8,16},{10,18},{12,4},{14,6},{16,24},{18,... | collective-permute-start | bytes 786440 | tf_op jit(solution)/shard_map/ppermute | solution.py:749
  54.1 8.2 %middle_part.1 = (f32[128,1024]{1,0:T(8,128)}, bf16[128,5504]{1,0:T(8,128)(2,1)}, bf16[128,1312]{1,0:T(8,128)(2,1)}, bf16[128,1024]{1,0:T(8,128)(2,1)}, bf16[2,8,64,128]{3,2,1,0:T(8,128)(2,1)}) custom-call(s32[1]{0:T(128)} %bitcast.refs_0_, bf16[2,512,128]{2,1,0:T(8,128)(2,1)} %bitcast.27, bf16[128,1024]{1,0:T(8,128)(2,1)} %refs_0_.2, ...), custom_call_target="tpu_custom_call" | custom-call | flops 1912602624 | bytes 5373952 | tf_op jit(solution)/shard_map/middle_part/pallas_call | solution.py:50
  62.9 5.2 %all-to-all-start.2 = ((bf16[16,64,128]{2,1,0:T(8,128)(2,1)}), bf16[16,64,128]{2,1,0:T(8,128)(2,1)S(1)}, u32[]{:S(2)}, u32[]{:S(2)}) async-start(bf16[16,64,128]{2,1,0:T(8,128)(2,1)} %bitcast.28), calls=%async_computation.2 | async-start | bytes 524288 | tf_op jit(solution)/shard_map/all_to_all | solution.py:709
  68.2 2.0 %collective-permute-start.10 = (bf16[128,1024]{1,0:T(8,128)(2,1)}, bf16[128,1024]{1,0:T(8,128)(2,1)S(1)}, u32[]{:S(2)}, u32[]{:S(2)}) collective-permute-start(bf16[128,1024]{1,0:T(8,128)(2,1)} %get-tuple-element.127.refs_3_), channel_id=1, source_target_pairs={{0,1},{1,0},{2,3},{3,2},{4,5},{5,4},{6,7},{7,6},{8,9},{9,8},{10,11... | collective-permute-start | bytes 786440 | tf_op jit(solution)/shard_map/ppermute | solution.py:727
  70.9 5.8 %mlp_weight.1 = (bf16[64,3968]{1,0:T(8,128)(2,1)}, bf16[64,3968]{1,0:T(8,128)(2,1)}, bf16[64,3968]{1,0:T(8,128)(2,1)}, bf16[64,3968]{1,0:T(8,128)(2,1)}, bf16[32...) custom-call(bf16[512,1024]{1,0:T(8,128)(2,1)} %fusion.refs_0_.pick_r, ...), custom_call_target="tpu_custom_call" | custom-call | flops 1442840576 | bytes 9699328 | tf_op jit(solution)/shard_map/mlp_weight/pallas_call | solution.py:50
  76.7 1.5 collective-permute-start.13
  79.8 2.7 %middle_back.1 = (f32[128,1024]{1,0:T(8,128)}, bf16[128,1024]{1,0:T(8,128)(2,1)}) custom-call(f32[128,1024]{1,0:T(8,128)} %get-tuple-element.112.refs_0_, bf16[128,1024]{1,0:T(8,128)(2,1)} %refs_1_.5, f32[1,1024]{1,0:T(1,128)} %bitcast.32, bf16[128,1024]{1,0:T(8,128)(2,1)} %get-tuple-element.127.refs_3_, bf16[128,1024]{1,0:T(8,128)(2,1)} %copy-done.17), custom_call_target="tpu_custom_call" | custom-call | flops 2621440 | bytes 2097152 | tf_op jit(solution)/shard_map/middle_back/pallas_call | solution.py:50
  82.6 1.5 collective-permute-start.11
  85.3 8.0 %attend_back.1 = (bf16[8,64,128]{2,1,0:T(8,128)(2,1)}, f32[8,128,128]{2,1,0:T(8,128)}, f32[8,128,128]{2,1,0:T(8,128)}) custom-call(bf16[8,192,128]{2,1,0:T(8,128)(2,1)} %copy-done.14, bf16[8,192,128]{2,1,0:T(8,128)(2,1)} %copy-done.29, bf16[2,8,64,128]{3,2,1,0:T(8,128)(2,1)} %bitcast.29, f32[8,64,128]{2,1,0:T(8,128)} %get-tuple-element.131.refs_3_, ...), custom_call_target="tpu_custom_call" | custom-call | flops 1342177280 | bytes 1572864 | tf_op jit(solution)/shard_map/attend_back/pallas_call | solution.py:50
  94.2 3.0 %out_weight.1 = (bf16[64,512]{1,0:T(8,128)(2,1)}, bf16[64,512]{1,0:T(8,128)(2,1)}, bf16[64,512]{1,0:T(8,128)(2,1)}, bf16[64,512]{1,0:T(8,128)(2,1)}, bf16[64,512...) custom-call(bf16[512,1024]{1,0:T(8,128)(2,1)} %fusion.refs_0_.pick_ref, ...), custom_call_target="tpu_custom_call" | custom-call | flops 268435456 | bytes 1048576 | tf_op jit(solution)/shard_map/out_weight/pallas_call | solution.py:530
  97.3 2.4 %ring_add.3 = (bf16[64,4480]{1,0:T(8,128)(2,1)}, bf16[64,4480]{1,0:T(8,128)(2,1)}) custom-call(bf16[64,3968]{1,0:T(8,128)(2,1)} %get-tuple-element.120.refs_0_, bf16[32,3968]{1,0:T(8,128)(2,1)} %copy-done.24, bf16[64,512]{1,0:T(8,128)(2,1)} %get-tuple-element.140.refs_2_, bf16[64,3968]{1,0:T(8,128)(2,1)} %get-tuple-element.123.refs_3_, ...), custom_call_target="tpu_custom_call" | custom-call | flops 1146880 | bytes 3440640 | tf_op jit(solution)/shard_map/ring_add/pallas_call | solution.py:50
  99.7 1.5 collective-permute-start.17
  102.5 2.2 %combine.1.refs_1_ = bf16[8,192,128]{2,1,0:T(8,128)(2,1)} custom-call(bf16[8,64,128]{2,1,0:T(8,128)(2,1)} %get-tuple-element.133.refs_0_, f32[8,128,128]{2,1,0:T(8,128)} %get-tuple-element.144.refs_1_, f32[8,128,128]{2,1,0:T(8,128)} %copy-done.13, f32[8,32,128]{2,1,0:T(8,128)} %get-tuple-element.173.refs_5_.refs_3_, ...), custom_call_target="tpu_custom_call" | custom-call | flops 65536 | bytes 1310720 | tf_op jit(solution)/shard_map/combine/pallas_call | solution.py:50
  104.7 5.5 %all-to-all-start.3 = ((bf16[8,192,128]{2,1,0:T(8,128)(2,1)}), bf16[8,192,128]{2,1,0:T(8,128)(2,1)S(1)}, u32[]{:S(2)}, u32[]{:S(2)}) async-start(bf16[8,192,128]{2,1,0:T(8,128)(2,1)} %combine.1.refs_1_), calls=%async_computation.3 | async-start | bytes 786432 | tf_op jit(solution)/shard_map/all_to_all | solution.py:712
  110.8 3.9 %head_weight.1 = (bf16[8,64,192]{2,1,0:T(8,128)(2,1)}, bf16[8,64,192]{2,1,0:T(8,128)(2,1)}) custom-call(s32[9]{0:T(128)} %pad_add_fusion.refs_0_, bf16[8,192,128]{2,1,0:T(8,128)(2,1)} %combine.1.refs_1_, bf16[128,1024]{1,0:T(8,128)(2,1)} %get-tuple-element.98.refs_2_, bf16[128,1024]{1,0:T(8,128)(2,1)} %collective-permute-done.1.refs_3_, ...), custom_call_target="tpu_custom_call" | custom-call | flops 402653184 | bytes 2097152 | tf_op jit(solution)/shard_map/head_weight/pallas_call | solution.py:50
  114.8 4.8 %collective-permute-start.22 = (bf16[64,512]{1,0:T(8,128)(2,1)S(1)}, bf16[64,512]{1,0:T(8,128)(2,1)S(1)}, u32[]{:S(2)}, u32[]{:S(2)}) collective-permute-start(bf16[64,512]{1,0:T(8,128)(2,1)S(1)} %copy-done.31), channel_id=1, source_target_pairs={{0,28},{2,30},{4,24},{6,26},{8,20},{10,22},{12,16},{14,18},{16,12}... | collective-permute-start | bytes 196616 | tf_op jit(solution)/shard_map/ppermute | solution.py:749
  120.6 2.6 %ring_add.4 = (bf16[64,4480]{1,0:T(8,128)(2,1)}, bf16[64,4480]{1,0:T(8,128)(2,1)}) custom-call(bf16[64,3968]{1,0:T(8,128)(2,1)} %get-tuple-element.119.refs_0_, bf16[64,4480]{1,0:T(8,128)(2,1)} %copy-done.11, bf16[64,512]{1,0:T(8,128)(2,1)} %get-tuple-element.149.refs_2_, bf16[64,3968]{1,0:T(8,128)(2,1)} %get-tuple-element.124.refs_3_, ...), custom_call_target="tpu_custom_call" | custom-call | flops 1146880 | bytes 3440640 | tf_op jit(solution)/shard_map/ring_add/pallas_call | solution.py:50
  123.3 2.0 %collective-permute-start.23 = (bf16[64,4480]{1,0:T(8,128)(2,1)}, bf16[64,4480]{1,0:T(8,128)(2,1)}, u32[]{:S(2)}, u32[]{:S(2)}) collective-permute-start(bf16[64,4480]{1,0:T(8,128)(2,1)} %get-tuple-element.152), channel_id=1, source_target_pairs={{0,4},{2,6},{4,12},{6,14},{8,0},{10,2},{12,20},{14,22},{16,8},{18,... | collective-permute-start | bytes 1720328 | tf_op jit(solution)/shard_map/ppermute | solution.py:749
  125.3 1.7 %add_convert_fusion.1 = bf16[8,64,192]{2,1,0:T(8,128)(2,1)} fusion(bf16[8,64,192]{2,1,0:T(8,128)(2,1)S(1)} %collective-permute-done.16, bf16[8,64,192]{2,1,0:T(8,128)(2,1)} %get-tuple-element.146), kind=kLoop, calls=%fused_computation.4 | loop fusion | flops 393216 | bytes 589824 | tf_op jit(solution)/shard_map/convert_element_type | solution.py:896
  127.0 1.0 all-to-all-done.3.refs_0_
  128.0 3.6 %all-to-all-start.4 = ((bf16[8,64,192]{2,1,0:T(8,128)(2,1)}), bf16[8,64,192]{2,1,0:T(8,128)(2,1)S(1)}, u32[]{:S(2)}, u32[]{:S(2)}) async-start(bf16[8,64,192]{2,1,0:T(8,128)(2,1)} %add_convert_fusion.1), calls=%async_computation.4 | async-start | bytes 524288 | tf_op jit(solution)/shard_map/all_to_all | solution.py:712
  131.7 3.9 %project_back.1.refs_2_ = bf16[128,1024]{1,0:T(8,128)(2,1)} custom-call(bf16[8,192,128]{2,1,0:T(8,128)(2,1)} %copy-done.3, bf16[3,1024,512]{2,1,0:T(8,128)(2,1)} %bitcast.23), custom_call_target="tpu_custom_call" | custom-call | flops 402653184 | bytes 3145728 | tf_op jit(solution)/shard_map/project_back/pallas_call | solution.py:50
  135.7 1.1 collective-permute-start.20
  137.4 1.9 %collective-permute-done.21.refs_1_ = bf16[64,4480]{1,0:T(8,128)(2,1)} collective-permute-done((bf16[64,4480]{1,0:T(8,128)(2,1)}, bf16[64,4480]{1,0:T(8,128)(2,1)}, u32[]{:S(2)}, u32[]{:S(2)}) %collective-permute-start.21) | collective-permute-done | bytes 573472 | tf_op jit(solution)/shard_map/ppermute | solution.py:749
  139.3 3.5 %collective-permute-done.20.refs_4_ = bf16[128,1024]{1,0:T(8,128)(2,1)} collective-permute-done((bf16[128,1024]{1,0:T(8,128)(2,1)}, bf16[128,1024]{1,0:T(8,128)(2,1)}, u32[]{:S(2)}, u32[]{:S(2)}) %collective-permute-start.20) | collective-permute-done | bytes 262176 | tf_op jit(solution)/shard_map/ppermute | solution.py:727
  142.8 2.6 %ring_add.5 = (bf16[64,4480]{1,0:T(8,128)(2,1)}, bf16[64,4480]{1,0:T(8,128)(2,1)}) custom-call(bf16[64,3968]{1,0:T(8,128)(2,1)} %get-tuple-element.118.refs_0_, bf16[64,4480]{1,0:T(8,128)(2,1)} %collective-permute-done.21.refs_1_, bf16[64,512]{1,0:T(8,128)(2,1)} %get-tuple-element.159.refs_2_, bf16[64,3968]{1,0:T(8,128)(2,1)} %get-tuple-element.125.refs_3_, ...), custom_call_target="tpu_custom_call" | custom-call | flops 1146880 | bytes 3440640 | tf_op jit(solution)/shard_map/ring_add/pallas_call | solution.py:50
  145.4 2.4 %collective-permute-start.24 = (bf16[64,4480]{1,0:T(8,128)(2,1)}, bf16[64,4480]{1,0:T(8,128)(2,1)S(1)}, u32[]{:S(2)}, u32[]{:S(2)}) collective-permute-start(bf16[64,4480]{1,0:T(8,128)(2,1)} %get-tuple-element.161), channel_id=1, source_target_pairs={{0,8},{2,10},{4,0},{6,2},{8,16},{10,18},{12,4},{14,6},{16,24},{18,... | collective-permute-start | bytes 1720328 | tf_op jit(solution)/shard_map/ppermute | solution.py:749
  150.1 2.6 %finish_qkv.1 = (f32[3,64,512]{2,1,0:T(8,128)}, f32[64,1]{1,0:T(8,128)}) custom-call(s32[1]{0:T(128)} %bitcast.11.first_ref, bf16[8,64,192]{2,1,0:T(8,128)(2,1)} %copy-done.5, bf16[3,1024,512]{2,1,0:T(8,128)(2,1)} %bitcast.24), custom_call_target="tpu_custom_call" | custom-call | flops 196608 | bytes 983040 | tf_op jit(solution)/shard_map/finish_qkv/pallas_call | solution.py:614
  152.8 2.6 %input_back.1 = f32[128,1024]{1,0:T(8,128)} custom-call(bf16[128,1024]{1,0:T(8,128)(2,1)} %refs_0_.2, f32[1,1024]{1,0:T(1,128)} %bitcast.35, bf16[128,1024]{1,0:T(8,128)(2,1)} %project_back.1.refs_2_, f32[128,1024]{1,0:T(8,128)} %get-tuple-element.155.refs_3_, bf16[128,1024]{1,0:T(8,128)(2,1)} %collective-permute-done.20.refs_4_), custom_call_target="tpu_custom_call" | custom-call | flops 2621440 | bytes 1835008 | tf_op jit(solution)/shard_map/input_back/pallas_call | solution.py:50
  156.2 2.0 %collective-permute-done.24.refs_1_ = bf16[64,4480]{1,0:T(8,128)(2,1)S(1)} collective-permute-done((bf16[64,4480]{1,0:T(8,128)(2,1)}, bf16[64,4480]{1,0:T(8,128)(2,1)S(1)}, u32[]{:S(2)}, u32[]{:S(2)}) %collective-permute-start.24) | collective-permute-done | bytes 573472 | tf_op jit(solution)/shard_map/ppermute | solution.py:749
  159.8 2.8 %finish_mlp.1 = (f32[64,2,1312]{2,1,0:T(2,128)}, f32[64,1312]{1,0:T(8,128)}, f32[2,64]{1,0:T(2,128)}) custom-call(bf16[64,3968]{1,0:T(8,128)(2,1)} %get-tuple-element.117.refs_0_, bf16[64,4480]{1,0:T(8,128)(2,1)} %copy-done.9, bf16[64,4480]{1,0:T(8,128)(2,1)} %copy-done.10, bf16[64,2624]{1,0:T(8,128)(2,1)} %copy.18.refs_3_, ...), custom_call_target="tpu_custom_call" | custom-call | flops 2031616 | bytes 3555328 | tf_op jit(solution)/shard_map/finish_mlp/pallas_call | solution.py:50
  163.5 1.6 add_bitcast_fusion
  165.1 1.4 collective-permute-done.26
  (122 shorter events, 20.2 us)
Async XLA Ops:
  0.6 12.2 %copy-start.7 = (bf16[512,1024]{1,0:T(8,128)(2,1)S(1)}, bf16[512,1024]{1,0:T(8,128)(2,1)}, u32[]{:S(2)}) copy-start(bf16[512,1024]{1,0:T(8,128)(2,1)} %refs_5_.1) | copy-start | bytes 3145732
  5.5 19.0 %all-to-all-start = ((bf16[8,192,128]{2,1,0:T(8,128)(2,1)}), bf16[8,192,128]{2,1,0:T(8,128)(2,1)S(1)}, u32[]{:S(2)}, u32[]{:S(2)}) async-start(bf16[8,192,128]{2,1,0:T(8,128)(2,1)} %get-tuple-element.90), calls=%async_computation | async-start | bytes 786432 | tf_op jit(solution)/shard_map/all_to_all | solution.py:712
  12.8 40.4 %collective-permute-start.5 = (bf16[512,1024]{1,0:T(8,128)(2,1)S(1)}, bf16[512,1024]{1,0:T(8,128)(2,1)S(1)}, u32[]{:S(2)}, u32[]{:S(2)}) collective-permute-start(bf16[512,1024]{1,0:T(8,128)(2,1)S(1)} %copy-done.7), channel_id=1, source_target_pairs={{0,1},{1,0},{2,3},{3,2},{4,5},{5,4},{6,7},{7,6},{8,9},{9,8},{10,11... | collective-permute-start | bytes 3145736 | tf_op jit(solution)/shard_map/ppermute | solution.py:727
  24.5 2.0 %collective-permute-start = (bf16[8,192,128]{2,1,0:T(8,128)(2,1)S(1)}, bf16[8,192,128]{2,1,0:T(8,128)(2,1)S(1)}, u32[]{:S(2)}, u32[]{:S(2)}) collective-permute-start(bf16[8,192,128]{2,1,0:T(8,128)(2,1)S(1)} %all-to-all-done.refs_0_), channel_id=1, source_target_pairs={{0,2},{2,0},{4,6},{6,4},{8,10},{10,8},{12,14},{14,12},{16,18},{18,... | collective-permute-start | bytes 1179656 | tf_op jit(solution)/shard_map/ppermute | solution.py:724
  24.5 9.0 %collective-permute-start.1 = (bf16[128,1024]{1,0:T(8,128)(2,1)}, bf16[128,1024]{1,0:T(8,128)(2,1)}, u32[]{:S(2)}, u32[]{:S(2)}) collective-permute-start(bf16[128,1024]{1,0:T(8,128)(2,1)} %get-tuple-element.98.refs_2_), channel_id=1, source_target_pairs={{0,8},{2,10},{4,0},{6,2},{8,16},{10,18},{12,4},{14,6},{16,24},{18,... | collective-permute-start | bytes 786440 | tf_op jit(solution)/shard_map/ppermute | solution.py:749
  25.4 8.8 %collective-permute-start.2 = (bf16[128,1024]{1,0:T(8,128)(2,1)}, bf16[128,1024]{1,0:T(8,128)(2,1)}, u32[]{:S(2)}, u32[]{:S(2)}) collective-permute-start(bf16[128,1024]{1,0:T(8,128)(2,1)} %get-tuple-element.98.refs_2_), channel_id=1, source_target_pairs={{0,4},{2,6},{4,12},{6,14},{8,0},{10,2},{12,20},{14,22},{16,8},{18,... | collective-permute-start | bytes 786440 | tf_op jit(solution)/shard_map/ppermute | solution.py:749
  34.2 16.5 %all-to-all-start.1 = ((bf16[16,64,128]{2,1,0:T(8,128)(2,1)}), bf16[16,64,128]{2,1,0:T(8,128)(2,1)S(1)}, u32[]{:S(2)}, u32[]{:S(2)}) async-start(bf16[16,64,128]{2,1,0:T(8,128)(2,1)} %bitcast.30), calls=%async_computation.1 | async-start | bytes 524288 | tf_op jit(solution)/shard_map/all_to_all | solution.py:709
  38.5 10.3 %collective-permute-start.3 = (bf16[128,1024]{1,0:T(8,128)(2,1)}, bf16[128,1024]{1,0:T(8,128)(2,1)S(1)}, u32[]{:S(2)}, u32[]{:S(2)}) collective-permute-start(bf16[128,1024]{1,0:T(8,128)(2,1)} %collective-permute-done.1.refs_3_), channel_id=1, source_target_pairs={{0,8},{2,10},{4,0},{6,2},{8,16},{10,18},{12,4},{14,6},{16,24},{18,... | collective-permute-start | bytes 786440 | tf_op jit(solution)/shard_map/ppermute | solution.py:749
  40.4 10.2 %collective-permute-start.4 = (bf16[128,1024]{1,0:T(8,128)(2,1)}, bf16[128,1024]{1,0:T(8,128)(2,1)S(1)}, u32[]{:S(2)}, u32[]{:S(2)}) collective-permute-start(bf16[128,1024]{1,0:T(8,128)(2,1)} %collective-permute-done.2.refs_4_), channel_id=1, source_target_pairs={{0,4},{2,6},{4,12},{6,14},{8,0},{10,2},{12,20},{14,22},{16,8},{18,... | collective-permute-start | bytes 786440 | tf_op jit(solution)/shard_map/ppermute | solution.py:749
  48.8 33.7 %copy-start.19 = (bf16[128,1024]{1,0:T(8,128)(2,1)}, bf16[128,1024]{1,0:T(8,128)(2,1)S(1)}, u32[]{:S(2)}) copy-start(bf16[128,1024]{1,0:T(8,128)(2,1)S(1)} %collective-permute-done.3.refs_5_) | copy-start | bytes 786436
  50.6 31.8 %copy-start.20 = (bf16[128,1024]{1,0:T(8,128)(2,1)}, bf16[128,1024]{1,0:T(8,128)(2,1)S(1)}, u32[]{:S(2)}) copy-start(bf16[128,1024]{1,0:T(8,128)(2,1)S(1)} %collective-permute-done.4.refs_6_) | copy-start | bytes 786436
  50.6 11.7 %collective-permute-start.6 = (bf16[128,1024]{1,0:T(8,128)(2,1)S(1)}, bf16[128,1024]{1,0:T(8,128)(2,1)S(1)}, u32[]{:S(2)}, u32[]{:S(2)}) collective-permute-start(bf16[128,1024]{1,0:T(8,128)(2,1)S(1)} %collective-permute-done.3.refs_5_), channel_id=1, source_target_pairs={{0,8},{2,10},{4,0},{6,2},{8,16},{10,18},{12,4},{14,6},{16,24},{18,... | collective-permute-start | bytes 786440 | tf_op jit(solution)/shard_map/ppermute | solution.py:749
  53.1 9.2 %collective-permute-start.7 = (bf16[128,1024]{1,0:T(8,128)(2,1)S(1)}, bf16[128,1024]{1,0:T(8,128)(2,1)S(1)}, u32[]{:S(2)}, u32[]{:S(2)}) collective-permute-start(bf16[128,1024]{1,0:T(8,128)(2,1)S(1)} %collective-permute-done.4.refs_6_), channel_id=1, source_target_pairs={{0,4},{2,6},{4,12},{6,14},{8,0},{10,2},{12,20},{14,22},{16,8},{18,... | collective-permute-start | bytes 786440 | tf_op jit(solution)/shard_map/ppermute | solution.py:749
  54.1 8.3 %copy-start.1 = (bf16[128,1024]{1,0:T(8,128)(2,1)S(1)}, bf16[128,1024]{1,0:T(8,128)(2,1)}, u32[]{:S(2)}) copy-start(bf16[128,1024]{1,0:T(8,128)(2,1)} %refs_1_.5) | copy-start | bytes 786436
  62.3 14.4 %copy-start.21 = (bf16[128,1024]{1,0:T(8,128)(2,1)}, bf16[128,1024]{1,0:T(8,128)(2,1)S(1)}, u32[]{:S(2)}) copy-start(bf16[128,1024]{1,0:T(8,128)(2,1)S(1)} %collective-permute-done.6.refs_7_) | copy-start | bytes 786436
  62.3 14.4 %copy-start.22 = (bf16[128,1024]{1,0:T(8,128)(2,1)}, bf16[128,1024]{1,0:T(8,128)(2,1)S(1)}, u32[]{:S(2)}) copy-start(bf16[128,1024]{1,0:T(8,128)(2,1)S(1)} %collective-permute-done.7.refs_8_) | copy-start | bytes 786436
  62.3 5.8 %collective-permute-start.9 = (bf16[128,5504]{1,0:T(8,128)(2,1)}, bf16[128,5504]{1,0:T(8,128)(2,1)S(1)}, u32[]{:S(2)}, u32[]{:S(2)}) collective-permute-start(bf16[128,5504]{1,0:T(8,128)(2,1)} %get-tuple-element.116.refs_3_.mid_ref), channel_id=1, source_target_pairs={{0,2},{2,0},{4,6},{6,4},{8,10},{10,8},{12,14},{14,12},{16,18},{18,... | collective-permute-start | bytes 4227080 | tf_op jit(solution)/shard_map/ppermute | solution.py:715
  62.4 7.7 %collective-permute-start.8 = (bf16[128,1024]{1,0:T(8,128)(2,1)S(1)}, bf16[128,1024]{1,0:T(8,128)(2,1)S(1)}, u32[]{:S(2)}, u32[]{:S(2)}) collective-permute-start(bf16[128,1024]{1,0:T(8,128)(2,1)S(1)} %copy-done.1), channel_id=1, source_target_pairs={{0,2},{2,0},{4,6},{6,4},{8,10},{10,8},{12,14},{14,12},{16,18},{18,... | collective-permute-start | bytes 786440 | tf_op jit(solution)/shard_map/ppermute | solution.py:715
  62.9 21.7 %all-to-all-start.2 = ((bf16[16,64,128]{2,1,0:T(8,128)(2,1)}), bf16[16,64,128]{2,1,0:T(8,128)(2,1)S(1)}, u32[]{:S(2)}, u32[]{:S(2)}) async-start(bf16[16,64,128]{2,1,0:T(8,128)(2,1)} %bitcast.28), calls=%async_computation.2 | async-start | bytes 524288 | tf_op jit(solution)/shard_map/all_to_all | solution.py:709
  68.2 10.9 %collective-permute-start.10 = (bf16[128,1024]{1,0:T(8,128)(2,1)}, bf16[128,1024]{1,0:T(8,128)(2,1)S(1)}, u32[]{:S(2)}, u32[]{:S(2)}) collective-permute-start(bf16[128,1024]{1,0:T(8,128)(2,1)} %get-tuple-element.127.refs_3_), channel_id=1, source_target_pairs={{0,1},{1,0},{2,3},{3,2},{4,5},{5,4},{6,7},{7,6},{8,9},{9,8},{10,11... | collective-permute-start | bytes 786440 | tf_op jit(solution)/shard_map/ppermute | solution.py:727
  76.7 16.7 %collective-permute-start.13 = (bf16[128,1024]{1,0:T(8,128)(2,1)S(1)}, bf16[128,1024]{1,0:T(8,128)(2,1)S(1)}, u32[]{:S(2)}, u32[]{:S(2)}) collective-permute-start(bf16[128,1024]{1,0:T(8,128)(2,1)S(1)} %collective-permute-done.6.refs_7_), channel_id=1, source_target_pairs={{0,8},{2,10},{4,0},{6,2},{8,16},{10,18},{12,4},{14,6},{16,24},{18,... | collective-permute-start | bytes 786440 | tf_op jit(solution)/shard_map/ppermute | solution.py:749
  82.5 10.9 %collective-permute-start.14 = (bf16[128,1024]{1,0:T(8,128)(2,1)}, bf16[128,1024]{1,0:T(8,128)(2,1)S(1)}, u32[]{:S(2)}, u32[]{:S(2)}) collective-permute-start(bf16[128,1024]{1,0:T(8,128)(2,1)} %get-tuple-element.139.own_ref), channel_id=1, source_target_pairs={{0,2},{2,0},{4,6},{6,4},{8,10},{10,8},{12,14},{14,12},{16,18},{18,... | collective-permute-start | bytes 786440 | tf_op jit(solution)/shard_map/ppermute | solution.py:715
  82.6 10.8 %collective-permute-start.11 = (bf16[32,3968]{1,0:T(8,128)(2,1)}, bf16[32,3968]{1,0:T(8,128)(2,1)S(1)}, u32[]{:S(2)}, u32[]{:S(2)}) collective-permute-start(bf16[32,3968]{1,0:T(8,128)(2,1)} %get-tuple-element.121), channel_id=1, source_target_pairs={{0,8},{2,10},{4,0},{6,2},{8,16},{10,18},{12,4},{14,6},{16,24},{18,... | collective-permute-start | bytes 761864 | tf_op jit(solution)/shard_map/ppermute | solution.py:749
  84.1 9.3 %collective-permute-start.12 = (bf16[32,3968]{1,0:T(8,128)(2,1)}, bf16[32,3968]{1,0:T(8,128)(2,1)S(1)}, u32[]{:S(2)}, u32[]{:S(2)}) collective-permute-start(bf16[32,3968]{1,0:T(8,128)(2,1)} %get-tuple-element.122), channel_id=1, source_target_pairs={{0,4},{2,6},{4,12},{6,14},{8,0},{10,2},{12,20},{14,22},{16,8},{18,... | collective-permute-start | bytes 761864 | tf_op jit(solution)/shard_map/ppermute | solution.py:749
  93.4 3.9 %copy-start.24 = (bf16[32,3968]{1,0:T(8,128)(2,1)}, bf16[32,3968]{1,0:T(8,128)(2,1)S(1)}, u32[]{:S(2)}) copy-start(bf16[32,3968]{1,0:T(8,128)(2,1)S(1)} %collective-permute-done.11.refs_1_) | copy-start | bytes 761860
  93.4 17.4 %copy-start.23 = (bf16[128,1024]{1,0:T(8,128)(2,1)}, bf16[128,1024]{1,0:T(8,128)(2,1)S(1)}, u32[]{:S(2)}) copy-start(bf16[128,1024]{1,0:T(8,128)(2,1)S(1)} %collective-permute-done.13.refs_9_) | copy-start | bytes 786436
  93.5 8.3 %collective-permute-start.15 = (f32[8,128,128]{2,1,0:T(8,128)}, f32[8,128,128]{2,1,0:T(8,128)S(1)}, u32[]{:S(2)}, u32[]{:S(2)}) collective-permute-start(f32[8,128,128]{2,1,0:T(8,128)} %get-tuple-element.145), channel_id=1, source_target_pairs={{0,2},{2,0},{4,6},{6,4},{8,10},{10,8},{12,14},{14,12},{16,18},{18,... | collective-permute-start | bytes 1572872 | tf_op jit(solution)/shard_map/ppermute | solution.py:724
  97.2 12.9 %copy-start.32 = (s32[8]{0:T(128)S(1)}, s32[8]{0:T(128)}, u32[]{:S(2)}) copy-start(s32[8]{0:T(128)} %constant.101.clone) | copy-start | bytes 100
  99.6 15.2 %copy-start.31 = (bf16[64,512]{1,0:T(8,128)(2,1)S(1)}, bf16[64,512]{1,0:T(8,128)(2,1)}, u32[]{:S(2)}) copy-start(bf16[64,512]{1,0:T(8,128)(2,1)} %get-tuple-element.157) | copy-start | bytes 196612
  99.7 19.9 %collective-permute-start.17 = (bf16[64,4480]{1,0:T(8,128)(2,1)}, bf16[64,4480]{1,0:T(8,128)(2,1)S(1)}, u32[]{:S(2)}, u32[]{:S(2)}) collective-permute-start(bf16[64,4480]{1,0:T(8,128)(2,1)} %get-tuple-element.142), channel_id=1, source_target_pairs={{0,8},{2,10},{4,0},{6,2},{8,16},{10,18},{12,4},{14,6},{16,24},{18,... | collective-permute-start | bytes 1720328 | tf_op jit(solution)/shard_map/ppermute | solution.py:749
  101.2 18.4 %collective-permute-start.18 = (bf16[64,4480]{1,0:T(8,128)(2,1)}, bf16[64,4480]{1,0:T(8,128)(2,1)S(1)}, u32[]{:S(2)}, u32[]{:S(2)}) collective-permute-start(bf16[64,4480]{1,0:T(8,128)(2,1)} %get-tuple-element.143), channel_id=1, source_target_pairs={{0,4},{2,6},{4,12},{6,14},{8,0},{10,2},{12,20},{14,22},{16,8},{18,... | collective-permute-start | bytes 1720328 | tf_op jit(solution)/shard_map/ppermute | solution.py:749
  104.7 23.3 %all-to-all-start.3 = ((bf16[8,192,128]{2,1,0:T(8,128)(2,1)}), bf16[8,192,128]{2,1,0:T(8,128)(2,1)S(1)}, u32[]{:S(2)}, u32[]{:S(2)}) async-start(bf16[8,192,128]{2,1,0:T(8,128)(2,1)} %combine.1.refs_1_), calls=%async_computation.3 | async-start | bytes 786432 | tf_op jit(solution)/shard_map/all_to_all | solution.py:712
  114.7 10.6 %collective-permute-start.16 = (bf16[8,64,192]{2,1,0:T(8,128)(2,1)}, bf16[8,64,192]{2,1,0:T(8,128)(2,1)S(1)}, u32[]{:S(2)}, u32[]{:S(2)}) collective-permute-start(bf16[8,64,192]{2,1,0:T(8,128)(2,1)} %get-tuple-element.147), channel_id=1, source_target_pairs={{0,2},{2,0},{4,6},{6,4},{8,10},{10,8},{12,14},{14,12},{16,18},{18,... | collective-permute-start | bytes 589832 | tf_op jit(solution)/shard_map/ppermute | solution.py:715
  114.8 22.6 %collective-permute-start.22 = (bf16[64,512]{1,0:T(8,128)(2,1)S(1)}, bf16[64,512]{1,0:T(8,128)(2,1)S(1)}, u32[]{:S(2)}, u32[]{:S(2)}) collective-permute-start(bf16[64,512]{1,0:T(8,128)(2,1)S(1)} %copy-done.31), channel_id=1, source_target_pairs={{0,28},{2,30},{4,24},{6,26},{8,20},{10,22},{12,16},{14,18},{16,12}... | collective-permute-start | bytes 196616 | tf_op jit(solution)/shard_map/ppermute | solution.py:749
  123.2 13.6 %copy-start = (bf16[1312,1024]{1,0:T(8,128)(2,1)S(1)}, bf16[1312,1024]{1,0:T(8,128)(2,1)}, u32[]{:S(2)}) copy-start(bf16[1312,1024]{1,0:T(8,128)(2,1)} %refs_1_.3) | copy-start | bytes 8060932
  123.2 16.1 %collective-permute-start.21 = (bf16[64,4480]{1,0:T(8,128)(2,1)}, bf16[64,4480]{1,0:T(8,128)(2,1)}, u32[]{:S(2)}, u32[]{:S(2)}) collective-permute-start(bf16[64,4480]{1,0:T(8,128)(2,1)} %get-tuple-element.151), channel_id=1, source_target_pairs={{0,8},{2,10},{4,0},{6,2},{8,16},{10,18},{12,4},{14,6},{16,24},{18,... | collective-permute-start | bytes 1720328 | tf_op jit(solution)/shard_map/ppermute | solution.py:749
  123.3 19.6 %collective-permute-start.23 = (bf16[64,4480]{1,0:T(8,128)(2,1)}, bf16[64,4480]{1,0:T(8,128)(2,1)}, u32[]{:S(2)}, u32[]{:S(2)}) collective-permute-start(bf16[64,4480]{1,0:T(8,128)(2,1)} %get-tuple-element.152), channel_id=1, source_target_pairs={{0,4},{2,6},{4,12},{6,14},{8,0},{10,2},{12,20},{14,22},{16,8},{18,... | collective-permute-start | bytes 1720328 | tf_op jit(solution)/shard_map/ppermute | solution.py:749
  128.0 21.4 %all-to-all-start.4 = ((bf16[8,64,192]{2,1,0:T(8,128)(2,1)}), bf16[8,64,192]{2,1,0:T(8,128)(2,1)S(1)}, u32[]{:S(2)}, u32[]{:S(2)}) async-start(bf16[8,64,192]{2,1,0:T(8,128)(2,1)} %add_convert_fusion.1), calls=%async_computation.4 | async-start | bytes 524288 | tf_op jit(solution)/shard_map/all_to_all | solution.py:712
  131.7 5.1 %copy-start.15 = (bf16[128,1312]{1,0:T(8,128)(2,1)S(1)}, bf16[128,1312]{1,0:T(8,128)(2,1)}, u32[]{:S(2)}) copy-start(bf16[128,1312]{1,0:T(8,128)(2,1)} %get-tuple-element.154) | copy-start | bytes 1007620
  135.6 13.1 %copy-start.27 = (f32[1024]{0:T(1024)S(1)}, f32[1024]{0:T(1024)}, u32[]{:S(2)}) copy-start(f32[1024]{0:T(1024)} %param.12) | copy-start | bytes 12292
  135.6 13.1 %copy-start.28 = (f32[1024]{0:T(1024)S(1)}, f32[1024]{0:T(1024)}, u32[]{:S(2)}) copy-start(f32[1024]{0:T(1024)} %param.11) | copy-start | bytes 12292
  135.7 7.2 %collective-permute-start.20 = (bf16[128,1024]{1,0:T(8,128)(2,1)}, bf16[128,1024]{1,0:T(8,128)(2,1)}, u32[]{:S(2)}, u32[]{:S(2)}) collective-permute-start(bf16[128,1024]{1,0:T(8,128)(2,1)} %project_back.1.refs_2_), channel_id=1, source_target_pairs={{0,1},{1,0},{2,3},{3,2},{4,5},{5,4},{6,7},{7,6},{8,9},{9,8},{10,11... | collective-permute-start | bytes 786440 | tf_op jit(solution)/shard_map/ppermute | solution.py:727
  145.4 10.0 %copy-start.2 = (f32[128,1024]{1,0:T(8,128)S(1)}, f32[128,1024]{1,0:T(8,128)}, u32[]{:S(2)}) copy-start(f32[128,1024]{1,0:T(8,128)} %get-tuple-element.112.refs_0_) | copy-start | bytes 1572868
  145.4 12.8 %collective-permute-start.24 = (bf16[64,4480]{1,0:T(8,128)(2,1)}, bf16[64,4480]{1,0:T(8,128)(2,1)S(1)}, u32[]{:S(2)}, u32[]{:S(2)}) collective-permute-start(bf16[64,4480]{1,0:T(8,128)(2,1)} %get-tuple-element.161), channel_id=1, source_target_pairs={{0,8},{2,10},{4,0},{6,2},{8,16},{10,18},{12,4},{14,6},{16,24},{18,... | collective-permute-start | bytes 1720328 | tf_op jit(solution)/shard_map/ppermute | solution.py:749
  147.8 11.2 %collective-permute-start.25 = (bf16[64,4480]{1,0:T(8,128)(2,1)}, bf16[64,4480]{1,0:T(8,128)(2,1)S(1)}, u32[]{:S(2)}, u32[]{:S(2)}) collective-permute-start(bf16[64,4480]{1,0:T(8,128)(2,1)} %get-tuple-element.162), channel_id=1, source_target_pairs={{0,4},{2,6},{4,12},{6,14},{8,0},{10,2},{12,20},{14,22},{16,8},{18,... | collective-permute-start | bytes 1720328 | tf_op jit(solution)/shard_map/ppermute | solution.py:749
  147.8 7.5 %collective-permute-start.19 = (bf16[128,1024]{1,0:T(8,128)(2,1)S(1)}, bf16[128,1024]{1,0:T(8,128)(2,1)S(1)}, u32[]{:S(2)}, u32[]{:S(2)}) collective-permute-start(bf16[128,1024]{1,0:T(8,128)(2,1)S(1)} %convolution_convert_fusion), channel_id=1, source_target_pairs={{0,1},{1,0},{2,3},{3,2},{4,5},{5,4},{6,7},{7,6},{8,9},{9,8},{10,11... | collective-permute-start | bytes 786440 | tf_op jit(solution)/shard_map/ppermute | solution.py:727
  152.8 10.8 %copy-start.26 = (bf16[64,512]{1,0:T(8,128)(2,1)S(1)}, bf16[64,512]{1,0:T(8,128)(2,1)}, u32[]{:S(2)}) copy-start(bf16[64,512]{1,0:T(8,128)(2,1)} %get-tuple-element.169) | copy-start | bytes 196612
  162.6 3.8 %collective-permute-start.26 = (f32[2,64]{1,0:T(2,128)}, f32[2,64]{1,0:T(2,128)S(1)}, u32[]{:S(2)}, u32[]{:S(2)}) collective-permute-start(f32[2,64]{1,0:T(2,128)} %get-tuple-element.167), channel_id=1, source_target_pairs={{0,1},{1,0},{2,3},{3,2},{4,5},{5,4},{6,7},{7,6},{8,9},{9,8},{10,11... | collective-permute-start | bytes 1544 | tf_op jit(solution)/shard_map/ppermute | solution.py:727
  (17 other events, 23.7 us)

commit v6 on v5

--- a/solution.py
+++ b/solution.py
@@ -512,38 +512,56 @@
         ref[...] = total[r * ref.shape[0] : (r + 1) * ref.shape[0]]
 
 
-def out_weight(count, inner, pick, own, other, mid, mid_other):
+def out_weight(count, inner, pick, own, other, mid, mid_other, ring=()):
     rows, (width, model) = pick.shape[0], own.shape
     vmem, hbm = pl.BlockSpec(memory_space=pltpu.VMEM), pl.BlockSpec(memory_space=pl.ANY)
 
+    size = 5 + len(ring)
+    sent = len(ring) // 2
+
     def kernel(pick_ref, own_ref, other_ref, mid_ref, mid_other_ref, *refs):
-        outs, held, sems = refs[:count], refs[count : count + 5], refs[count + 5]
+        ring_refs, refs = refs[: len(ring)], refs[len(ring) :]
+        outs, sent_refs, refs = refs[:count], refs[count : count + sent], refs[count + sent :]
+        held, sems = refs[:size], refs[size]
         columns = pl.ds(model, inner)
         given = [pick_ref, own_ref, other_ref, mid_ref.at[:, columns], mid_other_ref.at[:, columns]]
+        given += ring_refs
         copies = [pltpu.make_async_copy(g, h, sems.at[i]) for i, (g, h) in enumerate(zip(given, held))]
         for copy in copies:
             copy.start()
-        for copy in copies:
+        for copy in copies[:5]:
             copy.wait()
-        out_weight_kernel(rows // count, *held, *outs)
+        out_weight_kernel(rows // count, *held[:5], *outs)
+        for copy in copies[5:]:
+            copy.wait()
+        for side in range(sent):
+            block, got, out = held[5 + 2 * side], held[6 + 2 * side], sent_refs[side]
+            wide, cut = block.shape[1], got.shape[0]
+            part = slice(0, cut) if side == 0 else slice(cut, None)
+            rest = slice(cut, None) if side == 0 else slice(0, cut)
+            out[part, :wide] = (block[part].astype(F32) + got[...].astype(F32)).astype(BF)
+            out[rest, :wide] = block[rest]
+            out[:, wide:] = outs[count // 2 - 1 + 2 * side][...]
 
     return pl.pallas_call(
         kernel,
-        in_specs=[hbm] * 5,
-        out_specs=[vmem] * count,
-        out_shape=[shaped((rows // count, inner), BF)] * count,
+        in_specs=[hbm] * size,
+        out_specs=[vmem] * (count + sent),
+        out_shape=[shaped((rows // count, inner), BF)] * count
+        + [shaped((b.shape[0], b.shape[1] + inner), BF) for b in ring[::2]],
         scratch_shapes=[
             pltpu.VMEM(pick.shape, BF),
             pltpu.VMEM(own.shape, BF),
             pltpu.VMEM(own.shape, BF),
             pltpu.VMEM((width, inner), BF),
             pltpu.VMEM((width, inner), BF),
-            pltpu.SemaphoreType.DMA((5,)),
+            *[pltpu.VMEM(v.shape, BF) for v in ring],
+            pltpu.SemaphoreType.DMA((size,)),
         ],
         compiler_params=pltpu.CompilerParams(vmem_limit_bytes=GRANT),
         cost_estimate=work(4 * rows * own.size, 8 * own.size),
         name="out_weight",
-    )(pick, own, other, mid, mid_other)
+    )(pick, own, other, mid, mid_other, *ring)
 
 
 def ring_add_kernel(count, *refs):
@@ -857,6 +875,9 @@
     terms = [grad_kv[0]]
     for step in range(1, 2 * copies):
         terms.append(shift_keys(grad_kv[step], -step))
+    carried = ()
+    if ringed:
+        carried = (mlp_rights[1], after(got_right, dq), mlp_lefts[1], got_left)
     parts_out = out_weight(
         chips if ringed else 1,
         inner,
@@ -865,6 +886,7 @@
         low_other,
         mid,
         mid_other,
+        carried,
     )
     if ringed:
 
@@ -879,7 +901,8 @@
             got_right, got_left = turn(sent[0], 1), turn(sent[1], -1)
             return sent
 
-        sent = ring_step(1, True, dq)
+        parts_out, sent = parts_out[:chips], parts_out[chips:]
+        got_right, got_left = turn(sent[0], 1), turn(sent[1], -1)
         terms[0] = after(terms[0], sent)
     grad_own = combine(dq, terms, cos_all, sin_all)
     grad_back = exchange(grad_own)

time: 169 us -> 167 us (0.988)
  Pallas kernels: 67 us -> 65.3 us
    pallas_call x14 -> x13, Pallas kernels: 57.3 us -> 55 us  [staged(): pl.pallas_call(kernel, in_specs=[pl.BlockSpec(memory_space=pltpu.SMEM)] *...]
  transfers between devices with their start and end apart: 32 -> 32, of which waited for: 12 -> 12; matrix products, arithmetic and copies ran while one was open for 7% -> 7% of each run, Pallas kernels for 36% -> 35%
where the time goes in v6:
time: 167 us; the launch traced here: 166 us
  Pallas kernels  65.3 us (39%)
  starting transfers between devices  54.8 us (33%)
  waiting for transfers between devices  23.6 us (14%)
  local copies, waits for them, and re-layouts  11 us (7%)
  other arithmetic  9.37 us (6%)
    pallas_call x13, Pallas kernels, staged(): pl.pallas_call(kernel, in_specs=[pl.BlockSpec(memory_space=pltpu.SMEM)] *...  55 us
    ppermute x16, starting transfers between devices, turn(): return lax.ppermute(values, 'ctx', pairs)  21.6 us
    all_to_all x3, starting transfers between devices, exchange(): return lax.all_to_all(values, 'ctx', 0, 0, axis_index_groups=head_groups)  16.4 us
    ppermute x16, waiting for transfers between devices, turn(): return lax.ppermute(values, 'ctx', pairs)  9.56 us
    all_to_all x2, starting transfers between devices, exchange_wide(): lax.all_to_all(values, ('ctx', 'tp'), 0, 0, axis_index_groups=wide_groups)  9.53 us
    all_to_all x3, waiting for transfers between devices, exchange(): return lax.all_to_all(values, 'ctx', 0, 0, axis_index_groups=head_groups)  8.49 us
    unnamed x66, local copies, waits for them, and re-layouts  8.04 us
    ppermute x5, starting transfers between devices, swap_tp(): return lax.ppermute(values, 'tp', [(0, 1), (1, 0)])  6.53 us
  transfers between devices with their start and end apart: 32, of which 12 were waited for; matrix products, arithmetic and copies ran while one was open for 7% of the time, Pallas kernels for 35%

profile of v6, /device:TPU:0, one launch (start us, length us, event | category | flops | bytes accessed | tf_op | source)
XLA Modules:
  0.0 165.8 jit_solution(950703751512752303)
XLA Ops:
  1.4 4.1 %project.1 = (bf16[8,192,128]{2,1,0:T(8,128)(2,1)}, bf16[128,1024]{1,0:T(8,128)(2,1)}) custom-call(bf16[128,1024]{1,0:T(8,128)(2,1)} %refs_0_.2, f32[1,1024]{1,0:T(1,128)} %bitcast.34, f32[32,128]{1,0:T(8,128)} %get-tuple-element.173.c_ref, f32[32,128]{1,0:T(8,128)} %get-tuple-element.172.s_ref, bf16[3,1024,512]{2,1,0:T(8,128)(2,1)} %bitcast.22), custom_call_target="tpu_custom_call" | custom-call | flops 402653184 | bytes 3145728 | tf_op jit(solution)/shard_map/project/pallas_call | solution.py:304
  5.5 7.3 %all-to-all-start = ((bf16[8,192,128]{2,1,0:T(8,128)(2,1)}), bf16[8,192,128]{2,1,0:T(8,128)(2,1)S(1)}, u32[]{:S(2)}, u32[]{:S(2)}) async-start(bf16[8,192,128]{2,1,0:T(8,128)(2,1)} %get-tuple-element.88), calls=%async_computation | async-start | bytes 786432 | tf_op jit(solution)/shard_map/all_to_all | solution.py:730
  12.8 1.6 collective-permute-start.5
  14.6 1.2 fusion.refs_0_.pick_ref
  15.8 1.2 multiply_sine_fusion
  17.0 7.5 %all-to-all-done.refs_0_ = bf16[8,192,128]{2,1,0:T(8,128)(2,1)S(1)} async-done(((bf16[8,192,128]{2,1,0:T(8,128)(2,1)}), bf16[8,192,128]{2,1,0:T(8,128)(2,1)S(1)}, u32[]{:S(2)}, u32[]{:S(2)}) %all-to-all-start) | async-done | bytes 393248 | tf_op jit(solution)/shard_map/all_to_all | solution.py:730
  25.4 1.1 collective-permute-start.2
  27.3 6.0 %attend.1 = (f32[8,64,128]{2,1,0:T(8,128)}, bf16[2,8,64,128]{3,2,1,0:T(8,128)(2,1)}, f32[8,1,128]{2,1,0:T(1,128)}) custom-call(bf16[8,192,128]{2,1,0:T(8,128)(2,1)} %copy-done.14, bf16[8,192,128]{2,1,0:T(8,128)(2,1)} %copy-done.29), custom_call_target="tpu_custom_call" | custom-call | flops 536870912 | bytes 786432 | tf_op jit(solution)/shard_map/attend/pallas_call | solution.py:50
  34.2 4.3 %all-to-all-start.1 = ((bf16[16,64,128]{2,1,0:T(8,128)(2,1)}), bf16[16,64,128]{2,1,0:T(8,128)(2,1)S(1)}, u32[]{:S(2)}, u32[]{:S(2)}) async-start(bf16[16,64,128]{2,1,0:T(8,128)(2,1)} %bitcast.30), calls=%async_computation.1 | async-start | bytes 524288 | tf_op jit(solution)/shard_map/all_to_all | solution.py:727
  38.5 1.9 %collective-permute-start.3 = (bf16[128,1024]{1,0:T(8,128)(2,1)}, bf16[128,1024]{1,0:T(8,128)(2,1)S(1)}, u32[]{:S(2)}, u32[]{:S(2)}) collective-permute-start(bf16[128,1024]{1,0:T(8,128)(2,1)} %collective-permute-done.1.refs_3_), channel_id=1, source_target_pairs={{0,8},{2,10},{4,0},{6,2},{8,16},{10,18},{12,4},{14,6},{16,24},{18,... | collective-permute-start | bytes 786440 | tf_op jit(solution)/shard_map/ppermute | solution.py:767
  40.6 1.3 constant_dynamic-slice_fusion
  41.9 1.0 copy.18.refs_3_
  42.9 3.8 %unit_back.1.refs_7_ = f32[128,1312]{1,0:T(8,128)} custom-call(bf16[128,1024]{1,0:T(8,128)(2,1)} %refs_1_.5, bf16[1312,1024]{1,0:T(8,128)(2,1)} %refs_1_.3), custom_call_target="tpu_custom_call" | custom-call | flops 343932928 | bytes 2686976 | tf_op jit(solution)/shard_map/unit_back/pallas_call | solution.py:50
  46.7 2.1 %collective-permute-done.3.refs_5_ = bf16[128,1024]{1,0:T(8,128)(2,1)S(1)} collective-permute-done((bf16[128,1024]{1,0:T(8,128)(2,1)}, bf16[128,1024]{1,0:T(8,128)(2,1)S(1)}, u32[]{:S(2)}, u32[]{:S(2)}) %collective-permute-start.3) | collective-permute-done | bytes 262176 | tf_op jit(solution)/shard_map/ppermute | solution.py:767
  48.8 1.8 %collective-permute-done.4.refs_6_ = bf16[128,1024]{1,0:T(8,128)(2,1)S(1)} collective-permute-done((bf16[128,1024]{1,0:T(8,128)(2,1)}, bf16[128,1024]{1,0:T(8,128)(2,1)S(1)}, u32[]{:S(2)}, u32[]{:S(2)}) %collective-permute-start.4) | collective-permute-done | bytes 262176 | tf_op jit(solution)/shard_map/ppermute | solution.py:767
  50.6 2.5 %collective-permute-start.6 = (bf16[128,1024]{1,0:T(8,128)(2,1)S(1)}, bf16[128,1024]{1,0:T(8,128)(2,1)S(1)}, u32[]{:S(2)}, u32[]{:S(2)}) collective-permute-start(bf16[128,1024]{1,0:T(8,128)(2,1)S(1)} %collective-permute-done.3.refs_5_), channel_id=1, source_target_pairs={{0,8},{2,10},{4,0},{6,2},{8,16},{10,18},{12,4},{14,6},{16,24},{18,... | collective-permute-start | bytes 786440 | tf_op jit(solution)/shard_map/ppermute | solution.py:767
  53.2 1.0 copy-done.8
  54.1 8.2 %middle_part.1 = (f32[128,1024]{1,0:T(8,128)}, bf16[128,5504]{1,0:T(8,128)(2,1)}, bf16[128,1312]{1,0:T(8,128)(2,1)}, bf16[128,1024]{1,0:T(8,128)(2,1)}, bf16[2,8,64,128]{3,2,1,0:T(8,128)(2,1)}) custom-call(s32[1]{0:T(128)} %bitcast.refs_0_, bf16[2,512,128]{2,1,0:T(8,128)(2,1)} %bitcast.27, bf16[128,1024]{1,0:T(8,128)(2,1)} %refs_0_.2, ...), custom_call_target="tpu_custom_call" | custom-call | flops 1912602624 | bytes 5373952 | tf_op jit(solution)/shard_map/middle_part/pallas_call | solution.py:50
  62.9 5.2 %all-to-all-start.2 = ((bf16[16,64,128]{2,1,0:T(8,128)(2,1)}), bf16[16,64,128]{2,1,0:T(8,128)(2,1)S(1)}, u32[]{:S(2)}, u32[]{:S(2)}) async-start(bf16[16,64,128]{2,1,0:T(8,128)(2,1)} %bitcast.28), calls=%async_computation.2 | async-start | bytes 524288 | tf_op jit(solution)/shard_map/all_to_all | solution.py:727
  68.2 2.0 %collective-permute-start.10 = (bf16[128,1024]{1,0:T(8,128)(2,1)}, bf16[128,1024]{1,0:T(8,128)(2,1)S(1)}, u32[]{:S(2)}, u32[]{:S(2)}) collective-permute-start(bf16[128,1024]{1,0:T(8,128)(2,1)} %get-tuple-element.125.refs_3_), channel_id=1, source_target_pairs={{0,1},{1,0},{2,3},{3,2},{4,5},{5,4},{6,7},{7,6},{8,9},{9,8},{10,11... | collective-permute-start | bytes 786440 | tf_op jit(solution)/shard_map/ppermute | solution.py:745
  70.9 5.9 %mlp_weight.1 = (bf16[64,3968]{1,0:T(8,128)(2,1)}, bf16[64,3968]{1,0:T(8,128)(2,1)}, bf16[64,3968]{1,0:T(8,128)(2,1)}, bf16[64,3968]{1,0:T(8,128)(2,1)}, bf16[32...) custom-call(bf16[512,1024]{1,0:T(8,128)(2,1)} %fusion.refs_0_.pick_r, ...), custom_call_target="tpu_custom_call" | custom-call | flops 1442840576 | bytes 9699328 | tf_op jit(solution)/shard_map/mlp_weight/pallas_call | solution.py:50
  76.8 1.5 collective-permute-start.13
  79.8 2.7 %middle_back.1 = (f32[128,1024]{1,0:T(8,128)}, bf16[128,1024]{1,0:T(8,128)(2,1)}) custom-call(f32[128,1024]{1,0:T(8,128)} %get-tuple-element.110.refs_0_, bf16[128,1024]{1,0:T(8,128)(2,1)} %refs_1_.5, f32[1,1024]{1,0:T(1,128)} %bitcast.32, bf16[128,1024]{1,0:T(8,128)(2,1)} %get-tuple-element.125.refs_3_, bf16[128,1024]{1,0:T(8,128)(2,1)} %copy-done.17), custom_call_target="tpu_custom_call" | custom-call | flops 2621440 | bytes 2097152 | tf_op jit(solution)/shard_map/middle_back/pallas_call | solution.py:50
  82.6 1.5 collective-permute-start.11
  85.4 8.0 %attend_back.1 = (bf16[8,64,128]{2,1,0:T(8,128)(2,1)}, f32[8,128,128]{2,1,0:T(8,128)}, f32[8,128,128]{2,1,0:T(8,128)}) custom-call(bf16[8,192,128]{2,1,0:T(8,128)(2,1)} %copy-done.14, bf16[8,192,128]{2,1,0:T(8,128)(2,1)} %copy-done.29, bf16[2,8,64,128]{3,2,1,0:T(8,128)(2,1)} %bitcast.29, f32[8,64,128]{2,1,0:T(8,128)} %get-tuple-element.129.refs_3_, ...), custom_call_target="tpu_custom_call" | custom-call | flops 1342177280 | bytes 1572864 | tf_op jit(solution)/shard_map/attend_back/pallas_call | solution.py:50
  94.3 3.6 %out_weight.1 = (bf16[64,512]{1,0:T(8,128)(2,1)}, bf16[64,512]{1,0:T(8,128)(2,1)}, bf16[64,512]{1,0:T(8,128)(2,1)}, bf16[64,512]{1,0:T(8,128)(2,1)}, bf16[64,512...) custom-call(bf16[512,1024]{1,0:T(8,128)(2,1)} %fusion.refs_0_.pick_r, ...), custom_call_target="tpu_custom_call" | custom-call | flops 268435456 | bytes 1048576 | tf_op jit(solution)/shard_map/out_weight/pallas_call | solution.py:546
  97.9 1.5 collective-permute-start.17
  100.8 2.2 %combine.1.refs_1_ = bf16[8,192,128]{2,1,0:T(8,128)(2,1)} custom-call(bf16[8,64,128]{2,1,0:T(8,128)(2,1)} %get-tuple-element.131.refs_0_, f32[8,128,128]{2,1,0:T(8,128)} %get-tuple-element.140.refs_1_, f32[8,128,128]{2,1,0:T(8,128)} %copy-done.13, f32[8,32,128]{2,1,0:T(8,128)} %get-tuple-element.169.refs_5_.refs_3_, ...), custom_call_target="tpu_custom_call" | custom-call | flops 65536 | bytes 1310720 | tf_op jit(solution)/shard_map/combine/pallas_call | solution.py:50
  103.0 5.4 %all-to-all-start.3 = ((bf16[8,192,128]{2,1,0:T(8,128)(2,1)}), bf16[8,192,128]{2,1,0:T(8,128)(2,1)S(1)}, u32[]{:S(2)}, u32[]{:S(2)}) async-start(bf16[8,192,128]{2,1,0:T(8,128)(2,1)} %combine.1.refs_1_), calls=%async_computation.3 | async-start | bytes 786432 | tf_op jit(solution)/shard_map/all_to_all | solution.py:730
  109.0 3.9 %head_weight.1 = (bf16[8,64,192]{2,1,0:T(8,128)(2,1)}, bf16[8,64,192]{2,1,0:T(8,128)(2,1)}) custom-call(s32[9]{0:T(128)} %pad_add_fusion.refs_0_, bf16[8,192,128]{2,1,0:T(8,128)(2,1)} %combine.1.refs_1_, bf16[128,1024]{1,0:T(8,128)(2,1)} %get-tuple-element.96.refs_2_, bf16[128,1024]{1,0:T(8,128)(2,1)} %collective-permute-done.1.refs_3_, ...), custom_call_target="tpu_custom_call" | custom-call | flops 402653184 | bytes 2097152 | tf_op jit(solution)/shard_map/head_weight/pallas_call | solution.py:50
  113.0 4.8 %collective-permute-start.22 = (bf16[64,512]{1,0:T(8,128)(2,1)S(1)}, bf16[64,512]{1,0:T(8,128)(2,1)S(1)}, u32[]{:S(2)}, u32[]{:S(2)}) collective-permute-start(bf16[64,512]{1,0:T(8,128)(2,1)S(1)} %copy-done.31), channel_id=1, source_target_pairs={{0,28},{2,30},{4,24},{6,26},{8,20},{10,22},{12,16},{14,18},{16,12}... | collective-permute-start | bytes 196616 | tf_op jit(solution)/shard_map/ppermute | solution.py:767
  118.9 2.6 %ring_add.2 = (bf16[64,4480]{1,0:T(8,128)(2,1)}, bf16[64,4480]{1,0:T(8,128)(2,1)}) custom-call(bf16[64,3968]{1,0:T(8,128)(2,1)} %get-tuple-element.117.refs_0_, bf16[64,4480]{1,0:T(8,128)(2,1)} %copy-done.11, bf16[64,512]{1,0:T(8,128)(2,1)} %get-tuple-element.145.refs_2_, bf16[64,3968]{1,0:T(8,128)(2,1)} %get-tuple-element.122.refs_3_, ...), custom_call_target="tpu_custom_call" | custom-call | flops 1146880 | bytes 3440640 | tf_op jit(solution)/shard_map/ring_add/pallas_call | solution.py:50
  121.5 2.0 %collective-permute-start.23 = (bf16[64,4480]{1,0:T(8,128)(2,1)}, bf16[64,4480]{1,0:T(8,128)(2,1)}, u32[]{:S(2)}, u32[]{:S(2)}) collective-permute-start(bf16[64,4480]{1,0:T(8,128)(2,1)} %get-tuple-element.148), channel_id=1, source_target_pairs={{0,4},{2,6},{4,12},{6,14},{8,0},{10,2},{12,20},{14,22},{16,8},{18,... | collective-permute-start | bytes 1720328 | tf_op jit(solution)/shard_map/ppermute | solution.py:767
  123.5 1.7 %add_convert_fusion.1 = bf16[8,64,192]{2,1,0:T(8,128)(2,1)} fusion(bf16[8,64,192]{2,1,0:T(8,128)(2,1)S(1)} %collective-permute-done.16, bf16[8,64,192]{2,1,0:T(8,128)(2,1)} %get-tuple-element.142), kind=kLoop, calls=%fused_computation.4 | loop fusion | flops 393216 | bytes 589824 | tf_op jit(solution)/shard_map/convert_element_type | solution.py:919
  125.2 1.0 all-to-all-done.3.refs_0_
  126.3 3.6 %all-to-all-start.4 = ((bf16[8,64,192]{2,1,0:T(8,128)(2,1)}), bf16[8,64,192]{2,1,0:T(8,128)(2,1)S(1)}, u32[]{:S(2)}, u32[]{:S(2)}) async-start(bf16[8,64,192]{2,1,0:T(8,128)(2,1)} %add_convert_fusion.1), calls=%async_computation.4 | async-start | bytes 524288 | tf_op jit(solution)/shard_map/all_to_all | solution.py:730
  129.9 3.9 %project_back.1.refs_2_ = bf16[128,1024]{1,0:T(8,128)(2,1)} custom-call(bf16[8,192,128]{2,1,0:T(8,128)(2,1)} %copy-done.3, bf16[3,1024,512]{2,1,0:T(8,128)(2,1)} %bitcast.23), custom_call_target="tpu_custom_call" | custom-call | flops 402653184 | bytes 3145728 | tf_op jit(solution)/shard_map/project_back/pallas_call | solution.py:50
  133.9 1.1 collective-permute-start.20
  135.6 1.9 %collective-permute-done.21.refs_1_ = bf16[64,4480]{1,0:T(8,128)(2,1)} collective-permute-done((bf16[64,4480]{1,0:T(8,128)(2,1)}, bf16[64,4480]{1,0:T(8,128)(2,1)}, u32[]{:S(2)}, u32[]{:S(2)}) %collective-permute-start.21) | collective-permute-done | bytes 573472 | tf_op jit(solution)/shard_map/ppermute | solution.py:767
  137.5 3.5 %collective-permute-done.20.refs_4_ = bf16[128,1024]{1,0:T(8,128)(2,1)} collective-permute-done((bf16[128,1024]{1,0:T(8,128)(2,1)}, bf16[128,1024]{1,0:T(8,128)(2,1)}, u32[]{:S(2)}, u32[]{:S(2)}) %collective-permute-start.20) | collective-permute-done | bytes 262176 | tf_op jit(solution)/shard_map/ppermute | solution.py:745
  141.0 2.6 %ring_add.3 = (bf16[64,4480]{1,0:T(8,128)(2,1)}, bf16[64,4480]{1,0:T(8,128)(2,1)}) custom-call(bf16[64,3968]{1,0:T(8,128)(2,1)} %get-tuple-element.116.refs_0_, bf16[64,4480]{1,0:T(8,128)(2,1)} %collective-permute-done.21.refs_1_, bf16[64,512]{1,0:T(8,128)(2,1)} %get-tuple-element.155.refs_2_, bf16[64,3968]{1,0:T(8,128)(2,1)} %get-tuple-element.123.refs_3_, ...), custom_call_target="tpu_custom_call" | custom-call | flops 1146880 | bytes 3440640 | tf_op jit(solution)/shard_map/ring_add/pallas_call | solution.py:50
  143.6 2.4 %collective-permute-start.24 = (bf16[64,4480]{1,0:T(8,128)(2,1)}, bf16[64,4480]{1,0:T(8,128)(2,1)S(1)}, u32[]{:S(2)}, u32[]{:S(2)}) collective-permute-start(bf16[64,4480]{1,0:T(8,128)(2,1)} %get-tuple-element.157), channel_id=1, source_target_pairs={{0,8},{2,10},{4,0},{6,2},{8,16},{10,18},{12,4},{14,6},{16,24},{18,... | collective-permute-start | bytes 1720328 | tf_op jit(solution)/shard_map/ppermute | solution.py:767
  148.4 2.6 %finish_qkv.1 = (f32[3,64,512]{2,1,0:T(8,128)}, f32[64,1]{1,0:T(8,128)}) custom-call(s32[1]{0:T(128)} %bitcast.11.first_ref, bf16[8,64,192]{2,1,0:T(8,128)(2,1)} %copy-done.5, bf16[3,1024,512]{2,1,0:T(8,128)(2,1)} %bitcast.24), custom_call_target="tpu_custom_call" | custom-call | flops 196608 | bytes 983040 | tf_op jit(solution)/shard_map/finish_qkv/pallas_call | solution.py:632
  151.1 2.6 %input_back.1 = f32[128,1024]{1,0:T(8,128)} custom-call(bf16[128,1024]{1,0:T(8,128)(2,1)} %refs_0_.2, f32[1,1024]{1,0:T(1,128)} %bitcast.35, bf16[128,1024]{1,0:T(8,128)(2,1)} %project_back.1.refs_2_, f32[128,1024]{1,0:T(8,128)} %get-tuple-element.151.refs_3_, bf16[128,1024]{1,0:T(8,128)(2,1)} %collective-permute-done.20.refs_4_), custom_call_target="tpu_custom_call" | custom-call | flops 2621440 | bytes 1835008 | tf_op jit(solution)/shard_map/input_back/pallas_call | solution.py:50
  154.4 2.0 %collective-permute-done.24.refs_1_ = bf16[64,4480]{1,0:T(8,128)(2,1)S(1)} collective-permute-done((bf16[64,4480]{1,0:T(8,128)(2,1)}, bf16[64,4480]{1,0:T(8,128)(2,1)S(1)}, u32[]{:S(2)}, u32[]{:S(2)}) %collective-permute-start.24) | collective-permute-done | bytes 573472 | tf_op jit(solution)/shard_map/ppermute | solution.py:767
  158.1 2.8 %finish_mlp.1 = (f32[64,2,1312]{2,1,0:T(2,128)}, f32[64,1312]{1,0:T(8,128)}, f32[2,64]{1,0:T(2,128)}) custom-call(bf16[64,3968]{1,0:T(8,128)(2,1)} %get-tuple-element.115.refs_0_, bf16[64,4480]{1,0:T(8,128)(2,1)} %copy-done.9, bf16[64,4480]{1,0:T(8,128)(2,1)} %copy-done.10, bf16[64,2624]{1,0:T(8,128)(2,1)} %copy.18.refs_3_, ...), custom_call_target="tpu_custom_call" | custom-call | flops 2031616 | bytes 3555328 | tf_op jit(solution)/shard_map/finish_mlp/pallas_call | solution.py:50
  161.8 1.6 add_bitcast_fusion
  163.4 1.2 collective-permute-done.26
  (121 shorter events, 19.3 us)
Async XLA Ops:
  0.6 12.2 %copy-start.7 = (bf16[512,1024]{1,0:T(8,128)(2,1)S(1)}, bf16[512,1024]{1,0:T(8,128)(2,1)}, u32[]{:S(2)}) copy-start(bf16[512,1024]{1,0:T(8,128)(2,1)} %refs_5_.1) | copy-start | bytes 3145732
  5.5 19.0 %all-to-all-start = ((bf16[8,192,128]{2,1,0:T(8,128)(2,1)}), bf16[8,192,128]{2,1,0:T(8,128)(2,1)S(1)}, u32[]{:S(2)}, u32[]{:S(2)}) async-start(bf16[8,192,128]{2,1,0:T(8,128)(2,1)} %get-tuple-element.88), calls=%async_computation | async-start | bytes 786432 | tf_op jit(solution)/shard_map/all_to_all | solution.py:730
  12.8 40.4 %collective-permute-start.5 = (bf16[512,1024]{1,0:T(8,128)(2,1)S(1)}, bf16[512,1024]{1,0:T(8,128)(2,1)S(1)}, u32[]{:S(2)}, u32[]{:S(2)}) collective-permute-start(bf16[512,1024]{1,0:T(8,128)(2,1)S(1)} %copy-done.7), channel_id=1, source_target_pairs={{0,1},{1,0},{2,3},{3,2},{4,5},{5,4},{6,7},{7,6},{8,9},{9,8},{10,11... | collective-permute-start | bytes 3145736 | tf_op jit(solution)/shard_map/ppermute | solution.py:745
  24.5 2.0 %collective-permute-start = (bf16[8,192,128]{2,1,0:T(8,128)(2,1)S(1)}, bf16[8,192,128]{2,1,0:T(8,128)(2,1)S(1)}, u32[]{:S(2)}, u32[]{:S(2)}) collective-permute-start(bf16[8,192,128]{2,1,0:T(8,128)(2,1)S(1)} %all-to-all-done.refs_0_), channel_id=1, source_target_pairs={{0,2},{2,0},{4,6},{6,4},{8,10},{10,8},{12,14},{14,12},{16,18},{18,... | collective-permute-start | bytes 1179656 | tf_op jit(solution)/shard_map/ppermute | solution.py:742
  24.5 9.0 %collective-permute-start.1 = (bf16[128,1024]{1,0:T(8,128)(2,1)}, bf16[128,1024]{1,0:T(8,128)(2,1)}, u32[]{:S(2)}, u32[]{:S(2)}) collective-permute-start(bf16[128,1024]{1,0:T(8,128)(2,1)} %get-tuple-element.96.refs_2_), channel_id=1, source_target_pairs={{0,8},{2,10},{4,0},{6,2},{8,16},{10,18},{12,4},{14,6},{16,24},{18,... | collective-permute-start | bytes 786440 | tf_op jit(solution)/shard_map/ppermute | solution.py:767
  25.4 8.8 %collective-permute-start.2 = (bf16[128,1024]{1,0:T(8,128)(2,1)}, bf16[128,1024]{1,0:T(8,128)(2,1)}, u32[]{:S(2)}, u32[]{:S(2)}) collective-permute-start(bf16[128,1024]{1,0:T(8,128)(2,1)} %get-tuple-element.96.refs_2_), channel_id=1, source_target_pairs={{0,4},{2,6},{4,12},{6,14},{8,0},{10,2},{12,20},{14,22},{16,8},{18,... | collective-permute-start | bytes 786440 | tf_op jit(solution)/shard_map/ppermute | solution.py:767
  34.2 16.5 %all-to-all-start.1 = ((bf16[16,64,128]{2,1,0:T(8,128)(2,1)}), bf16[16,64,128]{2,1,0:T(8,128)(2,1)S(1)}, u32[]{:S(2)}, u32[]{:S(2)}) async-start(bf16[16,64,128]{2,1,0:T(8,128)(2,1)} %bitcast.30), calls=%async_computation.1 | async-start | bytes 524288 | tf_op jit(solution)/shard_map/all_to_all | solution.py:727
  38.5 10.3 %collective-permute-start.3 = (bf16[128,1024]{1,0:T(8,128)(2,1)}, bf16[128,1024]{1,0:T(8,128)(2,1)S(1)}, u32[]{:S(2)}, u32[]{:S(2)}) collective-permute-start(bf16[128,1024]{1,0:T(8,128)(2,1)} %collective-permute-done.1.refs_3_), channel_id=1, source_target_pairs={{0,8},{2,10},{4,0},{6,2},{8,16},{10,18},{12,4},{14,6},{16,24},{18,... | collective-permute-start | bytes 786440 | tf_op jit(solution)/shard_map/ppermute | solution.py:767
  40.4 10.2 %collective-permute-start.4 = (bf16[128,1024]{1,0:T(8,128)(2,1)}, bf16[128,1024]{1,0:T(8,128)(2,1)S(1)}, u32[]{:S(2)}, u32[]{:S(2)}) collective-permute-start(bf16[128,1024]{1,0:T(8,128)(2,1)} %collective-permute-done.2.refs_4_), channel_id=1, source_target_pairs={{0,4},{2,6},{4,12},{6,14},{8,0},{10,2},{12,20},{14,22},{16,8},{18,... | collective-permute-start | bytes 786440 | tf_op jit(solution)/shard_map/ppermute | solution.py:767
  48.8 33.7 %copy-start.19 = (bf16[128,1024]{1,0:T(8,128)(2,1)}, bf16[128,1024]{1,0:T(8,128)(2,1)S(1)}, u32[]{:S(2)}) copy-start(bf16[128,1024]{1,0:T(8,128)(2,1)S(1)} %collective-permute-done.3.refs_5_) | copy-start | bytes 786436
  50.6 31.9 %copy-start.20 = (bf16[128,1024]{1,0:T(8,128)(2,1)}, bf16[128,1024]{1,0:T(8,128)(2,1)S(1)}, u32[]{:S(2)}) copy-start(bf16[128,1024]{1,0:T(8,128)(2,1)S(1)} %collective-permute-done.4.refs_6_) | copy-start | bytes 786436
  50.6 11.7 %collective-permute-start.6 = (bf16[128,1024]{1,0:T(8,128)(2,1)S(1)}, bf16[128,1024]{1,0:T(8,128)(2,1)S(1)}, u32[]{:S(2)}, u32[]{:S(2)}) collective-permute-start(bf16[128,1024]{1,0:T(8,128)(2,1)S(1)} %collective-permute-done.3.refs_5_), channel_id=1, source_target_pairs={{0,8},{2,10},{4,0},{6,2},{8,16},{10,18},{12,4},{14,6},{16,24},{18,... | collective-permute-start | bytes 786440 | tf_op jit(solution)/shard_map/ppermute | solution.py:767
  53.1 9.2 %collective-permute-start.7 = (bf16[128,1024]{1,0:T(8,128)(2,1)S(1)}, bf16[128,1024]{1,0:T(8,128)(2,1)S(1)}, u32[]{:S(2)}, u32[]{:S(2)}) collective-permute-start(bf16[128,1024]{1,0:T(8,128)(2,1)S(1)} %collective-permute-done.4.refs_6_), channel_id=1, source_target_pairs={{0,4},{2,6},{4,12},{6,14},{8,0},{10,2},{12,20},{14,22},{16,8},{18,... | collective-permute-start | bytes 786440 | tf_op jit(solution)/shard_map/ppermute | solution.py:767
  54.1 8.3 %copy-start.1 = (bf16[128,1024]{1,0:T(8,128)(2,1)S(1)}, bf16[128,1024]{1,0:T(8,128)(2,1)}, u32[]{:S(2)}) copy-start(bf16[128,1024]{1,0:T(8,128)(2,1)} %refs_1_.5) | copy-start | bytes 786436
  62.3 14.4 %copy-start.21 = (bf16[128,1024]{1,0:T(8,128)(2,1)}, bf16[128,1024]{1,0:T(8,128)(2,1)S(1)}, u32[]{:S(2)}) copy-start(bf16[128,1024]{1,0:T(8,128)(2,1)S(1)} %collective-permute-done.6.refs_7_) | copy-start | bytes 786436
  62.3 14.4 %copy-start.22 = (bf16[128,1024]{1,0:T(8,128)(2,1)}, bf16[128,1024]{1,0:T(8,128)(2,1)S(1)}, u32[]{:S(2)}) copy-start(bf16[128,1024]{1,0:T(8,128)(2,1)S(1)} %collective-permute-done.7.refs_8_) | copy-start | bytes 786436
  62.4 5.8 %collective-permute-start.9 = (bf16[128,5504]{1,0:T(8,128)(2,1)}, bf16[128,5504]{1,0:T(8,128)(2,1)S(1)}, u32[]{:S(2)}, u32[]{:S(2)}) collective-permute-start(bf16[128,5504]{1,0:T(8,128)(2,1)} %get-tuple-element.114.refs_3_.mid_ref), channel_id=1, source_target_pairs={{0,2},{2,0},{4,6},{6,4},{8,10},{10,8},{12,14},{14,12},{16,18},{18,... | collective-permute-start | bytes 4227080 | tf_op jit(solution)/shard_map/ppermute | solution.py:733
  62.4 7.7 %collective-permute-start.8 = (bf16[128,1024]{1,0:T(8,128)(2,1)S(1)}, bf16[128,1024]{1,0:T(8,128)(2,1)S(1)}, u32[]{:S(2)}, u32[]{:S(2)}) collective-permute-start(bf16[128,1024]{1,0:T(8,128)(2,1)S(1)} %copy-done.1), channel_id=1, source_target_pairs={{0,2},{2,0},{4,6},{6,4},{8,10},{10,8},{12,14},{14,12},{16,18},{18,... | collective-permute-start | bytes 786440 | tf_op jit(solution)/shard_map/ppermute | solution.py:733
  62.9 21.7 %all-to-all-start.2 = ((bf16[16,64,128]{2,1,0:T(8,128)(2,1)}), bf16[16,64,128]{2,1,0:T(8,128)(2,1)S(1)}, u32[]{:S(2)}, u32[]{:S(2)}) async-start(bf16[16,64,128]{2,1,0:T(8,128)(2,1)} %bitcast.28), calls=%async_computation.2 | async-start | bytes 524288 | tf_op jit(solution)/shard_map/all_to_all | solution.py:727
  68.2 10.9 %collective-permute-start.10 = (bf16[128,1024]{1,0:T(8,128)(2,1)}, bf16[128,1024]{1,0:T(8,128)(2,1)S(1)}, u32[]{:S(2)}, u32[]{:S(2)}) collective-permute-start(bf16[128,1024]{1,0:T(8,128)(2,1)} %get-tuple-element.125.refs_3_), channel_id=1, source_target_pairs={{0,1},{1,0},{2,3},{3,2},{4,5},{5,4},{6,7},{7,6},{8,9},{9,8},{10,11... | collective-permute-start | bytes 786440 | tf_op jit(solution)/shard_map/ppermute | solution.py:745
  76.8 16.7 %collective-permute-start.13 = (bf16[128,1024]{1,0:T(8,128)(2,1)S(1)}, bf16[128,1024]{1,0:T(8,128)(2,1)S(1)}, u32[]{:S(2)}, u32[]{:S(2)}) collective-permute-start(bf16[128,1024]{1,0:T(8,128)(2,1)S(1)} %collective-permute-done.6.refs_7_), channel_id=1, source_target_pairs={{0,8},{2,10},{4,0},{6,2},{8,16},{10,18},{12,4},{14,6},{16,24},{18,... | collective-permute-start | bytes 786440 | tf_op jit(solution)/shard_map/ppermute | solution.py:767
  82.5 10.9 %collective-permute-start.14 = (bf16[128,1024]{1,0:T(8,128)(2,1)}, bf16[128,1024]{1,0:T(8,128)(2,1)S(1)}, u32[]{:S(2)}, u32[]{:S(2)}) collective-permute-start(bf16[128,1024]{1,0:T(8,128)(2,1)} %get-tuple-element.136.own_ref), channel_id=1, source_target_pairs={{0,2},{2,0},{4,6},{6,4},{8,10},{10,8},{12,14},{14,12},{16,18},{18,... | collective-permute-start | bytes 786440 | tf_op jit(solution)/shard_map/ppermute | solution.py:733
  82.6 10.8 %collective-permute-start.11 = (bf16[32,3968]{1,0:T(8,128)(2,1)}, bf16[32,3968]{1,0:T(8,128)(2,1)S(1)}, u32[]{:S(2)}, u32[]{:S(2)}) collective-permute-start(bf16[32,3968]{1,0:T(8,128)(2,1)} %get-tuple-element.119), channel_id=1, source_target_pairs={{0,8},{2,10},{4,0},{6,2},{8,16},{10,18},{12,4},{14,6},{16,24},{18,... | collective-permute-start | bytes 761864 | tf_op jit(solution)/shard_map/ppermute | solution.py:767
  84.1 9.3 %collective-permute-start.12 = (bf16[32,3968]{1,0:T(8,128)(2,1)}, bf16[32,3968]{1,0:T(8,128)(2,1)S(1)}, u32[]{:S(2)}, u32[]{:S(2)}) collective-permute-start(bf16[32,3968]{1,0:T(8,128)(2,1)} %get-tuple-element.120), channel_id=1, source_target_pairs={{0,4},{2,6},{4,12},{6,14},{8,0},{10,2},{12,20},{14,22},{16,8},{18,... | collective-permute-start | bytes 761864 | tf_op jit(solution)/shard_map/ppermute | solution.py:767
  93.5 15.6 %copy-start.23 = (bf16[128,1024]{1,0:T(8,128)(2,1)}, bf16[128,1024]{1,0:T(8,128)(2,1)S(1)}, u32[]{:S(2)}) copy-start(bf16[128,1024]{1,0:T(8,128)(2,1)S(1)} %collective-permute-done.13.refs_9_) | copy-start | bytes 786436
  93.5 6.5 %collective-permute-start.15 = (f32[8,128,128]{2,1,0:T(8,128)}, f32[8,128,128]{2,1,0:T(8,128)S(1)}, u32[]{:S(2)}, u32[]{:S(2)}) collective-permute-start(f32[8,128,128]{2,1,0:T(8,128)} %get-tuple-element.141), channel_id=1, source_target_pairs={{0,2},{2,0},{4,6},{6,4},{8,10},{10,8},{12,14},{14,12},{16,18},{18,... | collective-permute-start | bytes 1572872 | tf_op jit(solution)/shard_map/ppermute | solution.py:742
  94.3 14.1 %copy-start.32 = (s32[8]{0:T(128)S(1)}, s32[8]{0:T(128)}, u32[]{:S(2)}) copy-start(s32[8]{0:T(128)} %constant.101.clone) | copy-start | bytes 100
  97.9 15.2 %copy-start.31 = (bf16[64,512]{1,0:T(8,128)(2,1)S(1)}, bf16[64,512]{1,0:T(8,128)(2,1)}, u32[]{:S(2)}) copy-start(bf16[64,512]{1,0:T(8,128)(2,1)} %get-tuple-element.153) | copy-start | bytes 196612
  97.9 19.9 %collective-permute-start.17 = (bf16[64,4480]{1,0:T(8,128)(2,1)}, bf16[64,4480]{1,0:T(8,128)(2,1)S(1)}, u32[]{:S(2)}, u32[]{:S(2)}) collective-permute-start(bf16[64,4480]{1,0:T(8,128)(2,1)} %get-tuple-element.138), channel_id=1, source_target_pairs={{0,8},{2,10},{4,0},{6,2},{8,16},{10,18},{12,4},{14,6},{16,24},{18,... | collective-permute-start | bytes 1720328 | tf_op jit(solution)/shard_map/ppermute | solution.py:767
  99.4 18.4 %collective-permute-start.18 = (bf16[64,4480]{1,0:T(8,128)(2,1)}, bf16[64,4480]{1,0:T(8,128)(2,1)S(1)}, u32[]{:S(2)}, u32[]{:S(2)}) collective-permute-start(bf16[64,4480]{1,0:T(8,128)(2,1)} %get-tuple-element.139), channel_id=1, source_target_pairs={{0,4},{2,6},{4,12},{6,14},{8,0},{10,2},{12,20},{14,22},{16,8},{18,... | collective-permute-start | bytes 1720328 | tf_op jit(solution)/shard_map/ppermute | solution.py:767
  103.0 23.3 %all-to-all-start.3 = ((bf16[8,192,128]{2,1,0:T(8,128)(2,1)}), bf16[8,192,128]{2,1,0:T(8,128)(2,1)S(1)}, u32[]{:S(2)}, u32[]{:S(2)}) async-start(bf16[8,192,128]{2,1,0:T(8,128)(2,1)} %combine.1.refs_1_), calls=%async_computation.3 | async-start | bytes 786432 | tf_op jit(solution)/shard_map/all_to_all | solution.py:730
  113.0 10.6 %collective-permute-start.16 = (bf16[8,64,192]{2,1,0:T(8,128)(2,1)}, bf16[8,64,192]{2,1,0:T(8,128)(2,1)S(1)}, u32[]{:S(2)}, u32[]{:S(2)}) collective-permute-start(bf16[8,64,192]{2,1,0:T(8,128)(2,1)} %get-tuple-element.143), channel_id=1, source_target_pairs={{0,2},{2,0},{4,6},{6,4},{8,10},{10,8},{12,14},{14,12},{16,18},{18,... | collective-permute-start | bytes 589832 | tf_op jit(solution)/shard_map/ppermute | solution.py:733
  113.0 22.6 %collective-permute-start.22 = (bf16[64,512]{1,0:T(8,128)(2,1)S(1)}, bf16[64,512]{1,0:T(8,128)(2,1)S(1)}, u32[]{:S(2)}, u32[]{:S(2)}) collective-permute-start(bf16[64,512]{1,0:T(8,128)(2,1)S(1)} %copy-done.31), channel_id=1, source_target_pairs={{0,28},{2,30},{4,24},{6,26},{8,20},{10,22},{12,16},{14,18},{16,12}... | collective-permute-start | bytes 196616 | tf_op jit(solution)/shard_map/ppermute | solution.py:767
  121.4 13.6 %copy-start = (bf16[1312,1024]{1,0:T(8,128)(2,1)S(1)}, bf16[1312,1024]{1,0:T(8,128)(2,1)}, u32[]{:S(2)}) copy-start(bf16[1312,1024]{1,0:T(8,128)(2,1)} %refs_1_.3) | copy-start | bytes 8060932
  121.4 16.1 %collective-permute-start.21 = (bf16[64,4480]{1,0:T(8,128)(2,1)}, bf16[64,4480]{1,0:T(8,128)(2,1)}, u32[]{:S(2)}, u32[]{:S(2)}) collective-permute-start(bf16[64,4480]{1,0:T(8,128)(2,1)} %get-tuple-element.147), channel_id=1, source_target_pairs={{0,8},{2,10},{4,0},{6,2},{8,16},{10,18},{12,4},{14,6},{16,24},{18,... | collective-permute-start | bytes 1720328 | tf_op jit(solution)/shard_map/ppermute | solution.py:767
  121.5 19.5 %collective-permute-start.23 = (bf16[64,4480]{1,0:T(8,128)(2,1)}, bf16[64,4480]{1,0:T(8,128)(2,1)}, u32[]{:S(2)}, u32[]{:S(2)}) collective-permute-start(bf16[64,4480]{1,0:T(8,128)(2,1)} %get-tuple-element.148), channel_id=1, source_target_pairs={{0,4},{2,6},{4,12},{6,14},{8,0},{10,2},{12,20},{14,22},{16,8},{18,... | collective-permute-start | bytes 1720328 | tf_op jit(solution)/shard_map/ppermute | solution.py:767
  126.3 3.6 %copy-start.3 = (bf16[8,192,128]{2,1,0:T(8,128)(2,1)}, bf16[8,192,128]{2,1,0:T(8,128)(2,1)S(1)}, u32[]{:S(2)}) copy-start(bf16[8,192,128]{2,1,0:T(8,128)(2,1)S(1)} %all-to-all-done.3.refs_0_) | copy-start | bytes 1179652
  126.3 21.4 %all-to-all-start.4 = ((bf16[8,64,192]{2,1,0:T(8,128)(2,1)}), bf16[8,64,192]{2,1,0:T(8,128)(2,1)S(1)}, u32[]{:S(2)}, u32[]{:S(2)}) async-start(bf16[8,64,192]{2,1,0:T(8,128)(2,1)} %add_convert_fusion.1), calls=%async_computation.4 | async-start | bytes 524288 | tf_op jit(solution)/shard_map/all_to_all | solution.py:730
  129.9 5.1 %copy-start.15 = (bf16[128,1312]{1,0:T(8,128)(2,1)S(1)}, bf16[128,1312]{1,0:T(8,128)(2,1)}, u32[]{:S(2)}) copy-start(bf16[128,1312]{1,0:T(8,128)(2,1)} %get-tuple-element.150) | copy-start | bytes 1007620
  133.9 13.2 %copy-start.27 = (f32[1024]{0:T(1024)S(1)}, f32[1024]{0:T(1024)}, u32[]{:S(2)}) copy-start(f32[1024]{0:T(1024)} %param.12) | copy-start | bytes 12292
  133.9 13.1 %copy-start.28 = (f32[1024]{0:T(1024)S(1)}, f32[1024]{0:T(1024)}, u32[]{:S(2)}) copy-start(f32[1024]{0:T(1024)} %param.11) | copy-start | bytes 12292
  133.9 7.2 %collective-permute-start.20 = (bf16[128,1024]{1,0:T(8,128)(2,1)}, bf16[128,1024]{1,0:T(8,128)(2,1)}, u32[]{:S(2)}, u32[]{:S(2)}) collective-permute-start(bf16[128,1024]{1,0:T(8,128)(2,1)} %project_back.1.refs_2_), channel_id=1, source_target_pairs={{0,1},{1,0},{2,3},{3,2},{4,5},{5,4},{6,7},{7,6},{8,9},{9,8},{10,11... | collective-permute-start | bytes 786440 | tf_op jit(solution)/shard_map/ppermute | solution.py:745
  143.6 10.0 %copy-start.2 = (f32[128,1024]{1,0:T(8,128)S(1)}, f32[128,1024]{1,0:T(8,128)}, u32[]{:S(2)}) copy-start(f32[128,1024]{1,0:T(8,128)} %get-tuple-element.110.refs_0_) | copy-start | bytes 1572868
  143.6 12.8 %collective-permute-start.24 = (bf16[64,4480]{1,0:T(8,128)(2,1)}, bf16[64,4480]{1,0:T(8,128)(2,1)S(1)}, u32[]{:S(2)}, u32[]{:S(2)}) collective-permute-start(bf16[64,4480]{1,0:T(8,128)(2,1)} %get-tuple-element.157), channel_id=1, source_target_pairs={{0,8},{2,10},{4,0},{6,2},{8,16},{10,18},{12,4},{14,6},{16,24},{18,... | collective-permute-start | bytes 1720328 | tf_op jit(solution)/shard_map/ppermute | solution.py:767
  146.1 11.2 %collective-permute-start.25 = (bf16[64,4480]{1,0:T(8,128)(2,1)}, bf16[64,4480]{1,0:T(8,128)(2,1)S(1)}, u32[]{:S(2)}, u32[]{:S(2)}) collective-permute-start(bf16[64,4480]{1,0:T(8,128)(2,1)} %get-tuple-element.158), channel_id=1, source_target_pairs={{0,4},{2,6},{4,12},{6,14},{8,0},{10,2},{12,20},{14,22},{16,8},{18,... | collective-permute-start | bytes 1720328 | tf_op jit(solution)/shard_map/ppermute | solution.py:767
  146.1 7.5 %collective-permute-start.19 = (bf16[128,1024]{1,0:T(8,128)(2,1)S(1)}, bf16[128,1024]{1,0:T(8,128)(2,1)S(1)}, u32[]{:S(2)}, u32[]{:S(2)}) collective-permute-start(bf16[128,1024]{1,0:T(8,128)(2,1)S(1)} %convolution_convert_fusion), channel_id=1, source_target_pairs={{0,1},{1,0},{2,3},{3,2},{4,5},{5,4},{6,7},{7,6},{8,9},{9,8},{10,11... | collective-permute-start | bytes 786440 | tf_op jit(solution)/shard_map/ppermute | solution.py:745
  151.0 10.8 %copy-start.26 = (bf16[64,512]{1,0:T(8,128)(2,1)S(1)}, bf16[64,512]{1,0:T(8,128)(2,1)}, u32[]{:S(2)}) copy-start(bf16[64,512]{1,0:T(8,128)(2,1)} %get-tuple-element.165) | copy-start | bytes 196612
  160.9 3.7 %collective-permute-start.26 = (f32[2,64]{1,0:T(2,128)}, f32[2,64]{1,0:T(2,128)S(1)}, u32[]{:S(2)}, u32[]{:S(2)}) collective-permute-start(f32[2,64]{1,0:T(2,128)} %get-tuple-element.163), channel_id=1, source_target_pairs={{0,1},{1,0},{2,3},{3,2},{4,5},{5,4},{6,7},{7,6},{8,9},{9,8},{10,11... | collective-permute-start | bytes 1544 | tf_op jit(solution)/shard_map/ppermute | solution.py:745
  (17 other events, 17.8 us)
